TPU v7x, 32 devices: a whole 2x2x4 slice. The times are simulated.
32 devices in a mesh: dp: 8 (over z, x), mp: 4 (over y, core).
Axes of the slice: x: 2, y: 2, z: 4, core: 2. Of those that a mesh axis runs over, the one named last changes fastest.
Arguments:
- hidden: bfloat16 [128, 4096], P('dp'), may hold values from -6 to 6
- wq_direct: bfloat16 [4096, 2048], P(None, 'mp'), may hold values from -0.09375 to 0.09375
- wkv_direct: bfloat16 [2, 4096, 2048], P(None, None, 'mp'), may hold values from -0.09375 to 0.09375
- wo_direct: bfloat16 [2048, 4096], P(None, 'mp'), may hold values from -0.125 to 0.125
- kv_cache: bfloat16 [2, 128, 32, 2048], P(None, 'dp', None, 'mp'), may hold values from -6 to 6
- parent: int32 [128], P('dp'), may hold values from 0 to 15
- lengths: int32 [128], P('dp'), may hold values from 1 to 32
- cand_embed: bfloat16 [128, 32, 4096], P('dp', None, 'mp'), may hold values from -6 to 6
- source: bfloat16 [8, 8, 4096], P('dp', None, 'mp'), may hold values from -6 to 6
- enc_qkv: bfloat16 [3, 4096, 2048], P(None, 'dp', 'mp'), may hold values from -0.09375 to 0.09375
- enc_out: bfloat16 [2048, 4096], P('dp', 'mp'), may hold values from -0.125 to 0.125
- cross_q: bfloat16 [4096, 2048], P('dp', 'mp'), may hold values from -0.09375 to 0.09375
- cross_kv: bfloat16 [2, 4096, 2048], P(None, 'dp', 'mp'), may hold values from -0.09375 to 0.09375
- cross_out: bfloat16 [2048, 4096], P('dp', 'mp'), may hold values from -0.125 to 0.125
- w_direct: bfloat16 [4096], P('mp'), may hold values from -0.09375 to 0.09375
- w_channel: bfloat16 [4096], P('mp'), may hold values from -0.09375 to 0.09375
- target_shard: int32 [128], P('dp'), may hold values from 0 to 7, as said below
Outputs:
- direct_state: bfloat16 [128, 4096], P('dp', 'mp')
- rerank_score: float32 [128], P('dp')
- channel_score: float32 [128], P('dp')
Inputs may be any that keep to these rules, and one draw needn't show every extreme that they name: `target_shard`: every shard receives exactly one candidate of each beam index; a device sends exactly 2 of its candidates to each shard that it sends to.
All inputs are finite; a program needn't handle non-finite values.
Results may differ from a plain program's by a relative error of at most 0.0075.
Values may be sent and summed in bfloat16 or wider, within the bound.
No kernel may reach another device: no remote copies, remote signals or barrier semaphores. Data moves between devices by JAX's collectives and lax.ppermute only.
A program may use at most 128 MiB of HBM per device.

v0:
```python
import math

import jax
import jax.numpy as jnp
from jax import lax
from jax.sharding import PartitionSpec as P

D = 4096
HD = 64


EPSILON = 1e-06


def attend(queries, keys, values, valid):
    group_n, query_n, columns = queries.shape
    key_n = keys.shape[1]
    head_n = columns // HD
    query_heads = queries.reshape(group_n, query_n, head_n, HD)
    key_heads = keys.reshape(group_n, key_n, head_n, HD)
    value_heads = values.reshape(group_n, key_n, head_n, HD)
    scores = jnp.einsum(
        "bqhd,bkhd->bhqk", query_heads, key_heads, preferred_element_type=jnp.float32
    ) / math.sqrt(HD)
    scores = jnp.where(valid[:, None, None, :], scores, -1e30)
    weights = jax.nn.softmax(scores, axis=-1).astype(jnp.bfloat16)
    context = jnp.einsum(
        "bhqk,bkhd->bqhd", weights, value_heads, preferred_element_type=jnp.float32
    )
    return context.astype(jnp.bfloat16).reshape(group_n, query_n, columns)


def project(inputs, matrices):
    segment = lax.all_gather(inputs, "mp", axis=1, tiled=True)
    return tuple(
        (jnp.dot(segment, matrix, preferred_element_type=jnp.float32) for matrix in matrices)
    )


def row_sums(parts):
    return lax.psum(parts, "mp")


def shards(
    hidden,
    wq_direct,
    wkv_direct,
    wo_direct,
    kv_cache,
    parent,
    lengths,
    cand_embed,
    source,
    enc_qkv,
    enc_out,
    cross_q,
    cross_kv,
    cross_out,
    w_direct,
    w_channel,
    target_shard,
):
    enc_full, out_full, query_full, memory_full, cross_full = (
        lax.all_gather(enc_qkv, "dp", axis=1, tiled=True),
        lax.all_gather(enc_out, "dp", axis=0, tiled=True),
        lax.all_gather(cross_q, "dp", axis=0, tiled=True),
        lax.all_gather(cross_kv, "dp", axis=1, tiled=True),
        lax.all_gather(cross_out, "dp", axis=0, tiled=True),
    )
    beam_n = hidden.shape[0]
    local_width = wo_direct.shape[1]
    cache_len = kv_cache.shape[2]
    beam_index = jnp.arange(beam_n, dtype=jnp.int32)
    positions = jnp.arange(cache_len, dtype=jnp.int32)
    own_start = lax.axis_index("mp") * local_width
    hidden_share = lax.dynamic_slice_in_dim(hidden, own_start, local_width, 1).astype(jnp.float32)
    query_new = jnp.dot(hidden, wq_direct, preferred_element_type=jnp.float32).astype(jnp.bfloat16)
    key_new = jnp.dot(hidden, wkv_direct[0], preferred_element_type=jnp.float32).astype(
        jnp.bfloat16
    )
    value_new = jnp.dot(hidden, wkv_direct[1], preferred_element_type=jnp.float32).astype(
        jnp.bfloat16
    )
    all_keys = jnp.concatenate([kv_cache[0][parent], key_new[:, None]], axis=1)
    all_values = jnp.concatenate([kv_cache[1][parent], value_new[:, None]], axis=1)
    cache_valid = jnp.concatenate(
        [positions[None, :] < lengths[:, None], jnp.ones((beam_n, 1), dtype=bool)], axis=1
    )
    context = attend(query_new[:, None], all_keys, all_values, cache_valid)[:, 0]
    (update,) = project(context, (wo_direct,))
    new_state = hidden_share + update
    squares, direct_dot = row_sums(
        (
            jnp.sum(new_state * new_state, axis=1),
            jnp.sum(new_state * w_direct.astype(jnp.float32), axis=1),
        )
    )
    direct_score = direct_dot / jnp.sqrt(squares / D + EPSILON)
    peer_count = lax.axis_size("dp")
    per_peer = max(1, beam_n // peer_count)
    slots_total = peer_count * per_peer
    same_shard = target_shard[:, None] == target_shard[None, :]
    earlier = beam_index[None, :] < beam_index[:, None]
    rank_within = jnp.sum(same_shard & earlier, axis=1)
    send_slot = target_shard * per_peer + rank_within
    tokens = cand_embed[parent]
    own_source = source[0]
    src_len = own_source.shape[0]
    send_tokens = (
        jnp.zeros((slots_total,) + tokens.shape[1:], jnp.bfloat16).at[send_slot].set(tokens)
    )
    send_source = (
        jnp.zeros((slots_total, src_len, local_width), jnp.bfloat16)
        .at[send_slot]
        .set(jnp.broadcast_to(own_source[None], (beam_n, src_len, local_width)))
    )
    labels = jnp.stack([beam_index, lengths], axis=1).astype(jnp.bfloat16)
    send_labels = jnp.full((slots_total, 2), -1.0, jnp.bfloat16).at[send_slot].set(labels)
    (owner_query,) = project(own_source, (query_full,))
    owner_query = owner_query.astype(jnp.bfloat16)
    send_query = (
        jnp.zeros((slots_total, src_len, owner_query.shape[1]), jnp.bfloat16)
        .at[send_slot]
        .set(jnp.broadcast_to(owner_query[None], (beam_n,) + owner_query.shape))
    )
    got_tokens, got_source, got_labels, got_query = (
        lax.all_to_all(send_tokens, "dp", split_axis=0, concat_axis=0, tiled=True),
        lax.all_to_all(send_source, "dp", split_axis=0, concat_axis=0, tiled=True),
        lax.all_to_all(send_labels, "dp", split_axis=0, concat_axis=0, tiled=True),
        lax.all_to_all(send_query, "dp", split_axis=0, concat_axis=0, tiled=True),
    )
    beam_match = got_labels[:, 0].astype(jnp.int32)[None, :] == beam_index[:, None]
    arrival = jnp.argmax(beam_match, axis=1)
    cand_tokens = got_tokens[arrival]
    cand_source = got_source[arrival]
    cand_len = got_labels[arrival, 1].astype(jnp.int32)
    token_rows = cand_tokens.reshape(beam_n * cache_len, local_width)
    enc_queries, enc_keys, enc_values = project(token_rows, (enc_full[0], enc_full[1], enc_full[2]))
    enc_queries = enc_queries.astype(jnp.bfloat16).reshape(beam_n, cache_len, -1)
    enc_keys = enc_keys.astype(jnp.bfloat16).reshape(beam_n, cache_len, -1)
    enc_values = enc_values.astype(jnp.bfloat16).reshape(beam_n, cache_len, -1)
    key_valid = positions[None, :] < cand_len[:, None]
    enc_context = attend(enc_queries, enc_keys, enc_values, key_valid).reshape(
        beam_n * cache_len, -1
    )
    (enc_update,) = project(enc_context, (out_full,))
    summed = token_rows.astype(jnp.float32) + enc_update
    (enc_squares,) = row_sums((jnp.sum(summed * summed, axis=1),))
    memory = (summed / jnp.sqrt(enc_squares / D + EPSILON)[:, None]).astype(jnp.bfloat16)
    cross_keys, cross_values = project(memory, (memory_full[0], memory_full[1]))
    cross_keys = cross_keys.astype(jnp.bfloat16).reshape(beam_n, cache_len, -1)
    cross_values = cross_values.astype(jnp.bfloat16).reshape(beam_n, cache_len, -1)
    source_rows = cand_source.reshape(beam_n * src_len, local_width)
    cross_queries = got_query[arrival]
    cross_context = attend(cross_queries, cross_keys, cross_values, key_valid).reshape(
        beam_n * src_len, -1
    )
    (cross_update,) = project(cross_context, (cross_full,))
    decoded = source_rows.astype(jnp.float32) + cross_update
    dec_squares, dec_dot = row_sums(
        (
            jnp.sum(decoded * decoded, axis=1),
            jnp.sum(decoded * w_channel.astype(jnp.float32), axis=1),
        )
    )
    position_score = (dec_dot / jnp.sqrt(dec_squares / D + EPSILON)).reshape(beam_n, src_len)
    channel_score = jnp.mean(position_score, axis=1)
    send_back = jnp.zeros((slots_total,), jnp.float32).at[arrival].set(channel_score)
    returned = lax.all_to_all(send_back, "dp", split_axis=0, concat_axis=0, tiled=True)
    rerank_score = direct_score + returned[send_slot]
    return (new_state.astype(jnp.bfloat16), rerank_score, channel_score)


def solution(mesh):
    in_specs = (
        P("dp", None),
        P(None, "mp"),
        P(None, None, "mp"),
        P(None, "mp"),
        P(None, "dp", None, "mp"),
        P("dp"),
        P("dp"),
        P("dp", None, "mp"),
        P("dp", None, "mp"),
        P(None, "dp", "mp"),
        P("dp", "mp"),
        P("dp", "mp"),
        P(None, "dp", "mp"),
        P("dp", "mp"),
        P("mp"),
        P("mp"),
        P("dp"),
    )
    out_specs = (P("dp", "mp"), P("dp"), P("dp"))
    return jax.shard_map(shards, mesh=mesh, in_specs=in_specs, out_specs=out_specs, check_vma=False)
```

profile of v0, /device:TPU:0, one launch (start us, length us, event | category | flops | bytes accessed | tf_op | source)
XLA Modules:
  0.0 713.0 jit_solution(14737660215632062058)
XLA Ops:
  7.2 0.9 convert_reduce_fusion
  10.9 7.3 %all-to-all-start = ((bf16[8,2,2]{1,2,0:T(2,128)(2,1)}), bf16[8,2,2]{1,2,0:T(2,128)(2,1)S(1)}, u32[]{:S(2)}, u32[]{:S(2)}) async-start(bf16[8,2,2]{1,2,0:T(2,128)(2,1)} %copy.61), calls=%async_computation | async-start | bytes 8192 | tf_op jit(solution)/shard_map/all_to_all | solution.py:129
  19.5 1.1 broadcast_in_dim.69
  20.6 3.0 scatter_fusion.1
  23.6 1.0 all-to-all-done
  24.6 5.0 all-to-all-start.2
  30.4 24.6 %all-to-all-done.2 = bf16[16,32,1024]{2,1,0:T(8,128)(2,1)S(1)} async-done(((bf16[16,32,1024]{2,1,0:T(8,128)(2,1)}), bf16[16,32,1024]{2,1,0:T(8,128)(2,1)S(1)}, u32[]{:S(2)}, u32[]{:S(2)}) %all-to-all-start.2) | async-done | bytes 1048608 | tf_op jit(solution)/shard_map/all_to_all | solution.py:127
  55.0 1.6 gather_fusion.4
  58.9 31.2 %all-gather.10.cloned.1.call-done = bf16[512,4096]{1,0:T(8,128)(2,1)} async-done(((bf16[512,1024]{1,0:T(8,128)(2,1)}), bf16[512,4096]{1,0:T(8,128)(2,1)}) %all-gather.10.cloned.1.call-update) | async-done | bytes 4194320 | tf_op jit(solution)/shard_map/all_gather | solution.py:34
  90.1 178.6 %all-gather.12.cloned.1.call-done = bf16[3,4096,512]{2,1,0:T(8,128)(2,1)} async-done(((bf16[3,512,512]{2,1,0:T(8,128)(2,1)}), bf16[3,4096,512]{2,1,0:T(8,128)(2,1)}) %all-gather.12.cloned.1.call-update) | async-done | bytes 12582928 | tf_op jit(solution)/shard_map/all_gather | solution.py:64
  268.7 5.8 fusion.22
  275.0 6.3 fusion.23
  281.9 6.6 fusion.21
  288.5 1.6 reshape_reshape.21
  290.2 2.4 fusion.80
  292.6 2.2 fusion.16
  295.2 1.4 reshape_reshape.24
  298.1 44.4 %all-gather.16.cloned.1.call-done = bf16[2048,1024]{1,0:T(8,128)(2,1)} async-done(((bf16[256,1024]{1,0:T(8,128)(2,1)}), bf16[2048,1024]{1,0:T(8,128)(2,1)}) %all-gather.16.cloned.1.call-update) | async-done | bytes 4194320 | tf_op jit(solution)/shard_map/all_gather | solution.py:65
  342.5 22.3 %all-gather.14.cloned.1.call-done = bf16[512,2048]{1,0:T(8,128)(2,1)} async-done(((bf16[512,512]{1,0:T(8,128)(2,1)}), bf16[512,2048]{1,0:T(8,128)(2,1)}) %all-gather.14.cloned.1.call-update) | async-done | bytes 2097168 | tf_op jit(solution)/shard_map/all_gather | solution.py:34
  364.8 5.3 multiply_reduce_fusion
  370.0 5.9 psum.37
  375.9 1.3 divide_convert_fusion
  378.8 2.5 scatter_fusion
  381.2 5.7 all-to-all-start.1
  386.9 1.3 slice_bitcast_fusion.20
  389.3 2.9 fusion.38
  392.3 2.8 convolution_convert_fusion.2
  396.4 2.8 fusion.35
  399.6 0.8 fusion.19
  401.5 5.2 all-gather
  406.7 5.2 all_gather.33
  412.0 33.8 %all-gather.22.cloned.1.call-done = bf16[4096,512]{1,0:T(8,128)(2,1)} async-done(((bf16[512,512]{1,0:T(8,128)(2,1)}), bf16[4096,512]{1,0:T(8,128)(2,1)}) %all-gather.22.cloned.1.call-update) | async-done | bytes 4194320 | tf_op jit(solution)/shard_map/all_gather | solution.py:66
  445.7 2.8 convolution_convert_fusion.3
  449.2 2.2 scatter_fusion.2
  451.4 3.6 all-to-all-start.3
  455.0 3.9 multiply_reduce_fusion.3
  459.5 5.7 all-to-all-done.3
  466.0 107.1 %all-gather.20.cloned.1.call-done = bf16[2,4096,512]{2,1,0:T(8,128)(2,1)} async-done(((bf16[2,512,512]{2,1,0:T(8,128)(2,1)}), bf16[2,4096,512]{2,1,0:T(8,128)(2,1)}) %all-gather.20.cloned.1.call-update) | async-done | bytes 8388624 | tf_op jit(solution)/shard_map/all_gather | solution.py:67
  573.1 34.3 %all-gather.18.cloned.1.call-done = bf16[512,4096]{1,0:T(8,128)(2,1)} async-done(((bf16[512,1024]{1,0:T(8,128)(2,1)}), bf16[512,4096]{1,0:T(8,128)(2,1)}) %all-gather.18.cloned.1.call-update) | async-done | bytes 4194320 | tf_op jit(solution)/shard_map/all_gather | solution.py:34
  607.4 5.8 fusion.25
  613.7 5.9 fusion.24
  621.2 1.9 fusion.29
  623.4 7.2 %all_gather.42 = bf16[128,2048]{1,0:T(8,128)(2,1)S(1)} all-gather(bf16[128,512]{1,0:T(8,128)(2,1)S(1)} %reshape_reshape.27), channel_id=1, replica_groups=mesh['dp'=8,'mp'=4] {'mp'}, dimensions={1}, use_global_device_ids=true | all-gather | bytes 655360 | tf_op jit(solution)/shard_map/all_gather | solution.py:34
  630.6 52.4 %all-gather.24.cloned.1.call-done = bf16[2048,1024]{1,0:T(8,128)(2,1)} async-done(((bf16[256,1024]{1,0:T(8,128)(2,1)}), bf16[2048,1024]{1,0:T(8,128)(2,1)}) %all-gather.24.cloned.1.call-update) | async-done | bytes 4194320 | tf_op jit(solution)/shard_map/all_gather | solution.py:68
  682.9 3.1 multiply_reduce_fusion.1
  686.0 5.7 all-reduce.2
  693.2 4.0 all-to-all-start.4
  697.2 6.5 all-to-all-done.4
  (100 shorter events, 23.7 us)
Async XLA Ops:
  7.2 11.7 %copy-start = (bf16[16,32,1024]{2,1,0:T(8,128)(2,1)S(1)}, bf16[16,32,1024]{2,1,0:T(8,128)(2,1)}, u32[]{:S(2)}) copy-start(bf16[16,32,1024]{2,1,0:T(8,128)(2,1)} %param.24) | copy-start | bytes 3145732
  10.9 13.6 %all-to-all-start = ((bf16[8,2,2]{1,2,0:T(2,128)(2,1)}), bf16[8,2,2]{1,2,0:T(2,128)(2,1)S(1)}, u32[]{:S(2)}, u32[]{:S(2)}) async-start(bf16[8,2,2]{1,2,0:T(2,128)(2,1)} %copy.61), calls=%async_computation | async-start | bytes 8192 | tf_op jit(solution)/shard_map/all_to_all | solution.py:129
  24.6 30.4 %all-to-all-start.2 = ((bf16[16,32,1024]{2,1,0:T(8,128)(2,1)}), bf16[16,32,1024]{2,1,0:T(8,128)(2,1)S(1)}, u32[]{:S(2)}, u32[]{:S(2)}) async-start(bf16[16,32,1024]{2,1,0:T(8,128)(2,1)} %scatter_fusion.1), calls=%async_computation.2 | async-start | bytes 2097152 | tf_op jit(solution)/shard_map/all_to_all | solution.py:127
  29.6 60.5 %all-gather.10.cloned.1.call-start = ((), (), s32[]{:S(2)}) async-start(), calls=%async_computation.5 | async-start | bytes 5242880 | tf_op jit(solution)/shard_map/all_gather | solution.py:34
  56.6 212.1 %all-gather.12.cloned.1.call-start = ((), (), s32[]{:S(2)}) async-start(), calls=%async_computation.6 | async-start | bytes 14155776 | tf_op jit(solution)/shard_map/all_gather | solution.py:64
  57.4 285.1 %all-gather.16.cloned.1.call-start = ((), (), s32[]{:S(2)}) async-start(), calls=%async_computation.8 | async-start | bytes 4718592 | tf_op jit(solution)/shard_map/all_gather | solution.py:65
  58.1 306.7 %all-gather.14.cloned.1.call-start = ((), (), s32[]{:S(2)}) async-start(), calls=%async_computation.7 | async-start | bytes 2621440 | tf_op jit(solution)/shard_map/all_gather | solution.py:34
  294.7 70.0 %copy-start.2 = (bf16[16,32,1024]{2,1,0:T(8,128)(2,1)S(1)}, bf16[16,32,1024]{2,1,0:T(8,128)(2,1)}, u32[]{:S(2)}) copy-start(bf16[16,32,1024]{2,1,0:T(8,128)(2,1)} %gather_fusion.4) | copy-start | bytes 3145732
  296.7 149.1 %all-gather.22.cloned.1.call-start = ((), (), s32[]{:S(2)}) async-start(), calls=%async_computation.11 | async-start | bytes 4718592 | tf_op jit(solution)/shard_map/all_gather | solution.py:66
  297.3 275.9 %all-gather.20.cloned.1.call-start = ((), (), s32[]{:S(2)}) async-start(), calls=%async_computation.10 | async-start | bytes 9437184 | tf_op jit(solution)/shard_map/all_gather | solution.py:67
  297.8 309.5 %all-gather.18.cloned.1.call-start = ((), (), s32[]{:S(2)}) async-start(), calls=%async_computation.9 | async-start | bytes 5242880 | tf_op jit(solution)/shard_map/all_gather | solution.py:34
  370.0 8.0 %copy-start.4 = (bf16[1,8,1024]{2,1,0:T(8,128)(2,1)S(1)}, bf16[1,8,1024]{2,1,0:T(8,128)(2,1)}, u32[]{:S(2)}) copy-start(bf16[1,8,1024]{2,1,0:T(8,128)(2,1)} %param.25) | copy-start | bytes 49156
  377.2 12.1 %copy-start.3 = (bf16[16,4096]{1,0:T(8,128)(2,1)S(1)}, bf16[16,4096]{1,0:T(8,128)(2,1)}, u32[]{:S(2)}) copy-start(bf16[16,4096]{1,0:T(8,128)(2,1)} %param.17) | copy-start | bytes 393220
  377.2 305.7 %all-gather.24.cloned.1.call-start = ((), (), s32[]{:S(2)}) async-start(), calls=%async_computation.12 | async-start | bytes 4718592 | tf_op jit(solution)/shard_map/all_gather | solution.py:68
  381.2 70.2 %all-to-all-start.1 = ((bf16[16,8,1024]{2,1,0:T(8,128)(2,1)}), bf16[16,8,1024]{2,1,0:T(8,128)(2,1)S(1)}, u32[]{:S(2)}, u32[]{:S(2)}) async-start(bf16[16,8,1024]{2,1,0:T(8,128)(2,1)} %scatter_fusion), calls=%async_computation.1 | async-start | bytes 524288 | tf_op jit(solution)/shard_map/all_to_all | solution.py:128
  395.1 4.2 copy-start.7
  399.2 2.1 copy-start.5
  399.4 2.1 copy-start.6
  451.4 13.8 %all-to-all-start.3 = ((bf16[16,8,512]{2,1,0:T(8,128)(2,1)}), bf16[16,8,512]{2,1,0:T(8,128)(2,1)S(1)}, u32[]{:S(2)}, u32[]{:S(2)}) async-start(bf16[16,8,512]{2,1,0:T(8,128)(2,1)} %scatter_fusion.2), calls=%async_computation.3 | async-start | bytes 262144 | tf_op jit(solution)/shard_map/all_to_all | solution.py:130
  621.2 85.0 %copy-start.1 = (bf16[16,32,1024]{2,1,0:T(8,128)(2,1)S(1)}, bf16[16,32,1024]{2,1,0:T(8,128)(2,1)}, u32[]{:S(2)}) copy-start(bf16[16,32,1024]{2,1,0:T(8,128)(2,1)} %param.24) | copy-start | bytes 3145732
  691.9 14.3 %copy-start.8 = (f32[16]{0:T(128)}, f32[16]{0:T(128)S(1)}, u32[]{:S(2)}) copy-start(f32[16]{0:T(128)S(1)} %broadcast_multiply_fusion) | copy-start | bytes 196
  693.2 10.5 %all-to-all-start.4 = ((f32[8,2,1]{1,2,0:T(1,128)}), f32[8,2,1]{1,2,0:T(1,128)S(1)}, u32[]{:S(2)}, u32[]{:S(2)}) async-start(f32[8,2,1]{1,2,0:T(1,128)} %bitcast.25), calls=%async_computation.4 | async-start | bytes 8192 | tf_op jit(solution)/shard_map/all_to_all | solution.py:169
Sparse Core Ops, SparseCore 0:
  56.7 33.2 all-gather.9
  92.2 176.4 all-gather.11
  270.8 71.5 all-gather.15
  343.9 20.8 all-gather.13
  366.7 78.9 all-gather.21
  447.8 125.3 all-gather.19
  574.7 32.6 all-gather.17
  609.5 73.3 all-gather.23
where the time goes:
time: 714 us; the launch traced here: 713 us
  waiting for transfers between devices  545 us (76%)
  matrix products  62.3 us (9%)
  blocking collectives  29.2 us (4%)
  local copies, waits for them, and re-layouts  28.5 us (4%)
  starting transfers between devices  26.1 us (4%)
  between operations  14.5 us (2%)
  other arithmetic  7.38 us (1%)
    all_gather x1, waiting for transfers between devices, shards(): lax.all_gather(enc_qkv, 'dp', axis=1, tiled=True)  179 us
    all_gather x1, waiting for transfers between devices, shards(): lax.all_gather(cross_kv, 'dp', axis=1, tiled=True)  107 us
    all_gather x3, waiting for transfers between devices, project(): segment = lax.all_gather(inputs, 'mp', axis=1, tiled=True)  87.7 us
    all_gather x1, waiting for transfers between devices, shards(): lax.all_gather(cross_out, 'dp', axis=0, tiled=True)  52.4 us
    dot_general x9, matrix products, project(): jnp.dot(segment, matrix, preferred_element_type=jnp.float32)  45.5 us
    all_gather x1, waiting for transfers between devices, shards(): lax.all_gather(enc_out, 'dp', axis=0, tiled=True)  44.4 us
    all_gather x1, waiting for transfers between devices, shards(): lax.all_gather(cross_q, 'dp', axis=0, tiled=True)  33.8 us
    all_to_all x1, waiting for transfers between devices, shards(): lax.all_to_all(send_tokens, 'dp', split_axis=0, concat_axis=0, tiled=True)  24.6 us
  transfers between devices with their start and end apart: 13, of which 12 were waited for; matrix products, arithmetic and copies ran while one was open for 12% of the time, Pallas kernels for 0%

commit v1 on v0

v1 whole, which is shorter than its diff:
```python
import functools
import math

import jax
import jax.numpy as jnp
from jax import lax
from jax.experimental import pallas as pl
from jax.experimental.pallas import tpu as pltpu
from jax.sharding import PartitionSpec as P

HD = 64
EPSILON = 1e-06
NEG = -1e30
LANES = 128
F32 = jnp.float32
BF16 = jnp.bfloat16


def dot(a, b):
    return jnp.dot(a, b, preferred_element_type=F32)


def after(value, *others):
    return lax.optimization_barrier((value, others))[0]


def copy_kernel(index_ref, in_ref, out_ref):
    out_ref[...] = in_ref[...]


def take_rows(rows, index, axis):
    n = index.shape[0]
    block = rows.shape[:axis] + (1,) + rows.shape[axis + 1 :]
    tail = (0,) * (rows.ndim - axis - 1)
    lead = (0,) * axis
    out_shape = rows.shape[:axis] + (n,) + rows.shape[axis + 1 :]
    return pl.pallas_call(
        copy_kernel,
        grid_spec=pltpu.PrefetchScalarGridSpec(
            num_scalar_prefetch=1,
            grid=(n,),
            in_specs=[pl.BlockSpec(block, lambda i, at: lead + (at[i],) + tail)],
            out_specs=pl.BlockSpec(block, lambda i, at: lead + (i,) + tail),
        ),
        out_shape=jax.ShapeDtypeStruct(out_shape, rows.dtype),
        cost_estimate=pl.CostEstimate(
            flops=0, bytes_accessed=4 * math.prod(out_shape), transcendentals=0
        ),
    )(index, rows)


def enc_kernel(width, span, qkv_ref, live_ref, out_ref):
    rows = qkv_ref.shape[0]
    own = lax.broadcasted_iota(jnp.int32, (rows, rows), 0) // span
    other = lax.broadcasted_iota(jnp.int32, (rows, rows), 1) // span
    valid = (own == other) & (live_ref[...] > 0)
    for head in range(width // HD):
        q, k, v = (
            qkv_ref[:, part * width + head * HD : part * width + (head + 1) * HD]
            for part in range(3)
        )
        scores = lax.dot_general(q, k, (((1,), (1,)), ((), ())), preferred_element_type=F32)
        scores = jnp.where(valid, scores * (1.0 / math.sqrt(HD)), NEG)
        top = jnp.max(scores, axis=1, keepdims=True)
        weights = jnp.exp(scores - top)
        weights = (weights / jnp.sum(weights, axis=1, keepdims=True)).astype(BF16)
        out_ref[:, head * HD : (head + 1) * HD] = dot(weights, v).astype(BF16)


def enc_attention(qkv, live, span):
    rows, width = qkv.shape[0], qkv.shape[1] // 3
    return pl.pallas_call(
        functools.partial(enc_kernel, width, span),
        grid=(rows // LANES,),
        in_specs=[
            pl.BlockSpec((LANES, 3 * width), lambda i: (i, 0)),
            pl.BlockSpec((1, LANES), lambda i: (0, i)),
        ],
        out_specs=pl.BlockSpec((LANES, width), lambda i: (i, 0)),
        out_shape=jax.ShapeDtypeStruct((rows, width), BF16),
        cost_estimate=pl.CostEstimate(
            flops=4 * rows * LANES * width,
            bytes_accessed=8 * rows * width,
            transcendentals=rows * LANES * (width // HD),
        ),
    )(qkv, live)


def cross_kernel(span, query_n, scores_ref, scale_ref, live_ref, values_ref, out_ref):
    pairs, lanes = scores_ref.shape[1:]
    width = values_ref.shape[1]
    cands = lanes // span
    scores = scores_ref[0] * (scale_ref[...] * (1.0 / math.sqrt(HD)))
    live = live_ref[...] > 0
    cand = lax.broadcasted_iota(jnp.int32, (pairs, lanes), 1) // span
    scores = jnp.concatenate(
        [jnp.where((cand == c) & live, scores, NEG) for c in range(cands)], axis=0
    )
    top = jnp.max(scores, axis=1, keepdims=True)
    weights = jnp.exp(scores - top)
    weights = (weights / jnp.sum(weights, axis=1, keepdims=True)).astype(BF16)
    context = dot(weights, values_ref[...])
    heads = pairs // query_n
    head = lax.broadcasted_iota(jnp.int32, (query_n, width), 1) // HD
    for c in range(cands):
        total = jnp.zeros((query_n, width), F32)
        for h in range(heads):
            start = (c * heads + h) * query_n
            total = total + jnp.where(head == h, context[start : start + query_n], 0.0)
        out_ref[c * query_n : (c + 1) * query_n] = total.astype(BF16)


def cross_attention(scores, scale, live, values, span, query_n):
    source_n, pairs, rows = scores.shape
    width = values.shape[1]
    per_source = rows // source_n // LANES
    made = LANES // span * query_n
    return pl.pallas_call(
        functools.partial(cross_kernel, span, query_n),
        grid=(rows // LANES,),
        in_specs=[
            pl.BlockSpec((1, pairs, LANES), lambda i: (i // per_source, 0, i)),
            pl.BlockSpec((1, LANES), lambda i: (0, i)),
            pl.BlockSpec((1, LANES), lambda i: (0, i)),
            pl.BlockSpec((LANES, width), lambda i: (i, 0)),
        ],
        out_specs=pl.BlockSpec((made, width), lambda i: (i, 0)),
        out_shape=jax.ShapeDtypeStruct((rows // LANES * made, width), BF16),
        cost_estimate=pl.CostEstimate(
            flops=4 * rows * pairs * width,
            bytes_accessed=2 * rows * width + 4 * pairs * rows,
            transcendentals=rows * pairs * (LANES // span),
        ),
    )(scores, scale, live, values)


def direct_attend(query, keys, values, valid):
    group_n, columns = query.shape
    key_n, head_n = keys.shape[1], columns // HD
    query_heads = query.reshape(group_n, 1, head_n, HD)
    key_heads = keys.reshape(group_n, key_n, head_n, HD)
    value_heads = values.reshape(group_n, key_n, head_n, HD)
    scores = jnp.einsum(
        "bqhd,bkhd->bhqk", query_heads, key_heads, preferred_element_type=F32
    ) / math.sqrt(HD)
    scores = jnp.where(valid[:, None, None, :], scores, NEG)
    weights = jax.nn.softmax(scores, axis=-1).astype(BF16)
    context = jnp.einsum("bhqk,bkhd->bqhd", weights, value_heads, preferred_element_type=F32)
    return context.astype(BF16).reshape(group_n, columns)


def shards(
    hidden,
    wq_direct,
    wkv_direct,
    wo_direct,
    kv_cache,
    parent,
    lengths,
    cand_embed,
    source,
    enc_qkv,
    enc_out,
    cross_q,
    cross_kv,
    cross_out,
    w_direct,
    w_channel,
    target_shard,
):
    dp_n, mp_n = lax.axis_size("dp"), lax.axis_size("mp")
    side_n = dp_n // mp_n
    line_n = dp_n // side_n
    me, own_mp = lax.axis_index("dp"), lax.axis_index("mp")
    side, line = me % side_n, me // side_n
    beam_n, features = hidden.shape
    span = kv_cache.shape[2]
    query_n = source.shape[1]
    rung = [(i, i - i % side_n + (i + 1) % side_n) for i in range(dp_n)]

    def swap(a):
        return lax.ppermute(a, "dp", rung)

    def ordered(own, got, axis):
        return jnp.where(
            side == 0, jnp.concatenate([own, got], axis), jnp.concatenate([got, own], axis)
        )

    def both(a, axis):
        return ordered(a, swap(a), axis)

    def side_part(a, at):
        width = a.shape[-1] // side_n
        return lax.dynamic_slice_in_dim(a, at * width, width, a.ndim - 1)

    def rung_sum(a):
        a = lax.psum(a, "mp")
        return a + swap(a)

    def hop(a, step, up):
        if up:
            lines = [(k, k + 1) for k in range(step - 1, line_n - 1)]
        else:
            lines = [(k, k - 1) for k in range(1, line_n - step + 1)]
        return lax.ppermute(
            a, "dp", [(s * side_n + i, t * side_n + i) for s, t in lines for i in range(side_n)]
        )

    def line_gather(parts):
        ups, downs = [list(parts)], [list(parts)]
        for step in range(1, line_n):
            next_up, next_down = [], []
            for at in range(len(parts)):
                next_up.append(hop(ups[-1][at], step, True))
                next_down.append(hop(downs[-1][at], step, False))
            ups.append(next_up)
            downs.append(next_down)
        slots = [list(parts)]
        for j in range(1, line_n):
            slots.append(
                [
                    jnp.where(line >= j, up, down)
                    for up, down in zip(ups[j], downs[line_n - j], strict=True)
                ]
            )
        return slots, (ups[-1], downs[-1])

    def spread_dot(blocks, slots):
        total = None
        for j, slot in enumerate(slots):
            block = lax.dynamic_index_in_dim(blocks, (line - j) % line_n, 0, keepdims=False)
            part = dot(block, slot)
            total = part if total is None else total + part
        return total

    qkv_own = jnp.concatenate([side_part(w, side) for w in enc_qkv], axis=1)
    qkv_other = jnp.concatenate([side_part(w, 1 - side) for w in enc_qkv], axis=1)
    qkv_got = swap(qkv_other)
    qkv_slots, sent = line_gather([qkv_own, qkv_got])
    qkv_slots = [ordered(own, got, 0) for own, got in qkv_slots]

    def slab(w):
        return ordered(side_part(w, side), swap(side_part(w, 1 - side)), 0)

    out_slots, sent = line_gather([after(slab(enc_out), sent)])
    value_slots, sent = line_gather([after(slab(cross_kv[1]), sent)])
    last_slots, sent = line_gather([after(slab(cross_out), sent)])
    out_slots, value_slots, last_slots = (
        [s for (s,) in slots] for slots in (out_slots, value_slots, last_slots)
    )

    tokens = take_rows(cand_embed, parent, 0)
    local_width = tokens.shape[2]
    token_rows = both(tokens.reshape(beam_n * span, local_width), 0)
    token_blocks = lax.all_gather(token_rows, "mp", axis=0)
    lens = both(lengths, 0)
    positions = jnp.arange(span, dtype=jnp.int32)
    live = (positions[None, :] < lens[:, None]).astype(jnp.int32).reshape(1, -1)

    sources = lax.all_gather(source[0], "dp", axis=0)
    source_blocks = lax.all_gather(sources, "mp", axis=0)
    source_block = lax.dynamic_index_in_dim(source_blocks, line, 0, keepdims=False)
    source_part = side_part(source_block.reshape(dp_n * query_n, local_width), side)
    queries = lax.psum(dot(source_part, cross_q), "dp").astype(BF16)
    head_n = queries.shape[1] // HD
    mixed = jnp.einsum(
        "rhc,khc->hrk",
        queries.reshape(-1, head_n, HD),
        cross_kv[0].reshape(-1, head_n, HD),
        preferred_element_type=F32,
    ).astype(BF16)
    depth = mixed.shape[2]
    side_heads = head_n // side_n
    mixed = mixed.reshape(side_n, side_heads, line_n, side_n, query_n, depth)
    mixed = mixed.transpose(2, 0, 3, 1, 4, 5).reshape(dp_n, -1, depth)
    mixed = lax.all_to_all(mixed, "dp", split_axis=0, concat_axis=0, tiled=True)
    pairs = side_heads * query_n
    mixed = mixed.reshape(line_n, side_n, side_n * pairs, depth).transpose(0, 2, 1, 3)
    mixed = mixed.reshape(line_n, side_n * pairs, side_n * depth)

    own_start = own_mp * local_width
    hidden_share = lax.dynamic_slice_in_dim(hidden, own_start, local_width, 1).astype(F32)
    query_new = dot(hidden, wq_direct).astype(BF16)
    key_new = dot(hidden, wkv_direct[0]).astype(BF16)
    value_new = dot(hidden, wkv_direct[1]).astype(BF16)
    cache = take_rows(kv_cache, parent, 1)
    all_keys = jnp.concatenate([cache[0], key_new[:, None]], axis=1)
    all_values = jnp.concatenate([cache[1], value_new[:, None]], axis=1)
    cache_valid = jnp.concatenate(
        [positions[None, :] < lengths[:, None], jnp.ones((beam_n, 1), dtype=bool)], axis=1
    )
    context = direct_attend(query_new, all_keys, all_values, cache_valid)
    context = lax.all_gather(context, "mp", axis=1, tiled=True)
    new_state = hidden_share + dot(context, wo_direct)
    squares, direct_dot = lax.psum(
        (
            jnp.sum(new_state * new_state, axis=1),
            jnp.sum(new_state * w_direct.astype(F32), axis=1),
        ),
        "mp",
    )
    direct_score = direct_dot / jnp.sqrt(squares / features + EPSILON)

    qkv = spread_dot(token_blocks, qkv_slots).astype(BF16)
    enc_context = enc_attention(qkv, live, span)
    enc_blocks = lax.all_gather(both(enc_context, 1), "mp", axis=0)
    summed = side_part(token_rows, side).astype(F32) + spread_dot(enc_blocks, out_slots)
    enc_squares = rung_sum(jnp.sum(summed * summed, axis=1))
    scale = 1.0 / jnp.sqrt(enc_squares / features + EPSILON)
    memory_blocks = lax.all_gather(both(summed.astype(BF16), 1), "mp", axis=0)

    scores = None
    for k in range(line_n):
        part = lax.dot_general(
            mixed[k], memory_blocks[k], (((1,), (1,)), ((), ())), preferred_element_type=F32
        )
        scores = part if scores is None else scores + part
    cross_values = (spread_dot(memory_blocks, value_slots) * scale[:, None]).astype(BF16)
    cross_context = cross_attention(
        scores.reshape(side_n, pairs, -1), scale[None, :], live, cross_values, span, query_n
    )
    cross_blocks = lax.all_gather(both(cross_context, 1), "mp", axis=0)
    update = spread_dot(cross_blocks, last_slots)
    rung_source = lax.dynamic_slice_in_dim(sources, line * side_n, side_n, 0)
    rung_source = side_part(rung_source, side).astype(F32)
    decoded = rung_source[:, None] + update.reshape(side_n, beam_n, query_n, -1)
    channel_weight = side_part(w_channel, side).astype(F32)
    sums = jnp.stack(
        [jnp.sum(decoded * decoded, axis=-1), jnp.sum(decoded * channel_weight, axis=-1)]
    )
    dec_squares, dec_dot = rung_sum(sums)
    cand_channel = jnp.mean(dec_dot / jnp.sqrt(dec_squares / features + EPSILON), axis=-1)
    own_channel = lax.dynamic_index_in_dim(cand_channel, side, 0, keepdims=False)

    targets = lax.all_gather(target_shard, "dp", axis=0)
    all_channel = lax.all_gather(own_channel, "dp", axis=0)
    channel_score = jnp.sum(jnp.where(targets == me, all_channel, 0.0), axis=0)
    return (new_state.astype(BF16), direct_score + own_channel, channel_score)


def solution(mesh):
    in_specs = (
        P("dp", None),
        P(None, "mp"),
        P(None, None, "mp"),
        P(None, "mp"),
        P(None, "dp", None, "mp"),
        P("dp"),
        P("dp"),
        P("dp", None, "mp"),
        P("dp", None, "mp"),
        P(None, "dp", "mp"),
        P("dp", "mp"),
        P("dp", "mp"),
        P(None, "dp", "mp"),
        P("dp", "mp"),
        P("mp"),
        P("mp"),
        P("dp"),
    )
    out_specs = (P("dp", "mp"), P("dp"), P("dp"))
    return jax.shard_map(shards, mesh=mesh, in_specs=in_specs, out_specs=out_specs, check_vma=False)
```

time: 714 us -> 563 us (0.79)
  waiting for transfers between devices: 545 us -> 176 us
  blocking collectives: 29.2 us -> 141 us
  starting transfers between devices: 26.1 us -> 82.1 us
  Pallas kernels: 0 us -> 39.2 us
  other arithmetic: 7.38 us -> 24.2 us
  matrix products: 62.3 us -> 48.8 us
    all_gather x8 -> x4, waiting for transfers between devices: 504 us -> 2.68 us  [the longest x1 2.65 us: shards(): enc_blocks = lax.all_gather(both(enc_context, 1), 'mp', axis=0)]
    ppermute x0 -> x41, waiting for transfers between devices: none -> 173 us  [the longest x30 94.4 us: hop(): lax.ppermute(a, 'dp', [(s * side_n + i, t * side_n + i) for s, t in lines...]
    ppermute x0 -> x41, starting transfers between devices: none -> 77.6 us  [the longest x30 62.6 us: hop(): lax.ppermute(a, 'dp', [(s * side_n + i, t * side_n + i) for s, t in lines...]
    all_gather x3 -> x4, blocking collectives: 17.7 us -> 75.6 us  [the longest x1 30.9 us: shards(): sources = lax.all_gather(source[0], 'dp', axis=0)]
    psum x2 -> x3, blocking collectives: 11.6 us -> 53.8 us  [the longest x1 37.5 us: shards(): queries = lax.psum(dot(source_part, cross_q), 'dp').astype(BF16)]
    pallas_call x0 -> x4, Pallas kernels: none -> 39.2 us  [the longest x2 19.2 us: take_rows(): pl.pallas_call(copy_kernel, grid_spec=pltpu.PrefetchScalarGridSpec(num_sc...]
    all_to_all x5 -> x1, waiting for transfers between devices: 37.8 us -> 0.01 us  [shards(): mixed = lax.all_to_all(mixed, 'dp', split_axis=0, concat_axis=0, tiled=True)]
    all_to_all x5 -> x1, starting transfers between devices: 25.6 us -> 4.16 us  [shards(): mixed = lax.all_to_all(mixed, 'dp', split_axis=0, concat_axis=0, tiled=True)]
  transfers between devices with their start and end apart: 13 -> 46, of which waited for: 12 -> 19; matrix products, arithmetic and copies ran while one was open for 12% -> 12% of each run, Pallas kernels for 0% -> 3%
where the time goes in v1:
time: 563 us; the launch traced here: 559 us
  waiting for transfers between devices  176 us (31%)
  blocking collectives  141 us (25%)
  starting transfers between devices  82.1 us (15%)
  matrix products  48.8 us (9%)
  Pallas kernels  39.2 us (7%)
  local copies, waits for them, and re-layouts  32.9 us (6%)
  other arithmetic  24.2 us (4%)
  between operations  15.4 us (3%)
    ppermute x30, waiting for transfers between devices, hop(): lax.ppermute(a, 'dp', [(s * side_n + i, t * side_n + i) for s, t in lines...  94.4 us
    ppermute x11, waiting for transfers between devices, swap(): return lax.ppermute(a, 'dp', rung)  78.5 us
    ppermute x30, starting transfers between devices, hop(): lax.ppermute(a, 'dp', [(s * side_n + i, t * side_n + i) for s, t in lines...  62.6 us
    dot_general x21, matrix products, dot(): return jnp.dot(a, b, preferred_element_type=F32)  41.4 us
    psum x1, blocking collectives, shards(): queries = lax.psum(dot(source_part, cross_q), 'dp').astype(BF16)  37.5 us
    all_gather x1, blocking collectives, shards(): sources = lax.all_gather(source[0], 'dp', axis=0)  30.9 us
    all_gather x1, blocking collectives, shards(): all_channel = lax.all_gather(own_channel, 'dp', axis=0)  29.4 us
    pallas_call x2, Pallas kernels, take_rows(): pl.pallas_call(copy_kernel, grid_spec=pltpu.PrefetchScalarGridSpec(num_sc...  19.2 us
  transfers between devices with their start and end apart: 46, of which 19 were waited for; matrix products, arithmetic and copies ran while one was open for 12% of the time, Pallas kernels for 3%

profile of v1, /device:TPU:0, one launch (start us, length us, event | category | flops | bytes accessed | tf_op | source)
XLA Modules:
  0.0 559.0 jit_solution(14322207380855495045)
XLA Ops:
  7.2 9.6 %shard_map.185 = bf16[16,32,1024]{2,1,0:T(8,128)(2,1)} custom-call(s32[16]{0:T(128)} %index_ref.3, bf16[16,32,1024]{2,1,0:T(8,128)(2,1)} %in_ref.3), custom_call_target="tpu_custom_call" | custom-call | bytes 2097152 | tf_op jit(solution)/shard_map/pallas_call | solution.py:37
  19.2 2.9 collective-permute-start
  23.5 22.0 %collective-permute-done = bf16[512,1024]{0,1:T(8,128)(2,1)S(1)} collective-permute-done((bf16[512,1024]{0,1:T(8,128)(2,1)}, bf16[512,1024]{0,1:T(8,128)(2,1)S(1)}, u32[]{:S(2)}, u32[]{:S(2)}) %collective-permute-start) | collective-permute-done | bytes 1048608 | tf_op jit(solution)/shard_map/ppermute | solution.py:182
  46.6 3.1 maximum_select_fusion
  49.7 2.6 copy.64
  57.2 5.5 collective-permute-start.2
  62.6 10.2 %collective-permute-done.1 = bf16[512,768]{1,0:T(8,128)(2,1)S(1)} collective-permute-done((bf16[512,768]{1,0:T(8,128)(2,1)S(1)}, bf16[512,768]{1,0:T(8,128)(2,1)S(1)}, u32[]{:S(2)}, u32[]{:S(2)}) %collective-permute-start.1) | collective-permute-done | bytes 786464 | tf_op jit(solution)/shard_map/ppermute | solution.py:182
  74.1 5.5 collective-permute-start.6
  82.4 12.7 %collective-permute-done.7 = bf16[512,768]{1,0:T(8,128)(2,1)S(1)} collective-permute-done((bf16[512,768]{1,0:T(8,128)(2,1)S(1)}, bf16[512,768]{1,0:T(8,128)(2,1)S(1)}, u32[]{:S(2)}, u32[]{:S(2)}) %collective-permute-start.7) | collective-permute-done | bytes 786464 | tf_op jit(solution)/shard_map/ppermute | solution.py:205
  101.7 10.5 %collective-permute-done.4 = bf16[512,768]{1,0:T(8,128)(2,1)} collective-permute-done((bf16[512,768]{1,0:T(8,128)(2,1)S(1)}, bf16[512,768]{1,0:T(8,128)(2,1)}, u32[]{:S(2)}, u32[]{:S(2)}) %collective-permute-start.4) | collective-permute-done | bytes 786464 | tf_op jit(solution)/shard_map/ppermute | solution.py:205
  117.0 12.0 %collective-permute-done.8 = bf16[512,768]{1,0:T(8,128)(2,1)} collective-permute-done((bf16[512,768]{1,0:T(8,128)(2,1)S(1)}, bf16[512,768]{1,0:T(8,128)(2,1)}, u32[]{:S(2)}, u32[]{:S(2)}) %collective-permute-start.8) | collective-permute-done | bytes 786464 | tf_op jit(solution)/shard_map/ppermute | solution.py:205
  133.1 12.7 %collective-permute-done.5 = bf16[512,768]{1,0:T(8,128)(2,1)} collective-permute-done((bf16[512,768]{1,0:T(8,128)(2,1)}, bf16[512,768]{1,0:T(8,128)(2,1)}, u32[]{:S(2)}, u32[]{:S(2)}) %collective-permute-start.5) | collective-permute-done | bytes 786464 | tf_op jit(solution)/shard_map/ppermute | solution.py:205
  148.9 11.3 %collective-permute-done.9 = bf16[512,768]{1,0:T(8,128)(2,1)S(1)} collective-permute-done((bf16[512,768]{1,0:T(8,128)(2,1)}, bf16[512,768]{1,0:T(8,128)(2,1)S(1)}, u32[]{:S(2)}, u32[]{:S(2)}) %collective-permute-start.9) | collective-permute-done | bytes 786464 | tf_op jit(solution)/shard_map/ppermute | solution.py:205
  161.3 4.0 fusion.26
  169.7 3.1 add_convert_fusion.qkv_ref
  172.8 14.0 %shard_map.186 = bf16[1024,256]{1,0:T(8,128)(2,1)} custom-call(bf16[1024,768]{1,0:T(8,128)(2,1)} %add_convert_fusion.qkv_ref, s32[1,1024]{1,0:T(1,128)} %reshape.395.live_ref), custom_call_target="tpu_custom_call" | custom-call | flops 134217728 | bytes 2097152 | tf_op jit(solution)/shard_map/pallas_call | solution.py:72
  187.7 10.8 %collective-permute-done.15 = bf16[1024,256]{1,0:T(8,128)(2,1)S(1)} collective-permute-done((bf16[1024,256]{1,0:T(8,128)(2,1)}, bf16[1024,256]{1,0:T(8,128)(2,1)S(1)}, u32[]{:S(2)}, u32[]{:S(2)}) %collective-permute-start.15) | collective-permute-done | bytes 524320 | tf_op jit(solution)/shard_map/ppermute | solution.py:182
  201.9 5.9 %collective-permute-done.16 = bf16[256,512]{1,0:T(8,128)(2,1)S(1)} collective-permute-done((bf16[256,512]{1,0:T(8,128)(2,1)S(1)}, bf16[256,512]{1,0:T(8,128)(2,1)S(1)}, u32[]{:S(2)}, u32[]{:S(2)}) %collective-permute-start.16) | collective-permute-done | bytes 262176 | tf_op jit(solution)/shard_map/ppermute | solution.py:182
  209.3 4.6 collective-permute-start.17
  213.9 5.5 collective-permute-done.18
  221.3 11.3 %collective-permute-done.19 = bf16[512,512]{1,0:T(8,128)(2,1)S(1)} collective-permute-done((bf16[512,512]{1,0:T(8,128)(2,1)S(1)}, bf16[512,512]{1,0:T(8,128)(2,1)S(1)}, u32[]{:S(2)}, u32[]{:S(2)}) %collective-permute-start.19) | collective-permute-done | bytes 524320 | tf_op jit(solution)/shard_map/ppermute | solution.py:205
  235.4 2.7 all-gather.10.cloned.1.call-done
  240.2 3.5 collective-permute-done.20
  248.4 21.6 %collective-permute-done.23 = bf16[1024,512]{0,1:T(8,128)(2,1)S(1)} collective-permute-done((bf16[1024,512]{0,1:T(8,128)(2,1)S(1)}, bf16[1024,512]{0,1:T(8,128)(2,1)S(1)}, u32[]{:S(2)}, u32[]{:S(2)}) %collective-permute-start.23) | collective-permute-done | bytes 1048608 | tf_op jit(solution)/shard_map/ppermute | solution.py:182
  271.0 2.6 copy.65
  276.5 30.9 %all_gather.39 = bf16[8,8,1024]{2,1,0:T(8,128)(2,1)S(1)} all-gather(bf16[1,8,1024]{2,1,0:T(8,128)(2,1)S(1)} %copy-done.28), channel_id=1, replica_groups=mesh['dp'=8,'mp'=4] {'dp'}, dimensions={0}, use_global_device_ids=true | all-gather | bytes 147456 | tf_op jit(solution)/shard_map/all_gather | solution.py:260
  308.1 10.1 %all-gather = bf16[32,8,1024]{2,1,0:T(8,128)(2,1)S(1)} all-gather(bf16[8,8,1024]{2,1,0:T(8,128)(2,1)S(1)} %all_gather.39), channel_id=2, replica_groups=mesh['dp'=8,'mp'=4] {'mp'}, dimensions={0}, use_global_device_ids=true | all-gather | bytes 655360 | tf_op jit(solution)/shard_map/all_gather | solution.py:261
  318.4 37.5 %all-reduce.4 = bf16[64,512]{1,0:T(8,128)(2,1)S(1)} all-reduce(f32[64,512]{1,0:T(8,128)S(1)} %fusion.149), channel_id=1, replica_groups=mesh['dp'=8,'mp'=4] {'dp'}, use_global_device_ids=true, to_apply=%region_6.7 | all-reduce | flops 32768 | bytes 196608 | tf_op jit(solution)/shard_map/psum | solution.py:264
  357.3 4.2 all-to-all-start
  364.2 9.5 %shard_map.184 = bf16[2,16,32,512]{3,2,1,0:T(8,128)(2,1)} custom-call(s32[16]{0:T(128)} %index_ref.3, bf16[2,16,32,512]{3,2,1,0:T(8,128)(2,1)} %in_ref.2), custom_call_target="tpu_custom_call" | custom-call | bytes 2097152 | tf_op jit(solution)/shard_map/pallas_call | solution.py:37
  379.7 5.3 collective-permute-start.26
  385.1 2.8 fusion.100
  389.9 2.8 convolution_convert_fusion.1
  396.6 2.8 fusion.97
  403.8 5.7 %psum.38 = f32[1024]{0:T(1024)S(1)} all-reduce(f32[1024]{0:T(1024)} %get-tuple-element.16), channel_id=1, replica_groups=mesh['dp'=8,'mp'=4] {'mp'}, use_global_device_ids=true, to_apply=%region_8.9 | all-reduce | flops 1024 | bytes 8192 | tf_op jit(solution)/shard_map/psum | solution.py:197
  415.4 2.5 fusion.14
  417.9 2.9 fusion.16
  428.2 6.0 %shard_map.187 = bf16[256,256]{1,0:T(8,128)(2,1)} custom-call(f32[2,32,1024]{2,1,0:T(8,128)} %bitcast.188, f32[1,1024]{1,0:T(1,128)} %bitcast.204, s32[1,1024]{1,0:T(1,128)} %reshape.395.live_ref, bf16[1024,256]{1,0:T(8,128)(2,1)} %fusion.84.values_ref), custom_call_target="tpu_custom_call" | custom-call | flops 33554432 | bytes 655360 | tf_op jit(solution)/shard_map/pallas_call | solution.py:118
  436.1 3.3 collective-permute-done.32
  446.3 10.6 %collective-permute-start.34 = (bf16[512,512]{1,0:T(8,128)(2,1)S(1)}, bf16[512,512]{1,0:T(8,128)(2,1)S(1)}, u32[]{:S(2)}, u32[]{:S(2)}) collective-permute-start(bf16[512,512]{1,0:T(8,128)(2,1)S(1)} %maximum_select_fusion.15), channel_id=1, source_target_pairs={{0,8},{4,12},{8,16},{12,20},{16,24},{20,28},{1,9},{5,13},{9,17},{1... | collective-permute-start | bytes 1572872 | tf_op jit(solution)/shard_map/ppermute | solution.py:205
  458.2 4.4 collective-permute-done.35
  467.5 11.4 %all-reduce.1 = s32[128]{0:T(128)S(1)} all-reduce(s32[128]{0:T(128)S(1)} %dynamic-update-slice), channel_id=3, replica_groups=mesh['dp'=8,'mp'=4] {'dp'}, use_global_device_ids=true, to_apply=%add.1 | all-reduce | flops 128 | bytes 1024
  478.9 5.2 all_gather.38
  487.0 3.6 multiply_reduce_fusion.3
  493.4 10.6 %collective-permute-done.37 = bf16[512,512]{1,0:T(8,128)(2,1)S(1)} collective-permute-done((bf16[512,512]{1,0:T(8,128)(2,1)S(1)}, bf16[512,512]{1,0:T(8,128)(2,1)S(1)}, u32[]{:S(2)}, u32[]{:S(2)}) %collective-permute-start.37) | collective-permute-done | bytes 524320 | tf_op jit(solution)/shard_map/ppermute | solution.py:205
  507.3 10.7 %all-reduce.2 = (f32[16]{0:T(128)S(1)}, f32[16]{0:T(128)S(1)}, f32[2,2,16,8]{3,2,1,0:T(8,128)S(1)}) all-reduce(f32[16]{0:T(128)S(1)} %get-tuple-element.12, f32[16]{0:T(128)S(1)} %get-tuple-element.11, f32[2,2,16,8]{3,2,1,0:T(8,128)S(1)} %pad_maximum_fusion.4), channel_id=1, replica_groups=mesh['dp'=8,'mp'=4] {'mp'}, use_global_device_ids=true, to_apply=%region_3.4 | all-reduce | flops 544 | bytes 4352 | tf_op jit(solution)/shard_map/psum | solution.py:295
  519.4 2.6 collective-permute-done.40
  522.1 29.4 %all-gather.2 = f32[8,1,16]{2,1,0:T(1,128)S(1)} all-gather(f32[1,1,16]{2,1,0:T(1,128)S(1)} %fusion.177), channel_id=1, replica_groups=mesh['dp'=8,'mp'=4] {'dp'}, dimensions={0}, use_global_device_ids=true | all-gather | bytes 576 | tf_op jit(solution)/shard_map/all_gather | solution.py:336
  (233 shorter events, 118.9 us)
Async XLA Ops:
  7.2 311.0 %copy-start = (bf16[512,512]{1,0:T(8,128)(2,1)S(1)}, bf16[512,512]{1,0:T(8,128)(2,1)}, u32[]{:S(2)}) copy-start(bf16[512,512]{1,0:T(8,128)(2,1)} %param.28) | copy-start | bytes 1572868
  7.2 154.1 %all-gather.8.cloned.1.call-start = ((), (), s32[]{:S(2)}) async-start(), calls=%async_computation.1 | async-start | bytes 10485760 | tf_op jit(solution)/shard_map/all_gather | solution.py:255
  19.2 26.3 %collective-permute-start = (bf16[512,1024]{0,1:T(8,128)(2,1)}, bf16[512,1024]{0,1:T(8,128)(2,1)S(1)}, u32[]{:S(2)}, u32[]{:S(2)}) collective-permute-start(bf16[512,1024]{0,1:T(8,128)(2,1)} %copy.60), channel_id=1, source_target_pairs={{0,4},{4,0},{8,12},{12,8},{16,20},{20,16},{24,28},{28,24},{1,5},{5... | collective-permute-start | bytes 3145736 | tf_op jit(solution)/shard_map/ppermute | solution.py:182
  52.3 185.7 %all-gather.10.cloned.1.call-start = ((), (), s32[]{:S(2)}) async-start(), calls=%async_computation.2 | async-start | bytes 5242880 | tf_op jit(solution)/shard_map/all_gather | solution.py:306
  53.9 44.1 %copy-start.30 = (s32[16]{0:T(128)S(1)}, s32[16]{0:T(128)}, u32[]{:S(2)}) copy-start(s32[16]{0:T(128)} %param.23) | copy-start | bytes 196
  54.0 18.8 %collective-permute-start.1 = (bf16[512,768]{1,0:T(8,128)(2,1)S(1)}, bf16[512,768]{1,0:T(8,128)(2,1)S(1)}, u32[]{:S(2)}, u32[]{:S(2)}) collective-permute-start(bf16[512,768]{1,0:T(8,128)(2,1)S(1)} %pad_maximum_fusion.3), channel_id=1, source_target_pairs={{0,4},{4,0},{8,12},{12,8},{16,20},{20,16},{24,28},{28,24},{1,5},{5... | collective-permute-start | bytes 2359304 | tf_op jit(solution)/shard_map/ppermute | solution.py:182
  55.9 23.7 %collective-permute-start.3 = (bf16[512,768]{1,0:T(8,128)(2,1)S(1)}, bf16[512,768]{1,0:T(8,128)(2,1)S(1)}, u32[]{:S(2)}, u32[]{:S(2)}) collective-permute-start(bf16[512,768]{1,0:T(8,128)(2,1)S(1)} %pad_maximum_fusion.2), channel_id=1, source_target_pairs={{8,0},{12,4},{16,8},{20,12},{24,16},{28,20},{9,1},{13,5},{17,9},{2... | collective-permute-start | bytes 2359304 | tf_op jit(solution)/shard_map/ppermute | solution.py:205
  57.2 23.7 %collective-permute-start.2 = (bf16[512,768]{1,0:T(8,128)(2,1)S(1)}, bf16[512,768]{1,0:T(8,128)(2,1)}, u32[]{:S(2)}, u32[]{:S(2)}) collective-permute-start(bf16[512,768]{1,0:T(8,128)(2,1)S(1)} %pad_maximum_fusion.2), channel_id=1, source_target_pairs={{0,8},{4,12},{8,16},{12,20},{16,24},{20,28},{1,9},{5,13},{9,17},{1... | collective-permute-start | bytes 2359304 | tf_op jit(solution)/shard_map/ppermute | solution.py:205
  72.8 22.4 %collective-permute-start.7 = (bf16[512,768]{1,0:T(8,128)(2,1)S(1)}, bf16[512,768]{1,0:T(8,128)(2,1)S(1)}, u32[]{:S(2)}, u32[]{:S(2)}) collective-permute-start(bf16[512,768]{1,0:T(8,128)(2,1)S(1)} %collective-permute-done.1), channel_id=1, source_target_pairs={{8,0},{12,4},{16,8},{20,12},{24,16},{28,20},{9,1},{13,5},{17,9},{2... | collective-permute-start | bytes 2359304 | tf_op jit(solution)/shard_map/ppermute | solution.py:205
  74.1 22.4 %collective-permute-start.6 = (bf16[512,768]{1,0:T(8,128)(2,1)S(1)}, bf16[512,768]{1,0:T(8,128)(2,1)}, u32[]{:S(2)}, u32[]{:S(2)}) collective-permute-start(bf16[512,768]{1,0:T(8,128)(2,1)S(1)} %collective-permute-done.1), channel_id=1, source_target_pairs={{0,8},{4,12},{8,16},{12,20},{16,24},{20,28},{1,9},{5,13},{9,17},{1... | collective-permute-start | bytes 2359304 | tf_op jit(solution)/shard_map/ppermute | solution.py:205
  79.6 32.6 %collective-permute-start.4 = (bf16[512,768]{1,0:T(8,128)(2,1)S(1)}, bf16[512,768]{1,0:T(8,128)(2,1)}, u32[]{:S(2)}, u32[]{:S(2)}) collective-permute-start(bf16[512,768]{1,0:T(8,128)(2,1)S(1)} %collective-permute-done.3), channel_id=1, source_target_pairs={{8,0},{12,4},{16,8},{20,12},{9,1},{13,5},{17,9},{21,13},{10,2},{14... | collective-permute-start | bytes 2359304 | tf_op jit(solution)/shard_map/ppermute | solution.py:205
  80.9 33.3 %collective-permute-start.10 = (bf16[512,768]{1,0:T(8,128)(2,1)}, bf16[512,768]{1,0:T(8,128)(2,1)}, u32[]{:S(2)}, u32[]{:S(2)}) collective-permute-start(bf16[512,768]{1,0:T(8,128)(2,1)} %collective-permute-done.2), channel_id=1, source_target_pairs={{8,16},{12,20},{16,24},{20,28},{9,17},{13,21},{17,25},{21,29},{10,... | collective-permute-start | bytes 2359304 | tf_op jit(solution)/shard_map/ppermute | solution.py:205
  95.2 33.8 %collective-permute-start.8 = (bf16[512,768]{1,0:T(8,128)(2,1)S(1)}, bf16[512,768]{1,0:T(8,128)(2,1)}, u32[]{:S(2)}, u32[]{:S(2)}) collective-permute-start(bf16[512,768]{1,0:T(8,128)(2,1)S(1)} %collective-permute-done.7), channel_id=1, source_target_pairs={{8,0},{12,4},{16,8},{20,12},{9,1},{13,5},{17,9},{21,13},{10,2},{14... | collective-permute-start | bytes 2359304 | tf_op jit(solution)/shard_map/ppermute | solution.py:205
  96.5 33.8 %collective-permute-start.11 = (bf16[512,768]{1,0:T(8,128)(2,1)}, bf16[512,768]{1,0:T(8,128)(2,1)}, u32[]{:S(2)}, u32[]{:S(2)}) collective-permute-start(bf16[512,768]{1,0:T(8,128)(2,1)} %collective-permute-done.6), channel_id=1, source_target_pairs={{8,16},{12,20},{16,24},{20,28},{9,17},{13,21},{17,25},{21,29},{10,... | collective-permute-start | bytes 2359304 | tf_op jit(solution)/shard_map/ppermute | solution.py:205
  98.1 3.5 collective-permute-start.14
  112.1 33.7 %collective-permute-start.5 = (bf16[512,768]{1,0:T(8,128)(2,1)}, bf16[512,768]{1,0:T(8,128)(2,1)}, u32[]{:S(2)}, u32[]{:S(2)}) collective-permute-start(bf16[512,768]{1,0:T(8,128)(2,1)} %collective-permute-done.4), channel_id=1, source_target_pairs={{8,0},{12,4},{9,1},{13,5},{10,2},{14,6},{11,3},{15,7}} | collective-permute-start | bytes 2359304 | tf_op jit(solution)/shard_map/ppermute | solution.py:205
  114.2 33.8 %collective-permute-start.12 = (bf16[512,768]{1,0:T(8,128)(2,1)}, bf16[512,768]{1,0:T(8,128)(2,1)S(1)}, u32[]{:S(2)}, u32[]{:S(2)}) collective-permute-start(bf16[512,768]{1,0:T(8,128)(2,1)} %collective-permute-done.10), channel_id=1, source_target_pairs={{16,24},{20,28},{17,25},{21,29},{18,26},{22,30},{19,27},{23,31}} | collective-permute-start | bytes 2359304 | tf_op jit(solution)/shard_map/ppermute | solution.py:205
  129.0 31.2 %collective-permute-start.9 = (bf16[512,768]{1,0:T(8,128)(2,1)}, bf16[512,768]{1,0:T(8,128)(2,1)S(1)}, u32[]{:S(2)}, u32[]{:S(2)}) collective-permute-start(bf16[512,768]{1,0:T(8,128)(2,1)} %collective-permute-done.8), channel_id=1, source_target_pairs={{8,0},{12,4},{9,1},{13,5},{10,2},{14,6},{11,3},{15,7}} | collective-permute-start | bytes 2359304 | tf_op jit(solution)/shard_map/ppermute | solution.py:205
  130.3 30.0 %collective-permute-start.13 = (bf16[512,768]{1,0:T(8,128)(2,1)}, bf16[512,768]{1,0:T(8,128)(2,1)S(1)}, u32[]{:S(2)}, u32[]{:S(2)}) collective-permute-start(bf16[512,768]{1,0:T(8,128)(2,1)} %collective-permute-done.11), channel_id=1, source_target_pairs={{16,24},{20,28},{17,25},{21,29},{18,26},{22,30},{19,27},{23,31}} | collective-permute-start | bytes 2359304 | tf_op jit(solution)/shard_map/ppermute | solution.py:205
  186.8 11.7 %collective-permute-start.15 = (bf16[1024,256]{1,0:T(8,128)(2,1)}, bf16[1024,256]{1,0:T(8,128)(2,1)S(1)}, u32[]{:S(2)}, u32[]{:S(2)}) collective-permute-start(bf16[1024,256]{1,0:T(8,128)(2,1)} %shard_map.186), channel_id=1, source_target_pairs={{0,4},{4,0},{8,12},{12,8},{16,20},{20,16},{24,28},{28,24},{1,5},{5... | collective-permute-start | bytes 1572872 | tf_op jit(solution)/shard_map/ppermute | solution.py:182
  201.0 214.3 %all-gather.12.cloned.1.call-start = ((), (), s32[]{:S(2)}) async-start(), calls=%async_computation.3 | async-start | bytes 10485760 | tf_op jit(solution)/shard_map/all_gather | solution.py:310
  201.3 6.4 %collective-permute-start.16 = (bf16[256,512]{1,0:T(8,128)(2,1)S(1)}, bf16[256,512]{1,0:T(8,128)(2,1)S(1)}, u32[]{:S(2)}, u32[]{:S(2)}) collective-permute-start(bf16[256,512]{1,0:T(8,128)(2,1)S(1)} %get-tuple-element.36), channel_id=1, source_target_pairs={{0,4},{4,0},{8,12},{12,8},{16,20},{20,16},{24,28},{28,24},{1,5},{5... | collective-permute-start | bytes 786440 | tf_op jit(solution)/shard_map/ppermute | solution.py:182
  208.0 11.3 %collective-permute-start.18 = (bf16[512,512]{1,0:T(8,128)(2,1)S(1)}, bf16[512,512]{1,0:T(8,128)(2,1)S(1)}, u32[]{:S(2)}, u32[]{:S(2)}) collective-permute-start(bf16[512,512]{1,0:T(8,128)(2,1)S(1)} %maximum_select_fusion.13), channel_id=1, source_target_pairs={{8,0},{12,4},{16,8},{20,12},{24,16},{28,20},{9,1},{13,5},{17,9},{2... | collective-permute-start | bytes 1572872 | tf_op jit(solution)/shard_map/ppermute | solution.py:205
  209.3 11.3 %collective-permute-start.17 = (bf16[512,512]{1,0:T(8,128)(2,1)S(1)}, bf16[512,512]{1,0:T(8,128)(2,1)S(1)}, u32[]{:S(2)}, u32[]{:S(2)}) collective-permute-start(bf16[512,512]{1,0:T(8,128)(2,1)S(1)} %maximum_select_fusion.13), channel_id=1, source_target_pairs={{0,8},{4,12},{8,16},{12,20},{16,24},{20,28},{1,9},{5,13},{9,17},{1... | collective-permute-start | bytes 1572872 | tf_op jit(solution)/shard_map/ppermute | solution.py:205
  219.3 13.3 %collective-permute-start.19 = (bf16[512,512]{1,0:T(8,128)(2,1)S(1)}, bf16[512,512]{1,0:T(8,128)(2,1)S(1)}, u32[]{:S(2)}, u32[]{:S(2)}) collective-permute-start(bf16[512,512]{1,0:T(8,128)(2,1)S(1)} %collective-permute-done.18), channel_id=1, source_target_pairs={{8,0},{12,4},{16,8},{20,12},{9,1},{13,5},{17,9},{21,13},{10,2},{14... | collective-permute-start | bytes 1572872 | tf_op jit(solution)/shard_map/ppermute | solution.py:205
  220.6 13.3 %collective-permute-start.21 = (bf16[512,512]{1,0:T(8,128)(2,1)S(1)}, bf16[512,512]{1,0:T(8,128)(2,1)S(1)}, u32[]{:S(2)}, u32[]{:S(2)}) collective-permute-start(bf16[512,512]{1,0:T(8,128)(2,1)S(1)} %collective-permute-done.17), channel_id=1, source_target_pairs={{8,16},{12,20},{16,24},{20,28},{9,17},{13,21},{17,25},{21,29},{10,... | collective-permute-start | bytes 1572872 | tf_op jit(solution)/shard_map/ppermute | solution.py:205
  232.6 11.1 %collective-permute-start.20 = (bf16[512,512]{1,0:T(8,128)(2,1)S(1)}, bf16[512,512]{1,0:T(8,128)(2,1)S(1)}, u32[]{:S(2)}, u32[]{:S(2)}) collective-permute-start(bf16[512,512]{1,0:T(8,128)(2,1)S(1)} %collective-permute-done.19), channel_id=1, source_target_pairs={{8,0},{12,4},{9,1},{13,5},{10,2},{14,6},{11,3},{15,7}} | collective-permute-start | bytes 1572872 | tf_op jit(solution)/shard_map/ppermute | solution.py:205
  233.9 10.5 %collective-permute-start.22 = (bf16[512,512]{1,0:T(8,128)(2,1)S(1)}, bf16[512,512]{1,0:T(8,128)(2,1)}, u32[]{:S(2)}, u32[]{:S(2)}) collective-permute-start(bf16[512,512]{1,0:T(8,128)(2,1)S(1)} %collective-permute-done.21), channel_id=1, source_target_pairs={{16,24},{20,28},{17,25},{21,29},{18,26},{22,30},{19,27},{23,31}} | collective-permute-start | bytes 1572872 | tf_op jit(solution)/shard_map/ppermute | solution.py:205
  247.8 22.2 %collective-permute-start.23 = (bf16[1024,512]{0,1:T(8,128)(2,1)S(1)}, bf16[1024,512]{0,1:T(8,128)(2,1)S(1)}, u32[]{:S(2)}, u32[]{:S(2)}) collective-permute-start(bf16[1024,512]{0,1:T(8,128)(2,1)S(1)} %get-tuple-element.17), channel_id=1, source_target_pairs={{0,4},{4,0},{8,12},{12,8},{16,20},{20,16},{24,28},{28,24},{1,5},{5... | collective-permute-start | bytes 3145736 | tf_op jit(solution)/shard_map/ppermute | solution.py:182
  274.9 98.8 %collective-permute-start.25 = (bf16[512,256]{1,0:T(8,128)(2,1)S(1)}, bf16[512,256]{1,0:T(8,128)(2,1)S(1)}, u32[]{:S(2)}, u32[]{:S(2)}) collective-permute-start(bf16[512,256]{1,0:T(8,128)(2,1)S(1)} %get-tuple-element.38), channel_id=1, source_target_pairs={{0,4},{4,0},{8,12},{12,8},{16,20},{20,16},{24,28},{28,24},{1,5},{5... | collective-permute-start | bytes 786440 | tf_op jit(solution)/shard_map/ppermute | solution.py:182
  357.3 42.8 %all-to-all-start = ((bf16[8,64,512]{2,1,0:T(8,128)(2,1)}), bf16[8,64,512]{2,1,0:T(8,128)(2,1)}, u32[]{:S(2)}, u32[]{:S(2)}) async-start(bf16[8,64,512]{2,1,0:T(8,128)(2,1)} %bitcast.15), calls=%async_computation | async-start | bytes 1048576 | tf_op jit(solution)/shard_map/all_to_all | solution.py:276
  361.5 130.5 %all-gather.14.cloned.1.call-start = ((), (), s32[]{:S(2)}) async-start(), calls=%async_computation.4 | async-start | bytes 1310720 | tf_op jit(solution)/shard_map/all_gather | solution.py:322
  362.3 78.9 %collective-permute-start.33 = (bf16[256,512]{1,0:T(8,128)(2,1)}, bf16[256,512]{1,0:T(8,128)(2,1)}, u32[]{:S(2)}, u32[]{:S(2)}) collective-permute-start(bf16[256,512]{1,0:T(8,128)(2,1)} %get-tuple-element.40), channel_id=1, source_target_pairs={{0,4},{4,0},{8,12},{12,8},{16,20},{20,16},{24,28},{28,24},{1,5},{5... | collective-permute-start | bytes 786440 | tf_op jit(solution)/shard_map/ppermute | solution.py:182
  375.7 13.0 %collective-permute-start.27 = (bf16[1024,256]{1,0:T(8,128)(2,1)S(1)}, bf16[1024,256]{1,0:T(8,128)(2,1)}, u32[]{:S(2)}, u32[]{:S(2)}) collective-permute-start(bf16[1024,256]{1,0:T(8,128)(2,1)S(1)} %maximum_select_fusion.14), channel_id=1, source_target_pairs={{8,0},{12,4},{16,8},{20,12},{24,16},{28,20},{9,1},{13,5},{17,9},{2... | collective-permute-start | bytes 1572872 | tf_op jit(solution)/shard_map/ppermute | solution.py:205
  379.7 15.4 %collective-permute-start.26 = (bf16[1024,256]{1,0:T(8,128)(2,1)S(1)}, bf16[1024,256]{1,0:T(8,128)(2,1)}, u32[]{:S(2)}, u32[]{:S(2)}) collective-permute-start(bf16[1024,256]{1,0:T(8,128)(2,1)S(1)} %maximum_select_fusion.14), channel_id=1, source_target_pairs={{0,8},{4,12},{8,16},{12,20},{16,24},{20,28},{1,9},{5,13},{9,17},{1... | collective-permute-start | bytes 1572872 | tf_op jit(solution)/shard_map/ppermute | solution.py:205
  388.6 13.9 %collective-permute-start.28 = (bf16[1024,256]{1,0:T(8,128)(2,1)}, bf16[1024,256]{1,0:T(8,128)(2,1)}, u32[]{:S(2)}, u32[]{:S(2)}) collective-permute-start(bf16[1024,256]{1,0:T(8,128)(2,1)} %collective-permute-done.27), channel_id=1, source_target_pairs={{8,0},{12,4},{16,8},{20,12},{9,1},{13,5},{17,9},{21,13},{10,2},{14... | collective-permute-start | bytes 1572872 | tf_op jit(solution)/shard_map/ppermute | solution.py:205
  395.2 18.7 %collective-permute-start.30 = (bf16[1024,256]{1,0:T(8,128)(2,1)}, bf16[1024,256]{1,0:T(8,128)(2,1)}, u32[]{:S(2)}, u32[]{:S(2)}) collective-permute-start(bf16[1024,256]{1,0:T(8,128)(2,1)} %collective-permute-done.26), channel_id=1, source_target_pairs={{8,16},{12,20},{16,24},{20,28},{9,17},{13,21},{17,25},{21,29},{10,... | collective-permute-start | bytes 1572872 | tf_op jit(solution)/shard_map/ppermute | solution.py:205
  402.5 15.4 %collective-permute-start.29 = (bf16[1024,256]{1,0:T(8,128)(2,1)}, bf16[1024,256]{1,0:T(8,128)(2,1)}, u32[]{:S(2)}, u32[]{:S(2)}) collective-permute-start(bf16[1024,256]{1,0:T(8,128)(2,1)} %collective-permute-done.28), channel_id=1, source_target_pairs={{8,0},{12,4},{9,1},{13,5},{10,2},{14,6},{11,3},{15,7}} | collective-permute-start | bytes 1572872 | tf_op jit(solution)/shard_map/ppermute | solution.py:205
  409.5 5.8 %collective-permute-start.24 = (f32[1024]{0:T(1024)S(1)}, f32[1024]{0:T(1024)S(1)}, u32[]{:S(2)}, u32[]{:S(2)}) collective-permute-start(f32[1024]{0:T(1024)S(1)} %psum.38), channel_id=1, source_target_pairs={{0,4},{4,0},{8,12},{12,8},{16,20},{20,16},{24,28},{28,24},{1,5},{5... | collective-permute-start | bytes 12296 | tf_op jit(solution)/shard_map/ppermute | solution.py:182
  413.9 7.0 %collective-permute-start.31 = (bf16[1024,256]{1,0:T(8,128)(2,1)}, bf16[1024,256]{1,0:T(8,128)(2,1)}, u32[]{:S(2)}, u32[]{:S(2)}) collective-permute-start(bf16[1024,256]{1,0:T(8,128)(2,1)} %collective-permute-done.30), channel_id=1, source_target_pairs={{16,24},{20,28},{17,25},{21,29},{18,26},{22,30},{19,27},{23,31}} | collective-permute-start | bytes 1572872 | tf_op jit(solution)/shard_map/ppermute | solution.py:205
  434.2 5.3 collective-permute-start.32
  442.4 20.2 %collective-permute-start.35 = (bf16[512,512]{1,0:T(8,128)(2,1)S(1)}, bf16[512,512]{1,0:T(8,128)(2,1)}, u32[]{:S(2)}, u32[]{:S(2)}) collective-permute-start(bf16[512,512]{1,0:T(8,128)(2,1)S(1)} %maximum_select_fusion.15), channel_id=1, source_target_pairs={{8,0},{12,4},{16,8},{20,12},{24,16},{28,20},{9,1},{13,5},{17,9},{2... | collective-permute-start | bytes 1572872 | tf_op jit(solution)/shard_map/ppermute | solution.py:205
  446.3 37.8 %collective-permute-start.34 = (bf16[512,512]{1,0:T(8,128)(2,1)S(1)}, bf16[512,512]{1,0:T(8,128)(2,1)S(1)}, u32[]{:S(2)}, u32[]{:S(2)}) collective-permute-start(bf16[512,512]{1,0:T(8,128)(2,1)S(1)} %maximum_select_fusion.15), channel_id=1, source_target_pairs={{0,8},{4,12},{8,16},{12,20},{16,24},{20,28},{1,9},{5,13},{9,17},{1... | collective-permute-start | bytes 1572872 | tf_op jit(solution)/shard_map/ppermute | solution.py:205
  462.6 23.1 %collective-permute-start.36 = (bf16[512,512]{1,0:T(8,128)(2,1)}, bf16[512,512]{1,0:T(8,128)(2,1)S(1)}, u32[]{:S(2)}, u32[]{:S(2)}) collective-permute-start(bf16[512,512]{1,0:T(8,128)(2,1)} %collective-permute-done.35), channel_id=1, source_target_pairs={{8,0},{12,4},{16,8},{20,12},{9,1},{13,5},{17,9},{21,13},{10,2},{14... | collective-permute-start | bytes 1572872 | tf_op jit(solution)/shard_map/ppermute | solution.py:205
  484.1 6.5 %collective-permute-start.38 = (bf16[512,512]{1,0:T(8,128)(2,1)S(1)}, bf16[512,512]{1,0:T(8,128)(2,1)S(1)}, u32[]{:S(2)}, u32[]{:S(2)}) collective-permute-start(bf16[512,512]{1,0:T(8,128)(2,1)S(1)} %collective-permute-done.34), channel_id=1, source_target_pairs={{8,16},{12,20},{16,24},{20,28},{9,17},{13,21},{17,25},{21,29},{10,... | collective-permute-start | bytes 1572872 | tf_op jit(solution)/shard_map/ppermute | solution.py:205
  485.7 18.3 %collective-permute-start.37 = (bf16[512,512]{1,0:T(8,128)(2,1)S(1)}, bf16[512,512]{1,0:T(8,128)(2,1)S(1)}, u32[]{:S(2)}, u32[]{:S(2)}) collective-permute-start(bf16[512,512]{1,0:T(8,128)(2,1)S(1)} %collective-permute-done.36), channel_id=1, source_target_pairs={{8,0},{12,4},{9,1},{13,5},{10,2},{14,6},{11,3},{15,7}} | collective-permute-start | bytes 1572872 | tf_op jit(solution)/shard_map/ppermute | solution.py:205
  490.6 15.0 %collective-permute-start.39 = (bf16[512,512]{1,0:T(8,128)(2,1)S(1)}, bf16[512,512]{1,0:T(8,128)(2,1)}, u32[]{:S(2)}, u32[]{:S(2)}) collective-permute-start(bf16[512,512]{1,0:T(8,128)(2,1)S(1)} %collective-permute-done.38), channel_id=1, source_target_pairs={{16,24},{20,28},{17,25},{21,29},{18,26},{22,30},{19,27},{23,31}} | collective-permute-start | bytes 1572872 | tf_op jit(solution)/shard_map/ppermute | solution.py:205
  518.0 4.0 collective-permute-start.40
  (35 other events, 233.1 us)
Sparse Core Ops, SparseCore 0:
  52.4 59.7 all-gather.7
  201.1 36.8 all-gather.9
  273.7 61.4 all-gather.11
  441.3 26.5 all-gather.13

commit v2 on v1

v2 whole, which is shorter than its diff:
```python
import functools
import math

import jax
import jax.numpy as jnp
from jax import lax
from jax.experimental import pallas as pl
from jax.experimental.pallas import tpu as pltpu
from jax.sharding import PartitionSpec as P

HD = 64
EPSILON = 1e-06
NEG = -1e30
LANES = 128
F32 = jnp.float32
BF16 = jnp.bfloat16


def dot(a, b):
    return jnp.dot(a, b, preferred_element_type=F32)


def fence(*values):
    return lax.optimization_barrier(values)


def take_kernel(axis, index_ref, in_ref, out_ref):
    lead = (slice(None),) * axis
    for i in range(index_ref.shape[0]):
        out_ref[lead + (i,)] = in_ref[lead + (index_ref[i],)]


def take_rows(rows, index, axis):
    shape = rows.shape[:axis] + index.shape + rows.shape[axis + 1 :]
    return pl.pallas_call(
        functools.partial(take_kernel, axis),
        in_specs=[
            pl.BlockSpec(memory_space=pltpu.SMEM),
            pl.BlockSpec(memory_space=pltpu.VMEM),
        ],
        out_specs=pl.BlockSpec(memory_space=pltpu.VMEM),
        out_shape=jax.ShapeDtypeStruct(shape, rows.dtype),
        compiler_params=pltpu.CompilerParams(vmem_limit_bytes=16 << 20),
        cost_estimate=pl.CostEstimate(
            flops=0, bytes_accessed=4 * math.prod(shape), transcendentals=0
        ),
    )(index, rows)


def enc_kernel(width, span, qkv_ref, live_ref, out_ref):
    own = lax.broadcasted_iota(jnp.int32, (LANES, LANES), 0) // span
    other = lax.broadcasted_iota(jnp.int32, (LANES, LANES), 1) // span
    same = own == other
    ones = jnp.ones((LANES, HD), BF16)
    for start in range(0, qkv_ref.shape[0], LANES):
        rows = slice(start, start + LANES)
        bias = jnp.where(same & (live_ref[:, rows] > 0), 0.0, NEG)
        for head in range(width // HD):
            q, k, v = (
                qkv_ref[rows, part * width + head * HD : part * width + (head + 1) * HD]
                for part in range(3)
            )
            scores = lax.dot_general(q, k, (((1,), (1,)), ((), ())), preferred_element_type=F32)
            scores = scores * (1.0 / math.sqrt(HD)) + bias
            weights = jnp.exp(scores - jnp.max(scores, axis=1, keepdims=True)).astype(BF16)
            context = dot(weights, v) / dot(weights, ones)
            out_ref[rows, head * HD : (head + 1) * HD] = context.astype(BF16)


def enc_attention(qkv, live, span):
    rows, width = qkv.shape[0], qkv.shape[1] // 3
    block = 2 * LANES
    return pl.pallas_call(
        functools.partial(enc_kernel, width, span),
        grid=(rows // block,),
        in_specs=[
            pl.BlockSpec((block, 3 * width), lambda i: (i, 0)),
            pl.BlockSpec((1, block), lambda i: (0, i)),
        ],
        out_specs=pl.BlockSpec((block, width), lambda i: (i, 0)),
        out_shape=jax.ShapeDtypeStruct((rows, width), BF16),
        cost_estimate=pl.CostEstimate(
            flops=4 * rows * LANES * width,
            bytes_accessed=8 * rows * width,
            transcendentals=rows * LANES * (width // HD),
        ),
    )(qkv, live)


def cross_kernel(span, query_n, scores_ref, scale_ref, live_ref, values_ref, out_ref):
    pairs = scores_ref.shape[0]
    width = values_ref.shape[1]
    cands = LANES // span
    heads = pairs // query_n
    cand = lax.broadcasted_iota(jnp.int32, (pairs, LANES), 1) // span
    head = lax.broadcasted_iota(jnp.int32, (query_n, width), 1) // HD
    for at in range(values_ref.shape[0] // LANES):
        rows = slice(at * LANES, (at + 1) * LANES)
        scores = scores_ref[:, rows] * (scale_ref[:, rows] * (1.0 / math.sqrt(HD)))
        live = live_ref[:, rows] > 0
        scores = jnp.concatenate(
            [jnp.where((cand == c) & live, scores, NEG) for c in range(cands)], axis=0
        )
        weights = jnp.exp(scores - jnp.max(scores, axis=1, keepdims=True))
        weights = (weights / jnp.sum(weights, axis=1, keepdims=True)).astype(BF16)
        context = dot(weights, values_ref[rows])
        for c in range(cands):
            total = jnp.zeros((query_n, width), F32)
            for h in range(heads):
                start = (c * heads + h) * query_n
                total = total + jnp.where(head == h, context[start : start + query_n], 0.0)
            start = (at * cands + c) * query_n
            out_ref[start : start + query_n] = total.astype(BF16)


def cross_attention(scores, scale, live, values, span, query_n):
    pairs, rows = scores.shape
    width = values.shape[1]
    return pl.pallas_call(
        functools.partial(cross_kernel, span, query_n),
        in_specs=[pl.BlockSpec(memory_space=pltpu.VMEM)] * 4,
        out_specs=pl.BlockSpec(memory_space=pltpu.VMEM),
        out_shape=jax.ShapeDtypeStruct((rows // span * query_n, width), BF16),
        compiler_params=pltpu.CompilerParams(vmem_limit_bytes=16 << 20),
        cost_estimate=pl.CostEstimate(
            flops=4 * rows * pairs * width,
            bytes_accessed=2 * rows * width + 4 * pairs * rows,
            transcendentals=rows * pairs * (LANES // span),
        ),
    )(scores, scale, live, values)


def direct_attend(query, keys, values, valid):
    group_n, columns = query.shape
    key_n, head_n = keys.shape[1], columns // HD
    query_heads = query.reshape(group_n, 1, head_n, HD)
    key_heads = keys.reshape(group_n, key_n, head_n, HD)
    value_heads = values.reshape(group_n, key_n, head_n, HD)
    scores = jnp.einsum(
        "bqhd,bkhd->bhqk", query_heads, key_heads, preferred_element_type=F32
    ) / math.sqrt(HD)
    scores = jnp.where(valid[:, None, None, :], scores, NEG)
    weights = jax.nn.softmax(scores, axis=-1).astype(BF16)
    context = jnp.einsum("bhqk,bkhd->bqhd", weights, value_heads, preferred_element_type=F32)
    return context.astype(BF16).reshape(group_n, columns)


class Feed:
    def __init__(self, hop, swap, line_n, shards):
        self.hop, self.swap, self.line_n = hop, swap, line_n
        self.shards, self.group, self.step = list(shards), 0, 0
        self.came = [{(0, 0): s} for s in shards]
        self.crossed = [{} for _ in shards]
        self.fresh = None

    def run(self):
        new = []
        if self.fresh is not None:
            group, step = self.fresh
            for way in (1, -1):
                got = self.swap(self.came[group][way, step], way * step)
                new.append((self.crossed[group], (way, step), got))
            self.fresh = None
        if self.group < len(self.shards):
            came = self.came[self.group]
            for way in (1, -1):
                last = came[(way, self.step) if self.step else (0, 0)]
                new.append((came, (way, self.step + 1), self.hop(last, self.step + 1, way > 0)))
            if self.step == 0:
                got = self.swap(came[0, 0], 0)
                new.append((self.crossed[self.group], (0, 0), got))
            self.fresh = (self.group, self.step + 1)
            self.step += 1
            if self.step == self.line_n - 1:
                self.group, self.step = self.group + 1, 0
        return new

    def advance(self, *values):
        new = self.run()
        arrived, values = fence([got for _, _, got in new], values)
        for (store, key, _), got in zip(new, arrived, strict=True):
            store[key] = got
        return values

    def finish(self, group):
        while len(self.crossed[group]) < 2 * self.line_n - 1:
            self.advance()


def shards(
    hidden,
    wq_direct,
    wkv_direct,
    wo_direct,
    kv_cache,
    parent,
    lengths,
    cand_embed,
    source,
    enc_qkv,
    enc_out,
    cross_q,
    cross_kv,
    cross_out,
    w_direct,
    w_channel,
    target_shard,
):
    dp_n, mp_n = lax.axis_size("dp"), lax.axis_size("mp")
    side_n = dp_n // mp_n
    line_n = dp_n // side_n
    me, own_mp = lax.axis_index("dp"), lax.axis_index("mp")
    side, line = me % side_n, me // side_n
    beam_n, features = hidden.shape
    span, query_n = kv_cache.shape[2], source.shape[1]
    local_width = cand_embed.shape[2]

    def swap(a, steps=0):
        lines = range(max(steps, 0), line_n + min(steps, 0))
        pairs = [(k * side_n + i, k * side_n + (i + 1) % side_n) for k in lines for i in range(side_n)]
        return lax.ppermute(a, "dp", pairs)

    def hop(a, step, up):
        if up:
            lines = [(k, k + 1) for k in range(step - 1, line_n - 1)]
        else:
            lines = [(k, k - 1) for k in range(1, line_n - step + 1)]
        pairs = [(s * side_n + i, t * side_n + i) for s, t in lines for i in range(side_n)]
        return lax.ppermute(a, "dp", pairs)

    def ordered(own, got, axis):
        return jnp.where(
            side == 0, jnp.concatenate([own, got], axis), jnp.concatenate([got, own], axis)
        )

    def side_part(a, at):
        width = a.shape[-1] // side_n
        return lax.dynamic_slice_in_dim(a, at * width, width, a.ndim - 1)

    def slots_of(came, crossed):
        slots = [ordered(came[0, 0], crossed[0, 0], 0)]
        for j in range(1, line_n):
            own, got = (
                jnp.where(line >= j, store[1, j], store[-1, line_n - j])
                for store in (came, crossed)
            )
            slots.append(ordered(own, got, 0))
        return slots

    def spread_dot(blocks, slots):
        total = None
        for j, slot in enumerate(slots):
            block = lax.dynamic_index_in_dim(blocks, (line - j) % line_n, 0, keepdims=False)
            part = dot(block, slot)
            total = part if total is None else total + part
        return total

    def everyone(a):
        return lax.all_gather(a, "mp", axis=0)

    feed = Feed(hop, swap, line_n, [enc_out, cross_kv[1], cross_out])
    unit = (line_n - 1) // 3
    positions = jnp.arange(span, dtype=jnp.int32)

    own = jnp.concatenate([side_part(w, side) for w in enc_qkv], axis=1)
    other = jnp.concatenate([side_part(w, 1 - side) for w in enc_qkv], axis=1)
    came, crossed = {(0, 0): own}, {}

    def stage(step, *values):
        new = []
        if step == 0:
            new.append((crossed, (0, 0), swap(other)))
        for store, hops in ((came, step + 1), (crossed, step)):
            if 1 <= hops < line_n:
                for way in (1, -1):
                    last = store[(way, hops - 1) if hops > 1 else (0, 0)]
                    new.append((store, (way, hops), hop(last, hops, way > 0)))
        arrived, values = fence([got for _, _, got in new], values)
        for (store, key, _), got in zip(new, arrived, strict=True):
            store[key] = got
        return values

    tokens = take_rows(cand_embed, parent, 0).reshape(beam_n * span, local_width)
    source_rows = lax.all_gather(source[0], "mp", axis=1, tiled=True)
    tokens, source_rows = stage(0, tokens, source_rows)

    own_blocks = everyone(tokens)
    tokens_got = swap(tokens)
    lengths_got = swap(lengths)
    source_cut = source_rows.reshape(query_n, dp_n, -1).transpose(1, 0, 2)
    source_cut = lax.all_to_all(source_cut, "dp", split_axis=0, concat_axis=0, tiled=True)
    partial = dot(source_cut.reshape(dp_n * query_n, -1), cross_q)
    partial = partial + swap(partial)
    targets = lax.all_gather(target_shard, "dp", axis=0)
    cache = take_rows(kv_cache, parent, 1)
    tokens_got, partial, targets, cache = stage(1, tokens_got, partial, targets, cache)

    got_blocks = everyone(tokens_got)
    total = partial
    for j in range(1, line_n):
        total = total + lax.ppermute(
            partial, "dp", [(i, (i + j * side_n) % dp_n) for i in range(dp_n)]
        )
    queries = total.astype(BF16)
    query_new = dot(hidden, wq_direct).astype(BF16)
    key_new = dot(hidden, wkv_direct[0]).astype(BF16)
    value_new = dot(hidden, wkv_direct[1]).astype(BF16)
    queries, query_new, key_new, value_new = stage(2, queries, query_new, key_new, value_new)

    head_n = queries.shape[1] // HD
    mixed = jnp.einsum(
        "rhc,khc->rhk",
        queries.reshape(-1, head_n, HD),
        cross_kv[0].reshape(-1, head_n, HD),
        preferred_element_type=F32,
    ).astype(BF16)
    depth = mixed.shape[2]
    pairs = head_n * query_n
    mixed = mixed.reshape(dp_n, query_n, head_n, depth).transpose(0, 2, 1, 3)
    mixed = lax.all_to_all(
        mixed.reshape(dp_n, pairs, depth), "dp", split_axis=0, concat_axis=0, tiled=True
    )
    mixed = mixed.reshape(line_n, side_n, pairs, depth).transpose(0, 2, 1, 3)
    mixed = mixed.reshape(line_n, pairs, side_n * depth)
    all_keys = jnp.concatenate([cache[0], key_new[:, None]], axis=1)
    all_values = jnp.concatenate([cache[1], value_new[:, None]], axis=1)
    cache_valid = jnp.concatenate(
        [positions[None, :] < lengths[:, None], jnp.ones((beam_n, 1), dtype=bool)], axis=1
    )
    context = direct_attend(query_new, all_keys, all_values, cache_valid)
    for step in range(3, line_n - 1):
        stage(step)
    for _ in range(unit):
        context, mixed = feed.advance(context, mixed)
    context, mixed, own_blocks, got_blocks = stage(
        line_n - 1, context, mixed, own_blocks, got_blocks
    )

    def live_of(lens):
        return (positions[None, :] < lens[:, None]).astype(jnp.int32).reshape(1, -1)

    qkv_slots = slots_of(came, crossed)
    qkv_got = spread_dot(got_blocks, qkv_slots).astype(BF16)
    context_got = enc_attention(qkv_got, live_of(lengths_got), span)
    for _ in range(unit):
        (context_got,) = feed.advance(context_got)
    live = live_of(lengths)
    qkv_own = spread_dot(own_blocks, qkv_slots).astype(BF16)
    context_own = enc_attention(qkv_own, live, span)
    enc_context = ordered(context_own, swap(context_got), 1)
    for _ in range(unit):
        (enc_context,) = feed.advance(enc_context)
    enc_blocks = everyone(enc_context)
    for _ in range(unit):
        feed.advance()
    feed.finish(0)
    (enc_blocks,) = fence(enc_blocks)
    summed = tokens.astype(F32) + spread_dot(enc_blocks, slots_of(feed.came[0], feed.crossed[0]))
    summed_sent = summed.astype(BF16)
    for _ in range(unit):
        summed, summed_sent = feed.advance(summed, summed_sent)
    memory_blocks = everyone(summed_sent)
    enc_squares = lax.psum(jnp.sum(summed * summed, axis=1), "mp")
    scale = 1.0 / jnp.sqrt(enc_squares / features + EPSILON)
    for _ in range(2 * unit):
        feed.advance()
    feed.finish(1)
    (context,) = feed.advance(context)

    context = lax.all_gather(context, "mp", axis=1, tiled=True)
    own_start = own_mp * local_width
    hidden_share = lax.dynamic_slice_in_dim(hidden, own_start, local_width, 1).astype(F32)
    new_state = hidden_share + dot(context, wo_direct)
    squares, direct_dot = lax.psum(
        (
            jnp.sum(new_state * new_state, axis=1),
            jnp.sum(new_state * w_direct.astype(F32), axis=1),
        ),
        "mp",
    )
    direct_score = direct_dot / jnp.sqrt(squares / features + EPSILON)
    (memory_blocks,) = fence(memory_blocks)

    scores = None
    for k in range(line_n):
        part = lax.dot_general(
            mixed[k], memory_blocks[k], (((1,), (1,)), ((), ())), preferred_element_type=F32
        )
        scores = part if scores is None else scores + part
    value_slots = slots_of(feed.came[1], feed.crossed[1])
    cross_values = (spread_dot(memory_blocks, value_slots) * scale[:, None]).astype(BF16)
    cross_context = cross_attention(scores, scale[None, :], live, cross_values, span, query_n)
    cross_blocks = everyone(cross_context)
    feed.finish(2)
    update = spread_dot(cross_blocks, slots_of(feed.came[2], feed.crossed[2]))
    decoded = source.astype(F32) + update.reshape(beam_n, query_n, -1)
    sums = jnp.stack(
        [jnp.sum(decoded * decoded, axis=-1), jnp.sum(decoded * w_channel.astype(F32), axis=-1)]
    )
    places = lax.broadcasted_iota(jnp.int32, (dp_n, 1, 1, 1), 0) == me
    dec_squares, dec_dot = lax.psum(jnp.where(places, sums[None], 0.0), ("dp", "mp")).swapaxes(0, 1)
    all_channel = jnp.mean(dec_dot / jnp.sqrt(dec_squares / features + EPSILON), axis=-1)
    own_channel = lax.dynamic_index_in_dim(all_channel, me, 0, keepdims=False)
    channel_score = jnp.sum(jnp.where(targets == me, all_channel, 0.0), axis=0)
    return (new_state.astype(BF16), direct_score + own_channel, channel_score)


def solution(mesh):
    in_specs = (
        P("dp", None),
        P(None, "mp"),
        P(None, None, "mp"),
        P(None, "mp"),
        P(None, "dp", None, "mp"),
        P("dp"),
        P("dp"),
        P("dp", None, "mp"),
        P("dp", None, "mp"),
        P(None, "dp", "mp"),
        P("dp", "mp"),
        P("dp", "mp"),
        P(None, "dp", "mp"),
        P("dp", "mp"),
        P("mp"),
        P("mp"),
        P("dp"),
    )
    out_specs = (P("dp", "mp"), P("dp"), P("dp"))
    return jax.shard_map(shards, mesh=mesh, in_specs=in_specs, out_specs=out_specs, check_vma=False)
```

time: 563 us -> 449 us (0.80)
  waiting for transfers between devices: 176 us -> 119 us
  blocking collectives: 141 us -> 84.2 us
  starting transfers between devices: 82.1 us -> 116 us
  Pallas kernels: 39.2 us -> 10.6 us
  local copies, waits for them, and re-layouts: 32.9 us -> 20.5 us
  other arithmetic: 24.2 us -> 35 us
    ppermute x41 -> x59, waiting for transfers between devices: 173 us -> 109 us  [the longest x26 52.8 us: swap(): return lax.ppermute(a, 'dp', pairs)]
    all_gather x3 -> x2, blocking collectives: 70.4 us -> 13.2 us  [the longest x1 7.51 us: everyone(): return lax.all_gather(a, 'mp', axis=0)]
    ppermute x41 -> x59, starting transfers between devices: 77.6 us -> 105 us  [the longest x30 56.8 us: hop(): return lax.ppermute(a, 'dp', pairs)]
    pallas_call x3, Pallas kernels: 25.2 us -> 3.03 us  [the longest x2 2.21 us: take_rows(): pl.pallas_call(functools.partial(take_kernel, axis), in_specs=[pl.BlockSp...]
    select_n x6 -> x24, other arithmetic: 8.41 us -> 28.9 us  [slots_of(): jnp.where(line >= j, store[1, j], store[-1, line_n - j])]
    all_to_all x1 -> x2, waiting for transfers between devices: 0.01 us -> 10 us  [the longest x1 5.11 us: shards(): lax.all_to_all(mixed.reshape(dp_n, pairs, depth), 'dp', split_axis=0, con...]
    select_n x8 -> x1, other arithmetic: 11 us -> 1.95 us  [ordered(): jnp.where(side == 0, jnp.concatenate([own, got], axis), jnp.concatenate([...]
    unnamed x1, blocking collectives: 11.4 us -> 20.4 us
  transfers between devices with their start and end apart: 46 -> 65, of which waited for: 19 -> 21; matrix products, arithmetic and copies ran while one was open for 12% -> 19% of each run, Pallas kernels for 3% -> 2%
where the time goes in v2:
time: 449 us; the launch traced here: 446 us
  waiting for transfers between devices  119 us (27%)
  starting transfers between devices  116 us (26%)
  blocking collectives  84.2 us (19%)
  matrix products  44.9 us (10%)
  other arithmetic  35 us (8%)
  local copies, waits for them, and re-layouts  20.5 us (5%)
  between operations  15.7 us (3%)
  Pallas kernels  10.6 us (2%)
    ppermute x30, starting transfers between devices, hop(): return lax.ppermute(a, 'dp', pairs)  56.8 us
    ppermute x26, waiting for transfers between devices, swap(): return lax.ppermute(a, 'dp', pairs)  52.8 us
    ppermute x26, starting transfers between devices, swap(): return lax.ppermute(a, 'dp', pairs)  44.7 us
    dot_general x25, matrix products, dot(): return jnp.dot(a, b, preferred_element_type=F32)  41.7 us
    psum x1, blocking collectives, shards(): lax.psum(jnp.where(places, sums[None], 0.0), ('dp', 'mp')).swapaxes(0, 1)  37.8 us
    ppermute x3, waiting for transfers between devices, shards(): lax.ppermute(partial, 'dp', [(i, (i + j * side_n) % dp_n) for i in range(...  29.1 us
    select_n x24, other arithmetic, slots_of(): jnp.where(line >= j, store[1, j], store[-1, line_n - j])  28.9 us
    ppermute x30, waiting for transfers between devices, hop(): return lax.ppermute(a, 'dp', pairs)  27.3 us
  transfers between devices with their start and end apart: 65, of which 21 were waited for; matrix products, arithmetic and copies ran while one was open for 19% of the time, Pallas kernels for 2%

profile of v2, /device:TPU:0, one launch (start us, length us, event | category | flops | bytes accessed | tf_op | source)
XLA Modules:
  0.0 446.1 jit_solution(18289439446794450911)
XLA Ops:
  9.0 6.0 %collective-permute-start.4 = (bf16[512,768]{1,0:T(8,128)(2,1)S(1)}, bf16[512,768]{1,0:T(8,128)(2,1)}, u32[]{:S(2)}, u32[]{:S(2)}) collective-permute-start(bf16[512,768]{1,0:T(8,128)(2,1)S(1)} %pad_maximum_fusion.3), channel_id=1, source_target_pairs={{0,8},{4,12},{8,16},{12,20},{16,24},{20,28},{1,9},{5,13},{9,17},{1... | collective-permute-start | bytes 2359304 | tf_op jit(solution)/shard_map/ppermute | solution.py:229
  19.6 5.7 %all-gather = bf16[1,8,4096]{2,1,0:T(8,128)(2,1)} all-gather(bf16[1,8,1024]{2,1,0:T(8,128)(2,1)S(1)} %copy-done.38), channel_id=2, replica_groups=mesh['dp'=8,'mp'=4] {'mp'}, dimensions={2}, use_global_device_ids=true | all-gather | bytes 81920 | tf_op jit(solution)/shard_map/all_gather | solution.py:284
  25.2 5.6 %collective-permute-done.4 = bf16[512,768]{1,0:T(8,128)(2,1)} collective-permute-done((bf16[512,768]{1,0:T(8,128)(2,1)S(1)}, bf16[512,768]{1,0:T(8,128)(2,1)}, u32[]{:S(2)}, u32[]{:S(2)}) %collective-permute-start.4) | collective-permute-done | bytes 786464 | tf_op jit(solution)/shard_map/ppermute | solution.py:229
  30.9 5.1 %collective-permute-done.5 = bf16[512,768]{1,0:T(8,128)(2,1)} collective-permute-done((bf16[512,768]{1,0:T(8,128)(2,1)S(1)}, bf16[512,768]{1,0:T(8,128)(2,1)}, u32[]{:S(2)}, u32[]{:S(2)}) %collective-permute-start.5) | collective-permute-done | bytes 786464 | tf_op jit(solution)/shard_map/ppermute | solution.py:229
  36.0 6.2 %all-to-all-start = ((bf16[8,8,512]{2,1,0:T(8,128)(2,1)}), bf16[8,8,512]{2,1,0:T(8,128)(2,1)S(1)}, u32[]{:S(2)}, u32[]{:S(2)}) async-start(bf16[8,8,512]{2,1,0:T(8,128)(2,1)} %bitcast.9), calls=%async_computation | async-start | bytes 131072 | tf_op jit(solution)/shard_map/all_to_all | solution.py:291
  44.3 4.9 %all-to-all-done = bf16[8,8,512]{2,1,0:T(8,128)(2,1)S(1)} async-done(((bf16[8,8,512]{2,1,0:T(8,128)(2,1)}), bf16[8,8,512]{2,1,0:T(8,128)(2,1)S(1)}, u32[]{:S(2)}, u32[]{:S(2)}) %all-to-all-start) | async-done | bytes 65568 | tf_op jit(solution)/shard_map/all_to_all | solution.py:291
  52.6 5.7 %collective-permute-start.8 = (bf16[512,768]{1,0:T(8,128)(2,1)}, bf16[512,768]{1,0:T(8,128)(2,1)}, u32[]{:S(2)}, u32[]{:S(2)}) collective-permute-start(bf16[512,768]{1,0:T(8,128)(2,1)} %collective-permute-done.3), channel_id=1, source_target_pairs={{0,8},{4,12},{8,16},{12,20},{16,24},{20,28},{1,9},{5,13},{9,17},{1... | collective-permute-start | bytes 2359304 | tf_op jit(solution)/shard_map/ppermute | solution.py:229
  58.3 10.8 %collective-permute-done.11 = f32[64,512]{1,0:T(8,128)S(1)} collective-permute-done((f32[64,512]{1,0:T(8,128)S(1)}, f32[64,512]{1,0:T(8,128)S(1)}, u32[]{:S(2)}, u32[]{:S(2)}) %collective-permute-start.11) | collective-permute-done | bytes 131104 | tf_op jit(solution)/shard_map/ppermute | solution.py:221
  71.9 20.4 %all-reduce.1 = s32[128]{0:T(128)S(1)} all-reduce(s32[128]{0:T(128)S(1)} %dynamic-update-slice), channel_id=3, replica_groups=mesh['dp'=8,'mp'=4] {'dp'}, use_global_device_ids=true, to_apply=%add.1 | all-reduce | flops 128 | bytes 1024
  99.2 3.8 fusion.21
  103.1 3.0 fusion.24
  116.2 2.1 broadcast_select_fusion.3
  123.5 28.1 %collective-permute-done.18 = f32[64,512]{1,0:T(8,128)} collective-permute-done((f32[64,512]{1,0:T(8,128)}, f32[64,512]{1,0:T(8,128)}, u32[]{:S(2)}, u32[]{:S(2)}) %collective-permute-start.18) | collective-permute-done | bytes 131104 | tf_op jit(solution)/shard_map/ppermute | solution.py:301
  151.7 2.2 collective-permute-start
  160.1 4.8 %all-to-all-start.1 = ((bf16[8,64,512]{2,1,0:T(8,128)(2,1)}), bf16[8,64,512]{2,1,0:T(8,128)(2,1)S(1)}, u32[]{:S(2)}, u32[]{:S(2)}) async-start(bf16[8,64,512]{2,1,0:T(8,128)(2,1)} %bitcast.172), calls=%async_computation.1 | async-start | bytes 1048576 | tf_op jit(solution)/shard_map/all_to_all | solution.py:320
  174.5 5.1 %all-to-all-done.1 = bf16[8,64,512]{2,1,0:T(8,128)(2,1)S(1)} async-done(((bf16[8,64,512]{2,1,0:T(8,128)(2,1)}), bf16[8,64,512]{2,1,0:T(8,128)(2,1)S(1)}, u32[]{:S(2)}, u32[]{:S(2)}) %all-to-all-start.1) | async-done | bytes 524320 | tf_op jit(solution)/shard_map/all_to_all | solution.py:320
  187.6 9.0 %collective-permute-done.24 = bf16[512,768]{1,0:T(8,128)(2,1)} collective-permute-done((bf16[512,768]{1,0:T(8,128)(2,1)}, bf16[512,768]{1,0:T(8,128)(2,1)}, u32[]{:S(2)}, u32[]{:S(2)}) %collective-permute-start.24) | collective-permute-done | bytes 786464 | tf_op jit(solution)/shard_map/ppermute | solution.py:229
  199.1 2.5 fusion.108
  204.2 3.3 add_convert_fusion.1.qkv_ref
  207.5 3.4 fusion.101
  210.9 3.8 shard_map.186
  214.7 2.4 fusion.99
  225.2 3.3 add_convert_fusion.qkv_ref
  228.5 3.8 shard_map.187
  232.3 3.8 collective-permute-done.30
  238.2 2.3 collective-permute-start.33
  245.4 2.9 collective-permute-start.32
  251.8 3.6 collective-permute-done.35
  255.4 5.6 %collective-permute-done.32 = bf16[256,1024]{1,0:T(8,128)(2,1)S(1)} collective-permute-done((bf16[256,1024]{1,0:T(8,128)(2,1)S(1)}, bf16[256,1024]{1,0:T(8,128)(2,1)S(1)}, u32[]{:S(2)}, u32[]{:S(2)}) %collective-permute-start.32) | collective-permute-done | bytes 524320 | tf_op jit(solution)/shard_map/ppermute | solution.py:221
  263.9 3.5 collective-permute-start.37
  270.2 2.2 fusion.28
  274.5 3.3 fusion.217
  278.9 7.4 %collective-permute-start.46 = (bf16[256,1024]{1,0:T(8,128)(2,1)}, bf16[256,1024]{1,0:T(8,128)(2,1)S(1)}, u32[]{:S(2)}, u32[]{:S(2)}) collective-permute-start(bf16[256,1024]{1,0:T(8,128)(2,1)} %param.30), channel_id=1, source_target_pairs={{0,8},{4,12},{8,16},{12,20},{16,24},{20,28},{1,9},{5,13},{9,17},{1... | collective-permute-start | bytes 1572872 | tf_op jit(solution)/shard_map/ppermute | solution.py:229
  287.8 3.7 collective-permute-start.41
  295.4 8.8 %collective-permute-done.41 = bf16[512,512]{1,0:T(8,128)(2,1)S(1)} collective-permute-done((bf16[512,512]{1,0:T(8,128)(2,1)}, bf16[512,512]{1,0:T(8,128)(2,1)S(1)}, u32[]{:S(2)}, u32[]{:S(2)}) %collective-permute-start.41) | collective-permute-done | bytes 524320 | tf_op jit(solution)/shard_map/ppermute | solution.py:221
  308.3 2.2 collective-permute-start.45
  313.2 2.7 collective-permute-done.48
  316.7 6.9 %collective-permute-done.45 = bf16[512,512]{1,0:T(8,128)(2,1)S(1)} collective-permute-done((bf16[512,512]{1,0:T(8,128)(2,1)S(1)}, bf16[512,512]{1,0:T(8,128)(2,1)S(1)}, u32[]{:S(2)}, u32[]{:S(2)}) %collective-permute-start.45) | collective-permute-done | bytes 524320 | tf_op jit(solution)/shard_map/ppermute | solution.py:221
  325.8 3.7 collective-permute-start.50
  333.5 4.8 %collective-permute-done.50 = bf16[256,1024]{1,0:T(8,128)(2,1)S(1)} collective-permute-done((bf16[256,1024]{1,0:T(8,128)(2,1)S(1)}, bf16[256,1024]{1,0:T(8,128)(2,1)S(1)}, u32[]{:S(2)}, u32[]{:S(2)}) %collective-permute-start.50) | collective-permute-done | bytes 524320 | tf_op jit(solution)/shard_map/ppermute | solution.py:221
  338.3 2.8 collective-permute-done.52
  347.4 5.2 %all_gather.51 = bf16[16,2048]{1,0:T(8,128)(2,1)S(1)} all-gather(bf16[16,512]{1,0:T(8,128)(2,1)S(1)} %reshape.164), channel_id=1, replica_groups=mesh['dp'=8,'mp'=4] {'mp'}, dimensions={1}, use_global_device_ids=true | all-gather | bytes 81920 | tf_op jit(solution)/shard_map/all_gather | solution.py:370
  354.0 7.6 %all-reduce.2 = (f32[512]{0:T(512)S(1)}, f32[16]{0:T(128)S(1)}, f32[16]{0:T(128)S(1)}) all-reduce(f32[512]{0:T(512)S(1)} %multiply_reduce_fusion, f32[16]{0:T(128)S(1)} %get-tuple-element.152, f32[16]{0:T(128)S(1)} %get-tuple-element.151), channel_id=1, replica_groups=mesh['dp'=8,'mp'=4] {'mp'}, use_global_device_ids=true, to_apply=%region_7.8 | all-reduce | flops 544 | bytes 4352 | tf_op jit(solution)/shard_map/psum | solution.py:363
  364.4 3.3 collective-permute-start.58
  372.7 5.9 %collective-permute-done.58 = bf16[256,1024]{1,0:T(8,128)(2,1)S(1)} collective-permute-done((bf16[256,1024]{1,0:T(8,128)(2,1)}, bf16[256,1024]{1,0:T(8,128)(2,1)S(1)}, u32[]{:S(2)}, u32[]{:S(2)}) %collective-permute-start.58) | collective-permute-done | bytes 524320 | tf_op jit(solution)/shard_map/ppermute | solution.py:221
  380.3 2.7 fusion.51
  388.8 7.5 %all-gather.6 = bf16[512,512]{1,0:T(8,128)(2,1)S(1)} all-gather(bf16[128,512]{1,0:T(8,128)(2,1)S(1)} %shard_map.188), channel_id=8, replica_groups=mesh['dp'=8,'mp'=4] {'mp'}, dimensions={0}, use_global_device_ids=true | all-gather | bytes 655360 | tf_op jit(solution)/shard_map/all_gather | solution.py:259
  400.7 37.8 %psum.31 = f32[2,8,16,8]{2,3,1,0:T(8,128)S(1)} all-reduce(f32[2,8,16,8]{2,3,1,0:T(8,128)S(1)} %select_bitcast_fusion), channel_id=1, replica_groups=mesh['dp'=8,'mp'=4] {'dp','mp'}, use_global_device_ids=true, to_apply=%region_10.11 | all-reduce | flops 2048 | bytes 16384 | tf_op jit(solution)/shard_map/psum | solution.py:401
  (311 shorter events, 139.2 us)
Async XLA Ops:
  7.2 189.3 %all-gather.12.cloned.1.call-start = ((), (), s32[]{:S(2)}) async-start(), calls=%async_computation.2 | async-start | bytes 5242880 | tf_op jit(solution)/shard_map/all_gather | solution.py:259
  9.0 21.9 %collective-permute-start.4 = (bf16[512,768]{1,0:T(8,128)(2,1)S(1)}, bf16[512,768]{1,0:T(8,128)(2,1)}, u32[]{:S(2)}, u32[]{:S(2)}) collective-permute-start(bf16[512,768]{1,0:T(8,128)(2,1)S(1)} %pad_maximum_fusion.3), channel_id=1, source_target_pairs={{0,8},{4,12},{8,16},{12,20},{16,24},{20,28},{1,9},{5,13},{9,17},{1... | collective-permute-start | bytes 2359304 | tf_op jit(solution)/shard_map/ppermute | solution.py:229
  15.0 21.0 %collective-permute-start.5 = (bf16[512,768]{1,0:T(8,128)(2,1)S(1)}, bf16[512,768]{1,0:T(8,128)(2,1)}, u32[]{:S(2)}, u32[]{:S(2)}) collective-permute-start(bf16[512,768]{1,0:T(8,128)(2,1)S(1)} %pad_maximum_fusion.3), channel_id=1, source_target_pairs={{8,0},{12,4},{16,8},{20,12},{24,16},{28,20},{9,1},{13,5},{17,9},{2... | collective-permute-start | bytes 2359304 | tf_op jit(solution)/shard_map/ppermute | solution.py:229
  16.4 19.6 %collective-permute-start.3 = (bf16[512,768]{1,0:T(8,128)(2,1)S(1)}, bf16[512,768]{1,0:T(8,128)(2,1)}, u32[]{:S(2)}, u32[]{:S(2)}) collective-permute-start(bf16[512,768]{1,0:T(8,128)(2,1)S(1)} %pad_maximum_fusion.2), channel_id=1, source_target_pairs={{0,4},{4,0},{8,12},{12,8},{16,20},{20,16},{24,28},{28,24},{1,5},{5... | collective-permute-start | bytes 2359304 | tf_op jit(solution)/shard_map/ppermute | solution.py:221
  42.2 154.3 %all-gather.14.cloned.1.call-start = ((), (), s32[]{:S(2)}) async-start(), calls=%async_computation.3 | async-start | bytes 5242880 | tf_op jit(solution)/shard_map/all_gather | solution.py:259
  42.3 52.1 %collective-permute-start.10 = (bf16[512,1024]{1,0:T(8,128)(2,1)}, bf16[512,1024]{1,0:T(8,128)(2,1)}, u32[]{:S(2)}, u32[]{:S(2)}) collective-permute-start(bf16[512,1024]{1,0:T(8,128)(2,1)} %bitcast.6), channel_id=1, source_target_pairs={{0,4},{4,0},{8,12},{12,8},{16,20},{20,16},{24,28},{28,24},{1,5},{5... | collective-permute-start | bytes 3145736 | tf_op jit(solution)/shard_map/ppermute | solution.py:221
  49.4 19.7 %collective-permute-start.11 = (f32[64,512]{1,0:T(8,128)S(1)}, f32[64,512]{1,0:T(8,128)S(1)}, u32[]{:S(2)}, u32[]{:S(2)}) collective-permute-start(f32[64,512]{1,0:T(8,128)S(1)} %fusion.160), channel_id=1, source_target_pairs={{0,4},{4,0},{8,12},{12,8},{16,20},{20,16},{24,28},{28,24},{1,5},{5... | collective-permute-start | bytes 393224 | tf_op jit(solution)/shard_map/ppermute | solution.py:221
  49.8 44.5 %collective-permute-start.6 = (bf16[512,768]{1,0:T(8,128)(2,1)}, bf16[512,768]{1,0:T(8,128)(2,1)}, u32[]{:S(2)}, u32[]{:S(2)}) collective-permute-start(bf16[512,768]{1,0:T(8,128)(2,1)} %collective-permute-done.4), channel_id=1, source_target_pairs={{8,16},{12,20},{16,24},{20,28},{9,17},{13,21},{17,25},{21,29},{10,... | collective-permute-start | bytes 2359304 | tf_op jit(solution)/shard_map/ppermute | solution.py:229
  51.3 43.0 %collective-permute-start.7 = (bf16[512,768]{1,0:T(8,128)(2,1)}, bf16[512,768]{1,0:T(8,128)(2,1)}, u32[]{:S(2)}, u32[]{:S(2)}) collective-permute-start(bf16[512,768]{1,0:T(8,128)(2,1)} %collective-permute-done.5), channel_id=1, source_target_pairs={{8,0},{12,4},{16,8},{20,12},{9,1},{13,5},{17,9},{21,13},{10,2},{14... | collective-permute-start | bytes 2359304 | tf_op jit(solution)/shard_map/ppermute | solution.py:229
  52.6 41.7 %collective-permute-start.8 = (bf16[512,768]{1,0:T(8,128)(2,1)}, bf16[512,768]{1,0:T(8,128)(2,1)}, u32[]{:S(2)}, u32[]{:S(2)}) collective-permute-start(bf16[512,768]{1,0:T(8,128)(2,1)} %collective-permute-done.3), channel_id=1, source_target_pairs={{0,8},{4,12},{8,16},{12,20},{16,24},{20,28},{1,9},{5,13},{9,17},{1... | collective-permute-start | bytes 2359304 | tf_op jit(solution)/shard_map/ppermute | solution.py:229
  69.1 25.2 %collective-permute-start.9 = (bf16[512,768]{1,0:T(8,128)(2,1)}, bf16[512,768]{1,0:T(8,128)(2,1)}, u32[]{:S(2)}, u32[]{:S(2)}) collective-permute-start(bf16[512,768]{1,0:T(8,128)(2,1)} %collective-permute-done.3), channel_id=1, source_target_pairs={{8,0},{12,4},{16,8},{20,12},{24,16},{28,20},{9,1},{13,5},{17,9},{2... | collective-permute-start | bytes 2359304 | tf_op jit(solution)/shard_map/ppermute | solution.py:229
  109.7 45.4 %collective-permute-start.12 = (bf16[512,768]{1,0:T(8,128)(2,1)}, bf16[512,768]{1,0:T(8,128)(2,1)}, u32[]{:S(2)}, u32[]{:S(2)}) collective-permute-start(bf16[512,768]{1,0:T(8,128)(2,1)} %collective-permute-done.6), channel_id=1, source_target_pairs={{16,24},{20,28},{17,25},{21,29},{18,26},{22,30},{19,27},{23,31}} | collective-permute-start | bytes 2359304 | tf_op jit(solution)/shard_map/ppermute | solution.py:229
  111.2 45.2 %collective-permute-start.13 = (bf16[512,768]{1,0:T(8,128)(2,1)}, bf16[512,768]{1,0:T(8,128)(2,1)}, u32[]{:S(2)}, u32[]{:S(2)}) collective-permute-start(bf16[512,768]{1,0:T(8,128)(2,1)} %collective-permute-done.7), channel_id=1, source_target_pairs={{8,0},{12,4},{9,1},{13,5},{10,2},{14,6},{11,3},{15,7}} | collective-permute-start | bytes 2359304 | tf_op jit(solution)/shard_map/ppermute | solution.py:229
  112.5 44.7 %collective-permute-start.14 = (bf16[512,768]{1,0:T(8,128)(2,1)}, bf16[512,768]{1,0:T(8,128)(2,1)}, u32[]{:S(2)}, u32[]{:S(2)}) collective-permute-start(bf16[512,768]{1,0:T(8,128)(2,1)} %collective-permute-done.8), channel_id=1, source_target_pairs={{8,16},{12,20},{16,24},{20,28},{9,17},{13,21},{17,25},{21,29},{10,... | collective-permute-start | bytes 2359304 | tf_op jit(solution)/shard_map/ppermute | solution.py:229
  115.0 42.2 %collective-permute-start.15 = (bf16[512,768]{1,0:T(8,128)(2,1)}, bf16[512,768]{1,0:T(8,128)(2,1)}, u32[]{:S(2)}, u32[]{:S(2)}) collective-permute-start(bf16[512,768]{1,0:T(8,128)(2,1)} %collective-permute-done.9), channel_id=1, source_target_pairs={{8,0},{12,4},{16,8},{20,12},{9,1},{13,5},{17,9},{21,13},{10,2},{14... | collective-permute-start | bytes 2359304 | tf_op jit(solution)/shard_map/ppermute | solution.py:229
  118.4 33.3 %collective-permute-start.18 = (f32[64,512]{1,0:T(8,128)}, f32[64,512]{1,0:T(8,128)}, u32[]{:S(2)}, u32[]{:S(2)}) collective-permute-start(f32[64,512]{1,0:T(8,128)} %add.202), channel_id=1, source_target_pairs={{0,24},{4,28},{8,0},{12,4},{16,8},{20,12},{24,16},{28,20},{1,25},{... | collective-permute-start | bytes 393224 | tf_op jit(solution)/shard_map/ppermute | solution.py:301
  151.7 29.6 %collective-permute-start = (bf16[256,1024]{1,0:T(8,128)(2,1)}, bf16[256,1024]{1,0:T(8,128)(2,1)}, u32[]{:S(2)}, u32[]{:S(2)}) collective-permute-start(bf16[256,1024]{1,0:T(8,128)(2,1)} %param.27), channel_id=1, source_target_pairs={{0,8},{4,12},{8,16},{12,20},{16,24},{20,28},{1,9},{5,13},{9,17},{1... | collective-permute-start | bytes 1572872 | tf_op jit(solution)/shard_map/ppermute | solution.py:229
  155.1 26.2 %collective-permute-start.1 = (bf16[256,1024]{1,0:T(8,128)(2,1)}, bf16[256,1024]{1,0:T(8,128)(2,1)}, u32[]{:S(2)}, u32[]{:S(2)}) collective-permute-start(bf16[256,1024]{1,0:T(8,128)(2,1)} %param.27), channel_id=1, source_target_pairs={{8,0},{12,4},{16,8},{20,12},{24,16},{28,20},{9,1},{13,5},{17,9},{2... | collective-permute-start | bytes 1572872 | tf_op jit(solution)/shard_map/ppermute | solution.py:229
  156.4 24.9 %collective-permute-start.2 = (bf16[256,1024]{1,0:T(8,128)(2,1)}, bf16[256,1024]{1,0:T(8,128)(2,1)}, u32[]{:S(2)}, u32[]{:S(2)}) collective-permute-start(bf16[256,1024]{1,0:T(8,128)(2,1)} %param.27), channel_id=1, source_target_pairs={{0,4},{4,0},{8,12},{12,8},{16,20},{20,16},{24,28},{28,24},{1,5},{5... | collective-permute-start | bytes 1572872 | tf_op jit(solution)/shard_map/ppermute | solution.py:221
  160.1 19.4 %all-to-all-start.1 = ((bf16[8,64,512]{2,1,0:T(8,128)(2,1)}), bf16[8,64,512]{2,1,0:T(8,128)(2,1)S(1)}, u32[]{:S(2)}, u32[]{:S(2)}) async-start(bf16[8,64,512]{2,1,0:T(8,128)(2,1)} %bitcast.172), calls=%async_computation.1 | async-start | bytes 1048576 | tf_op jit(solution)/shard_map/all_to_all | solution.py:320
  165.0 105.2 %all-gather.16.cloned.1.call-start = ((), (), s32[]{:S(2)}) async-start(), calls=%async_computation.4 | async-start | bytes 2621440 | tf_op jit(solution)/shard_map/all_gather | solution.py:259
  167.0 19.0 %collective-permute-start.23 = (bf16[512,768]{1,0:T(8,128)(2,1)}, bf16[512,768]{1,0:T(8,128)(2,1)}, u32[]{:S(2)}, u32[]{:S(2)}) collective-permute-start(bf16[512,768]{1,0:T(8,128)(2,1)} %collective-permute-done.14), channel_id=1, source_target_pairs={{16,24},{20,28},{17,25},{21,29},{18,26},{22,30},{19,27},{23,31}} | collective-permute-start | bytes 2359304 | tf_op jit(solution)/shard_map/ppermute | solution.py:229
  168.6 27.9 %collective-permute-start.24 = (bf16[512,768]{1,0:T(8,128)(2,1)}, bf16[512,768]{1,0:T(8,128)(2,1)}, u32[]{:S(2)}, u32[]{:S(2)}) collective-permute-start(bf16[512,768]{1,0:T(8,128)(2,1)} %collective-permute-done.15), channel_id=1, source_target_pairs={{8,0},{12,4},{9,1},{13,5},{10,2},{14,6},{11,3},{15,7}} | collective-permute-start | bytes 2359304 | tf_op jit(solution)/shard_map/ppermute | solution.py:229
  181.3 37.2 %collective-permute-start.19 = (bf16[256,1024]{1,0:T(8,128)(2,1)}, bf16[256,1024]{1,0:T(8,128)(2,1)}, u32[]{:S(2)}, u32[]{:S(2)}) collective-permute-start(bf16[256,1024]{1,0:T(8,128)(2,1)} %collective-permute-done), channel_id=1, source_target_pairs={{8,12},{12,8},{16,20},{20,16},{24,28},{28,24},{9,13},{13,9},{17,21... | collective-permute-start | bytes 1572872 | tf_op jit(solution)/shard_map/ppermute | solution.py:221
  182.7 35.8 %collective-permute-start.21 = (bf16[256,1024]{1,0:T(8,128)(2,1)}, bf16[256,1024]{1,0:T(8,128)(2,1)}, u32[]{:S(2)}, u32[]{:S(2)}) collective-permute-start(bf16[256,1024]{1,0:T(8,128)(2,1)} %collective-permute-done), channel_id=1, source_target_pairs={{8,16},{12,20},{16,24},{20,28},{9,17},{13,21},{17,25},{21,29},{10,... | collective-permute-start | bytes 1572872 | tf_op jit(solution)/shard_map/ppermute | solution.py:229
  184.2 34.3 %collective-permute-start.20 = (bf16[256,1024]{1,0:T(8,128)(2,1)}, bf16[256,1024]{1,0:T(8,128)(2,1)}, u32[]{:S(2)}, u32[]{:S(2)}) collective-permute-start(bf16[256,1024]{1,0:T(8,128)(2,1)} %collective-permute-done.1), channel_id=1, source_target_pairs={{0,4},{4,0},{8,12},{12,8},{16,20},{20,16},{1,5},{5,1},{9,13},{13,9... | collective-permute-start | bytes 1572872 | tf_op jit(solution)/shard_map/ppermute | solution.py:221
  186.1 32.4 %collective-permute-start.22 = (bf16[256,1024]{1,0:T(8,128)(2,1)}, bf16[256,1024]{1,0:T(8,128)(2,1)}, u32[]{:S(2)}, u32[]{:S(2)}) collective-permute-start(bf16[256,1024]{1,0:T(8,128)(2,1)} %collective-permute-done.1), channel_id=1, source_target_pairs={{8,0},{12,4},{16,8},{20,12},{9,1},{13,5},{17,9},{21,13},{10,2},{14... | collective-permute-start | bytes 1572872 | tf_op jit(solution)/shard_map/ppermute | solution.py:229
  218.5 19.6 %collective-permute-start.26 = (bf16[256,1024]{1,0:T(8,128)(2,1)}, bf16[256,1024]{1,0:T(8,128)(2,1)S(1)}, u32[]{:S(2)}, u32[]{:S(2)}) collective-permute-start(bf16[256,1024]{1,0:T(8,128)(2,1)} %collective-permute-done.21), channel_id=1, source_target_pairs={{16,20},{20,16},{24,28},{28,24},{17,21},{21,17},{25,29},{29,25},{1... | collective-permute-start | bytes 1572872 | tf_op jit(solution)/shard_map/ppermute | solution.py:221
  219.2 18.9 %collective-permute-start.28 = (bf16[256,1024]{1,0:T(8,128)(2,1)}, bf16[256,1024]{1,0:T(8,128)(2,1)S(1)}, u32[]{:S(2)}, u32[]{:S(2)}) collective-permute-start(bf16[256,1024]{1,0:T(8,128)(2,1)} %collective-permute-done.21), channel_id=1, source_target_pairs={{16,24},{20,28},{17,25},{21,29},{18,26},{22,30},{19,27},{23,31}} | collective-permute-start | bytes 1572872 | tf_op jit(solution)/shard_map/ppermute | solution.py:229
  219.9 18.2 %collective-permute-start.27 = (bf16[256,1024]{1,0:T(8,128)(2,1)}, bf16[256,1024]{1,0:T(8,128)(2,1)S(1)}, u32[]{:S(2)}, u32[]{:S(2)}) collective-permute-start(bf16[256,1024]{1,0:T(8,128)(2,1)} %collective-permute-done.22), channel_id=1, source_target_pairs={{0,4},{4,0},{8,12},{12,8},{1,5},{5,1},{9,13},{13,9},{2,6},{6,2},{1... | collective-permute-start | bytes 1572872 | tf_op jit(solution)/shard_map/ppermute | solution.py:221
  221.8 16.3 %collective-permute-start.29 = (bf16[256,1024]{1,0:T(8,128)(2,1)}, bf16[256,1024]{1,0:T(8,128)(2,1)S(1)}, u32[]{:S(2)}, u32[]{:S(2)}) collective-permute-start(bf16[256,1024]{1,0:T(8,128)(2,1)} %collective-permute-done.22), channel_id=1, source_target_pairs={{8,0},{12,4},{9,1},{13,5},{10,2},{14,6},{11,3},{15,7}} | collective-permute-start | bytes 1572872 | tf_op jit(solution)/shard_map/ppermute | solution.py:229
  238.1 142.2 %all-gather.18.cloned.1.call-start = ((), (), s32[]{:S(2)}) async-start(), calls=%async_computation.5 | async-start | bytes 5242880 | tf_op jit(solution)/shard_map/all_gather | solution.py:259
  245.4 15.6 %collective-permute-start.32 = (bf16[256,1024]{1,0:T(8,128)(2,1)S(1)}, bf16[256,1024]{1,0:T(8,128)(2,1)S(1)}, u32[]{:S(2)}, u32[]{:S(2)}) collective-permute-start(bf16[256,1024]{1,0:T(8,128)(2,1)S(1)} %collective-permute-done.29), channel_id=1, source_target_pairs={{0,4},{4,0},{1,5},{5,1},{2,6},{6,2},{3,7},{7,3}} | collective-permute-start | bytes 1572872 | tf_op jit(solution)/shard_map/ppermute | solution.py:221
  261.0 16.7 %collective-permute-start.36 = (bf16[512,512]{1,0:T(8,128)(2,1)}, bf16[512,512]{1,0:T(8,128)(2,1)}, u32[]{:S(2)}, u32[]{:S(2)}) collective-permute-start(bf16[512,512]{1,0:T(8,128)(2,1)} %collective-permute-done.33), channel_id=1, source_target_pairs={{8,12},{12,8},{16,20},{20,16},{24,28},{28,24},{9,13},{13,9},{17,21... | collective-permute-start | bytes 1572872 | tf_op jit(solution)/shard_map/ppermute | solution.py:221
  262.5 15.3 %collective-permute-start.38 = (bf16[512,512]{1,0:T(8,128)(2,1)}, bf16[512,512]{1,0:T(8,128)(2,1)}, u32[]{:S(2)}, u32[]{:S(2)}) collective-permute-start(bf16[512,512]{1,0:T(8,128)(2,1)} %collective-permute-done.33), channel_id=1, source_target_pairs={{8,16},{12,20},{16,24},{20,28},{9,17},{13,21},{17,25},{21,29},{10,... | collective-permute-start | bytes 1572872 | tf_op jit(solution)/shard_map/ppermute | solution.py:229
  263.9 13.8 %collective-permute-start.37 = (bf16[512,512]{1,0:T(8,128)(2,1)}, bf16[512,512]{1,0:T(8,128)(2,1)}, u32[]{:S(2)}, u32[]{:S(2)}) collective-permute-start(bf16[512,512]{1,0:T(8,128)(2,1)} %collective-permute-done.34), channel_id=1, source_target_pairs={{0,4},{4,0},{8,12},{12,8},{16,20},{20,16},{1,5},{5,1},{9,13},{13,9... | collective-permute-start | bytes 1572872 | tf_op jit(solution)/shard_map/ppermute | solution.py:221
  278.9 32.9 %collective-permute-start.46 = (bf16[256,1024]{1,0:T(8,128)(2,1)}, bf16[256,1024]{1,0:T(8,128)(2,1)S(1)}, u32[]{:S(2)}, u32[]{:S(2)}) collective-permute-start(bf16[256,1024]{1,0:T(8,128)(2,1)} %param.30), channel_id=1, source_target_pairs={{0,8},{4,12},{8,16},{12,20},{16,24},{20,28},{1,9},{5,13},{9,17},{1... | collective-permute-start | bytes 1572872 | tf_op jit(solution)/shard_map/ppermute | solution.py:229
  287.1 18.9 %collective-permute-start.42 = (bf16[512,512]{1,0:T(8,128)(2,1)}, bf16[512,512]{1,0:T(8,128)(2,1)S(1)}, u32[]{:S(2)}, u32[]{:S(2)}) collective-permute-start(bf16[512,512]{1,0:T(8,128)(2,1)} %collective-permute-done.38), channel_id=1, source_target_pairs={{16,24},{20,28},{17,25},{21,29},{18,26},{22,30},{19,27},{23,31}} | collective-permute-start | bytes 1572872 | tf_op jit(solution)/shard_map/ppermute | solution.py:229
  287.8 16.5 %collective-permute-start.41 = (bf16[512,512]{1,0:T(8,128)(2,1)}, bf16[512,512]{1,0:T(8,128)(2,1)S(1)}, u32[]{:S(2)}, u32[]{:S(2)}) collective-permute-start(bf16[512,512]{1,0:T(8,128)(2,1)} %collective-permute-done.39), channel_id=1, source_target_pairs={{0,4},{4,0},{8,12},{12,8},{1,5},{5,1},{9,13},{13,9},{2,6},{6,2},{1... | collective-permute-start | bytes 1572872 | tf_op jit(solution)/shard_map/ppermute | solution.py:221
  291.4 16.2 %collective-permute-start.43 = (bf16[512,512]{1,0:T(8,128)(2,1)}, bf16[512,512]{1,0:T(8,128)(2,1)S(1)}, u32[]{:S(2)}, u32[]{:S(2)}) collective-permute-start(bf16[512,512]{1,0:T(8,128)(2,1)} %collective-permute-done.39), channel_id=1, source_target_pairs={{8,0},{12,4},{9,1},{13,5},{10,2},{14,6},{11,3},{15,7}} | collective-permute-start | bytes 1572872 | tf_op jit(solution)/shard_map/ppermute | solution.py:229
  294.1 19.1 %collective-permute-start.47 = (bf16[256,1024]{1,0:T(8,128)(2,1)}, bf16[256,1024]{1,0:T(8,128)(2,1)S(1)}, u32[]{:S(2)}, u32[]{:S(2)}) collective-permute-start(bf16[256,1024]{1,0:T(8,128)(2,1)} %param.30), channel_id=1, source_target_pairs={{8,0},{12,4},{16,8},{20,12},{24,16},{28,20},{9,1},{13,5},{17,9},{2... | collective-permute-start | bytes 1572872 | tf_op jit(solution)/shard_map/ppermute | solution.py:229
  308.3 15.3 %collective-permute-start.45 = (bf16[512,512]{1,0:T(8,128)(2,1)S(1)}, bf16[512,512]{1,0:T(8,128)(2,1)S(1)}, u32[]{:S(2)}, u32[]{:S(2)}) collective-permute-start(bf16[512,512]{1,0:T(8,128)(2,1)S(1)} %collective-permute-done.43), channel_id=1, source_target_pairs={{0,4},{4,0},{1,5},{5,1},{2,6},{6,2},{3,7},{7,3}} | collective-permute-start | bytes 1572872 | tf_op jit(solution)/shard_map/ppermute | solution.py:221
  324.3 14.0 %collective-permute-start.51 = (bf16[256,1024]{1,0:T(8,128)(2,1)S(1)}, bf16[256,1024]{1,0:T(8,128)(2,1)}, u32[]{:S(2)}, u32[]{:S(2)}) collective-permute-start(bf16[256,1024]{1,0:T(8,128)(2,1)S(1)} %collective-permute-done.46), channel_id=1, source_target_pairs={{8,16},{12,20},{16,24},{20,28},{9,17},{13,21},{17,25},{21,29},{10,... | collective-permute-start | bytes 1572872 | tf_op jit(solution)/shard_map/ppermute | solution.py:229
  341.1 22.4 %collective-permute-start.53 = (bf16[256,1024]{1,0:T(8,128)(2,1)}, bf16[256,1024]{1,0:T(8,128)(2,1)}, u32[]{:S(2)}, u32[]{:S(2)}) collective-permute-start(bf16[256,1024]{1,0:T(8,128)(2,1)} %collective-permute-done.51), channel_id=1, source_target_pairs={{16,20},{20,16},{24,28},{28,24},{17,21},{21,17},{25,29},{29,25},{1... | collective-permute-start | bytes 1572872 | tf_op jit(solution)/shard_map/ppermute | solution.py:221
  342.5 21.0 %collective-permute-start.55 = (bf16[256,1024]{1,0:T(8,128)(2,1)}, bf16[256,1024]{1,0:T(8,128)(2,1)}, u32[]{:S(2)}, u32[]{:S(2)}) collective-permute-start(bf16[256,1024]{1,0:T(8,128)(2,1)} %collective-permute-done.51), channel_id=1, source_target_pairs={{16,24},{20,28},{17,25},{21,29},{18,26},{22,30},{19,27},{23,31}} | collective-permute-start | bytes 1572872 | tf_op jit(solution)/shard_map/ppermute | solution.py:229
  344.0 19.5 %collective-permute-start.54 = (bf16[256,1024]{1,0:T(8,128)(2,1)}, bf16[256,1024]{1,0:T(8,128)(2,1)}, u32[]{:S(2)}, u32[]{:S(2)}) collective-permute-start(bf16[256,1024]{1,0:T(8,128)(2,1)} %collective-permute-done.52), channel_id=1, source_target_pairs={{0,4},{4,0},{8,12},{12,8},{1,5},{5,1},{9,13},{13,9},{2,6},{6,2},{1... | collective-permute-start | bytes 1572872 | tf_op jit(solution)/shard_map/ppermute | solution.py:221
  346.1 17.4 %collective-permute-start.56 = (bf16[256,1024]{1,0:T(8,128)(2,1)}, bf16[256,1024]{1,0:T(8,128)(2,1)}, u32[]{:S(2)}, u32[]{:S(2)}) collective-permute-start(bf16[256,1024]{1,0:T(8,128)(2,1)} %collective-permute-done.52), channel_id=1, source_target_pairs={{8,0},{12,4},{9,1},{13,5},{10,2},{14,6},{11,3},{15,7}} | collective-permute-start | bytes 1572872 | tf_op jit(solution)/shard_map/ppermute | solution.py:229
  364.4 14.2 %collective-permute-start.58 = (bf16[256,1024]{1,0:T(8,128)(2,1)}, bf16[256,1024]{1,0:T(8,128)(2,1)S(1)}, u32[]{:S(2)}, u32[]{:S(2)}) collective-permute-start(bf16[256,1024]{1,0:T(8,128)(2,1)} %collective-permute-done.56), channel_id=1, source_target_pairs={{0,4},{4,0},{1,5},{5,1},{2,6},{6,2},{3,7},{7,3}} | collective-permute-start | bytes 1572872 | tf_op jit(solution)/shard_map/ppermute | solution.py:221
  (72 other events, 875.2 us)
Sparse Core Ops, SparseCore 0:
  36.1 36.0 all-gather.11
  94.5 32.5 all-gather.13
  238.3 20.8 all-gather.15
  279.0 40.4 all-gather.17

commit v3 on v2

v3 whole, which is shorter than its diff:
```python
import functools
import math

import jax
import jax.numpy as jnp
from jax import lax
from jax.experimental import pallas as pl
from jax.experimental.pallas import tpu as pltpu
from jax.sharding import PartitionSpec as P

HD = 64
EPSILON = 1e-06
NEG = -1e30
LANES = 128
F32 = jnp.float32
BF16 = jnp.bfloat16


def dot(a, b):
    return jnp.dot(a, b, preferred_element_type=F32)


def fence(*values):
    return lax.optimization_barrier(values)


def take_kernel(axis, index_ref, in_ref, out_ref):
    lead = (slice(None),) * axis
    for i in range(index_ref.shape[0]):
        out_ref[lead + (i,)] = in_ref[lead + (index_ref[i],)]


def take_rows(rows, index, axis):
    shape = rows.shape[:axis] + index.shape + rows.shape[axis + 1 :]
    return pl.pallas_call(
        functools.partial(take_kernel, axis),
        in_specs=[
            pl.BlockSpec(memory_space=pltpu.SMEM),
            pl.BlockSpec(memory_space=pltpu.VMEM),
        ],
        out_specs=pl.BlockSpec(memory_space=pltpu.VMEM),
        out_shape=jax.ShapeDtypeStruct(shape, rows.dtype),
        compiler_params=pltpu.CompilerParams(vmem_limit_bytes=16 << 20),
        cost_estimate=pl.CostEstimate(
            flops=0, bytes_accessed=4 * math.prod(shape), transcendentals=0
        ),
    )(index, rows)


def enc_kernel(width, span, qkv_ref, live_ref, out_ref):
    own = lax.broadcasted_iota(jnp.int32, (LANES, LANES), 0) // span
    other = lax.broadcasted_iota(jnp.int32, (LANES, LANES), 1) // span
    same = own == other
    ones = jnp.ones((LANES, HD), BF16)
    for start in range(0, qkv_ref.shape[0], LANES):
        rows = slice(start, start + LANES)
        bias = jnp.where(same & (live_ref[:, rows] > 0), 0.0, NEG)
        for head in range(width // HD):
            q, k, v = (
                qkv_ref[rows, part * width + head * HD : part * width + (head + 1) * HD]
                for part in range(3)
            )
            scores = lax.dot_general(q, k, (((1,), (1,)), ((), ())), preferred_element_type=F32)
            scores = scores * (1.0 / math.sqrt(HD)) + bias
            weights = jnp.exp(scores - jnp.max(scores, axis=1, keepdims=True)).astype(BF16)
            context = dot(weights, v) / dot(weights, ones)
            out_ref[rows, head * HD : (head + 1) * HD] = context.astype(BF16)


def enc_attention(qkv, live, span):
    rows, width = qkv.shape[0], qkv.shape[1] // 3
    block = 2 * LANES
    return pl.pallas_call(
        functools.partial(enc_kernel, width, span),
        grid=(rows // block,),
        in_specs=[
            pl.BlockSpec((block, 3 * width), lambda i: (i, 0)),
            pl.BlockSpec((1, block), lambda i: (0, i)),
        ],
        out_specs=pl.BlockSpec((block, width), lambda i: (i, 0)),
        out_shape=jax.ShapeDtypeStruct((rows, width), BF16),
        cost_estimate=pl.CostEstimate(
            flops=4 * rows * LANES * width,
            bytes_accessed=8 * rows * width,
            transcendentals=rows * LANES * (width // HD),
        ),
    )(qkv, live)


def cross_kernel(span, query_n, scores_ref, scale_ref, live_ref, values_ref, out_ref):
    pairs = scores_ref.shape[0]
    width = values_ref.shape[1]
    cands = LANES // span
    heads = pairs // query_n
    cand = lax.broadcasted_iota(jnp.int32, (pairs, LANES), 1) // span
    head = lax.broadcasted_iota(jnp.int32, (query_n, width), 1) // HD
    for at in range(values_ref.shape[0] // LANES):
        rows = slice(at * LANES, (at + 1) * LANES)
        scores = scores_ref[:, rows] * (scale_ref[:, rows] * (1.0 / math.sqrt(HD)))
        live = live_ref[:, rows] > 0
        scores = jnp.concatenate(
            [jnp.where((cand == c) & live, scores, NEG) for c in range(cands)], axis=0
        )
        weights = jnp.exp(scores - jnp.max(scores, axis=1, keepdims=True))
        weights = (weights / jnp.sum(weights, axis=1, keepdims=True)).astype(BF16)
        context = dot(weights, values_ref[rows])
        for c in range(cands):
            total = jnp.zeros((query_n, width), F32)
            for h in range(heads):
                start = (c * heads + h) * query_n
                total = total + jnp.where(head == h, context[start : start + query_n], 0.0)
            start = (at * cands + c) * query_n
            out_ref[start : start + query_n] = total.astype(BF16)


def cross_attention(scores, scale, live, values, span, query_n):
    pairs, rows = scores.shape
    width = values.shape[1]
    return pl.pallas_call(
        functools.partial(cross_kernel, span, query_n),
        in_specs=[pl.BlockSpec(memory_space=pltpu.VMEM)] * 4,
        out_specs=pl.BlockSpec(memory_space=pltpu.VMEM),
        out_shape=jax.ShapeDtypeStruct((rows // span * query_n, width), BF16),
        compiler_params=pltpu.CompilerParams(vmem_limit_bytes=16 << 20),
        cost_estimate=pl.CostEstimate(
            flops=4 * rows * pairs * width,
            bytes_accessed=2 * rows * width + 4 * pairs * rows,
            transcendentals=rows * pairs * (LANES // span),
        ),
    )(scores, scale, live, values)


def direct_attend(query, keys, values, valid):
    group_n, columns = query.shape
    key_n, head_n = keys.shape[1], columns // HD
    query_heads = query.reshape(group_n, 1, head_n, HD)
    key_heads = keys.reshape(group_n, key_n, head_n, HD)
    value_heads = values.reshape(group_n, key_n, head_n, HD)
    scores = jnp.einsum(
        "bqhd,bkhd->bhqk", query_heads, key_heads, preferred_element_type=F32
    ) / math.sqrt(HD)
    scores = jnp.where(valid[:, None, None, :], scores, NEG)
    weights = jax.nn.softmax(scores, axis=-1).astype(BF16)
    context = jnp.einsum("bhqk,bkhd->bqhd", weights, value_heads, preferred_element_type=F32)
    return context.astype(BF16).reshape(group_n, columns)


def shards(
    hidden,
    wq_direct,
    wkv_direct,
    wo_direct,
    kv_cache,
    parent,
    lengths,
    cand_embed,
    source,
    enc_qkv,
    enc_out,
    cross_q,
    cross_kv,
    cross_out,
    w_direct,
    w_channel,
    target_shard,
):
    dp_n, mp_n = lax.axis_size("dp"), lax.axis_size("mp")
    side_n = dp_n // mp_n
    line_n = dp_n // side_n
    me, own_mp = lax.axis_index("dp"), lax.axis_index("mp")
    side, line = me % side_n, me // side_n
    beam_n, features = hidden.shape
    span, query_n = kv_cache.shape[2], source.shape[1]
    local_width = cand_embed.shape[2]
    by_pairs = line_n == 4
    inner = (line == 1) | (line == 2)

    def move(a, pairs):
        return lax.ppermute(
            a, "dp", [(s * side_n + i, t * side_n + i) for s, t in pairs for i in range(side_n)]
        )

    def swap(a):
        return lax.ppermute(
            a, "dp", [(i, i - i % side_n + (i + 1) % side_n) for i in range(dp_n)]
        )

    def near(store):
        if not by_pairs:
            return []
        return [
            (store, "next", move(store["own"], [(0, 1), (1, 0), (2, 3), (3, 2)])),
            (store, "inner", move(store["own"], [(1, 2), (2, 1)])),
        ]

    def far(store):
        if not by_pairs:
            lines = [[k * side_n + i for k in range(line_n)] for i in range(side_n)]
            return [(store, "far", lax.all_gather(store["own"], "dp", axis_index_groups=lines))]
        return [
            (store, "outer", move(store["inner"], [(1, 0), (2, 3)])),
            (store, "inner_last", move(store["next"], [(1, 2), (2, 1)])),
            (store, "outer_last", move(store["next"], [(1, 3), (2, 0)])),
        ]

    def join(store):
        if by_pairs:
            store["far"] = jnp.stack(
                [
                    jnp.where(inner, store["inner"], store["outer"]),
                    jnp.where(inner, store["inner_last"], store["outer_last"]),
                ]
            )

    def cross(store, crossed, *keys):
        return [(crossed, key, swap(store[key])) for key in keys if key in store]

    def settle(made, held, *values):
        places = [(store, key) for store, key, _ in made]
        places += [(store, key) for store, key in held if key in store]
        arrays = [a for _, _, a in made]
        arrays += [store[key] for store, key in held if key in store]
        arrays, values = fence(arrays, values)
        for (store, key), a in zip(places, arrays, strict=True):
            store[key] = a
        return values

    def slots_of(store):
        if not by_pairs:
            return [(k, store["far"][k]) for k in range(line_n)]
        low = line < 2
        return [
            (line, store["own"]),
            (line ^ 1, store["next"]),
        ] + [
            (jnp.where(low, 2 + k, 1 - k), store["far"][k]) for k in range(2) if "far" in store
        ]

    def ordered(own, got, axis):
        return jnp.where(
            side == 0, jnp.concatenate([own, got], axis), jnp.concatenate([got, own], axis)
        )

    def slots_across(store, crossed):
        pairs = zip(slots_of(store), slots_of(crossed), strict=True)
        return [(place, ordered(own, got, 0)) for (place, own), (_, got) in pairs]

    def side_part(a, at):
        width = a.shape[-1] // side_n
        return lax.dynamic_slice_in_dim(a, at * width, width, a.ndim - 1)

    def spread_dot(blocks, slots, total=None):
        for place, slot in slots:
            part = dot(lax.dynamic_index_in_dim(blocks, place, 0, keepdims=False), slot)
            total = part if total is None else total + part
        return total

    def everyone(a):
        return lax.all_gather(a, "mp", axis=0)

    def exchange(a):
        return lax.all_to_all(a, "dp", split_axis=0, concat_axis=0, tiled=True)

    positions = jnp.arange(span, dtype=jnp.int32)

    out, out_other = {"own": enc_out}, {}
    val, val_other = {"own": cross_kv[1]}, {}
    last, last_other = {"own": cross_out}, {}
    qkv_own = jnp.concatenate([side_part(w, side) for w in enc_qkv], axis=1)
    qkv_got = swap(jnp.concatenate([side_part(w, 1 - side) for w in enc_qkv], axis=1))
    out_near = near(out)
    last_near = near(last)
    tokens = take_rows(cand_embed, parent, 0).reshape(beam_n * span, local_width)
    source_rows = lax.all_gather(source[0], "mp", axis=1, tiled=True)
    source_cut = source_rows.reshape(query_n, dp_n, -1).transpose(1, 0, 2)
    source_cut = exchange(source_cut)
    qkv_got, tokens, source_cut = settle(out_near, [], qkv_got, tokens, source_cut)

    both = jnp.zeros((side_n,) + qkv_own.shape, BF16)
    both = lax.dynamic_update_index_in_dim(both, qkv_own, side, 0)
    both = lax.dynamic_update_index_in_dim(both, qkv_got, 1 - side, 0)
    qkv = {"own": both.reshape(-1, both.shape[2])}
    qkv_near = near(qkv)
    tokens_got = swap(tokens)
    own_blocks = everyone(tokens)
    cache = take_rows(kv_cache, parent, 1)
    partial = exchange(dot(source_cut.reshape(dp_n * query_n, -1), cross_q))
    query_new = dot(hidden, wq_direct).astype(BF16)
    key_new = dot(hidden, wkv_direct[0]).astype(BF16)
    value_new = dot(hidden, wkv_direct[1]).astype(BF16)
    bases = [(store, "own") for store in (out, val, last)]
    tokens_got, partial, cache, query_new, key_new, value_new = settle(
        qkv_near + last_near, bases, tokens_got, partial, cache, query_new, key_new, value_new
    )

    qkv_far = far(qkv)
    got_blocks = everyone(tokens_got)
    lengths_got = swap(lengths)
    (lengths_got,) = settle(cross(out, out_other, "own", "next"), bases, lengths_got)
    queries = jnp.sum(partial.reshape(dp_n, query_n, -1), axis=0).astype(BF16)
    queries = exchange(jnp.broadcast_to(queries, (dp_n,) + queries.shape).reshape(dp_n * query_n, -1))
    (queries,) = settle(
        cross(val, val_other, "own") + cross(last, last_other, "own"), [(last, "next")], queries
    )
    last_cross = cross(last, last_other, "next")
    head_n = queries.shape[1] // HD
    mixed = jnp.einsum(
        "rhc,khc->rhk",
        queries.reshape(-1, head_n, HD),
        cross_kv[0].reshape(-1, head_n, HD),
        preferred_element_type=F32,
    ).astype(BF16)
    depth = mixed.shape[2]
    pairs = head_n * query_n
    mixed = mixed.reshape(dp_n, query_n, head_n, depth).transpose(0, 2, 1, 3)
    mixed = exchange(mixed.reshape(dp_n, pairs, depth))
    all_keys = jnp.concatenate([cache[0], key_new[:, None]], axis=1)
    all_values = jnp.concatenate([cache[1], value_new[:, None]], axis=1)
    cache_valid = jnp.concatenate(
        [positions[None, :] < lengths[:, None], jnp.ones((beam_n, 1), dtype=bool)], axis=1
    )
    context = direct_attend(query_new, all_keys, all_values, cache_valid)
    context = lax.all_gather(context, "mp", axis=1, tiled=True)
    own_start = own_mp * local_width
    hidden_share = lax.dynamic_slice_in_dim(hidden, own_start, local_width, 1).astype(F32)
    new_state = hidden_share + dot(context, wo_direct)
    squares, direct_dot = lax.psum(
        (
            jnp.sum(new_state * new_state, axis=1),
            jnp.sum(new_state * w_direct.astype(F32), axis=1),
        ),
        "mp",
    )
    direct_score = direct_dot / jnp.sqrt(squares / features + EPSILON)
    new_state = new_state.astype(BF16)
    early = slots_of(qkv)[:2] if by_pairs else []
    rows_got = spread_dot(got_blocks, early)
    rows_own = spread_dot(own_blocks, early)
    new_state, direct_score, own_blocks, got_blocks, rows_got, rows_own = settle(
        qkv_far + last_cross,
        [(out, "inner"), (out, "next"), (val, "own")],
        new_state,
        direct_score,
        own_blocks,
        got_blocks,
        rows_got,
        rows_own,
    )

    def live_of(lens):
        return (positions[None, :] < lens[:, None]).astype(jnp.int32).reshape(1, -1)

    out_far = far(out)
    join(qkv)
    qkv_slots = slots_of(qkv)[len(early) :]
    rows_got = spread_dot(got_blocks, qkv_slots, rows_got).astype(BF16)
    context_got = enc_attention(rows_got, live_of(lengths_got), span)
    live = live_of(lengths)
    rows_own = spread_dot(own_blocks, qkv_slots, rows_own).astype(BF16)
    context_own = enc_attention(rows_own, live, span)
    context_got, context_own, mixed = settle(
        out_far, [(val, "own")], context_got, context_own, mixed
    )

    join(out)
    context_got = swap(context_got)
    out_cross = cross(out, out_other, "far")
    enc_context = ordered(context_own, context_got, 1)
    (enc_context,) = settle(near(val), [], enc_context)
    enc_blocks = everyone(enc_context)
    val_far = far(val)
    settle(out_cross, [(val, "next")])
    val_cross = cross(val, val_other, "next")
    (enc_blocks,) = fence(enc_blocks)
    summed = tokens.astype(F32) + spread_dot(enc_blocks, slots_across(out, out_other))
    summed_sent = summed.astype(BF16)
    summed, summed_sent = settle(
        val_far, [(last, "inner"), (last, "next")], summed, summed_sent
    )
    memory_blocks = everyone(summed_sent)
    join(val)
    val_cross += cross(val, val_other, "far")
    last_far = far(last)
    enc_squares = lax.psum(jnp.sum(summed * summed, axis=1), "mp")
    scale = 1.0 / jnp.sqrt(enc_squares / features + EPSILON)
    (scale,) = settle(val_cross + last_far, [], scale)
    join(last)
    last_cross = cross(last, last_other, "far")
    (memory_blocks,) = fence(memory_blocks)

    mixed = mixed.reshape(line_n, side_n, pairs, depth).transpose(0, 2, 1, 3)
    mixed = mixed.reshape(line_n, pairs, side_n * depth)

    scores = None
    for k in range(line_n):
        part = lax.dot_general(
            mixed[k], memory_blocks[k], (((1,), (1,)), ((), ())), preferred_element_type=F32
        )
        scores = part if scores is None else scores + part
    cross_values = spread_dot(memory_blocks, slots_across(val, val_other))
    cross_values = (cross_values * scale[:, None]).astype(BF16)
    cross_context = cross_attention(scores, scale[None, :], live, cross_values, span, query_n)
    cross_blocks = everyone(cross_context)
    (cross_blocks,) = settle(last_cross, [], cross_blocks)
    update = spread_dot(cross_blocks, slots_across(last, last_other))
    decoded = source.astype(F32) + update.reshape(beam_n, query_n, -1)
    dec_squares, dec_dot = lax.psum(
        (
            jnp.sum(decoded * decoded, axis=-1).reshape(1, -1),
            jnp.sum(decoded * w_channel.astype(F32), axis=-1).reshape(1, -1),
        ),
        "mp",
    )
    position_score = dec_dot / jnp.sqrt(dec_squares / features + EPSILON)
    own_channel = jnp.mean(position_score.reshape(beam_n, query_n), axis=1)
    shard_ids = lax.broadcasted_iota(jnp.int32, (dp_n, beam_n), 0)
    sent_scores = jnp.where(shard_ids == target_shard[None], own_channel[None], 0.0)
    return (new_state, direct_score + own_channel, jnp.sum(exchange(sent_scores), axis=0))


def solution(mesh):
    in_specs = (
        P("dp", None),
        P(None, "mp"),
        P(None, None, "mp"),
        P(None, "mp"),
        P(None, "dp", None, "mp"),
        P("dp"),
        P("dp"),
        P("dp", None, "mp"),
        P("dp", None, "mp"),
        P(None, "dp", "mp"),
        P("dp", "mp"),
        P("dp", "mp"),
        P(None, "dp", "mp"),
        P("dp", "mp"),
        P("mp"),
        P("mp"),
        P("dp"),
    )
    out_specs = (P("dp", "mp"), P("dp"), P("dp"))
    return jax.shard_map(shards, mesh=mesh, in_specs=in_specs, out_specs=out_specs, check_vma=False)
```

time: 449 us -> 359 us (0.80)
  starting transfers between devices: 116 us -> 68.9 us
  blocking collectives: 84.2 us -> 48.3 us
  other arithmetic: 35 us -> 17.1 us
  matrix products: 44.9 us -> 58.7 us
    ppermute x59 -> x33, starting transfers between devices: 105 us -> 49.4 us  [the longest x20 31.6 us: move(): lax.ppermute(a, 'dp', [(s * side_n + i, t * side_n + i) for s, t in pairs...]
    ppermute x59 -> x33, waiting for transfers between devices: 109 us -> 75.9 us  [the longest x13 46.1 us: swap(): lax.ppermute(a, 'dp', [(i, i - i % side_n + (i + 1) % side_n) for i in ra...]
    all_to_all x2 -> x4, waiting for transfers between devices: 10 us -> 39.4 us  [exchange(): return lax.all_to_all(a, 'dp', split_axis=0, concat_axis=0, tiled=True)]
    psum x1 -> x2, blocking collectives: 37.8 us -> 12.4 us  [the longest x1 6.67 us: shards(): lax.psum((jnp.sum(new_state * new_state, axis=1), jnp.sum(new_state * w_d...]
    select_n x24 -> x7, other arithmetic: 28.9 us -> 6.86 us  [the longest x3 3.52 us: join(): jnp.where(inner, store['inner_last'], store['outer_last'])]
    unnamed x1 -> x0, blocking collectives: 20.4 us -> none
    dot_general x25, matrix products: 41.7 us -> 54.1 us  [dot(): return jnp.dot(a, b, preferred_element_type=F32)]
    all_to_all x0 -> x1, blocking collectives: none -> 11.9 us  [exchange(): return lax.all_to_all(a, 'dp', split_axis=0, concat_axis=0, tiled=True)]
  transfers between devices with their start and end apart: 65 -> 41, of which waited for: 21 -> 10; matrix products, arithmetic and copies ran while one was open for 19% -> 24% of each run, Pallas kernels for 2% -> 3%
where the time goes in v3:
time: 359 us; the launch traced here: 357 us
  waiting for transfers between devices  116 us (32%)
  starting transfers between devices  68.9 us (19%)
  matrix products  58.7 us (16%)
  blocking collectives  48.3 us (13%)
  local copies, waits for them, and re-layouts  23.3 us (6%)
  other arithmetic  17.1 us (5%)
  between operations  14.6 us (4%)
  Pallas kernels  10.6 us (3%)
    dot_general x25, matrix products, dot(): return jnp.dot(a, b, preferred_element_type=F32)  54.1 us
    ppermute x13, waiting for transfers between devices, swap(): lax.ppermute(a, 'dp', [(i, i - i % side_n + (i + 1) % side_n) for i in ra...  46.1 us
    all_to_all x4, waiting for transfers between devices, exchange(): return lax.all_to_all(a, 'dp', split_axis=0, concat_axis=0, tiled=True)  39.4 us
    ppermute x20, starting transfers between devices, move(): lax.ppermute(a, 'dp', [(s * side_n + i, t * side_n + i) for s, t in pairs...  31.6 us
    ppermute x20, waiting for transfers between devices, move(): lax.ppermute(a, 'dp', [(s * side_n + i, t * side_n + i) for s, t in pairs...  29.8 us
    all_to_all x4, starting transfers between devices, exchange(): return lax.all_to_all(a, 'dp', split_axis=0, concat_axis=0, tiled=True)  19.2 us
    ppermute x13, starting transfers between devices, swap(): lax.ppermute(a, 'dp', [(i, i - i % side_n + (i + 1) % side_n) for i in ra...  17.8 us
    all_to_all x1, blocking collectives, exchange(): return lax.all_to_all(a, 'dp', split_axis=0, concat_axis=0, tiled=True)  11.9 us
  transfers between devices with their start and end apart: 41, of which 10 were waited for; matrix products, arithmetic and copies ran while one was open for 24% of the time, Pallas kernels for 3%

profile of v3, /device:TPU:0, one launch (start us, length us, event | category | flops | bytes accessed | tf_op | source)
XLA Modules:
  0.0 357.4 jit_solution(8115608618866494917)
XLA Ops:
  10.6 2.9 collective-permute-start.2
  16.6 5.7 %all-gather = bf16[1,8,4096]{2,1,0:T(8,128)(2,1)} all-gather(bf16[1,8,1024]{2,1,0:T(8,128)(2,1)S(1)} %copy-done.27), channel_id=2, replica_groups=mesh['dp'=8,'mp'=4] {'mp'}, dimensions={2}, use_global_device_ids=true | all-gather | bytes 81920 | tf_op jit(solution)/shard_map/all_gather | solution.py:274
  22.3 4.9 %all-to-all-start = ((bf16[8,8,512]{2,1,0:T(8,128)(2,1)}), bf16[8,8,512]{2,1,0:T(8,128)(2,1)S(1)}, u32[]{:S(2)}, u32[]{:S(2)}) async-start(bf16[8,8,512]{2,1,0:T(8,128)(2,1)} %bitcast.9), calls=%async_computation | async-start | bytes 131072 | tf_op jit(solution)/shard_map/all_to_all | solution.py:262
  28.8 5.2 %all-to-all-done = bf16[8,8,512]{2,1,0:T(8,128)(2,1)S(1)} async-done(((bf16[8,8,512]{2,1,0:T(8,128)(2,1)}), bf16[8,8,512]{2,1,0:T(8,128)(2,1)S(1)}, u32[]{:S(2)}, u32[]{:S(2)}) %all-to-all-start) | async-done | bytes 65568 | tf_op jit(solution)/shard_map/all_to_all | solution.py:262
  37.5 2.0 collective-permute-start.4
  39.5 2.7 collective-permute-start.5
  43.7 2.8 fusion.19
  51.7 4.2 %all-to-all-start.1 = ((f32[8,8,512]{2,1,0:T(8,128)}), f32[8,8,512]{2,1,0:T(8,128)S(1)}, u32[]{:S(2)}, u32[]{:S(2)}) async-start(f32[8,8,512]{2,1,0:T(8,128)} %fusion.144), calls=%async_computation.1 | async-start | bytes 262144 | tf_op jit(solution)/shard_map/all_to_all | solution.py:262
  55.9 2.1 fusion.202
  58.0 26.7 %collective-permute-done.5 = bf16[256,1024]{1,0:T(8,128)(2,1)} collective-permute-done((bf16[256,1024]{1,0:T(8,128)(2,1)}, bf16[256,1024]{1,0:T(8,128)(2,1)}, u32[]{:S(2)}, u32[]{:S(2)}) %collective-permute-start.5) | collective-permute-done | bytes 524320 | tf_op jit(solution)/shard_map/ppermute | solution.py:179
  84.8 5.1 %all-to-all-done.1 = f32[8,8,512]{2,1,0:T(8,128)S(1)} async-done(((f32[8,8,512]{2,1,0:T(8,128)}), f32[8,8,512]{2,1,0:T(8,128)S(1)}, u32[]{:S(2)}, u32[]{:S(2)}) %all-to-all-start.1) | async-done | bytes 131104 | tf_op jit(solution)/shard_map/all_to_all | solution.py:262
  96.1 1.9 collective-permute-start.9
  101.5 2.4 concatenate.105
  107.8 1.7 fusion.8
  109.6 5.6 %all_gather.37 = bf16[16,2048]{1,0:T(8,128)(2,1)S(1)} all-gather(bf16[16,512]{1,0:T(8,128)(2,1)S(1)} %reshape.231), channel_id=1, replica_groups=mesh['dp'=8,'mp'=4] {'mp'}, dimensions={1}, use_global_device_ids=true | all-gather | bytes 81920 | tf_op jit(solution)/shard_map/all_gather | solution.py:323
  115.8 6.4 %all-to-all-start.2 = ((bf16[8,8,512]{2,1,0:T(8,128)(2,1)}), bf16[8,8,512]{2,1,0:T(8,128)(2,1)S(1)}, u32[]{:S(2)}, u32[]{:S(2)}) async-start(bf16[8,8,512]{2,1,0:T(8,128)(2,1)} %broadcast_in_dim.59), calls=%async_computation.2 | async-start | bytes 131072 | tf_op jit(solution)/shard_map/all_to_all | solution.py:262
  123.5 2.1 collective-permute-start.14
  125.7 3.6 multiply_reduce_fusion.3
  129.3 6.7 %all-reduce.2 = (f32[16]{0:T(128)S(1)}, f32[16]{0:T(128)S(1)}) all-reduce(f32[16]{0:T(128)S(1)} %get-tuple-element.142, f32[16]{0:T(128)S(1)} %get-tuple-element.141), channel_id=1, replica_groups=mesh['dp'=8,'mp'=4] {'mp'}, use_global_device_ids=true, to_apply=%region_4.5 | all-reduce | flops 32 | bytes 256 | tf_op jit(solution)/shard_map/psum | solution.py:327
  137.3 29.1 %all-to-all-done.2 = bf16[8,8,512]{2,1,0:T(8,128)(2,1)S(1)} async-done(((bf16[8,8,512]{2,1,0:T(8,128)(2,1)}), bf16[8,8,512]{2,1,0:T(8,128)(2,1)S(1)}, u32[]{:S(2)}, u32[]{:S(2)}) %all-to-all-start.2) | async-done | bytes 65568 | tf_op jit(solution)/shard_map/all_to_all | solution.py:262
  168.8 3.7 %all-to-all-start.3 = ((bf16[8,64,512]{2,1,0:T(8,128)(2,1)}), bf16[8,64,512]{2,1,0:T(8,128)(2,1)S(1)}, u32[]{:S(2)}, u32[]{:S(2)}) async-start(bf16[8,64,512]{2,1,0:T(8,128)(2,1)} %bitcast.208), calls=%async_computation.3 | async-start | bytes 1048576 | tf_op jit(solution)/shard_map/all_to_all | solution.py:262
  172.8 2.7 fusion.110
  175.5 3.9 %convolution_add_fusion = f32[512,768]{1,0:T(8,128)} fusion(f32[512,768]{1,0:T(8,128)S(1)} %fusion.110, bf16[1024,768]{1,0:T(8,128)(2,1)} %collective-permute-done.3, bf16[4,512,1024]{2,1,0:T(8,128)(2,1)} %bitcast.241, s32[]{:T(128)S(6)} %select_n.205), kind=kOutput, calls=%fused_computation.14 | convolution fusion | flops 805699584 | bytes 5767172 | tf_op jit(solution)/shard_map/dot_general | solution.py:20
  179.4 2.9 fusion.113
  182.4 3.7 %convolution_add_fusion.1 = f32[512,768]{1,0:T(8,128)} fusion(f32[512,768]{1,0:T(8,128)S(1)} %fusion.113, bf16[1024,768]{1,0:T(8,128)(2,1)} %collective-permute-done.3, bf16[4,512,1024]{2,1,0:T(8,128)(2,1)S(1)} %bitcast.246, s32[]{:T(128)S(6)} %select_n.205), kind=kOutput, calls=%fused_computation.15 | convolution fusion | flops 805699584 | bytes 5767172 | tf_op jit(solution)/shard_map/dot_general | solution.py:20
  190.3 2.4 fusion.101
  192.8 2.0 add_convert_fusion.qkv_ref
  194.7 3.6 %fusion.107 = f32[512,768]{1,0:T(8,128)} fusion(bf16[4,512,1024]{2,1,0:T(8,128)(2,1)S(1)} %bitcast.247, s32[]{:T(128)S(6)} %select_n.207, bf16[1024,768]{1,0:T(8,128)(2,1)} %collective-permute-done.4, bf16[1024,768]{1,0:T(8,128)(2,1)} %collective-permute-done.8, pred[]{:T(512)S(6)} %or.5), kind=kOutput, calls=%fused_computation.140 | convolution fusion | flops 806092800 | bytes 5767173 | tf_op jit(solution)/shard_map/dot_general | solution.py:20
  198.3 3.8 %shard_map.187 = bf16[512,256]{1,0:T(8,128)(2,1)} custom-call(bf16[512,768]{1,0:T(8,128)(2,1)} %add_convert_fusion.qkv_ref, s32[1,512]{1,0:T(1,128)} %reshape.240.live_ref), custom_call_target="tpu_custom_call" | custom-call | flops 67108864 | bytes 1048576 | tf_op jit(solution)/shard_map/pallas_call | solution.py:73
  202.1 4.1 %add_convert_fusion.1.qkv_ref = bf16[512,768]{1,0:T(8,128)(2,1)} fusion(f32[512,768]{1,0:T(8,128)} %convolution_add_fusion.1, f32[512,768]{1,0:T(8,128)} %fusion.107, bf16[4,512,1024]{2,1,0:T(8,128)(2,1)} %bitcast.245, s32[]{:T(128)S(6)} %select_n.210, bf16[1024,768]{1,0:T(8,128)(2,1)} %collective-permute-done.9, ...), kind=kOutput, calls=%fused_computation.11 | convolution fusion | flops 807272448 | bytes 8126469 | tf_op jit(solution)/shard_map/dot_general | solution.py:20
  206.2 3.8 %shard_map.186 = bf16[512,256]{1,0:T(8,128)(2,1)} custom-call(bf16[512,768]{1,0:T(8,128)(2,1)} %add_convert_fusion.1.qkv_ref, s32[1,512]{1,0:T(1,128)} %reshape.239.live_ref), custom_call_target="tpu_custom_call" | custom-call | flops 67108864 | bytes 1048576 | tf_op jit(solution)/shard_map/pallas_call | solution.py:73
  210.0 3.0 collective-permute-done.17
  213.0 4.6 %collective-permute-start.20 = (bf16[512,512]{1,0:T(8,128)(2,1)}, bf16[512,512]{1,0:T(8,128)(2,1)}, u32[]{:S(2)}, u32[]{:S(2)}) collective-permute-start(bf16[512,512]{1,0:T(8,128)(2,1)} %get-tuple-element.105), channel_id=1, source_target_pairs={{0,8},{4,12},{8,0},{12,4},{16,24},{20,28},{24,16},{28,20},{1,9},{5... | collective-permute-start | bytes 1572872 | tf_op jit(solution)/shard_map/ppermute | solution.py:179
  220.5 6.1 %collective-permute-done.22 = bf16[512,256]{1,0:T(8,128)(2,1)S(1)} collective-permute-done((bf16[512,256]{1,0:T(8,128)(2,1)}, bf16[512,256]{1,0:T(8,128)(2,1)S(1)}, u32[]{:S(2)}, u32[]{:S(2)}) %collective-permute-start.22) | collective-permute-done | bytes 262176 | tf_op jit(solution)/shard_map/ppermute | solution.py:184
  235.9 12.2 %collective-permute-done.26 = bf16[2,256,1024]{2,1,0:T(8,128)(2,1)S(1)} collective-permute-done((bf16[2,256,1024]{2,1,0:T(8,128)(2,1)S(1)}, bf16[2,256,1024]{2,1,0:T(8,128)(2,1)S(1)}, u32[]{:S(2)}, u32[]{:S(2)}) %collective-permute-start.26) | collective-permute-done | bytes 1048608 | tf_op jit(solution)/shard_map/ppermute | solution.py:184
  249.5 2.6 fusion.32
  252.8 2.3 fusion.26
  255.2 3.3 fusion.205
  269.5 6.2 %psum.37 = f32[512]{0:T(512)S(1)} all-reduce(f32[512]{0:T(512)S(1)} %multiply_reduce_fusion), channel_id=1, replica_groups=mesh['dp'=8,'mp'=4] {'mp'}, use_global_device_ids=true, to_apply=%region_8.9 | all-reduce | flops 512 | bytes 4096 | tf_op jit(solution)/shard_map/psum | solution.py:384
  275.7 23.2 %collective-permute-done.27 = bf16[512,512]{1,0:T(8,128)(2,1)} collective-permute-done((bf16[512,512]{1,0:T(8,128)(2,1)}, bf16[512,512]{1,0:T(8,128)(2,1)}, u32[]{:S(2)}, u32[]{:S(2)}) %collective-permute-start.27) | collective-permute-done | bytes 524320 | tf_op jit(solution)/shard_map/ppermute | solution.py:184
  303.7 2.3 slice_bitcast_fusion.10
  306.0 2.7 fusion.49
  309.6 2.3 convolution_add_fusion.4
  316.0 6.5 %all-gather.5 = bf16[512,512]{1,0:T(8,128)(2,1)S(1)} all-gather(bf16[128,512]{1,0:T(8,128)(2,1)S(1)} %shard_map.188), channel_id=7, replica_groups=mesh['dp'=8,'mp'=4] {'mp'}, dimensions={0}, use_global_device_ids=true | all-gather | bytes 655360 | tf_op jit(solution)/shard_map/all_gather | solution.py:259
  322.5 4.4 %collective-permute-done.32 = bf16[2,256,1024]{2,1,0:T(8,128)(2,1)S(1)} collective-permute-done((bf16[2,256,1024]{2,1,0:T(8,128)(2,1)}, bf16[2,256,1024]{2,1,0:T(8,128)(2,1)S(1)}, u32[]{:S(2)}, u32[]{:S(2)}) %collective-permute-start.32) | collective-permute-done | bytes 1048608 | tf_op jit(solution)/shard_map/ppermute | solution.py:184
  327.0 2.1 fusion.72
  331.9 5.8 %all-reduce.1 = (f32[1,128]{1,0:T(1,128)S(1)}, f32[1,128]{1,0:T(1,128)S(1)}) all-reduce(f32[1,128]{1,0:T(1,128)S(1)} %bitcast.259, f32[1,128]{1,0:T(1,128)S(1)} %bitcast.258), channel_id=1, replica_groups=mesh['dp'=8,'mp'=4] {'mp'}, use_global_device_ids=true, to_apply=%region_10.11 | all-reduce | flops 256 | bytes 2048 | tf_op jit(solution)/shard_map/psum | solution.py:407
  338.4 11.9 %all_to_all.34 = f32[8,1,16]{2,1,0:T(1,128)S(1)} all-to-all(f32[8,1,16]{2,1,0:T(1,128)S(1)} %compare_select_fusion), channel_id=1, replica_groups=mesh['dp'=8,'mp'=4] {'dp'}, dimensions={0} | all-to-all | bytes 1024 | tf_op jit(solution)/shard_map/all_to_all | solution.py:262
  (214 shorter events, 80.9 us)
Async XLA Ops:
  7.2 43.4 %copy-start = (bf16[512,512]{1,0:T(8,128)(2,1)S(1)}, bf16[512,512]{1,0:T(8,128)(2,1)}, u32[]{:S(2)}) copy-start(bf16[512,512]{1,0:T(8,128)(2,1)} %param.28) | copy-start | bytes 1572868
  8.8 18.4 %copy-start.2 = (bf16[16,32,1024]{2,1,0:T(8,128)(2,1)S(1)}, bf16[16,32,1024]{2,1,0:T(8,128)(2,1)}, u32[]{:S(2)}) copy-start(bf16[16,32,1024]{2,1,0:T(8,128)(2,1)} %in_ref.2) | copy-start | bytes 3145732
  8.8 18.4 %copy-start.5 = (s32[16]{0:T(128)S(1)}, s32[16]{0:T(128)}, u32[]{:S(2)}) copy-start(s32[16]{0:T(128)} %index_ref.3) | copy-start | bytes 196
  10.6 23.5 %collective-permute-start.2 = (bf16[512,768]{1,0:T(8,128)(2,1)}, bf16[512,768]{1,0:T(8,128)(2,1)S(1)}, u32[]{:S(2)}, u32[]{:S(2)}) collective-permute-start(bf16[512,768]{1,0:T(8,128)(2,1)} %pad_maximum_fusion.5), channel_id=1, source_target_pairs={{0,4},{4,0},{8,12},{12,8},{16,20},{20,16},{24,28},{28,24},{1,5},{5... | collective-permute-start | bytes 2359304 | tf_op jit(solution)/shard_map/ppermute | solution.py:184
  13.5 20.5 %collective-permute-start = (bf16[256,1024]{1,0:T(8,128)(2,1)}, bf16[256,1024]{1,0:T(8,128)(2,1)}, u32[]{:S(2)}, u32[]{:S(2)}) collective-permute-start(bf16[256,1024]{1,0:T(8,128)(2,1)} %param.27), channel_id=1, source_target_pairs={{0,8},{4,12},{8,0},{12,4},{16,24},{20,28},{24,16},{28,20},{1,9},{5... | collective-permute-start | bytes 1572872 | tf_op jit(solution)/shard_map/ppermute | solution.py:179
  15.1 19.0 %collective-permute-start.1 = (bf16[256,1024]{1,0:T(8,128)(2,1)}, bf16[256,1024]{1,0:T(8,128)(2,1)}, u32[]{:S(2)}, u32[]{:S(2)}) collective-permute-start(bf16[256,1024]{1,0:T(8,128)(2,1)} %param.27), channel_id=1, source_target_pairs={{8,16},{12,20},{16,8},{20,12},{9,17},{13,21},{17,9},{21,13},{10,18... | collective-permute-start | bytes 1572872 | tf_op jit(solution)/shard_map/ppermute | solution.py:179
  22.3 11.8 %all-to-all-start = ((bf16[8,8,512]{2,1,0:T(8,128)(2,1)}), bf16[8,8,512]{2,1,0:T(8,128)(2,1)S(1)}, u32[]{:S(2)}, u32[]{:S(2)}) async-start(bf16[8,8,512]{2,1,0:T(8,128)(2,1)} %bitcast.9), calls=%async_computation | async-start | bytes 131072 | tf_op jit(solution)/shard_map/all_to_all | solution.py:262
  27.1 145.6 %all-gather.11.cloned.1.call-start = ((), (), s32[]{:S(2)}) async-start(), calls=%async_computation.5 | async-start | bytes 5242880 | tf_op jit(solution)/shard_map/all_gather | solution.py:259
  37.3 52.5 %collective-permute-start.3 = (bf16[1024,768]{1,0:T(8,128)(2,1)}, bf16[1024,768]{1,0:T(8,128)(2,1)}, u32[]{:S(2)}, u32[]{:S(2)}) collective-permute-start(bf16[1024,768]{1,0:T(8,128)(2,1)} %bitcast.11), channel_id=1, source_target_pairs={{0,8},{4,12},{8,0},{12,4},{16,24},{20,28},{24,16},{28,20},{1,9},{5... | collective-permute-start | bytes 4718600 | tf_op jit(solution)/shard_map/ppermute | solution.py:179
  37.5 52.3 %collective-permute-start.4 = (bf16[1024,768]{1,0:T(8,128)(2,1)}, bf16[1024,768]{1,0:T(8,128)(2,1)}, u32[]{:S(2)}, u32[]{:S(2)}) collective-permute-start(bf16[1024,768]{1,0:T(8,128)(2,1)} %bitcast.11), channel_id=1, source_target_pairs={{8,16},{12,20},{16,8},{20,12},{9,17},{13,21},{17,9},{21,13},{10,18... | collective-permute-start | bytes 4718600 | tf_op jit(solution)/shard_map/ppermute | solution.py:179
  39.5 45.3 %collective-permute-start.5 = (bf16[256,1024]{1,0:T(8,128)(2,1)}, bf16[256,1024]{1,0:T(8,128)(2,1)}, u32[]{:S(2)}, u32[]{:S(2)}) collective-permute-start(bf16[256,1024]{1,0:T(8,128)(2,1)} %param.30), channel_id=1, source_target_pairs={{0,8},{4,12},{8,0},{12,4},{16,24},{20,28},{24,16},{28,20},{1,9},{5... | collective-permute-start | bytes 1572872 | tf_op jit(solution)/shard_map/ppermute | solution.py:179
  42.2 42.6 %collective-permute-start.6 = (bf16[256,1024]{1,0:T(8,128)(2,1)}, bf16[256,1024]{1,0:T(8,128)(2,1)}, u32[]{:S(2)}, u32[]{:S(2)}) collective-permute-start(bf16[256,1024]{1,0:T(8,128)(2,1)} %param.30), channel_id=1, source_target_pairs={{8,16},{12,20},{16,8},{20,12},{9,17},{13,21},{17,9},{21,13},{10,18... | collective-permute-start | bytes 1572872 | tf_op jit(solution)/shard_map/ppermute | solution.py:179
  46.5 43.4 %collective-permute-start.7 = (bf16[512,1024]{1,0:T(8,128)(2,1)}, bf16[512,1024]{1,0:T(8,128)(2,1)}, u32[]{:S(2)}, u32[]{:S(2)}) collective-permute-start(bf16[512,1024]{1,0:T(8,128)(2,1)} %bitcast.7), channel_id=1, source_target_pairs={{0,4},{4,0},{8,12},{12,8},{16,20},{20,16},{24,28},{28,24},{1,5},{5... | collective-permute-start | bytes 3145736 | tf_op jit(solution)/shard_map/ppermute | solution.py:184
  50.8 40.4 %copy-start.30 = (bf16[1024]{0:T(1024)(128)(2,1)S(1)}, bf16[1024]{0:T(1024)(128)(2,1)}, u32[]{:S(2)}) copy-start(bf16[1024]{0:T(1024)(128)(2,1)} %param.31) | copy-start | bytes 6148
  51.7 38.2 %all-to-all-start.1 = ((f32[8,8,512]{2,1,0:T(8,128)}), f32[8,8,512]{2,1,0:T(8,128)S(1)}, u32[]{:S(2)}, u32[]{:S(2)}) async-start(f32[8,8,512]{2,1,0:T(8,128)} %fusion.144), calls=%async_computation.1 | async-start | bytes 262144 | tf_op jit(solution)/shard_map/all_to_all | solution.py:262
  55.9 123.6 %all-gather.13.cloned.1.call-start = ((), (), s32[]{:S(2)}) async-start(), calls=%async_computation.6 | async-start | bytes 5242880 | tf_op jit(solution)/shard_map/all_gather | solution.py:259
  89.9 32.3 %collective-permute-start.13 = (s32[16]{0:T(128)}, s32[16]{0:T(128)}, u32[]{:S(2)}, u32[]{:S(2)}) collective-permute-start(s32[16]{0:T(128)} %param.23), channel_id=1, source_target_pairs={{0,4},{4,0},{8,12},{12,8},{16,20},{20,16},{24,28},{28,24},{1,5},{5... | collective-permute-start | bytes 200 | tf_op jit(solution)/shard_map/ppermute | solution.py:184
  94.0 29.5 %collective-permute-start.12 = (bf16[256,1024]{1,0:T(8,128)(2,1)}, bf16[256,1024]{1,0:T(8,128)(2,1)}, u32[]{:S(2)}, u32[]{:S(2)}) collective-permute-start(bf16[256,1024]{1,0:T(8,128)(2,1)} %collective-permute-done), channel_id=1, source_target_pairs={{0,4},{4,0},{8,12},{12,8},{16,20},{20,16},{24,28},{28,24},{1,5},{5... | collective-permute-start | bytes 1572872 | tf_op jit(solution)/shard_map/ppermute | solution.py:184
  94.8 91.3 %collective-permute-start.10 = (bf16[1024,768]{1,0:T(8,128)(2,1)}, bf16[1024,768]{1,0:T(8,128)(2,1)S(1)}, u32[]{:S(2)}, u32[]{:S(2)}) collective-permute-start(bf16[1024,768]{1,0:T(8,128)(2,1)} %collective-permute-done.3), channel_id=1, source_target_pairs={{8,24},{12,28},{16,0},{20,4},{9,25},{13,29},{17,1},{21,5},{10,26},... | collective-permute-start | bytes 4718600 | tf_op jit(solution)/shard_map/ppermute | solution.py:179
  96.1 90.1 %collective-permute-start.9 = (bf16[1024,768]{1,0:T(8,128)(2,1)}, bf16[1024,768]{1,0:T(8,128)(2,1)}, u32[]{:S(2)}, u32[]{:S(2)}) collective-permute-start(bf16[1024,768]{1,0:T(8,128)(2,1)} %collective-permute-done.3), channel_id=1, source_target_pairs={{8,16},{12,20},{16,8},{20,12},{9,17},{13,21},{17,9},{21,13},{10,18... | collective-permute-start | bytes 4718600 | tf_op jit(solution)/shard_map/ppermute | solution.py:179
  104.0 19.5 %collective-permute-start.11 = (bf16[256,1024]{1,0:T(8,128)(2,1)}, bf16[256,1024]{1,0:T(8,128)(2,1)}, u32[]{:S(2)}, u32[]{:S(2)}) collective-permute-start(bf16[256,1024]{1,0:T(8,128)(2,1)} %param.27), channel_id=1, source_target_pairs={{0,4},{4,0},{8,12},{12,8},{16,20},{20,16},{24,28},{28,24},{1,5},{5... | collective-permute-start | bytes 1572872 | tf_op jit(solution)/shard_map/ppermute | solution.py:184
  106.4 19.3 %copy-start.29 = (f32[1024]{0:T(1024)S(1)}, f32[1024]{0:T(1024)}, u32[]{:S(2)}) copy-start(f32[1024]{0:T(1024)} %convert_element_type.88) | copy-start | bytes 12292
  115.8 50.6 %all-to-all-start.2 = ((bf16[8,8,512]{2,1,0:T(8,128)(2,1)}), bf16[8,8,512]{2,1,0:T(8,128)(2,1)S(1)}, u32[]{:S(2)}, u32[]{:S(2)}) async-start(bf16[8,8,512]{2,1,0:T(8,128)(2,1)} %broadcast_in_dim.59), calls=%async_computation.2 | async-start | bytes 131072 | tf_op jit(solution)/shard_map/all_to_all | solution.py:262
  122.2 63.9 %collective-permute-start.8 = (bf16[1024,768]{1,0:T(8,128)(2,1)}, bf16[1024,768]{1,0:T(8,128)(2,1)}, u32[]{:S(2)}, u32[]{:S(2)}) collective-permute-start(bf16[1024,768]{1,0:T(8,128)(2,1)} %collective-permute-done.4), channel_id=1, source_target_pairs={{8,0},{12,4},{16,24},{20,28},{9,1},{13,5},{17,25},{21,29},{10,2},{... | collective-permute-start | bytes 4718600 | tf_op jit(solution)/shard_map/ppermute | solution.py:179
  123.5 42.9 %collective-permute-start.14 = (bf16[512,512]{1,0:T(8,128)(2,1)S(1)}, bf16[512,512]{1,0:T(8,128)(2,1)}, u32[]{:S(2)}, u32[]{:S(2)}) collective-permute-start(bf16[512,512]{1,0:T(8,128)(2,1)S(1)} %copy-done.19), channel_id=1, source_target_pairs={{0,4},{4,0},{8,12},{12,8},{16,20},{20,16},{24,28},{28,24},{1,5},{5... | collective-permute-start | bytes 1572872 | tf_op jit(solution)/shard_map/ppermute | solution.py:184
  125.6 40.8 %collective-permute-start.15 = (bf16[256,1024]{1,0:T(8,128)(2,1)}, bf16[256,1024]{1,0:T(8,128)(2,1)}, u32[]{:S(2)}, u32[]{:S(2)}) collective-permute-start(bf16[256,1024]{1,0:T(8,128)(2,1)} %param.30), channel_id=1, source_target_pairs={{0,4},{4,0},{8,12},{12,8},{16,20},{20,16},{24,28},{28,24},{1,5},{5... | collective-permute-start | bytes 1572872 | tf_op jit(solution)/shard_map/ppermute | solution.py:184
  166.4 19.7 %collective-permute-start.16 = (bf16[256,1024]{1,0:T(8,128)(2,1)}, bf16[256,1024]{1,0:T(8,128)(2,1)S(1)}, u32[]{:S(2)}, u32[]{:S(2)}) collective-permute-start(bf16[256,1024]{1,0:T(8,128)(2,1)} %collective-permute-done.5), channel_id=1, source_target_pairs={{0,4},{4,0},{8,12},{12,8},{16,20},{20,16},{24,28},{28,24},{1,5},{5... | collective-permute-start | bytes 1572872 | tf_op jit(solution)/shard_map/ppermute | solution.py:184
  168.8 41.2 %all-to-all-start.3 = ((bf16[8,64,512]{2,1,0:T(8,128)(2,1)}), bf16[8,64,512]{2,1,0:T(8,128)(2,1)S(1)}, u32[]{:S(2)}, u32[]{:S(2)}) async-start(bf16[8,64,512]{2,1,0:T(8,128)(2,1)} %bitcast.208), calls=%async_computation.3 | async-start | bytes 1048576 | tf_op jit(solution)/shard_map/all_to_all | solution.py:262
  172.5 76.9 %all-gather.15.cloned.1.call-start = ((), (), s32[]{:S(2)}) async-start(), calls=%async_computation.7 | async-start | bytes 2621440 | tf_op jit(solution)/shard_map/all_gather | solution.py:259
  186.9 26.1 %collective-permute-start.18 = (bf16[256,1024]{1,0:T(8,128)(2,1)}, bf16[256,1024]{1,0:T(8,128)(2,1)S(1)}, u32[]{:S(2)}, u32[]{:S(2)}) collective-permute-start(bf16[256,1024]{1,0:T(8,128)(2,1)} %collective-permute-done), channel_id=1, source_target_pairs={{8,16},{12,20},{16,8},{20,12},{9,17},{13,21},{17,9},{21,13},{10,18... | collective-permute-start | bytes 1572872 | tf_op jit(solution)/shard_map/ppermute | solution.py:179
  187.7 25.3 %collective-permute-start.19 = (bf16[256,1024]{1,0:T(8,128)(2,1)}, bf16[256,1024]{1,0:T(8,128)(2,1)S(1)}, u32[]{:S(2)}, u32[]{:S(2)}) collective-permute-start(bf16[256,1024]{1,0:T(8,128)(2,1)} %collective-permute-done), channel_id=1, source_target_pairs={{8,24},{12,28},{16,0},{20,4},{9,25},{13,29},{17,1},{21,5},{10,26},... | collective-permute-start | bytes 1572872 | tf_op jit(solution)/shard_map/ppermute | solution.py:179
  189.0 24.0 %collective-permute-start.17 = (bf16[256,1024]{1,0:T(8,128)(2,1)}, bf16[256,1024]{1,0:T(8,128)(2,1)}, u32[]{:S(2)}, u32[]{:S(2)}) collective-permute-start(bf16[256,1024]{1,0:T(8,128)(2,1)} %collective-permute-done.1), channel_id=1, source_target_pairs={{8,0},{12,4},{16,24},{20,28},{9,1},{13,5},{17,25},{21,29},{10,2},{... | collective-permute-start | bytes 1572872 | tf_op jit(solution)/shard_map/ppermute | solution.py:179
  202.1 24.6 %copy-start.15 = (bf16[512,256]{1,0:T(8,128)(2,1)S(1)}, bf16[512,256]{1,0:T(8,128)(2,1)}, u32[]{:S(2)}) copy-start(bf16[512,256]{1,0:T(8,128)(2,1)} %shard_map.187) | copy-start | bytes 786436
  213.0 14.6 %collective-permute-start.20 = (bf16[512,512]{1,0:T(8,128)(2,1)}, bf16[512,512]{1,0:T(8,128)(2,1)}, u32[]{:S(2)}, u32[]{:S(2)}) collective-permute-start(bf16[512,512]{1,0:T(8,128)(2,1)} %get-tuple-element.105), channel_id=1, source_target_pairs={{0,8},{4,12},{8,0},{12,4},{16,24},{20,28},{24,16},{28,20},{1,9},{5... | collective-permute-start | bytes 1572872 | tf_op jit(solution)/shard_map/ppermute | solution.py:179
  217.6 10.0 %collective-permute-start.21 = (bf16[512,512]{1,0:T(8,128)(2,1)}, bf16[512,512]{1,0:T(8,128)(2,1)}, u32[]{:S(2)}, u32[]{:S(2)}) collective-permute-start(bf16[512,512]{1,0:T(8,128)(2,1)} %get-tuple-element.105), channel_id=1, source_target_pairs={{8,16},{12,20},{16,8},{20,12},{9,17},{13,21},{17,9},{21,13},{10,18... | collective-permute-start | bytes 1572872 | tf_op jit(solution)/shard_map/ppermute | solution.py:179
  219.1 7.6 %collective-permute-start.22 = (bf16[512,256]{1,0:T(8,128)(2,1)}, bf16[512,256]{1,0:T(8,128)(2,1)S(1)}, u32[]{:S(2)}, u32[]{:S(2)}) collective-permute-start(bf16[512,256]{1,0:T(8,128)(2,1)} %shard_map.186), channel_id=1, source_target_pairs={{0,4},{4,0},{8,12},{12,8},{16,20},{20,16},{24,28},{28,24},{1,5},{5... | collective-permute-start | bytes 786440 | tf_op jit(solution)/shard_map/ppermute | solution.py:184
  227.6 78.4 %all-gather.17.cloned.1.call-start = ((), (), s32[]{:S(2)}) async-start(), calls=%async_computation.8 | async-start | bytes 5242880 | tf_op jit(solution)/shard_map/all_gather | solution.py:259
  230.0 18.1 %collective-permute-start.26 = (bf16[2,256,1024]{2,1,0:T(8,128)(2,1)S(1)}, bf16[2,256,1024]{2,1,0:T(8,128)(2,1)S(1)}, u32[]{:S(2)}, u32[]{:S(2)}) collective-permute-start(bf16[2,256,1024]{2,1,0:T(8,128)(2,1)S(1)} %pad_maximum_fusion.2), channel_id=1, source_target_pairs={{0,4},{4,0},{8,12},{12,8},{16,20},{20,16},{24,28},{28,24},{1,5},{5... | collective-permute-start | bytes 3145736 | tf_op jit(solution)/shard_map/ppermute | solution.py:184
  231.6 26.9 %collective-permute-start.24 = (bf16[512,512]{1,0:T(8,128)(2,1)}, bf16[512,512]{1,0:T(8,128)(2,1)}, u32[]{:S(2)}, u32[]{:S(2)}) collective-permute-start(bf16[512,512]{1,0:T(8,128)(2,1)} %collective-permute-done.20), channel_id=1, source_target_pairs={{8,16},{12,20},{16,8},{20,12},{9,17},{13,21},{17,9},{21,13},{10,18... | collective-permute-start | bytes 1572872 | tf_op jit(solution)/shard_map/ppermute | solution.py:179
  233.1 25.4 %collective-permute-start.25 = (bf16[512,512]{1,0:T(8,128)(2,1)}, bf16[512,512]{1,0:T(8,128)(2,1)}, u32[]{:S(2)}, u32[]{:S(2)}) collective-permute-start(bf16[512,512]{1,0:T(8,128)(2,1)} %collective-permute-done.20), channel_id=1, source_target_pairs={{8,24},{12,28},{16,0},{20,4},{9,25},{13,29},{17,1},{21,5},{10,26},... | collective-permute-start | bytes 1572872 | tf_op jit(solution)/shard_map/ppermute | solution.py:179
  234.4 24.1 %collective-permute-start.23 = (bf16[512,512]{1,0:T(8,128)(2,1)}, bf16[512,512]{1,0:T(8,128)(2,1)}, u32[]{:S(2)}, u32[]{:S(2)}) collective-permute-start(bf16[512,512]{1,0:T(8,128)(2,1)} %collective-permute-done.21), channel_id=1, source_target_pairs={{8,0},{12,4},{16,24},{20,28},{9,1},{13,5},{17,25},{21,29},{10,2},{... | collective-permute-start | bytes 1572872 | tf_op jit(solution)/shard_map/ppermute | solution.py:179
  262.1 36.9 %collective-permute-start.28 = (bf16[2,512,512]{2,1,0:T(8,128)(2,1)}, bf16[2,512,512]{2,1,0:T(8,128)(2,1)}, u32[]{:S(2)}, u32[]{:S(2)}) collective-permute-start(bf16[2,512,512]{2,1,0:T(8,128)(2,1)} %pad_maximum_fusion.3), channel_id=1, source_target_pairs={{0,4},{4,0},{8,12},{12,8},{16,20},{20,16},{24,28},{28,24},{1,5},{5... | collective-permute-start | bytes 3145736 | tf_op jit(solution)/shard_map/ppermute | solution.py:184
  264.1 34.8 %collective-permute-start.27 = (bf16[512,512]{1,0:T(8,128)(2,1)}, bf16[512,512]{1,0:T(8,128)(2,1)}, u32[]{:S(2)}, u32[]{:S(2)}) collective-permute-start(bf16[512,512]{1,0:T(8,128)(2,1)} %collective-permute-done.20), channel_id=1, source_target_pairs={{0,4},{4,0},{8,12},{12,8},{16,20},{20,16},{24,28},{28,24},{1,5},{5... | collective-permute-start | bytes 1572872 | tf_op jit(solution)/shard_map/ppermute | solution.py:184
  264.7 34.2 %collective-permute-start.30 = (bf16[256,1024]{1,0:T(8,128)(2,1)}, bf16[256,1024]{1,0:T(8,128)(2,1)}, u32[]{:S(2)}, u32[]{:S(2)}) collective-permute-start(bf16[256,1024]{1,0:T(8,128)(2,1)} %collective-permute-done.5), channel_id=1, source_target_pairs={{8,16},{12,20},{16,8},{20,12},{9,17},{13,21},{17,9},{21,13},{10,18... | collective-permute-start | bytes 1572872 | tf_op jit(solution)/shard_map/ppermute | solution.py:179
  266.2 32.7 %collective-permute-start.31 = (bf16[256,1024]{1,0:T(8,128)(2,1)}, bf16[256,1024]{1,0:T(8,128)(2,1)}, u32[]{:S(2)}, u32[]{:S(2)}) collective-permute-start(bf16[256,1024]{1,0:T(8,128)(2,1)} %collective-permute-done.5), channel_id=1, source_target_pairs={{8,24},{12,28},{16,0},{20,4},{9,25},{13,29},{17,1},{21,5},{10,26},... | collective-permute-start | bytes 1572872 | tf_op jit(solution)/shard_map/ppermute | solution.py:179
  267.5 31.4 %collective-permute-start.29 = (bf16[256,1024]{1,0:T(8,128)(2,1)}, bf16[256,1024]{1,0:T(8,128)(2,1)}, u32[]{:S(2)}, u32[]{:S(2)}) collective-permute-start(bf16[256,1024]{1,0:T(8,128)(2,1)} %collective-permute-done.6), channel_id=1, source_target_pairs={{8,0},{12,4},{16,24},{20,28},{9,1},{13,5},{17,25},{21,29},{10,2},{... | collective-permute-start | bytes 1572872 | tf_op jit(solution)/shard_map/ppermute | solution.py:179
  302.3 24.7 %collective-permute-start.32 = (bf16[2,256,1024]{2,1,0:T(8,128)(2,1)}, bf16[2,256,1024]{2,1,0:T(8,128)(2,1)S(1)}, u32[]{:S(2)}, u32[]{:S(2)}) collective-permute-start(bf16[2,256,1024]{2,1,0:T(8,128)(2,1)} %pad_maximum_fusion.4), channel_id=1, source_target_pairs={{0,4},{4,0},{8,12},{12,8},{16,20},{20,16},{24,28},{28,24},{1,5},{5... | collective-permute-start | bytes 3145736 | tf_op jit(solution)/shard_map/ppermute | solution.py:184
  331.3 19.6 %copy-start.1 = (bf16[512,512]{1,0:T(8,128)(2,1)S(1)}, bf16[512,512]{1,0:T(8,128)(2,1)}, u32[]{:S(2)}) copy-start(bf16[512,512]{1,0:T(8,128)(2,1)} %param.28) | copy-start | bytes 1572868
  (29 other events, 145.8 us)
Sparse Core Ops, SparseCore 0:
  34.2 33.9 all-gather.10
  90.0 34.2 all-gather.12
  227.8 21.6 all-gather.14
  258.6 34.5 all-gather.16

commit v4 on v3

v4 whole, which is shorter than its diff:
```python
import functools
import math

import jax
import jax.numpy as jnp
from jax import lax
from jax.experimental import pallas as pl
from jax.experimental.pallas import tpu as pltpu
from jax.sharding import PartitionSpec as P

HD = 64
EPSILON = 1e-06
NEG = -1e30
LANES = 128
F32 = jnp.float32
BF16 = jnp.bfloat16


def dot(a, b):
    return jnp.dot(a, b, preferred_element_type=F32)


def fence(*values):
    return lax.optimization_barrier(values)


def take_kernel(axis, index_ref, in_ref, out_ref):
    lead = (slice(None),) * axis
    for i in range(index_ref.shape[0]):
        out_ref[lead + (i,)] = in_ref[lead + (index_ref[i],)]


def take_rows(rows, index, axis):
    shape = rows.shape[:axis] + index.shape + rows.shape[axis + 1 :]
    return pl.pallas_call(
        functools.partial(take_kernel, axis),
        in_specs=[
            pl.BlockSpec(memory_space=pltpu.SMEM),
            pl.BlockSpec(memory_space=pltpu.VMEM),
        ],
        out_specs=pl.BlockSpec(memory_space=pltpu.VMEM),
        out_shape=jax.ShapeDtypeStruct(shape, rows.dtype),
        compiler_params=pltpu.CompilerParams(vmem_limit_bytes=16 << 20),
        cost_estimate=pl.CostEstimate(
            flops=0, bytes_accessed=4 * math.prod(shape), transcendentals=0
        ),
    )(index, rows)


VMEM = pl.BlockSpec(memory_space=pltpu.VMEM)
SMEM = pl.BlockSpec(memory_space=pltpu.SMEM)


def local_call(kernel, inputs, out_shapes, scratch=()):
    return pl.pallas_call(
        kernel,
        in_specs=[SMEM] + [VMEM] * (len(inputs) - 1),
        out_specs=[VMEM] * len(out_shapes),
        out_shape=[jax.ShapeDtypeStruct(*shape) for shape in out_shapes],
        scratch_shapes=[pltpu.VMEM(*shape) for shape in scratch],
        compiler_params=pltpu.CompilerParams(vmem_limit_bytes=36 << 20),
        cost_estimate=pl.CostEstimate(flops=1000, bytes_accessed=1000, transcendentals=0),
    )(*inputs)


def tile_of(n):
    return 256 if n % 256 == 0 else n


def for_tiles(n, body):
    tile = tile_of(n)
    if tile == n:
        body(pl.ds(0, n))
        return

    def step(i, carry):
        body(pl.ds(pl.multiple_of(i * tile, tile), tile))
        return carry

    lax.fori_loop(0, n // tile, step, 0)


def spread_tile(at_ref, blocks_ref, slots, rows, cols, fold_at=0):
    here = at_ref[0] == 0
    total = None
    for j, parts in enumerate(slots):
        place = at_ref[j + 2]
        loaded = [load_part(ref, k, cols, fold_at) for ref, k, *_ in parts]
        if len(parts[0]) == 3:
            loaded = [jnp.where(at_ref[1] == 1, loaded[0], parts[0][2][:, cols])]
        if len(loaded) == 2:
            own, got = loaded
            loaded = [jnp.where(here, own, got), jnp.where(here, got, own)]
        depth = loaded[0].shape[0]
        for k, weights in enumerate(loaded):
            part = dot(blocks_ref[place, rows, k * depth : (k + 1) * depth], weights)
            total = part if total is None else total + part
    return total


def load_part(ref, index, cols, fold_at):
    lead = () if index is None else (index,)
    part = ref[lead + (slice(None), cols)]
    if fold_at:
        right = pl.ds(cols.start + fold_at, cols.size)
        part = jnp.concatenate([part, ref[lead + (slice(None), right)]], axis=0)
    return part


def bind(keys, *refs):
    pairs = [key if isinstance(key[0], tuple) else (key,) for key in keys]
    return [[(refs[key[0]], key[1], *(refs[k] for k in key[2:])) for key in parts] for parts in pairs]


def enc_kernel(keys, slot_n, span, at_ref, blocks_ref, live_ref, *refs):
    slots = bind(keys, *refs[:slot_n])
    out_ref, qkv_ref = refs[slot_n:]
    total_rows, width = out_ref.shape

    def project(rows):
        def columns(cols):
            qkv_ref[rows, cols] = spread_tile(at_ref, blocks_ref, slots, rows, cols).astype(BF16)

        for_tiles(qkv_ref.shape[1], columns)

    for_tiles(total_rows, project)
    own = lax.broadcasted_iota(jnp.int32, (LANES, LANES), 0) // span
    other = lax.broadcasted_iota(jnp.int32, (LANES, LANES), 1) // span
    same = own == other
    ones = jnp.ones((LANES, HD), BF16)
    for start in range(0, total_rows, LANES):
        rows = slice(start, start + LANES)
        bias = jnp.where(same & (live_ref[:, rows] > 0), 0.0, NEG)
        for head in range(width // HD):
            q, k, v = (
                qkv_ref[rows, part * width + head * HD : part * width + (head + 1) * HD]
                for part in range(3)
            )
            scores = lax.dot_general(q, k, (((1,), (1,)), ((), ())), preferred_element_type=F32)
            scores = scores * (1.0 / math.sqrt(HD)) + bias
            weights = jnp.exp(scores - jnp.max(scores, axis=1, keepdims=True)).astype(BF16)
            context = dot(weights, v) / dot(weights, ones)
            out_ref[rows, head * HD : (head + 1) * HD] = context.astype(BF16)


def enc_attention(at, blocks, live, keys, slots, span):
    rows, triple = blocks.shape[1], slots[0].shape[-1]
    return local_call(
        functools.partial(enc_kernel, keys, len(slots), span),
        (at, blocks, live, *slots),
        [((rows, triple // 3), BF16)],
        [((rows, triple), BF16)],
    )[0]


def out_kernel(keys, slot_n, at_ref, blocks_ref, tokens_ref, *refs):
    slots = bind(keys, *refs[:slot_n])
    summed_ref, squares_ref = refs[slot_n:]
    squares_ref[...] = jnp.zeros_like(squares_ref)

    def row_tile(rows):
        def columns(cols):
            summed = spread_tile(at_ref, blocks_ref, slots, rows, cols)
            summed = summed + tokens_ref[rows, cols].astype(F32)
            summed_ref[rows, cols] = summed.astype(BF16)
            squares_ref[rows] += jnp.sum(summed * summed, axis=1, keepdims=True)

        for_tiles(summed_ref.shape[1], columns)

    for_tiles(summed_ref.shape[0], row_tile)


def encode_out(at, blocks, tokens, keys, slots):
    return local_call(
        functools.partial(out_kernel, keys, len(slots)),
        (at, blocks, tokens, *slots),
        [(tokens.shape, BF16), ((tokens.shape[0], 1), F32)],
    )


def decode_kernel(keys, slot_n, span, query_n, at_ref, blocks_ref, mixed_ref, column_ref, row_ref, live_ref, *refs):
    slots = bind(keys, *refs[:slot_n])
    out_ref, values_ref, scores_ref = refs[slot_n:]
    total_rows, width = values_ref.shape

    def project(rows):
        def columns(cols):
            values = spread_tile(at_ref, blocks_ref, slots, rows, cols, width) * column_ref[rows]
            values_ref[rows, cols] = values.astype(BF16)

        for_tiles(width, columns)

    for_tiles(total_rows, project)
    total = None
    for k in range(blocks_ref.shape[0]):
        part = lax.dot_general(
            mixed_ref[k], blocks_ref[k], (((1,), (1,)), ((), ())), preferred_element_type=F32
        )
        total = part if total is None else total + part
    scores_ref[...] = total * (row_ref[...] * (1.0 / math.sqrt(HD)))
    pairs = scores_ref.shape[0]
    cands = LANES // span
    heads = pairs // query_n
    cand = lax.broadcasted_iota(jnp.int32, (pairs, LANES), 1) // span
    head = lax.broadcasted_iota(jnp.int32, (query_n, width), 1) // HD
    for at in range(total_rows // LANES):
        rows = slice(at * LANES, (at + 1) * LANES)
        scores = scores_ref[:, rows]
        live = live_ref[:, rows] > 0
        scores = jnp.concatenate(
            [jnp.where((cand == c) & live, scores, NEG) for c in range(cands)], axis=0
        )
        weights = jnp.exp(scores - jnp.max(scores, axis=1, keepdims=True))
        weights = (weights / jnp.sum(weights, axis=1, keepdims=True)).astype(BF16)
        context = dot(weights, values_ref[rows])
        made = []
        for c in range(cands):
            chosen = jnp.zeros((query_n, width), F32)
            for h in range(heads):
                start = (c * heads + h) * query_n
                chosen = chosen + jnp.where(head == h, context[start : start + query_n], 0.0)
            made.append(chosen)
        made = jnp.concatenate(made, axis=0).astype(BF16)
        out_ref[at * cands * query_n : (at + 1) * cands * query_n] = made


def decode(at, blocks, mixed, scale, live, keys, slots, span, query_n):
    rows, width = blocks.shape[1], slots[0].shape[-1] // 2
    return local_call(
        functools.partial(decode_kernel, keys, len(slots), span, query_n),
        (at, blocks, mixed, scale, scale.reshape(1, -1), live, *slots),
        [((rows // span * query_n, width), BF16)],
        [((rows, width), BF16), ((mixed.shape[1], rows), F32)],
    )[0]


def last_kernel(keys, slot_n, at_ref, blocks_ref, source_ref, weight_ref, *refs):
    slots = bind(keys, *refs[:slot_n])
    squares_ref, dots_ref = refs[slot_n:]
    squares_ref[...] = jnp.zeros_like(squares_ref)
    dots_ref[...] = jnp.zeros_like(dots_ref)
    total_rows, query_n = squares_ref.shape[0], source_ref.shape[0]

    def columns(cols):
        update = spread_tile(at_ref, blocks_ref, slots, pl.ds(0, total_rows), cols)
        source = source_ref[:, cols].astype(F32)
        decoded = update + jnp.concatenate([source] * (total_rows // query_n), axis=0)
        squares_ref[...] += jnp.sum(decoded * decoded, axis=1, keepdims=True)
        weighted = decoded * weight_ref[:, cols].astype(F32)
        dots_ref[...] += jnp.sum(weighted, axis=1, keepdims=True)

    for_tiles(source_ref.shape[1], columns)


def decode_out(at, blocks, source, weight, keys, slots):
    column = ((blocks.shape[1], 1), F32)
    return local_call(
        functools.partial(last_kernel, keys, len(slots)),
        (at, blocks, source, weight, *slots),
        [column, column],
    )


def direct_kernel(span, live_ref, hidden_ref, wq_ref, wkv_ref, cache_ref, out_ref):
    beams, width = out_ref.shape
    heads = width // HD
    hidden = hidden_ref[...]
    query, key, value = (
        dot(hidden, weights).astype(BF16) for weights in (wq_ref[...], wkv_ref[0], wkv_ref[1])
    )
    column_head = lax.broadcasted_iota(jnp.int32, (beams, width), 1) // HD
    spread = jnp.concatenate(
        [jnp.where(column_head == h, query.astype(F32), 0.0) for h in range(heads)], axis=0
    ).astype(BF16)
    rows = heads * beams

    def product(keys):
        return lax.dot_general(spread, keys, (((1,), (1,)), ((), ())), preferred_element_type=F32)

    def beam_of(shape, axis, n):
        index = lax.broadcasted_iota(jnp.int32, shape, axis)
        return index % beams if axis == 0 else index // n

    old = (rows, beams * span)
    valid = (beam_of(old, 0, 1) == beam_of(old, 1, span)) & (live_ref[...] > 0)
    scores = jnp.where(valid, product(cache_ref[0]) * (1.0 / math.sqrt(HD)), NEG)
    new = (rows, beams)
    fresh = beam_of(new, 0, 1) == beam_of(new, 1, 1)
    scores_new = jnp.where(fresh, product(key) * (1.0 / math.sqrt(HD)), NEG)
    top = jnp.maximum(
        jnp.max(scores, axis=1, keepdims=True), jnp.max(scores_new, axis=1, keepdims=True)
    )
    weights, weights_new = jnp.exp(scores - top), jnp.exp(scores_new - top)
    total = jnp.sum(weights, axis=1, keepdims=True) + jnp.sum(weights_new, axis=1, keepdims=True)
    context = dot((weights / total).astype(BF16), cache_ref[1])
    context = context + dot((weights_new / total).astype(BF16), value)
    chosen = jnp.zeros((beams, width), F32)
    for h in range(heads):
        chosen = chosen + jnp.where(column_head == h, context[h * beams : (h + 1) * beams], 0.0)
    out_ref[...] = chosen.astype(BF16)


def direct_context(live, hidden, wq, wkv, cache, span):
    return pl.pallas_call(
        functools.partial(direct_kernel, span),
        in_specs=[VMEM] * 5,
        out_specs=VMEM,
        out_shape=jax.ShapeDtypeStruct((hidden.shape[0], wq.shape[1]), BF16),
        compiler_params=pltpu.CompilerParams(vmem_limit_bytes=36 << 20),
        cost_estimate=pl.CostEstimate(flops=1000, bytes_accessed=1000, transcendentals=0),
    )(live, hidden, wq, wkv, cache)


def state_kernel(context_ref, wo_ref, hidden_ref, weight_ref, state_ref, squares_ref, dots_ref):
    state = hidden_ref[...].astype(F32) + dot(context_ref[...], wo_ref[...])
    state_ref[...] = state.astype(BF16)
    squares_ref[...] = jnp.sum(state * state, axis=1, keepdims=True)
    dots_ref[...] = jnp.sum(state * weight_ref[...].astype(F32), axis=1, keepdims=True)


def direct_state(context, wo, hidden, weight):
    column = jax.ShapeDtypeStruct((hidden.shape[0], 1), F32)
    return pl.pallas_call(
        state_kernel,
        in_specs=[VMEM] * 4,
        out_specs=[VMEM] * 3,
        out_shape=[jax.ShapeDtypeStruct(hidden.shape, BF16), column, column],
        compiler_params=pltpu.CompilerParams(vmem_limit_bytes=36 << 20),
        cost_estimate=pl.CostEstimate(flops=1000, bytes_accessed=1000, transcendentals=0),
    )(context, wo, hidden, weight)


def shards(
    hidden,
    wq_direct,
    wkv_direct,
    wo_direct,
    kv_cache,
    parent,
    lengths,
    cand_embed,
    source,
    enc_qkv,
    enc_out,
    cross_q,
    cross_kv,
    cross_out,
    w_direct,
    w_channel,
    target_shard,
):
    dp_n, mp_n = lax.axis_size("dp"), lax.axis_size("mp")
    side_n = dp_n // mp_n
    line_n = dp_n // side_n
    me, own_mp = lax.axis_index("dp"), lax.axis_index("mp")
    side, line = me % side_n, me // side_n
    beam_n, features = hidden.shape
    span, query_n = kv_cache.shape[2], source.shape[1]
    local_width = cand_embed.shape[2]
    by_pairs = line_n == 4
    inner = (line == 1) | (line == 2)

    def move(a, pairs):
        return lax.ppermute(
            a, "dp", [(s * side_n + i, t * side_n + i) for s, t in pairs for i in range(side_n)]
        )

    def swap(a):
        return lax.ppermute(
            a, "dp", [(i, i - i % side_n + (i + 1) % side_n) for i in range(dp_n)]
        )

    def to_next(a):
        return move(a, [(0, 1), (1, 0), (2, 3), (3, 2)])

    def to_inner(a):
        return move(a, [(1, 2), (2, 1)])

    def far(own, of_next, of_inner):
        if not by_pairs:
            lines = [[k * side_n + i for k in range(line_n)] for i in range(side_n)]
            return [lax.all_gather(own, "dp", axis_index_groups=lines)]
        return [
            move(of_inner, [(1, 0), (2, 3)]),
            move(of_next, [(1, 2), (2, 1)]),
            move(of_next, [(1, 3), (2, 0)]),
        ]

    def join(of_inner, made):
        if not by_pairs:
            return made[0]
        outer, inner_last, outer_last = made
        return jnp.stack(
            [jnp.where(inner, of_inner, outer), jnp.where(inner, inner_last, outer_last)]
        )

    low = line < 2
    if by_pairs:
        places = [line, line ^ 1, jnp.where(low, 2, 1), jnp.where(low, 3, 0)]
    else:
        places = list(range(line_n))
    at = jnp.stack([side, inner, *places]).astype(jnp.int32)

    def keys_of(*stacked):
        if not by_pairs:
            sides = [[(k, place) for place in range(line_n)] for k in range(len(stacked))]
        else:
            sides = [
                [(3 * k, own), (3 * k + 1, of_next), (3 * k + 2, 0), (3 * k + 2, 1)]
                for k, (own, of_next) in enumerate(stacked)
            ]
        return sides[0] if len(sides) == 1 else list(zip(*sides, strict=True))

    def slots_of(*sides):
        return [ref for parts in sides for ref in (parts if by_pairs else parts[2:])]

    def ordered(own, got, axis):
        return jnp.where(
            side == 0, jnp.concatenate([own, got], axis), jnp.concatenate([got, own], axis)
        )

    def side_part(a, of):
        width = a.shape[-1] // side_n
        return lax.dynamic_slice_in_dim(a, of * width, width, a.ndim - 1)

    def everyone(a):
        return lax.all_gather(a, "mp", axis=0)

    def exchange(a):
        return lax.all_to_all(a, "dp", split_axis=0, concat_axis=0, tiled=True)

    positions = jnp.arange(span, dtype=jnp.int32)

    def live_of(lens):
        return (positions[None, :] < lens[:, None]).astype(jnp.int32).reshape(1, -1)


    fold = cross_kv.shape[1] // enc_out.shape[0]
    qkv_sent = jnp.concatenate([side_part(w, 1 - side) for w in enc_qkv], axis=1)
    qkv_sent, enc_out, val = fence(qkv_sent, enc_out, cross_kv[1])
    qkv_got = swap(qkv_sent)
    val = jnp.concatenate(jnp.split(val, fold, axis=0), axis=1)
    own_pair = jnp.stack([enc_out, val])
    qkv_own = jnp.concatenate([side_part(w, side) for w in enc_qkv], axis=1)
    pair_next = to_next(own_pair) if by_pairs else own_pair
    pair_inner = to_inner(own_pair) if by_pairs else own_pair
    tokens = take_rows(cand_embed, parent, 0).reshape(beam_n * span, local_width)
    lengths_got = swap(lengths)
    qkv_got, pair_next, pair_inner, tokens, lengths_got, qkv_own = fence(
        qkv_got, pair_next, pair_inner, tokens, lengths_got, qkv_own
    )

    both = jnp.zeros((side_n,) + qkv_own.shape, BF16)
    both = lax.dynamic_update_index_in_dim(both, qkv_own, side, 0)
    both = lax.dynamic_update_index_in_dim(both, qkv_got, 1 - side, 0)
    qkv_own = both.reshape(-1, both.shape[2])
    qkv_next = to_next(qkv_own) if by_pairs else qkv_own
    qkv_inner = to_inner(qkv_own) if by_pairs else qkv_own
    tokens_got = swap(tokens)
    own_blocks = everyone(tokens)
    source_rows = lax.all_gather(source[0], "mp", axis=1, tiled=True)
    source_cut = source_rows.reshape(query_n, dp_n, -1).transpose(1, 0, 2)
    source_cut = exchange(source_cut)
    cache = take_rows(kv_cache, parent, 1)
    owns = jnp.stack([enc_out, val, cross_out])
    qkv_next, qkv_inner, tokens_got, owns, pair_next, cache, source_cut = fence(
        qkv_next, qkv_inner, tokens_got, owns, pair_next, cache, source_cut
    )

    qkv_far = far(qkv_own, qkv_next, qkv_inner)
    got_blocks = everyone(tokens_got)
    owns_cross = swap(owns)
    pair_cross = swap(pair_next) if by_pairs else pair_next
    partial = exchange(dot(source_cut.reshape(dp_n * query_n, -1), cross_q))
    live = live_of(lengths)
    context = direct_context(
        live, hidden, wq_direct, wkv_direct, cache.reshape(2, beam_n * span, -1), span
    )
    context = lax.all_gather(context, "mp", axis=1, tiled=True)
    own_start = own_mp * local_width
    hidden_share = lax.dynamic_slice_in_dim(hidden, own_start, local_width, 1)
    new_state, *sums = direct_state(context, wo_direct, hidden_share, w_direct[None])
    squares, direct_dot = lax.psum(tuple(a.reshape(-1) for a in sums), "mp")
    direct_score = direct_dot / jnp.sqrt(squares / features + EPSILON)
    out_next, out_inner, val_next, val_inner = pair_next[0], pair_inner[0], pair_next[1], pair_inner[1]
    (
        qkv_far,
        owns_cross,
        pair_cross,
        (out_next, out_inner, val_next, val_inner),
        last_own,
        partial,
        new_state,
        direct_score,
        own_blocks,
        got_blocks,
    ) = fence(
        qkv_far,
        owns_cross,
        pair_cross,
        (out_next, out_inner, val_next, val_inner),
        cross_out,
        partial,
        new_state,
        direct_score,
        own_blocks,
        got_blocks,
    )

    out_far = far(enc_out, out_next, out_inner)
    last_next = to_next(last_own) if by_pairs else last_own
    if by_pairs:
        qkv_keys = [(0, None), (1, None), (2, None, 3), (4, None, 5)]
        outer, inner_last, outer_last = qkv_far
        qkv_slots = [qkv_own, qkv_next, qkv_inner, outer, inner_last, outer_last]
    else:
        qkv_keys, qkv_slots = keys_of((None, None)), qkv_far
    queries = jnp.sum(partial.reshape(dp_n, query_n, -1), axis=0).astype(BF16)
    queries = exchange(jnp.broadcast_to(queries, (dp_n,) + queries.shape).reshape(dp_n * query_n, -1))
    live_got = live_of(lengths_got)
    context_got = swap(enc_attention(at, got_blocks, live_got, qkv_keys, qkv_slots, span))
    context_own = enc_attention(at, own_blocks, live, qkv_keys, qkv_slots, span)
    enc_context = ordered(context_own, context_got, 1)
    enc_context, out_far, last_next, last_own, val_next, val_inner, queries = fence(
        enc_context, out_far, last_next, last_own, val_next, val_inner, queries
    )

    enc_blocks = everyone(enc_context)
    out_far = join(out_inner, out_far)
    out_cross = swap(out_far)
    val_far = far(val, val_next, val_inner)
    enc_blocks, out_cross, val_far, last_next, last_own, queries = fence(
        enc_blocks, out_cross, val_far, last_next, last_own, queries
    )
    summed, squares = encode_out(
        at,
        enc_blocks,
        tokens,
        keys_of((None, 0), (0, 0)),
        slots_of((enc_out, pair_next, out_far), (owns_cross, pair_cross, out_cross)),
    )
    memory_blocks = everyone(summed)
    val_far = join(val_inner, val_far)
    val_cross = swap(val_far)
    last_cross = swap(last_next) if by_pairs else last_next
    last_inner = to_inner(last_own) if by_pairs else last_own
    (last_inner,) = fence(last_inner)
    last_far = far(last_own, last_next, last_inner)
    head_n = queries.shape[1] // HD
    mixed = jnp.einsum(
        "rhc,khc->rhk",
        queries.reshape(-1, head_n, HD),
        cross_kv[0].reshape(-1, head_n, HD),
        preferred_element_type=F32,
    ).astype(BF16)
    depth = mixed.shape[2]
    pairs = head_n * query_n
    mixed = mixed.reshape(dp_n, query_n, head_n, depth).transpose(0, 2, 1, 3)
    mixed = exchange(mixed.reshape(dp_n, pairs, depth))
    mixed = mixed.reshape(line_n, side_n, pairs, depth).transpose(0, 2, 1, 3)
    mixed = mixed.reshape(line_n, pairs, side_n * depth)
    enc_squares = lax.psum(squares.reshape(1, -1), "mp").reshape(-1, 1)
    scale = 1.0 / jnp.sqrt(enc_squares / features + EPSILON)
    val_cross, last_cross, last_far = fence(val_cross, last_cross, last_far)
    last_far = join(last_inner, last_far)
    last_far_cross = swap(last_far)
    memory_blocks, scale, mixed = fence(memory_blocks, scale, mixed)

    cross_context = decode(
        at,
        memory_blocks,
        mixed,
        scale,
        live,
        keys_of((None, 1), (1, 1)),
        slots_of((val, pair_next, val_far), (owns_cross, pair_cross, val_cross)),
        span,
        query_n,
    )
    cross_blocks = everyone(cross_context)
    cross_blocks, last_far_cross = fence(cross_blocks, last_far_cross)
    dec_sums = decode_out(
        at,
        cross_blocks,
        source[0],
        w_channel[None],
        keys_of((None, None), (2, None)),
        slots_of((cross_out, last_next, last_far), (owns_cross, last_cross, last_far_cross)),
    )
    dec_squares, dec_dot = lax.psum(tuple(a.reshape(1, -1) for a in dec_sums), "mp")
    position_score = dec_dot / jnp.sqrt(dec_squares / features + EPSILON)
    own_channel = jnp.mean(position_score.reshape(beam_n, query_n), axis=1)
    shard_ids = lax.broadcasted_iota(jnp.int32, (dp_n, beam_n), 0)
    sent_scores = jnp.where(shard_ids == target_shard[None], own_channel[None], 0.0)
    return (new_state, direct_score + own_channel, jnp.sum(exchange(sent_scores), axis=0))


def solution(mesh):
    in_specs = (
        P("dp", None),
        P(None, "mp"),
        P(None, None, "mp"),
        P(None, "mp"),
        P(None, "dp", None, "mp"),
        P("dp"),
        P("dp"),
        P("dp", None, "mp"),
        P("dp", None, "mp"),
        P(None, "dp", "mp"),
        P("dp", "mp"),
        P("dp", "mp"),
        P(None, "dp", "mp"),
        P("dp", "mp"),
        P("mp"),
        P("mp"),
        P("dp"),
    )
    out_specs = (P("dp", "mp"), P("dp"), P("dp"))
    return jax.shard_map(shards, mesh=mesh, in_specs=in_specs, out_specs=out_specs, check_vma=False)
```

time: 359 us -> 348 us (0.969)
  matrix products: 58.7 us -> 2.24 us
  Pallas kernels: 10.6 us -> 43.9 us
  local copies, waits for them, and re-layouts: 23.3 us -> 39.4 us
  waiting for transfers between devices: 116 us -> 102 us
  starting transfers between devices: 68.9 us -> 77.1 us
  blocking collectives: 48.3 us -> 52.6 us
    dot_general x25 -> x1, matrix products: 54.1 us -> 0.86 us  [dot(): return jnp.dot(a, b, preferred_element_type=F32)]
    pallas_call x3 -> x7, Pallas kernels: 8.37 us -> 41.6 us  [the longest x5 37.8 us: local_call(): pl.pallas_call(kernel, in_specs=[SMEM] + [VMEM] * (len(inputs) - 1), out_...]
    ppermute x13 -> x10, waiting for transfers between devices: 46.1 us -> 20.9 us  [swap(): lax.ppermute(a, 'dp', [(i, i - i % side_n + (i + 1) % side_n) for i in ra...]
    unnamed x76 -> x98, local copies, waits for them, and re-layouts: 2.67 us -> 25.4 us
    all_to_all x4, waiting for transfers between devices: 39.4 us -> 55.1 us  [exchange(): return lax.all_to_all(a, 'dp', split_axis=0, concat_axis=0, tiled=True)]
    all_to_all x4, starting transfers between devices: 19.2 us -> 28.9 us  [exchange(): return lax.all_to_all(a, 'dp', split_axis=0, concat_axis=0, tiled=True)]
    select_n x6 -> x0, other arithmetic: 6.86 us -> none  [the longest x3 3.52 us: join(): jnp.where(inner, store['inner_last'], store['outer_last'])]
    another operation x3 -> x11, other arithmetic: 2.29 us -> 7.64 us  [the longest x9 6.19 us: join(): jnp.stack([jnp.where(inner, of_inner, outer), jnp.where(inner, inner_last...]
  transfers between devices with their start and end apart: 41 -> 36, of which waited for: 10 -> 7; matrix products, arithmetic and copies ran while one was open for 24% -> 7% of each run, Pallas kernels for 3% -> 10%
where the time goes in v4:
time: 348 us; the launch traced here: 346 us
  waiting for transfers between devices  102 us (29%)
  starting transfers between devices  77.1 us (22%)
  blocking collectives  52.6 us (15%)
  Pallas kernels  43.9 us (13%)
  local copies, waits for them, and re-layouts  39.4 us (11%)
  other arithmetic  14.5 us (4%)
  between operations  14.5 us (4%)
    all_to_all x4, waiting for transfers between devices, exchange(): return lax.all_to_all(a, 'dp', split_axis=0, concat_axis=0, tiled=True)  55.1 us
    pallas_call x5, Pallas kernels, local_call(): pl.pallas_call(kernel, in_specs=[SMEM] + [VMEM] * (len(inputs) - 1), out_...  37.8 us
    ppermute x18, starting transfers between devices, move(): lax.ppermute(a, 'dp', [(s * side_n + i, t * side_n + i) for s, t in pairs...  35.2 us
    all_to_all x4, starting transfers between devices, exchange(): return lax.all_to_all(a, 'dp', split_axis=0, concat_axis=0, tiled=True)  28.9 us
    ppermute x18, waiting for transfers between devices, move(): lax.ppermute(a, 'dp', [(s * side_n + i, t * side_n + i) for s, t in pairs...  25.9 us
    unnamed x98, local copies, waits for them, and re-layouts  25.4 us
    ppermute x10, waiting for transfers between devices, swap(): lax.ppermute(a, 'dp', [(i, i - i % side_n + (i + 1) % side_n) for i in ra...  20.9 us
    all_to_all x1, blocking collectives, exchange(): return lax.all_to_all(a, 'dp', split_axis=0, concat_axis=0, tiled=True)  14.5 us
  transfers between devices with their start and end apart: 36, of which 7 were waited for; matrix products, arithmetic and copies ran while one was open for 7% of the time, Pallas kernels for 10%

profile of v4, /device:TPU:0, one launch (start us, length us, event | category | flops | bytes accessed | tf_op | source)
XLA Modules:
  0.0 346.2 jit_solution(7789441216829828576)
XLA Ops:
  7.3 2.2 fusion.9
  11.8 5.8 %collective-permute-start.1 = (bf16[2,256,1024]{2,1,0:T(8,128)(2,1)S(1)}, bf16[2,256,1024]{2,1,0:T(8,128)(2,1)S(1)}, u32[]{:S(2)}, u32[]{:S(2)}) collective-permute-start(bf16[2,256,1024]{2,1,0:T(8,128)(2,1)S(1)} %pad_maximum_fusion.1), channel_id=1, source_target_pairs={{0,8},{4,12},{8,0},{12,4},{16,24},{20,28},{24,16},{28,20},{1,9},{5... | collective-permute-start | bytes 3145736 | tf_op jit(solution)/shard_map/ppermute | solution.py:364
  17.6 1.5 collective-permute-start
  20.6 1.6 shard_map.184
  22.2 14.2 %collective-permute-done.3 = s32[16]{0:T(128)S(1)} collective-permute-done((s32[16]{0:T(128)S(1)}, s32[16]{0:T(128)S(1)}, u32[]{:S(2)}, u32[]{:S(2)}) %collective-permute-start.3) | collective-permute-done | bytes 96 | tf_op jit(solution)/shard_map/ppermute | solution.py:369
  36.5 4.1 %collective-permute-done.1.refs_1_ = bf16[2,256,1024]{2,1,0:T(8,128)(2,1)S(1)} collective-permute-done((bf16[2,256,1024]{2,1,0:T(8,128)(2,1)S(1)}, bf16[2,256,1024]{2,1,0:T(8,128)(2,1)S(1)}, u32[]{:S(2)}, u32[]{:S(2)}) %collective-permute-start.1) | collective-permute-done | bytes 1048608 | tf_op jit(solution)/shard_map/ppermute | solution.py:364
  42.1 1.8 collective-permute-start.5
  43.9 3.0 collective-permute-start.4
  48.4 6.0 %all-gather = bf16[1,8,4096]{2,1,0:T(8,128)(2,1)} all-gather(bf16[1,8,1024]{2,1,0:T(8,128)(2,1)S(1)} %copy-done.29), channel_id=2, replica_groups=mesh['dp'=8,'mp'=4] {'mp'}, dimensions={2}, use_global_device_ids=true | all-gather | bytes 81920 | tf_op jit(solution)/shard_map/all_gather | solution.py:461
  54.4 3.3 all-to-all-start
  62.1 21.2 %all-to-all-done = bf16[8,8,512]{2,1,0:T(8,128)(2,1)S(1)} async-done(((bf16[8,8,512]{2,1,0:T(8,128)(2,1)}), bf16[8,8,512]{2,1,0:T(8,128)(2,1)S(1)}, u32[]{:S(2)}, u32[]{:S(2)}) %all-to-all-start) | async-done | bytes 65568 | tf_op jit(solution)/shard_map/all_to_all | solution.py:430
  86.3 1.8 collective-permute-start.8
  88.2 1.6 collective-permute-start.11
  90.0 2.3 slice_bitcast_fusion
  93.2 7.7 %all-to-all-start.1 = ((f32[8,8,512]{2,1,0:T(8,128)}), f32[8,8,512]{2,1,0:T(8,128)}, u32[]{:S(2)}, u32[]{:S(2)}) async-start(f32[8,8,512]{2,1,0:T(8,128)} %fusion.1), calls=%async_computation.1 | async-start | bytes 262144 | tf_op jit(solution)/shard_map/all_to_all | solution.py:430
  100.9 3.4 copy-done.2
  104.3 2.2 copy-done.6
  107.8 2.5 shard_map.186
  111.4 5.2 %all_gather.37.context_ref = bf16[16,2048]{1,0:T(8,128)(2,1)S(1)} all-gather(bf16[16,512]{1,0:T(8,128)(2,1)S(1)} %shard_map.186), channel_id=1, replica_groups=mesh['dp'=8,'mp'=4] {'mp'}, dimensions={1}, use_global_device_ids=true | all-gather | bytes 81920 | tf_op jit(solution)/shard_map/all_gather | solution.py:479
  118.1 7.4 %all-reduce.1 = (f32[16]{0:T(128)S(1)}, f32[16]{0:T(128)S(1)}) all-reduce(f32[16]{0:T(128)S(1)} %reduce.1, f32[16]{0:T(128)S(1)} %reduce.2), channel_id=1, replica_groups=mesh['dp'=8,'mp'=4] {'mp'}, use_global_device_ids=true, to_apply=%region_0.1 | all-reduce | flops 32 | bytes 256 | tf_op jit(solution)/shard_map/psum | solution.py:483
  125.6 34.0 %all-to-all-done.1 = f32[8,8,512]{2,1,0:T(8,128)} async-done(((f32[8,8,512]{2,1,0:T(8,128)}), f32[8,8,512]{2,1,0:T(8,128)}, u32[]{:S(2)}, u32[]{:S(2)}) %all-to-all-start.1) | async-done | bytes 131104 | tf_op jit(solution)/shard_map/all_to_all | solution.py:430
  163.7 6.1 %collective-permute-start.16 = (bf16[256,1024]{1,0:T(8,128)(2,1)S(1)}, bf16[256,1024]{1,0:T(8,128)(2,1)}, u32[]{:S(2)}, u32[]{:S(2)}) collective-permute-start(bf16[256,1024]{1,0:T(8,128)(2,1)S(1)} %copy-done.17), channel_id=1, source_target_pairs={{0,8},{4,12},{8,0},{12,4},{16,24},{20,28},{24,16},{28,20},{1,9},{5... | collective-permute-start | bytes 1572872 | tf_op jit(solution)/shard_map/ppermute | solution.py:364
  170.0 2.2 copy-done.8
  172.2 9.7 %shard_map.189 = bf16[512,256]{1,0:T(8,128)(2,1)S(1)} custom-call(s32[6]{0:T(128)S(1)} %stack.80.at_ref, bf16[4,512,1024]{2,1,0:T(8,128)(2,1)S(1)} %bitcast.98, s32[1,512]{1,0:T(1,128)S(1)} %reshape.227.live_ref, bf16[1024,768]{1,0:T(8,128)(2,1)S(1)} %bitcast.93, bf16[1024,768]{1,0:T(8,128)(2,1)} %collective-permute-done.4.refs_1_, ...), custom_call_target="tpu_custom_call" | custom-call | flops 1000 | bytes 1000 | tf_op jit(solution)/shard_map/pallas_call | solution.py:55
  184.6 3.3 all-to-all-start.2
  188.0 2.2 copy-done.7
  190.2 9.7 %shard_map.188 = bf16[512,256]{1,0:T(8,128)(2,1)S(1)} custom-call(s32[6]{0:T(128)S(1)} %stack.80.at_ref, bf16[4,512,1024]{2,1,0:T(8,128)(2,1)S(1)} %bitcast.97, s32[1,512]{1,0:T(1,128)S(1)} %reshape.225.live_ref, bf16[1024,768]{1,0:T(8,128)(2,1)S(1)} %bitcast.94, bf16[1024,768]{1,0:T(8,128)(2,1)} %collective-permute-done.4.refs_1_, ...), custom_call_target="tpu_custom_call" | custom-call | flops 1000 | bytes 1000 | tf_op jit(solution)/shard_map/pallas_call | solution.py:55
  199.9 2.0 maximum_select_fusion
  204.5 1.9 collective-permute-start.17
  209.9 17.6 %collective-permute-done.18 = bf16[256,1024]{1,0:T(8,128)(2,1)S(1)} collective-permute-done((bf16[256,1024]{1,0:T(8,128)(2,1)S(1)}, bf16[256,1024]{1,0:T(8,128)(2,1)S(1)}, u32[]{:S(2)}, u32[]{:S(2)}) %collective-permute-start.18) | collective-permute-done | bytes 524320 | tf_op jit(solution)/shard_map/ppermute | solution.py:364
  231.0 1.6 copy-done.15
  233.8 6.9 %shard_map.190 = (bf16[512,1024]{1,0:T(8,128)(2,1)S(1)}, f32[512,1]{1,0:T(8,128)S(1)}) custom-call(s32[6]{0:T(128)S(1)} %stack.80.at_ref, bf16[4,512,512]{2,1,0:T(8,128)(2,1)S(1)} %bitcast.101, bf16[512,1024]{1,0:T(8,128)(2,1)} %bitcast.6.tokens_ref, bf16[256,1024]{1,0:T(8,128)(2,1)S(1)} %copy-done.5, ...), custom_call_target="tpu_custom_call" | custom-call | flops 1000 | bytes 1000 | tf_op jit(solution)/shard_map/pallas_call | solution.py:55
  241.8 1.6 collective-permute-start.23
  246.5 1.5 collective-permute-start.25
  248.0 1.6 collective-permute-start.22
  250.9 2.1 copy.31
  256.0 14.5 %all-to-all-start.3 = ((bf16[8,64,512]{2,1,0:T(8,128)(2,1)}), bf16[8,64,512]{2,1,0:T(8,128)(2,1)}, u32[]{:S(2)}, u32[]{:S(2)}) async-start(bf16[8,64,512]{2,1,0:T(8,128)(2,1)} %bitcast.107), calls=%async_computation.3 | async-start | bytes 1048576 | tf_op jit(solution)/shard_map/all_to_all | solution.py:430
  270.5 4.1 %collective-permute-done.26 = bf16[256,1024]{1,0:T(8,128)(2,1)} collective-permute-done((bf16[256,1024]{1,0:T(8,128)(2,1)}, bf16[256,1024]{1,0:T(8,128)(2,1)}, u32[]{:S(2)}, u32[]{:S(2)}) %collective-permute-start.26) | collective-permute-done | bytes 524320 | tf_op jit(solution)/shard_map/ppermute | solution.py:364
  274.7 6.7 %collective-permute-done.22.refs_4_ = bf16[256,1024]{1,0:T(8,128)(2,1)S(1)} collective-permute-done((bf16[256,1024]{1,0:T(8,128)(2,1)}, bf16[256,1024]{1,0:T(8,128)(2,1)S(1)}, u32[]{:S(2)}, u32[]{:S(2)}) %collective-permute-start.22) | collective-permute-done | bytes 524320 | tf_op jit(solution)/shard_map/ppermute | solution.py:369
  283.9 2.0 collective-permute-start.27
  286.0 6.1 %psum.37 = f32[1,512]{1,0:T(1,128)S(1)} all-reduce(f32[1,512]{1,0:T(1,128)S(1)} %bitcast.111), channel_id=1, replica_groups=mesh['dp'=8,'mp'=4] {'mp'}, use_global_device_ids=true, to_apply=%region_3.4 | all-reduce | flops 512 | bytes 4096 | tf_op jit(solution)/shard_map/psum | solution.py:562
  292.1 1.9 copy.37
  294.2 2.2 copy-done.12
  298.7 7.7 %shard_map.191 = bf16[128,512]{1,0:T(8,128)(2,1)S(1)} custom-call(s32[6]{0:T(128)S(1)} %stack.80.at_ref, bf16[4,512,1024]{2,1,0:T(8,128)(2,1)S(1)} %bitcast.100, bf16[4,64,1024]{2,1,0:T(8,128)(2,1)S(1)} %bitcast.104, f32[512,1]{1,0:T(8,128)S(1)} %copy.35.column_ref, f32[1,512]{1,0:T(1,128)S(1)} %bitcast.106, s32[1,512]{1,0:T(1,128)S(1)} %reshape.225.live_ref, ...), custom_call_target="tpu_custom_call" | custom-call | flops 1000 | bytes 1000 | tf_op jit(solution)/shard_map/pallas_call | solution.py:55
  306.4 6.5 %all-gather.5 = bf16[512,512]{1,0:T(8,128)(2,1)S(1)} all-gather(bf16[128,512]{1,0:T(8,128)(2,1)S(1)} %shard_map.191), channel_id=7, replica_groups=mesh['dp'=8,'mp'=4] {'mp'}, dimensions={0}, use_global_device_ids=true | all-gather | bytes 655360 | tf_op jit(solution)/shard_map/all_gather | solution.py:427
  312.9 3.9 %shard_map.192 = (f32[128,1]{1,0:T(8,128)S(1)}, f32[128,1]{1,0:T(8,128)S(1)}) custom-call(s32[6]{0:T(128)S(1)} %stack.80.at_ref, bf16[4,128,512]{2,1,0:T(8,128)(2,1)S(1)} %bitcast.102, bf16[8,1024]{1,0:T(8,128)(2,1)S(1)} %bitcast.105, bf16[1,1024]{1,0:T(2,128)(2,1)S(1)} %broadcast_in_dim.42.weight_ref, bf16[256,1024]{1,0:T(8,128)(2,1)S(1)} %copy-done.18, ...), custom_call_target="tpu_custom_call" | custom-call | flops 1000 | bytes 1000 | tf_op jit(solution)/shard_map/pallas_call | solution.py:55
  317.0 6.8 %all-reduce = (f32[1,128]{1,0:T(1,128)S(1)}, f32[1,128]{1,0:T(1,128)S(1)}) all-reduce(f32[1,128]{1,0:T(1,128)S(1)} %bitcast.112, f32[1,128]{1,0:T(1,128)S(1)} %bitcast.113), channel_id=1, replica_groups=mesh['dp'=8,'mp'=4] {'mp'}, use_global_device_ids=true, to_apply=%region_4.5 | all-reduce | flops 256 | bytes 2048 | tf_op jit(solution)/shard_map/psum | solution.py:590
  324.6 14.5 %all_to_all.34 = f32[8,1,16]{2,1,0:T(1,128)S(1)} all-to-all(f32[8,1,16]{2,1,0:T(1,128)S(1)} %compare_select_fusion), channel_id=1, replica_groups=mesh['dp'=8,'mp'=4] {'dp'}, dimensions={0} | all-to-all | bytes 1024 | tf_op jit(solution)/shard_map/all_to_all | solution.py:430
  (197 shorter events, 51.6 us)
Async XLA Ops:
  7.2 85.2 %copy-start = (bf16[512,512]{1,0:T(8,128)(2,1)S(1)}, bf16[512,512]{1,0:T(8,128)(2,1)}, u32[]{:S(2)}) copy-start(bf16[512,512]{1,0:T(8,128)(2,1)} %param.28) | copy-start | bytes 1572868
  7.2 152.4 %all-gather.11.cloned.1.call-start = ((), (), s32[]{:S(2)}) async-start(), calls=%async_computation.5 | async-start | bytes 5242880 | tf_op jit(solution)/shard_map/all_gather | solution.py:427
  10.8 9.8 %copy-start.31 = (bf16[1,256,1024]{2,1,0:T(8,128)(2,1)}, bf16[1,256,1024]{2,1,0:T(8,128)(2,1)S(1)}, u32[]{:S(2)}) copy-start(bf16[1,256,1024]{2,1,0:T(8,128)(2,1)S(1)} %get-tuple-element.147) | copy-start | bytes 1572868
  10.8 9.8 %copy-start.30 = (s32[16]{0:T(128)S(1)}, s32[16]{0:T(128)}, u32[]{:S(2)}) copy-start(s32[16]{0:T(128)} %index_ref.3) | copy-start | bytes 196
  10.9 25.5 %collective-permute-start.2 = (bf16[2,256,1024]{2,1,0:T(8,128)(2,1)S(1)}, bf16[2,256,1024]{2,1,0:T(8,128)(2,1)S(1)}, u32[]{:S(2)}, u32[]{:S(2)}) collective-permute-start(bf16[2,256,1024]{2,1,0:T(8,128)(2,1)S(1)} %pad_maximum_fusion.1), channel_id=1, source_target_pairs={{8,16},{12,20},{16,8},{20,12},{9,17},{13,21},{17,9},{21,13},{10,18... | collective-permute-start | bytes 3145736 | tf_op jit(solution)/shard_map/ppermute | solution.py:364
  11.8 28.7 %collective-permute-start.1 = (bf16[2,256,1024]{2,1,0:T(8,128)(2,1)S(1)}, bf16[2,256,1024]{2,1,0:T(8,128)(2,1)S(1)}, u32[]{:S(2)}, u32[]{:S(2)}) collective-permute-start(bf16[2,256,1024]{2,1,0:T(8,128)(2,1)S(1)} %pad_maximum_fusion.1), channel_id=1, source_target_pairs={{0,8},{4,12},{8,0},{12,4},{16,24},{20,28},{24,16},{28,20},{1,9},{5... | collective-permute-start | bytes 3145736 | tf_op jit(solution)/shard_map/ppermute | solution.py:364
  17.6 18.8 %collective-permute-start = (bf16[512,768]{1,0:T(8,128)(2,1)S(1)}, bf16[512,768]{1,0:T(8,128)(2,1)S(1)}, u32[]{:S(2)}, u32[]{:S(2)}) collective-permute-start(bf16[512,768]{1,0:T(8,128)(2,1)S(1)} %pad_maximum_fusion.5), channel_id=1, source_target_pairs={{0,4},{4,0},{8,12},{12,8},{16,20},{20,16},{24,28},{28,24},{1,5},{5... | collective-permute-start | bytes 2359304 | tf_op jit(solution)/shard_map/ppermute | solution.py:369
  19.1 17.3 %collective-permute-start.3 = (s32[16]{0:T(128)S(1)}, s32[16]{0:T(128)S(1)}, u32[]{:S(2)}, u32[]{:S(2)}) collective-permute-start(s32[16]{0:T(128)S(1)} %copy-done.47), channel_id=1, source_target_pairs={{0,4},{4,0},{8,12},{12,8},{16,20},{20,16},{24,28},{28,24},{1,5},{5... | collective-permute-start | bytes 200 | tf_op jit(solution)/shard_map/ppermute | solution.py:369
  42.1 41.2 %collective-permute-start.5 = (bf16[1024,768]{1,0:T(8,128)(2,1)S(1)}, bf16[1024,768]{1,0:T(8,128)(2,1)}, u32[]{:S(2)}, u32[]{:S(2)}) collective-permute-start(bf16[1024,768]{1,0:T(8,128)(2,1)S(1)} %bitcast.91), channel_id=1, source_target_pairs={{8,16},{12,20},{16,8},{20,12},{9,17},{13,21},{17,9},{21,13},{10,18... | collective-permute-start | bytes 4718600 | tf_op jit(solution)/shard_map/ppermute | solution.py:364
  43.9 39.4 %collective-permute-start.4 = (bf16[1024,768]{1,0:T(8,128)(2,1)S(1)}, bf16[1024,768]{1,0:T(8,128)(2,1)}, u32[]{:S(2)}, u32[]{:S(2)}) collective-permute-start(bf16[1024,768]{1,0:T(8,128)(2,1)S(1)} %bitcast.92), channel_id=1, source_target_pairs={{0,8},{4,12},{8,0},{12,4},{16,24},{20,28},{24,16},{28,20},{1,9},{5... | collective-permute-start | bytes 4718600 | tf_op jit(solution)/shard_map/ppermute | solution.py:364
  46.9 36.4 %collective-permute-start.6 = (bf16[512,1024]{1,0:T(8,128)(2,1)}, bf16[512,1024]{1,0:T(8,128)(2,1)}, u32[]{:S(2)}, u32[]{:S(2)}) collective-permute-start(bf16[512,1024]{1,0:T(8,128)(2,1)} %bitcast.6.tokens_ref), channel_id=1, source_target_pairs={{0,4},{4,0},{8,12},{12,8},{16,20},{20,16},{24,28},{28,24},{1,5},{5... | collective-permute-start | bytes 3145736 | tf_op jit(solution)/shard_map/ppermute | solution.py:369
  54.4 28.9 %all-to-all-start = ((bf16[8,8,512]{2,1,0:T(8,128)(2,1)}), bf16[8,8,512]{2,1,0:T(8,128)(2,1)S(1)}, u32[]{:S(2)}, u32[]{:S(2)}) async-start(bf16[8,8,512]{2,1,0:T(8,128)(2,1)} %bitcast.15), calls=%async_computation | async-start | bytes 131072 | tf_op jit(solution)/shard_map/all_to_all | solution.py:430
  57.7 101.9 %all-gather.13.cloned.1.call-start = ((), (), s32[]{:S(2)}) async-start(), calls=%async_computation.6 | async-start | bytes 5242880 | tf_op jit(solution)/shard_map/all_gather | solution.py:427
  60.7 29.1 %copy-start.28 = (bf16[16,4096]{1,0:T(8,128)(2,1)S(1)}, bf16[16,4096]{1,0:T(8,128)(2,1)}, u32[]{:S(2)}) copy-start(bf16[16,4096]{1,0:T(8,128)(2,1)} %hidden_ref.1) | copy-start | bytes 393220
  60.7 29.1 %copy-start.45 = (bf16[1024]{0:T(1024)(128)(2,1)S(1)}, bf16[1024]{0:T(1024)(128)(2,1)}, u32[]{:S(2)}) copy-start(bf16[1024]{0:T(1024)(128)(2,1)} %param.31) | copy-start | bytes 6148
  83.3 76.3 %collective-permute-start.10 = (bf16[3,256,1024]{2,1,0:T(8,128)(2,1)}, bf16[3,256,1024]{2,1,0:T(8,128)(2,1)}, u32[]{:S(2)}, u32[]{:S(2)}) collective-permute-start(bf16[3,256,1024]{2,1,0:T(8,128)(2,1)} %pad_maximum_fusion), channel_id=1, source_target_pairs={{0,4},{4,0},{8,12},{12,8},{16,20},{20,16},{24,28},{28,24},{1,5},{5... | collective-permute-start | bytes 4718600 | tf_op jit(solution)/shard_map/ppermute | solution.py:369
  83.7 75.8 %collective-permute-start.7 = (bf16[1024,768]{1,0:T(8,128)(2,1)}, bf16[1024,768]{1,0:T(8,128)(2,1)}, u32[]{:S(2)}, u32[]{:S(2)}) collective-permute-start(bf16[1024,768]{1,0:T(8,128)(2,1)} %collective-permute-done.5.refs_2_), channel_id=1, source_target_pairs={{8,0},{12,4},{16,24},{20,28},{9,1},{13,5},{17,25},{21,29},{10,2},{... | collective-permute-start | bytes 4718600 | tf_op jit(solution)/shard_map/ppermute | solution.py:364
  85.0 74.5 %collective-permute-start.9 = (bf16[1024,768]{1,0:T(8,128)(2,1)}, bf16[1024,768]{1,0:T(8,128)(2,1)}, u32[]{:S(2)}, u32[]{:S(2)}) collective-permute-start(bf16[1024,768]{1,0:T(8,128)(2,1)} %collective-permute-done.4.refs_1_), channel_id=1, source_target_pairs={{8,24},{12,28},{16,0},{20,4},{9,25},{13,29},{17,1},{21,5},{10,26},... | collective-permute-start | bytes 4718600 | tf_op jit(solution)/shard_map/ppermute | solution.py:364
  86.3 73.3 %collective-permute-start.8 = (bf16[1024,768]{1,0:T(8,128)(2,1)}, bf16[1024,768]{1,0:T(8,128)(2,1)}, u32[]{:S(2)}, u32[]{:S(2)}) collective-permute-start(bf16[1024,768]{1,0:T(8,128)(2,1)} %collective-permute-done.4.refs_1_), channel_id=1, source_target_pairs={{8,16},{12,20},{16,8},{20,12},{9,17},{13,21},{17,9},{21,13},{10,18... | collective-permute-start | bytes 4718600 | tf_op jit(solution)/shard_map/ppermute | solution.py:364
  88.2 71.3 %collective-permute-start.11 = (bf16[2,256,1024]{2,1,0:T(8,128)(2,1)S(1)}, bf16[2,256,1024]{2,1,0:T(8,128)(2,1)}, u32[]{:S(2)}, u32[]{:S(2)}) collective-permute-start(bf16[2,256,1024]{2,1,0:T(8,128)(2,1)S(1)} %collective-permute-done.1.refs_1_), channel_id=1, source_target_pairs={{0,4},{4,0},{8,12},{12,8},{16,20},{20,16},{24,28},{28,24},{1,5},{5... | collective-permute-start | bytes 3145736 | tf_op jit(solution)/shard_map/ppermute | solution.py:369
  93.2 66.3 %all-to-all-start.1 = ((f32[8,8,512]{2,1,0:T(8,128)}), f32[8,8,512]{2,1,0:T(8,128)}, u32[]{:S(2)}, u32[]{:S(2)}) async-start(f32[8,8,512]{2,1,0:T(8,128)} %fusion.1), calls=%async_computation.1 | async-start | bytes 262144 | tf_op jit(solution)/shard_map/all_to_all | solution.py:430
  116.6 47.1 %copy-start.17 = (bf16[256,1024]{1,0:T(8,128)(2,1)S(1)}, bf16[256,1024]{1,0:T(8,128)(2,1)}, u32[]{:S(2)}) copy-start(bf16[256,1024]{1,0:T(8,128)(2,1)} %refs_0_.2) | copy-start | bytes 1572868
  159.6 42.3 %collective-permute-start.15 = (bf16[256,1024]{1,0:T(8,128)(2,1)}, bf16[256,1024]{1,0:T(8,128)(2,1)}, u32[]{:S(2)}, u32[]{:S(2)}) collective-permute-start(bf16[256,1024]{1,0:T(8,128)(2,1)} %get-tuple-element.95), channel_id=1, source_target_pairs={{8,24},{12,28},{16,0},{20,4},{9,25},{13,29},{17,1},{21,5},{10,26},... | collective-permute-start | bytes 1572872 | tf_op jit(solution)/shard_map/ppermute | solution.py:364
  160.9 41.0 %collective-permute-start.14 = (bf16[256,1024]{1,0:T(8,128)(2,1)}, bf16[256,1024]{1,0:T(8,128)(2,1)}, u32[]{:S(2)}, u32[]{:S(2)}) collective-permute-start(bf16[256,1024]{1,0:T(8,128)(2,1)} %get-tuple-element.95), channel_id=1, source_target_pairs={{8,16},{12,20},{16,8},{20,12},{9,17},{13,21},{17,9},{21,13},{10,18... | collective-permute-start | bytes 1572872 | tf_op jit(solution)/shard_map/ppermute | solution.py:364
  162.4 39.5 %collective-permute-start.13 = (bf16[256,1024]{1,0:T(8,128)(2,1)}, bf16[256,1024]{1,0:T(8,128)(2,1)}, u32[]{:S(2)}, u32[]{:S(2)}) collective-permute-start(bf16[256,1024]{1,0:T(8,128)(2,1)} %get-tuple-element.94), channel_id=1, source_target_pairs={{8,0},{12,4},{16,24},{20,28},{9,1},{13,5},{17,25},{21,29},{10,2},{... | collective-permute-start | bytes 1572872 | tf_op jit(solution)/shard_map/ppermute | solution.py:364
  163.7 38.2 %collective-permute-start.16 = (bf16[256,1024]{1,0:T(8,128)(2,1)S(1)}, bf16[256,1024]{1,0:T(8,128)(2,1)}, u32[]{:S(2)}, u32[]{:S(2)}) collective-permute-start(bf16[256,1024]{1,0:T(8,128)(2,1)S(1)} %copy-done.17), channel_id=1, source_target_pairs={{0,8},{4,12},{8,0},{12,4},{16,24},{20,28},{24,16},{28,20},{1,9},{5... | collective-permute-start | bytes 1572872 | tf_op jit(solution)/shard_map/ppermute | solution.py:364
  181.9 18.0 %collective-permute-start.12 = (bf16[512,256]{1,0:T(8,128)(2,1)S(1)}, bf16[512,256]{1,0:T(8,128)(2,1)}, u32[]{:S(2)}, u32[]{:S(2)}) collective-permute-start(bf16[512,256]{1,0:T(8,128)(2,1)S(1)} %shard_map.189), channel_id=1, source_target_pairs={{0,4},{4,0},{8,12},{12,8},{16,20},{20,16},{24,28},{28,24},{1,5},{5... | collective-permute-start | bytes 786440 | tf_op jit(solution)/shard_map/ppermute | solution.py:369
  184.6 17.3 %all-to-all-start.2 = ((bf16[8,8,512]{2,1,0:T(8,128)(2,1)}), bf16[8,8,512]{2,1,0:T(8,128)(2,1)S(1)}, u32[]{:S(2)}, u32[]{:S(2)}) async-start(bf16[8,8,512]{2,1,0:T(8,128)(2,1)} %broadcast_in_dim.41), calls=%async_computation.2 | async-start | bytes 131072 | tf_op jit(solution)/shard_map/all_to_all | solution.py:430
  188.0 43.0 %all-gather.15.cloned.1.call-start = ((), (), s32[]{:S(2)}) async-start(), calls=%async_computation.7 | async-start | bytes 2621440 | tf_op jit(solution)/shard_map/all_gather | solution.py:427
  202.0 92.1 %all-gather.17.cloned.1.call-start = ((), (), s32[]{:S(2)}) async-start(), calls=%async_computation.8 | async-start | bytes 5242880 | tf_op jit(solution)/shard_map/all_gather | solution.py:427
  203.2 27.8 %copy-start.5 = (bf16[256,1024]{1,0:T(8,128)(2,1)S(1)}, bf16[256,1024]{1,0:T(8,128)(2,1)}, u32[]{:S(2)}) copy-start(bf16[256,1024]{1,0:T(8,128)(2,1)} %refs_0_.1) | copy-start | bytes 1572868
  204.5 25.5 %collective-permute-start.17 = (bf16[2,256,1024]{2,1,0:T(8,128)(2,1)S(1)}, bf16[2,256,1024]{2,1,0:T(8,128)(2,1)S(1)}, u32[]{:S(2)}, u32[]{:S(2)}) collective-permute-start(bf16[2,256,1024]{2,1,0:T(8,128)(2,1)S(1)} %pad_maximum_fusion.2.refs_2_), channel_id=1, source_target_pairs={{0,4},{4,0},{8,12},{12,8},{16,20},{20,16},{24,28},{28,24},{1,5},{5... | collective-permute-start | bytes 3145736 | tf_op jit(solution)/shard_map/ppermute | solution.py:369
  206.5 21.1 %collective-permute-start.18 = (bf16[256,1024]{1,0:T(8,128)(2,1)S(1)}, bf16[256,1024]{1,0:T(8,128)(2,1)S(1)}, u32[]{:S(2)}, u32[]{:S(2)}) collective-permute-start(bf16[256,1024]{1,0:T(8,128)(2,1)S(1)} %copy-done.33), channel_id=1, source_target_pairs={{8,0},{12,4},{16,24},{20,28},{9,1},{13,5},{17,25},{21,29},{10,2},{... | collective-permute-start | bytes 1572872 | tf_op jit(solution)/shard_map/ppermute | solution.py:364
  207.9 19.6 %collective-permute-start.20 = (bf16[256,1024]{1,0:T(8,128)(2,1)S(1)}, bf16[256,1024]{1,0:T(8,128)(2,1)S(1)}, u32[]{:S(2)}, u32[]{:S(2)}) collective-permute-start(bf16[256,1024]{1,0:T(8,128)(2,1)S(1)} %copy-done.44), channel_id=1, source_target_pairs={{8,24},{12,28},{16,0},{20,4},{9,25},{13,29},{17,1},{21,5},{10,26},... | collective-permute-start | bytes 1572872 | tf_op jit(solution)/shard_map/ppermute | solution.py:364
  209.2 19.1 %collective-permute-start.19 = (bf16[256,1024]{1,0:T(8,128)(2,1)S(1)}, bf16[256,1024]{1,0:T(8,128)(2,1)S(1)}, u32[]{:S(2)}, u32[]{:S(2)}) collective-permute-start(bf16[256,1024]{1,0:T(8,128)(2,1)S(1)} %copy-done.44), channel_id=1, source_target_pairs={{8,16},{12,20},{16,8},{20,12},{9,17},{13,21},{17,9},{21,13},{10,18... | collective-permute-start | bytes 1572872 | tf_op jit(solution)/shard_map/ppermute | solution.py:364
  241.8 7.8 %collective-permute-start.23 = (bf16[256,1024]{1,0:T(8,128)(2,1)S(1)}, bf16[256,1024]{1,0:T(8,128)(2,1)}, u32[]{:S(2)}, u32[]{:S(2)}) collective-permute-start(bf16[256,1024]{1,0:T(8,128)(2,1)S(1)} %copy-done.18), channel_id=1, source_target_pairs={{8,16},{12,20},{16,8},{20,12},{9,17},{13,21},{17,9},{21,13},{10,18... | collective-permute-start | bytes 1572872 | tf_op jit(solution)/shard_map/ppermute | solution.py:364
  244.7 11.3 %copy-start.13 = (bf16[2,256,1024]{2,1,0:T(8,128)(2,1)}, bf16[2,256,1024]{2,1,0:T(8,128)(2,1)S(1)}, u32[]{:S(2)}) copy-start(bf16[2,256,1024]{2,1,0:T(8,128)(2,1)S(1)} %pad_maximum_fusion.3.refs_2_) | copy-start | bytes 3145732
  244.7 36.7 %collective-permute-start.21 = (bf16[2,256,1024]{2,1,0:T(8,128)(2,1)S(1)}, bf16[2,256,1024]{2,1,0:T(8,128)(2,1)}, u32[]{:S(2)}, u32[]{:S(2)}) collective-permute-start(bf16[2,256,1024]{2,1,0:T(8,128)(2,1)S(1)} %pad_maximum_fusion.3.refs_2_), channel_id=1, source_target_pairs={{0,4},{4,0},{8,12},{12,8},{16,20},{20,16},{24,28},{28,24},{1,5},{5... | collective-permute-start | bytes 3145736 | tf_op jit(solution)/shard_map/ppermute | solution.py:369
  245.2 29.5 %collective-permute-start.26 = (bf16[256,1024]{1,0:T(8,128)(2,1)}, bf16[256,1024]{1,0:T(8,128)(2,1)}, u32[]{:S(2)}, u32[]{:S(2)}) collective-permute-start(bf16[256,1024]{1,0:T(8,128)(2,1)} %collective-permute-done.16.refs_1_), channel_id=1, source_target_pairs={{8,24},{12,28},{16,0},{20,4},{9,25},{13,29},{17,1},{21,5},{10,26},... | collective-permute-start | bytes 1572872 | tf_op jit(solution)/shard_map/ppermute | solution.py:364
  246.5 28.2 %collective-permute-start.25 = (bf16[256,1024]{1,0:T(8,128)(2,1)}, bf16[256,1024]{1,0:T(8,128)(2,1)}, u32[]{:S(2)}, u32[]{:S(2)}) collective-permute-start(bf16[256,1024]{1,0:T(8,128)(2,1)} %collective-permute-done.16.refs_1_), channel_id=1, source_target_pairs={{8,16},{12,20},{16,8},{20,12},{9,17},{13,21},{17,9},{21,13},{10,18... | collective-permute-start | bytes 1572872 | tf_op jit(solution)/shard_map/ppermute | solution.py:364
  248.0 33.4 %collective-permute-start.22 = (bf16[256,1024]{1,0:T(8,128)(2,1)}, bf16[256,1024]{1,0:T(8,128)(2,1)S(1)}, u32[]{:S(2)}, u32[]{:S(2)}) collective-permute-start(bf16[256,1024]{1,0:T(8,128)(2,1)} %collective-permute-done.16.refs_1_), channel_id=1, source_target_pairs={{0,4},{4,0},{8,12},{12,8},{16,20},{20,16},{24,28},{28,24},{1,5},{5... | collective-permute-start | bytes 1572872 | tf_op jit(solution)/shard_map/ppermute | solution.py:369
  249.6 31.8 %collective-permute-start.24 = (bf16[256,1024]{1,0:T(8,128)(2,1)}, bf16[256,1024]{1,0:T(8,128)(2,1)}, u32[]{:S(2)}, u32[]{:S(2)}) collective-permute-start(bf16[256,1024]{1,0:T(8,128)(2,1)} %collective-permute-done.23), channel_id=1, source_target_pairs={{8,0},{12,4},{16,24},{20,28},{9,1},{13,5},{17,25},{21,29},{10,2},{... | collective-permute-start | bytes 1572872 | tf_op jit(solution)/shard_map/ppermute | solution.py:364
  256.0 36.1 %all-to-all-start.3 = ((bf16[8,64,512]{2,1,0:T(8,128)(2,1)}), bf16[8,64,512]{2,1,0:T(8,128)(2,1)}, u32[]{:S(2)}, u32[]{:S(2)}) async-start(bf16[8,64,512]{2,1,0:T(8,128)(2,1)} %bitcast.107), calls=%async_computation.3 | async-start | bytes 1048576 | tf_op jit(solution)/shard_map/all_to_all | solution.py:430
  283.8 10.4 %copy-start.19 = (bf16[256,1024]{1,0:T(8,128)(2,1)S(1)}, bf16[256,1024]{1,0:T(8,128)(2,1)}, u32[]{:S(2)}) copy-start(bf16[256,1024]{1,0:T(8,128)(2,1)} %get-tuple-element.146.refs_0_) | copy-start | bytes 1572868
  283.9 29.0 %collective-permute-start.27 = (bf16[2,256,1024]{2,1,0:T(8,128)(2,1)S(1)}, bf16[2,256,1024]{2,1,0:T(8,128)(2,1)}, u32[]{:S(2)}, u32[]{:S(2)}) collective-permute-start(bf16[2,256,1024]{2,1,0:T(8,128)(2,1)S(1)} %pad_maximum_fusion.4.refs_2_), channel_id=1, source_target_pairs={{0,4},{4,0},{8,12},{12,8},{16,20},{20,16},{24,28},{28,24},{1,5},{5... | collective-permute-start | bytes 3145736 | tf_op jit(solution)/shard_map/ppermute | solution.py:369
  298.7 14.2 %copy-start.27 = (bf16[256,1024]{1,0:T(8,128)(2,1)S(1)}, bf16[256,1024]{1,0:T(8,128)(2,1)}, u32[]{:S(2)}) copy-start(bf16[256,1024]{1,0:T(8,128)(2,1)} %copy-done.26) | copy-start | bytes 1572868
  312.9 26.8 %copy-start.1 = (bf16[512,512]{1,0:T(8,128)(2,1)S(1)}, bf16[512,512]{1,0:T(8,128)(2,1)}, u32[]{:S(2)}) copy-start(bf16[512,512]{1,0:T(8,128)(2,1)} %param.28) | copy-start | bytes 1572868
  312.9 11.7 %copy-start.48 = (s32[16]{0:T(128)S(1)}, s32[16]{0:T(128)}, u32[]{:S(2)}) copy-start(s32[16]{0:T(128)} %param.33) | copy-start | bytes 196
  (37 other events, 107.1 us)
Sparse Core Ops, SparseCore 0:
  40.7 34.2 all-gather.10
  83.4 33.6 all-gather.12
  202.1 23.9 all-gather.14
  241.9 34.4 all-gather.16

commit v5 on v4

--- a/solution.py
+++ b/solution.py
@@ -63,12 +63,12 @@
     )(*inputs)
 
 
-def tile_of(n):
-    return 256 if n % 256 == 0 else n
-
-
-def for_tiles(n, body):
-    tile = tile_of(n)
+def tile_of(n, most):
+    return most if n % most == 0 else n
+
+
+def for_tiles(n, body, most=256):
+    tile = tile_of(n, most)
     if tile == n:
         body(pl.ds(0, n))
         return
@@ -81,19 +81,15 @@
 
 
 def spread_tile(at_ref, blocks_ref, slots, rows, cols, fold_at=0):
-    here = at_ref[0] == 0
     total = None
     for j, parts in enumerate(slots):
         place = at_ref[j + 2]
-        loaded = [load_part(ref, k, cols, fold_at) for ref, k, *_ in parts]
-        if len(parts[0]) == 3:
-            loaded = [jnp.where(at_ref[1] == 1, loaded[0], parts[0][2][:, cols])]
-        if len(loaded) == 2:
-            own, got = loaded
-            loaded = [jnp.where(here, own, got), jnp.where(here, got, own)]
-        depth = loaded[0].shape[0]
-        for k, weights in enumerate(loaded):
-            part = dot(blocks_ref[place, rows, k * depth : (k + 1) * depth], weights)
+        for k, (ref, index, *other) in enumerate(parts):
+            weights = load_part(ref, index, cols, fold_at)
+            if other:
+                weights = jnp.where(at_ref[1] == 1, weights, other[0][:, cols])
+            lead = (place,) if len(parts) == 1 else (place, k)
+            part = dot(blocks_ref[lead + (rows, slice(None))], weights)
             total = part if total is None else total + part
     return total
 
@@ -123,7 +119,7 @@
 
         for_tiles(qkv_ref.shape[1], columns)
 
-    for_tiles(total_rows, project)
+    for_tiles(total_rows, project, 512)
     own = lax.broadcasted_iota(jnp.int32, (LANES, LANES), 0) // span
     other = lax.broadcasted_iota(jnp.int32, (LANES, LANES), 1) // span
     same = own == other
@@ -158,23 +154,32 @@
     summed_ref, squares_ref = refs[slot_n:]
     squares_ref[...] = jnp.zeros_like(squares_ref)
 
+    side_n, total_rows, width = summed_ref.shape
+
     def row_tile(rows):
-        def columns(cols):
-            summed = spread_tile(at_ref, blocks_ref, slots, rows, cols)
-            summed = summed + tokens_ref[rows, cols].astype(F32)
-            summed_ref[rows, cols] = summed.astype(BF16)
-            squares_ref[rows] += jnp.sum(summed * summed, axis=1, keepdims=True)
-
-        for_tiles(summed_ref.shape[1], columns)
-
-    for_tiles(summed_ref.shape[0], row_tile)
+        for half in range(side_n):
+            order = jnp.where(at_ref[0] == half, 0, 1)
+
+            def columns(cols):
+                start = cols.start + half * width
+                if not isinstance(start, int):
+                    start = pl.multiple_of(start, LANES)
+                here = pl.ds(start, cols.size)
+                summed = spread_tile(at_ref, blocks_ref, slots, rows, here)
+                summed = summed + tokens_ref[rows, here].astype(F32)
+                summed_ref[order, rows, cols] = summed.astype(BF16)
+                squares_ref[rows] += jnp.sum(summed * summed, axis=1, keepdims=True)
+
+            for_tiles(width, columns)
+
+    for_tiles(total_rows, row_tile, 512)
 
 
 def encode_out(at, blocks, tokens, keys, slots):
     return local_call(
         functools.partial(out_kernel, keys, len(slots)),
         (at, blocks, tokens, *slots),
-        [(tokens.shape, BF16), ((tokens.shape[0], 1), F32)],
+        [((2, tokens.shape[0], tokens.shape[1] // 2), BF16), ((tokens.shape[0], 1), F32)],
     )
 
 
@@ -190,13 +195,17 @@
 
         for_tiles(width, columns)
 
-    for_tiles(total_rows, project)
+    for_tiles(total_rows, project, 512)
     total = None
     for k in range(blocks_ref.shape[0]):
-        part = lax.dot_general(
-            mixed_ref[k], blocks_ref[k], (((1,), (1,)), ((), ())), preferred_element_type=F32
-        )
-        total = part if total is None else total + part
+        for half in range(blocks_ref.shape[1]):
+            part = lax.dot_general(
+                mixed_ref[k, jnp.where(at_ref[0] == 0, half, blocks_ref.shape[1] - 1 - half)],
+                blocks_ref[k, half],
+                (((1,), (1,)), ((), ())),
+                preferred_element_type=F32,
+            )
+            total = part if total is None else total + part
     scores_ref[...] = total * (row_ref[...] * (1.0 / math.sqrt(HD)))
     pairs = scores_ref.shape[0]
     cands = LANES // span
@@ -221,16 +230,20 @@
                 chosen = chosen + jnp.where(head == h, context[start : start + query_n], 0.0)
             made.append(chosen)
         made = jnp.concatenate(made, axis=0).astype(BF16)
-        out_ref[at * cands * query_n : (at + 1) * cands * query_n] = made
+        half_width = width // 2
+        for half in range(2):
+            order = jnp.where(at_ref[0] == half, 0, 1)
+            made_half = made[:, half * half_width : (half + 1) * half_width]
+            out_ref[order, at * cands * query_n : (at + 1) * cands * query_n] = made_half
 
 
 def decode(at, blocks, mixed, scale, live, keys, slots, span, query_n):
-    rows, width = blocks.shape[1], slots[0].shape[-1] // 2
+    rows, width = blocks.shape[2], slots[0].shape[-1] // 2
     return local_call(
         functools.partial(decode_kernel, keys, len(slots), span, query_n),
         (at, blocks, mixed, scale, scale.reshape(1, -1), live, *slots),
-        [((rows // span * query_n, width), BF16)],
-        [((rows, width), BF16), ((mixed.shape[1], rows), F32)],
+        [((2, rows // span * query_n, width // 2), BF16)],
+        [((rows, width), BF16), ((mixed.shape[2], rows), F32)],
     )[0]
 
 
@@ -253,7 +266,7 @@
 
 
 def decode_out(at, blocks, source, weight, keys, slots):
-    column = ((blocks.shape[1], 1), F32)
+    column = ((blocks.shape[2], 1), F32)
     return local_call(
         functools.partial(last_kernel, keys, len(slots)),
         (at, blocks, source, weight, *slots),
@@ -414,11 +427,6 @@
     def slots_of(*sides):
         return [ref for parts in sides for ref in (parts if by_pairs else parts[2:])]
 
-    def ordered(own, got, axis):
-        return jnp.where(
-            side == 0, jnp.concatenate([own, got], axis), jnp.concatenate([got, own], axis)
-        )
-
     def side_part(a, of):
         width = a.shape[-1] // side_n
         return lax.dynamic_slice_in_dim(a, of * width, width, a.ndim - 1)
@@ -492,8 +500,6 @@
         partial,
         new_state,
         direct_score,
-        own_blocks,
-        got_blocks,
     ) = fence(
         qkv_far,
         owns_cross,
@@ -503,34 +509,31 @@
         partial,
         new_state,
         direct_score,
-        own_blocks,
-        got_blocks,
     )
 
     out_far = far(enc_out, out_next, out_inner)
-    last_next = to_next(last_own) if by_pairs else last_own
     if by_pairs:
         qkv_keys = [(0, None), (1, None), (2, None, 3), (4, None, 5)]
         outer, inner_last, outer_last = qkv_far
         qkv_slots = [qkv_own, qkv_next, qkv_inner, outer, inner_last, outer_last]
     else:
         qkv_keys, qkv_slots = keys_of((None, None)), qkv_far
-    queries = jnp.sum(partial.reshape(dp_n, query_n, -1), axis=0).astype(BF16)
-    queries = exchange(jnp.broadcast_to(queries, (dp_n,) + queries.shape).reshape(dp_n * query_n, -1))
     live_got = live_of(lengths_got)
     context_got = swap(enc_attention(at, got_blocks, live_got, qkv_keys, qkv_slots, span))
     context_own = enc_attention(at, own_blocks, live, qkv_keys, qkv_slots, span)
-    enc_context = ordered(context_own, context_got, 1)
-    enc_context, out_far, last_next, last_own, val_next, val_inner, queries = fence(
-        enc_context, out_far, last_next, last_own, val_next, val_inner, queries
+    enc_context = jnp.stack([context_own, context_got])
+    enc_context, out_far, last_own, val_next, val_inner, partial = fence(
+        enc_context, out_far, last_own, val_next, val_inner, partial
     )
 
     enc_blocks = everyone(enc_context)
     out_far = join(out_inner, out_far)
     out_cross = swap(out_far)
     val_far = far(val, val_next, val_inner)
-    enc_blocks, out_cross, val_far, last_next, last_own, queries = fence(
-        enc_blocks, out_cross, val_far, last_next, last_own, queries
+    queries = jnp.sum(partial.reshape(dp_n, query_n, -1), axis=0).astype(BF16)
+    queries = exchange(jnp.broadcast_to(queries, (dp_n,) + queries.shape).reshape(dp_n * query_n, -1))
+    enc_blocks, out_cross, val_far, last_own, queries = fence(
+        enc_blocks, out_cross, val_far, last_own, queries
     )
     summed, squares = encode_out(
         at,
@@ -542,9 +545,10 @@
     memory_blocks = everyone(summed)
     val_far = join(val_inner, val_far)
     val_cross = swap(val_far)
+    last_next = to_next(last_own) if by_pairs else last_own
+    last_inner = to_inner(last_own) if by_pairs else last_own
+    last_next, last_inner = fence(last_next, last_inner)
     last_cross = swap(last_next) if by_pairs else last_next
-    last_inner = to_inner(last_own) if by_pairs else last_own
-    (last_inner,) = fence(last_inner)
     last_far = far(last_own, last_next, last_inner)
     head_n = queries.shape[1] // HD
     mixed = jnp.einsum(
@@ -557,14 +561,13 @@
     pairs = head_n * query_n
     mixed = mixed.reshape(dp_n, query_n, head_n, depth).transpose(0, 2, 1, 3)
     mixed = exchange(mixed.reshape(dp_n, pairs, depth))
-    mixed = mixed.reshape(line_n, side_n, pairs, depth).transpose(0, 2, 1, 3)
-    mixed = mixed.reshape(line_n, pairs, side_n * depth)
+    mixed = mixed.reshape(line_n, side_n, pairs, depth)
     enc_squares = lax.psum(squares.reshape(1, -1), "mp").reshape(-1, 1)
     scale = 1.0 / jnp.sqrt(enc_squares / features + EPSILON)
-    val_cross, last_cross, last_far = fence(val_cross, last_cross, last_far)
+    val_cross, last_cross, last_far, scale = fence(val_cross, last_cross, last_far, scale)
     last_far = join(last_inner, last_far)
     last_far_cross = swap(last_far)
-    memory_blocks, scale, mixed = fence(memory_blocks, scale, mixed)
+    memory_blocks, mixed = fence(memory_blocks, mixed)
 
     cross_context = decode(
         at,

time: 348 us -> 334 us (0.960)
  blocking collectives: 52.6 us -> 75.3 us
  starting transfers between devices: 77.1 us -> 60.8 us
  waiting for transfers between devices: 102 us -> 87.7 us
  Pallas kernels: 43.9 us -> 40.1 us
    all_to_all x1 -> x2, blocking collectives: 14.5 us -> 37.2 us  [exchange(): return lax.all_to_all(a, 'dp', split_axis=0, concat_axis=0, tiled=True)]
    ppermute x18, waiting for transfers between devices: 25.9 us -> 14.3 us  [move(): lax.ppermute(a, 'dp', [(s * side_n + i, t * side_n + i) for s, t in pairs...]
    all_to_all x4 -> x3, starting transfers between devices: 28.9 us -> 21.1 us  [exchange(): return lax.all_to_all(a, 'dp', split_axis=0, concat_axis=0, tiled=True)]
    ppermute x18, starting transfers between devices: 35.2 us -> 29.5 us  [move(): lax.ppermute(a, 'dp', [(s * side_n + i, t * side_n + i) for s, t in pairs...]
    pallas_call x5, Pallas kernels: 37.8 us -> 34.1 us  [local_call(): pl.pallas_call(kernel, in_specs=[SMEM] + [VMEM] * (len(inputs) - 1), out_...]
    ppermute x10, waiting for transfers between devices: 20.9 us -> 17.2 us  [swap(): lax.ppermute(a, 'dp', [(i, i - i % side_n + (i + 1) % side_n) for i in ra...]
    all_to_all x4 -> x3, waiting for transfers between devices: 55.1 us -> 55.3 us  [exchange(): return lax.all_to_all(a, 'dp', split_axis=0, concat_axis=0, tiled=True)]
    unnamed x98 -> x96, local copies, waits for them, and re-layouts: 25.4 us -> 25.5 us
  transfers between devices with their start and end apart: 36 -> 35, of which waited for: 7 -> 7; matrix products, arithmetic and copies ran while one was open for 7% -> 6% of each run, Pallas kernels for 10% -> 9%
where the time goes in v5:
time: 334 us; the launch traced here: 333 us
  waiting for transfers between devices  87.7 us (26%)
  blocking collectives  75.3 us (23%)
  starting transfers between devices  60.8 us (18%)
  Pallas kernels  40.1 us (12%)
  local copies, waits for them, and re-layouts  37.9 us (11%)
  between operations  14.3 us (4%)
  other arithmetic  14.2 us (4%)
    all_to_all x3, waiting for transfers between devices, exchange(): return lax.all_to_all(a, 'dp', split_axis=0, concat_axis=0, tiled=True)  55.3 us
    all_to_all x2, blocking collectives, exchange(): return lax.all_to_all(a, 'dp', split_axis=0, concat_axis=0, tiled=True)  37.2 us
    pallas_call x5, Pallas kernels, local_call(): pl.pallas_call(kernel, in_specs=[SMEM] + [VMEM] * (len(inputs) - 1), out_...  34.1 us
    ppermute x18, starting transfers between devices, move(): lax.ppermute(a, 'dp', [(s * side_n + i, t * side_n + i) for s, t in pairs...  29.5 us
    unnamed x96, local copies, waits for them, and re-layouts  25.5 us
    all_to_all x3, starting transfers between devices, exchange(): return lax.all_to_all(a, 'dp', split_axis=0, concat_axis=0, tiled=True)  21.1 us
    ppermute x10, waiting for transfers between devices, swap(): lax.ppermute(a, 'dp', [(i, i - i % side_n + (i + 1) % side_n) for i in ra...  17.2 us
    ppermute x18, waiting for transfers between devices, move(): lax.ppermute(a, 'dp', [(s * side_n + i, t * side_n + i) for s, t in pairs...  14.3 us
  transfers between devices with their start and end apart: 35, of which 7 were waited for; matrix products, arithmetic and copies ran while one was open for 6% of the time, Pallas kernels for 9%

profile of v5, /device:TPU:0, one launch (start us, length us, event | category | flops | bytes accessed | tf_op | source)
XLA Modules:
  0.0 332.6 jit_solution(10177693450386942887)
XLA Ops:
  7.2 1.6 fusion.8
  13.8 3.0 collective-permute-start.1
  16.8 1.6 collective-permute-start.2
  18.5 1.5 collective-permute-start
  20.5 1.6 shard_map.184
  23.1 14.7 %collective-permute-done.3 = s32[16]{0:T(128)S(1)} collective-permute-done((s32[16]{0:T(128)S(1)}, s32[16]{0:T(128)S(1)}, u32[]{:S(2)}, u32[]{:S(2)}) %collective-permute-start.3) | collective-permute-done | bytes 96 | tf_op jit(solution)/shard_map/ppermute | solution.py:382
  37.8 2.4 collective-permute-done.1.refs_1_
  42.6 4.9 %collective-permute-start.4 = (bf16[1024,768]{1,0:T(8,128)(2,1)S(1)}, bf16[1024,768]{1,0:T(8,128)(2,1)}, u32[]{:S(2)}, u32[]{:S(2)}) collective-permute-start(bf16[1024,768]{1,0:T(8,128)(2,1)S(1)} %bitcast.89), channel_id=1, source_target_pairs={{0,8},{4,12},{8,0},{12,4},{16,24},{20,28},{24,16},{28,20},{1,9},{5... | collective-permute-start | bytes 4718600 | tf_op jit(solution)/shard_map/ppermute | solution.py:377
  47.5 1.9 collective-permute-start.5
  49.4 1.5 collective-permute-start.6
  50.9 5.7 %all-gather = bf16[1,8,4096]{2,1,0:T(8,128)(2,1)} all-gather(bf16[1,8,1024]{2,1,0:T(8,128)(2,1)S(1)} %copy-done.27), channel_id=2, replica_groups=mesh['dp'=8,'mp'=4] {'mp'}, dimensions={2}, use_global_device_ids=true | all-gather | bytes 81920 | tf_op jit(solution)/shard_map/all_gather | solution.py:469
  56.6 3.9 %all-to-all-start = ((bf16[8,8,512]{2,1,0:T(8,128)(2,1)}), bf16[8,8,512]{2,1,0:T(8,128)(2,1)S(1)}, u32[]{:S(2)}, u32[]{:S(2)}) async-start(bf16[8,8,512]{2,1,0:T(8,128)(2,1)} %bitcast.15), calls=%async_computation | async-start | bytes 131072 | tf_op jit(solution)/shard_map/all_to_all | solution.py:438
  63.4 1.4 pad_maximum_fusion
  64.8 21.4 %all-to-all-done = bf16[8,8,512]{2,1,0:T(8,128)(2,1)S(1)} async-done(((bf16[8,8,512]{2,1,0:T(8,128)(2,1)}), bf16[8,8,512]{2,1,0:T(8,128)(2,1)S(1)}, u32[]{:S(2)}, u32[]{:S(2)}) %all-to-all-start) | async-done | bytes 65568 | tf_op jit(solution)/shard_map/all_to_all | solution.py:438
  87.0 1.3 collective-permute-start.7
  88.3 1.8 collective-permute-start.8
  93.8 2.5 slice_bitcast_fusion
  97.1 7.8 %all-to-all-start.1 = ((f32[8,8,512]{2,1,0:T(8,128)}), f32[8,8,512]{2,1,0:T(8,128)S(1)}, u32[]{:S(2)}, u32[]{:S(2)}) async-start(f32[8,8,512]{2,1,0:T(8,128)} %fusion.1), calls=%async_computation.1 | async-start | bytes 262144 | tf_op jit(solution)/shard_map/all_to_all | solution.py:438
  105.0 3.4 %copy-done.2 = bf16[2,4096,512]{2,1,0:T(8,128)(2,1)S(1)} copy-done((bf16[2,4096,512]{2,1,0:T(8,128)(2,1)S(1)}, bf16[2,4096,512]{2,1,0:T(8,128)(2,1)}, u32[]{:S(2)}) %copy-start.2) | copy-done | bytes 8388632
  108.4 2.2 copy-done.6
  111.9 2.5 shard_map.186
  115.4 5.2 %all_gather.37.context_ref = bf16[16,2048]{1,0:T(8,128)(2,1)S(1)} all-gather(bf16[16,512]{1,0:T(8,128)(2,1)S(1)} %shard_map.186), channel_id=1, replica_groups=mesh['dp'=8,'mp'=4] {'mp'}, dimensions={1}, use_global_device_ids=true | all-gather | bytes 81920 | tf_op jit(solution)/shard_map/all_gather | solution.py:487
  122.2 7.5 %all-reduce.1 = (f32[16]{0:T(128)S(1)}, f32[16]{0:T(128)S(1)}) all-reduce(f32[16]{0:T(128)S(1)} %reduce.1, f32[16]{0:T(128)S(1)} %reduce.2), channel_id=1, replica_groups=mesh['dp'=8,'mp'=4] {'mp'}, use_global_device_ids=true, to_apply=%region_0.1 | all-reduce | flops 32 | bytes 256 | tf_op jit(solution)/shard_map/psum | solution.py:491
  129.7 34.0 %all-to-all-done.1 = f32[8,8,512]{2,1,0:T(8,128)S(1)} async-done(((f32[8,8,512]{2,1,0:T(8,128)}), f32[8,8,512]{2,1,0:T(8,128)S(1)}, u32[]{:S(2)}, u32[]{:S(2)}) %all-to-all-start.1) | async-done | bytes 131104 | tf_op jit(solution)/shard_map/all_to_all | solution.py:438
  163.7 1.5 collective-permute-start.14
  166.5 1.3 collective-permute-start.13
  168.0 2.2 copy-done.8
  170.2 9.1 %shard_map.189 = bf16[512,256]{1,0:T(8,128)(2,1)S(1)} custom-call(s32[6]{0:T(128)S(1)} %stack.89.at_ref, bf16[4,512,1024]{2,1,0:T(8,128)(2,1)S(1)} %bitcast.96, s32[1,512]{1,0:T(1,128)S(1)} %reshape.223.live_ref, bf16[1024,768]{1,0:T(8,128)(2,1)S(1)} %bitcast.91, bf16[1024,768]{1,0:T(8,128)(2,1)} %collective-permute-done.4.refs_1_, ...), custom_call_target="tpu_custom_call" | custom-call | flops 1000 | bytes 1000 | tf_op jit(solution)/shard_map/pallas_call | solution.py:55
  180.4 2.2 copy-done.7
  182.6 9.1 %shard_map.188 = bf16[512,256]{1,0:T(8,128)(2,1)S(1)} custom-call(s32[6]{0:T(128)S(1)} %stack.89.at_ref, bf16[4,512,1024]{2,1,0:T(8,128)(2,1)S(1)} %bitcast.95, s32[1,512]{1,0:T(1,128)S(1)} %reshape.221.live_ref, bf16[1024,768]{1,0:T(8,128)(2,1)S(1)} %bitcast.92, bf16[1024,768]{1,0:T(8,128)(2,1)} %collective-permute-done.4.refs_1_, ...), custom_call_target="tpu_custom_call" | custom-call | flops 1000 | bytes 1000 | tf_op jit(solution)/shard_map/pallas_call | solution.py:55
  199.7 26.3 %all_to_all.34 = bf16[8,8,512]{2,1,0:T(8,128)(2,1)S(1)} all-to-all(bf16[8,8,512]{2,1,0:T(8,128)(2,1)S(1)} %broadcast_in_dim.41), channel_id=1, replica_groups=mesh['dp'=8,'mp'=4] {'dp'}, dimensions={0} | all-to-all | bytes 131072 | tf_op jit(solution)/shard_map/all_to_all | solution.py:438
  229.4 1.6 copy-done.15
  232.2 5.3 %shard_map.190 = (bf16[2,512,512]{2,1,0:T(8,128)(2,1)S(1)}, f32[512,1]{1,0:T(8,128)S(1)}) custom-call(s32[6]{0:T(128)S(1)} %stack.89.at_ref, bf16[4,2,512,256]{3,2,1,0:T(8,128)(2,1)S(1)} %bitcast.99, bf16[512,1024]{1,0:T(8,128)(2,1)} %bitcast.6.tokens_ref, bf16[256,1024]{1,0:T(8,128)(2,1)S(1)} %copy-done.5, ...), custom_call_target="tpu_custom_call" | custom-call | flops 1000 | bytes 1000 | tf_op jit(solution)/shard_map/pallas_call | solution.py:55
  239.5 1.5 collective-permute-start.22
  242.8 5.1 %collective-permute-done.21.refs_1_ = bf16[256,1024]{1,0:T(8,128)(2,1)S(1)} collective-permute-done((bf16[256,1024]{1,0:T(8,128)(2,1)S(1)}, bf16[256,1024]{1,0:T(8,128)(2,1)S(1)}, u32[]{:S(2)}, u32[]{:S(2)}) %collective-permute-start.21) | collective-permute-done | bytes 524320 | tf_op jit(solution)/shard_map/ppermute | solution.py:377
  250.1 1.5 collective-permute-start.25
  252.8 2.1 copy.34
  255.7 1.4 fusion
  257.9 9.4 %all-to-all-start.3 = ((bf16[8,64,512]{2,1,0:T(8,128)(2,1)}), bf16[8,64,512]{2,1,0:T(8,128)(2,1)}, u32[]{:S(2)}, u32[]{:S(2)}) async-start(bf16[8,64,512]{2,1,0:T(8,128)(2,1)} %bitcast.105), calls=%async_computation.3 | async-start | bytes 1048576 | tf_op jit(solution)/shard_map/all_to_all | solution.py:438
  267.4 6.1 %psum.37 = f32[1,512]{1,0:T(1,128)S(1)} all-reduce(f32[1,512]{1,0:T(1,128)S(1)} %bitcast.111), channel_id=1, replica_groups=mesh['dp'=8,'mp'=4] {'mp'}, use_global_device_ids=true, to_apply=%region_3.4 | all-reduce | flops 512 | bytes 4096 | tf_op jit(solution)/shard_map/psum | solution.py:565
  273.5 2.5 collective-permute-done.23.refs_4_
  276.0 6.7 %collective-permute-done.26 = bf16[256,1024]{1,0:T(8,128)(2,1)} collective-permute-done((bf16[256,1024]{1,0:T(8,128)(2,1)S(1)}, bf16[256,1024]{1,0:T(8,128)(2,1)}, u32[]{:S(2)}, u32[]{:S(2)}) %collective-permute-start.26) | collective-permute-done | bytes 524320 | tf_op jit(solution)/shard_map/ppermute | solution.py:377
  286.0 2.2 copy-done.12
  289.4 7.0 %shard_map.191 = bf16[2,128,256]{2,1,0:T(8,128)(2,1)S(1)} custom-call(s32[6]{0:T(128)S(1)} %stack.89.at_ref, bf16[4,2,512,512]{3,2,1,0:T(8,128)(2,1)S(1)} %bitcast.98, bf16[4,2,64,512]{3,2,1,0:T(8,128)(2,1)} %bitcast.44.mixed_ref, f32[512,1]{1,0:T(8,128)S(1)} %copy.37.column_ref, f32[1,512]{1,0:T(1,128)S(1)} %bitcast.104, s32[1,512]{1,0:T(1,128)S(1)} %reshape.221.live_ref, ...), custom_call_target="tpu_custom_call" | custom-call | flops 1000 | bytes 1000 | tf_op jit(solution)/shard_map/pallas_call | solution.py:55
  296.4 7.2 %all-gather.5 = bf16[8,128,256]{2,1,0:T(8,128)(2,1)S(1)} all-gather(bf16[2,128,256]{2,1,0:T(8,128)(2,1)S(1)} %shard_map.191), channel_id=7, replica_groups=mesh['dp'=8,'mp'=4] {'mp'}, dimensions={0}, use_global_device_ids=true | all-gather | bytes 655360 | tf_op jit(solution)/shard_map/all_gather | solution.py:435
  303.6 3.6 %shard_map.192 = (f32[128,1]{1,0:T(8,128)S(1)}, f32[128,1]{1,0:T(8,128)S(1)}) custom-call(s32[6]{0:T(128)S(1)} %stack.89.at_ref, bf16[4,2,128,256]{3,2,1,0:T(8,128)(2,1)S(1)} %bitcast.100, bf16[8,1024]{1,0:T(8,128)(2,1)S(1)} %bitcast.103, bf16[1,1024]{1,0:T(2,128)(2,1)S(1)} %broadcast_in_dim.42.weight_ref, bf16[256,1024]{1,0:T(8,128)(2,1)S(1)} %copy-done.17, ...), custom_call_target="tpu_custom_call" | custom-call | flops 1000 | bytes 1000 | tf_op jit(solution)/shard_map/pallas_call | solution.py:55
  307.5 6.4 %all-reduce = (f32[1,128]{1,0:T(1,128)S(1)}, f32[1,128]{1,0:T(1,128)S(1)}) all-reduce(f32[1,128]{1,0:T(1,128)S(1)} %bitcast.112, f32[1,128]{1,0:T(1,128)S(1)} %bitcast.113), channel_id=1, replica_groups=mesh['dp'=8,'mp'=4] {'mp'}, use_global_device_ids=true, to_apply=%region_4.5 | all-reduce | flops 256 | bytes 2048 | tf_op jit(solution)/shard_map/psum | solution.py:593
  314.7 10.9 %all_to_all.35 = f32[8,1,16]{2,1,0:T(1,128)S(1)} all-to-all(f32[8,1,16]{2,1,0:T(1,128)S(1)} %compare_select_fusion), channel_id=1, replica_groups=mesh['dp'=8,'mp'=4] {'dp'}, dimensions={0} | all-to-all | bytes 1024 | tf_op jit(solution)/shard_map/all_to_all | solution.py:438
  (193 shorter events, 50.8 us)
Async XLA Ops:
  7.2 89.1 %copy-start = (bf16[512,512]{1,0:T(8,128)(2,1)S(1)}, bf16[512,512]{1,0:T(8,128)(2,1)}, u32[]{:S(2)}) copy-start(bf16[512,512]{1,0:T(8,128)(2,1)} %param.28) | copy-start | bytes 1572868
  11.7 8.8 %copy-start.21 = (bf16[16,32,1024]{2,1,0:T(8,128)(2,1)S(1)}, bf16[16,32,1024]{2,1,0:T(8,128)(2,1)}, u32[]{:S(2)}) copy-start(bf16[16,32,1024]{2,1,0:T(8,128)(2,1)} %in_ref.2) | copy-start | bytes 3145732
  12.7 9.5 %copy-start.29 = (bf16[1,256,1024]{2,1,0:T(8,128)(2,1)}, bf16[1,256,1024]{2,1,0:T(8,128)(2,1)S(1)}, u32[]{:S(2)}) copy-start(bf16[1,256,1024]{2,1,0:T(8,128)(2,1)S(1)} %get-tuple-element.143) | copy-start | bytes 1572868
  13.8 26.4 %collective-permute-start.1 = (bf16[2,256,1024]{2,1,0:T(8,128)(2,1)}, bf16[2,256,1024]{2,1,0:T(8,128)(2,1)S(1)}, u32[]{:S(2)}, u32[]{:S(2)}) collective-permute-start(bf16[2,256,1024]{2,1,0:T(8,128)(2,1)} %pad_maximum_fusion.1), channel_id=1, source_target_pairs={{0,8},{4,12},{8,0},{12,4},{16,24},{20,28},{24,16},{28,20},{1,9},{5... | collective-permute-start | bytes 3145736 | tf_op jit(solution)/shard_map/ppermute | solution.py:377
  16.8 23.4 %collective-permute-start.2 = (bf16[2,256,1024]{2,1,0:T(8,128)(2,1)}, bf16[2,256,1024]{2,1,0:T(8,128)(2,1)}, u32[]{:S(2)}, u32[]{:S(2)}) collective-permute-start(bf16[2,256,1024]{2,1,0:T(8,128)(2,1)} %pad_maximum_fusion.1), channel_id=1, source_target_pairs={{8,16},{12,20},{16,8},{20,12},{9,17},{13,21},{17,9},{21,13},{10,18... | collective-permute-start | bytes 3145736 | tf_op jit(solution)/shard_map/ppermute | solution.py:377
  18.5 19.3 %collective-permute-start = (bf16[512,768]{1,0:T(8,128)(2,1)}, bf16[512,768]{1,0:T(8,128)(2,1)}, u32[]{:S(2)}, u32[]{:S(2)}) collective-permute-start(bf16[512,768]{1,0:T(8,128)(2,1)} %pad_maximum_fusion.5), channel_id=1, source_target_pairs={{0,4},{4,0},{8,12},{12,8},{16,20},{20,16},{24,28},{28,24},{1,5},{5... | collective-permute-start | bytes 2359304 | tf_op jit(solution)/shard_map/ppermute | solution.py:382
  20.0 17.8 %collective-permute-start.3 = (s32[16]{0:T(128)S(1)}, s32[16]{0:T(128)S(1)}, u32[]{:S(2)}, u32[]{:S(2)}) collective-permute-start(s32[16]{0:T(128)S(1)} %copy-done.46), channel_id=1, source_target_pairs={{0,4},{4,0},{8,12},{12,8},{16,20},{20,16},{24,28},{28,24},{1,5},{5... | collective-permute-start | bytes 200 | tf_op jit(solution)/shard_map/ppermute | solution.py:382
  41.4 9.6 %copy-start.27 = (bf16[1,8,1024]{2,1,0:T(8,128)(2,1)S(1)}, bf16[1,8,1024]{2,1,0:T(8,128)(2,1)}, u32[]{:S(2)}) copy-start(bf16[1,8,1024]{2,1,0:T(8,128)(2,1)} %param.25) | copy-start | bytes 49156
  42.6 43.6 %collective-permute-start.4 = (bf16[1024,768]{1,0:T(8,128)(2,1)S(1)}, bf16[1024,768]{1,0:T(8,128)(2,1)}, u32[]{:S(2)}, u32[]{:S(2)}) collective-permute-start(bf16[1024,768]{1,0:T(8,128)(2,1)S(1)} %bitcast.89), channel_id=1, source_target_pairs={{0,8},{4,12},{8,0},{12,4},{16,24},{20,28},{24,16},{28,20},{1,9},{5... | collective-permute-start | bytes 4718600 | tf_op jit(solution)/shard_map/ppermute | solution.py:377
  47.5 38.7 %collective-permute-start.5 = (bf16[1024,768]{1,0:T(8,128)(2,1)S(1)}, bf16[1024,768]{1,0:T(8,128)(2,1)}, u32[]{:S(2)}, u32[]{:S(2)}) collective-permute-start(bf16[1024,768]{1,0:T(8,128)(2,1)S(1)} %bitcast.90), channel_id=1, source_target_pairs={{8,16},{12,20},{16,8},{20,12},{9,17},{13,21},{17,9},{21,13},{10,18... | collective-permute-start | bytes 4718600 | tf_op jit(solution)/shard_map/ppermute | solution.py:377
  49.4 36.8 %collective-permute-start.6 = (bf16[512,1024]{1,0:T(8,128)(2,1)}, bf16[512,1024]{1,0:T(8,128)(2,1)}, u32[]{:S(2)}, u32[]{:S(2)}) collective-permute-start(bf16[512,1024]{1,0:T(8,128)(2,1)} %bitcast.6.tokens_ref), channel_id=1, source_target_pairs={{0,4},{4,0},{8,12},{12,8},{16,20},{20,16},{24,28},{28,24},{1,5},{5... | collective-permute-start | bytes 3145736 | tf_op jit(solution)/shard_map/ppermute | solution.py:382
  56.6 29.6 %all-to-all-start = ((bf16[8,8,512]{2,1,0:T(8,128)(2,1)}), bf16[8,8,512]{2,1,0:T(8,128)(2,1)S(1)}, u32[]{:S(2)}, u32[]{:S(2)}) async-start(bf16[8,8,512]{2,1,0:T(8,128)(2,1)} %bitcast.15), calls=%async_computation | async-start | bytes 131072 | tf_op jit(solution)/shard_map/all_to_all | solution.py:438
  60.5 107.4 %all-gather.13.cloned.1.call-start = ((), (), s32[]{:S(2)}) async-start(), calls=%async_computation.6 | async-start | bytes 5242880 | tf_op jit(solution)/shard_map/all_gather | solution.py:435
  64.8 28.7 %copy-start.26 = (bf16[16,4096]{1,0:T(8,128)(2,1)S(1)}, bf16[16,4096]{1,0:T(8,128)(2,1)}, u32[]{:S(2)}) copy-start(bf16[16,4096]{1,0:T(8,128)(2,1)} %hidden_ref.1) | copy-start | bytes 393220
  64.8 28.8 %copy-start.44 = (bf16[1024]{0:T(1024)(128)(2,1)S(1)}, bf16[1024]{0:T(1024)(128)(2,1)}, u32[]{:S(2)}) copy-start(bf16[1024]{0:T(1024)(128)(2,1)} %param.31) | copy-start | bytes 6148
  86.3 94.1 %all-gather.11.cloned.1.call-start = ((), (), s32[]{:S(2)}) async-start(), calls=%async_computation.5 | async-start | bytes 5242880 | tf_op jit(solution)/shard_map/all_gather | solution.py:435
  87.0 76.7 %collective-permute-start.7 = (bf16[1024,768]{1,0:T(8,128)(2,1)}, bf16[1024,768]{1,0:T(8,128)(2,1)}, u32[]{:S(2)}, u32[]{:S(2)}) collective-permute-start(bf16[1024,768]{1,0:T(8,128)(2,1)} %collective-permute-done.5.refs_2_), channel_id=1, source_target_pairs={{8,0},{12,4},{16,24},{20,28},{9,1},{13,5},{17,25},{21,29},{10,2},{... | collective-permute-start | bytes 4718600 | tf_op jit(solution)/shard_map/ppermute | solution.py:377
  88.3 75.4 %collective-permute-start.8 = (bf16[1024,768]{1,0:T(8,128)(2,1)}, bf16[1024,768]{1,0:T(8,128)(2,1)}, u32[]{:S(2)}, u32[]{:S(2)}) collective-permute-start(bf16[1024,768]{1,0:T(8,128)(2,1)} %collective-permute-done.4.refs_1_), channel_id=1, source_target_pairs={{8,16},{12,20},{16,8},{20,12},{9,17},{13,21},{17,9},{21,13},{10,18... | collective-permute-start | bytes 4718600 | tf_op jit(solution)/shard_map/ppermute | solution.py:377
  90.1 73.6 %collective-permute-start.9 = (bf16[1024,768]{1,0:T(8,128)(2,1)}, bf16[1024,768]{1,0:T(8,128)(2,1)}, u32[]{:S(2)}, u32[]{:S(2)}) collective-permute-start(bf16[1024,768]{1,0:T(8,128)(2,1)} %collective-permute-done.4.refs_1_), channel_id=1, source_target_pairs={{8,24},{12,28},{16,0},{20,4},{9,25},{13,29},{17,1},{21,5},{10,26},... | collective-permute-start | bytes 4718600 | tf_op jit(solution)/shard_map/ppermute | solution.py:377
  91.4 72.3 %collective-permute-start.10 = (bf16[3,256,1024]{2,1,0:T(8,128)(2,1)}, bf16[3,256,1024]{2,1,0:T(8,128)(2,1)}, u32[]{:S(2)}, u32[]{:S(2)}) collective-permute-start(bf16[3,256,1024]{2,1,0:T(8,128)(2,1)} %pad_maximum_fusion), channel_id=1, source_target_pairs={{0,4},{4,0},{8,12},{12,8},{16,20},{20,16},{24,28},{28,24},{1,5},{5... | collective-permute-start | bytes 4718600 | tf_op jit(solution)/shard_map/ppermute | solution.py:382
  92.4 71.3 %collective-permute-start.11 = (bf16[2,256,1024]{2,1,0:T(8,128)(2,1)S(1)}, bf16[2,256,1024]{2,1,0:T(8,128)(2,1)}, u32[]{:S(2)}, u32[]{:S(2)}) collective-permute-start(bf16[2,256,1024]{2,1,0:T(8,128)(2,1)S(1)} %collective-permute-done.1.refs_1_), channel_id=1, source_target_pairs={{0,4},{4,0},{8,12},{12,8},{16,20},{20,16},{24,28},{28,24},{1,5},{5... | collective-permute-start | bytes 3145736 | tf_op jit(solution)/shard_map/ppermute | solution.py:382
  97.1 66.6 %all-to-all-start.1 = ((f32[8,8,512]{2,1,0:T(8,128)}), f32[8,8,512]{2,1,0:T(8,128)S(1)}, u32[]{:S(2)}, u32[]{:S(2)}) async-start(f32[8,8,512]{2,1,0:T(8,128)} %fusion.1), calls=%async_computation.1 | async-start | bytes 262144 | tf_op jit(solution)/shard_map/all_to_all | solution.py:438
  104.9 124.5 %all-gather.15.cloned.1.call-start = ((), (), s32[]{:S(2)}) async-start(), calls=%async_computation.7 | async-start | bytes 2621440 | tf_op jit(solution)/shard_map/all_gather | solution.py:435
  111.9 8.8 %copy-start.11 = (bf16[2048,1024]{1,0:T(8,128)(2,1)S(1)}, bf16[2048,1024]{1,0:T(8,128)(2,1)}, u32[]{:S(2)}) copy-start(bf16[2048,1024]{1,0:T(8,128)(2,1)} %wo_ref.1) | copy-start | bytes 12582916
  163.7 28.9 %collective-permute-start.14 = (bf16[256,1024]{1,0:T(8,128)(2,1)}, bf16[256,1024]{1,0:T(8,128)(2,1)}, u32[]{:S(2)}, u32[]{:S(2)}) collective-permute-start(bf16[256,1024]{1,0:T(8,128)(2,1)} %get-tuple-element.91), channel_id=1, source_target_pairs={{8,16},{12,20},{16,8},{20,12},{9,17},{13,21},{17,9},{21,13},{10,18... | collective-permute-start | bytes 1572872 | tf_op jit(solution)/shard_map/ppermute | solution.py:377
  165.2 27.4 %collective-permute-start.15 = (bf16[256,1024]{1,0:T(8,128)(2,1)}, bf16[256,1024]{1,0:T(8,128)(2,1)}, u32[]{:S(2)}, u32[]{:S(2)}) collective-permute-start(bf16[256,1024]{1,0:T(8,128)(2,1)} %get-tuple-element.91), channel_id=1, source_target_pairs={{8,24},{12,28},{16,0},{20,4},{9,25},{13,29},{17,1},{21,5},{10,26},... | collective-permute-start | bytes 1572872 | tf_op jit(solution)/shard_map/ppermute | solution.py:377
  166.5 26.1 %collective-permute-start.13 = (bf16[256,1024]{1,0:T(8,128)(2,1)}, bf16[256,1024]{1,0:T(8,128)(2,1)}, u32[]{:S(2)}, u32[]{:S(2)}) collective-permute-start(bf16[256,1024]{1,0:T(8,128)(2,1)} %get-tuple-element.90), channel_id=1, source_target_pairs={{8,0},{12,4},{16,24},{20,28},{9,1},{13,5},{17,25},{21,29},{10,2},{... | collective-permute-start | bytes 1572872 | tf_op jit(solution)/shard_map/ppermute | solution.py:377
  179.2 12.4 %collective-permute-start.12 = (bf16[512,256]{1,0:T(8,128)(2,1)S(1)}, bf16[512,256]{1,0:T(8,128)(2,1)S(1)}, u32[]{:S(2)}, u32[]{:S(2)}) collective-permute-start(bf16[512,256]{1,0:T(8,128)(2,1)S(1)} %shard_map.189), channel_id=1, source_target_pairs={{0,4},{4,0},{8,12},{12,8},{16,20},{20,16},{24,28},{28,24},{1,5},{5... | collective-permute-start | bytes 786440 | tf_op jit(solution)/shard_map/ppermute | solution.py:382
  192.6 93.4 %all-gather.17.cloned.1.call-start = ((), (), s32[]{:S(2)}) async-start(), calls=%async_computation.8 | async-start | bytes 5242880 | tf_op jit(solution)/shard_map/all_gather | solution.py:435
  195.2 34.2 %copy-start.5 = (bf16[256,1024]{1,0:T(8,128)(2,1)S(1)}, bf16[256,1024]{1,0:T(8,128)(2,1)}, u32[]{:S(2)}) copy-start(bf16[256,1024]{1,0:T(8,128)(2,1)} %refs_0_.1) | copy-start | bytes 1572868
  195.3 33.1 %collective-permute-start.16 = (bf16[2,256,1024]{2,1,0:T(8,128)(2,1)S(1)}, bf16[2,256,1024]{2,1,0:T(8,128)(2,1)S(1)}, u32[]{:S(2)}, u32[]{:S(2)}) collective-permute-start(bf16[2,256,1024]{2,1,0:T(8,128)(2,1)S(1)} %pad_maximum_fusion.2.refs_2_), channel_id=1, source_target_pairs={{0,4},{4,0},{8,12},{12,8},{16,20},{20,16},{24,28},{28,24},{1,5},{5... | collective-permute-start | bytes 3145736 | tf_op jit(solution)/shard_map/ppermute | solution.py:382
  196.3 29.6 %collective-permute-start.17 = (bf16[256,1024]{1,0:T(8,128)(2,1)S(1)}, bf16[256,1024]{1,0:T(8,128)(2,1)S(1)}, u32[]{:S(2)}, u32[]{:S(2)}) collective-permute-start(bf16[256,1024]{1,0:T(8,128)(2,1)S(1)} %copy-done.32), channel_id=1, source_target_pairs={{8,0},{12,4},{16,24},{20,28},{9,1},{13,5},{17,25},{21,29},{10,2},{... | collective-permute-start | bytes 1572872 | tf_op jit(solution)/shard_map/ppermute | solution.py:377
  197.6 28.3 %collective-permute-start.18 = (bf16[256,1024]{1,0:T(8,128)(2,1)S(1)}, bf16[256,1024]{1,0:T(8,128)(2,1)S(1)}, u32[]{:S(2)}, u32[]{:S(2)}) collective-permute-start(bf16[256,1024]{1,0:T(8,128)(2,1)S(1)} %copy-done.43), channel_id=1, source_target_pairs={{8,16},{12,20},{16,8},{20,12},{9,17},{13,21},{17,9},{21,13},{10,18... | collective-permute-start | bytes 1572872 | tf_op jit(solution)/shard_map/ppermute | solution.py:377
  198.3 28.4 %collective-permute-start.19 = (bf16[256,1024]{1,0:T(8,128)(2,1)S(1)}, bf16[256,1024]{1,0:T(8,128)(2,1)S(1)}, u32[]{:S(2)}, u32[]{:S(2)}) collective-permute-start(bf16[256,1024]{1,0:T(8,128)(2,1)S(1)} %copy-done.43), channel_id=1, source_target_pairs={{8,24},{12,28},{16,0},{20,4},{9,25},{13,29},{17,1},{21,5},{10,26},... | collective-permute-start | bytes 1572872 | tf_op jit(solution)/shard_map/ppermute | solution.py:377
  238.6 9.2 %collective-permute-start.21 = (bf16[256,1024]{1,0:T(8,128)(2,1)S(1)}, bf16[256,1024]{1,0:T(8,128)(2,1)S(1)}, u32[]{:S(2)}, u32[]{:S(2)}) collective-permute-start(bf16[256,1024]{1,0:T(8,128)(2,1)S(1)} %copy-done.17), channel_id=1, source_target_pairs={{0,8},{4,12},{8,0},{12,4},{16,24},{20,28},{24,16},{28,20},{1,9},{5... | collective-permute-start | bytes 1572872 | tf_op jit(solution)/shard_map/ppermute | solution.py:377
  239.5 8.4 %collective-permute-start.22 = (bf16[256,1024]{1,0:T(8,128)(2,1)S(1)}, bf16[256,1024]{1,0:T(8,128)(2,1)}, u32[]{:S(2)}, u32[]{:S(2)}) collective-permute-start(bf16[256,1024]{1,0:T(8,128)(2,1)S(1)} %copy-done.17), channel_id=1, source_target_pairs={{8,16},{12,20},{16,8},{20,12},{9,17},{13,21},{17,9},{21,13},{10,18... | collective-permute-start | bytes 1572872 | tf_op jit(solution)/shard_map/ppermute | solution.py:377
  242.2 15.7 %copy-start.13 = (bf16[2,256,1024]{2,1,0:T(8,128)(2,1)}, bf16[2,256,1024]{2,1,0:T(8,128)(2,1)S(1)}, u32[]{:S(2)}) copy-start(bf16[2,256,1024]{2,1,0:T(8,128)(2,1)S(1)} %pad_maximum_fusion.3.refs_2_) | copy-start | bytes 3145732
  242.2 31.3 %collective-permute-start.20 = (bf16[2,256,1024]{2,1,0:T(8,128)(2,1)S(1)}, bf16[2,256,1024]{2,1,0:T(8,128)(2,1)}, u32[]{:S(2)}, u32[]{:S(2)}) collective-permute-start(bf16[2,256,1024]{2,1,0:T(8,128)(2,1)S(1)} %pad_maximum_fusion.3.refs_2_), channel_id=1, source_target_pairs={{0,4},{4,0},{8,12},{12,8},{16,20},{20,16},{24,28},{28,24},{1,5},{5... | collective-permute-start | bytes 3145736 | tf_op jit(solution)/shard_map/ppermute | solution.py:382
  247.9 10.0 %copy-start.24 = (bf16[256,1024]{1,0:T(8,128)(2,1)}, bf16[256,1024]{1,0:T(8,128)(2,1)S(1)}, u32[]{:S(2)}) copy-start(bf16[256,1024]{1,0:T(8,128)(2,1)S(1)} %collective-permute-done.21.refs_1_) | copy-start | bytes 1572868
  247.9 28.1 %collective-permute-start.23 = (bf16[256,1024]{1,0:T(8,128)(2,1)S(1)}, bf16[256,1024]{1,0:T(8,128)(2,1)}, u32[]{:S(2)}, u32[]{:S(2)}) collective-permute-start(bf16[256,1024]{1,0:T(8,128)(2,1)S(1)} %collective-permute-done.21.refs_1_), channel_id=1, source_target_pairs={{0,4},{4,0},{8,12},{12,8},{16,20},{20,16},{24,28},{28,24},{1,5},{5... | collective-permute-start | bytes 1572872 | tf_op jit(solution)/shard_map/ppermute | solution.py:382
  248.8 27.2 %collective-permute-start.24 = (bf16[256,1024]{1,0:T(8,128)(2,1)}, bf16[256,1024]{1,0:T(8,128)(2,1)}, u32[]{:S(2)}, u32[]{:S(2)}) collective-permute-start(bf16[256,1024]{1,0:T(8,128)(2,1)} %collective-permute-done.22), channel_id=1, source_target_pairs={{8,0},{12,4},{16,24},{20,28},{9,1},{13,5},{17,25},{21,29},{10,2},{... | collective-permute-start | bytes 1572872 | tf_op jit(solution)/shard_map/ppermute | solution.py:377
  250.1 26.0 %collective-permute-start.25 = (bf16[256,1024]{1,0:T(8,128)(2,1)S(1)}, bf16[256,1024]{1,0:T(8,128)(2,1)}, u32[]{:S(2)}, u32[]{:S(2)}) collective-permute-start(bf16[256,1024]{1,0:T(8,128)(2,1)S(1)} %collective-permute-done.21.refs_1_), channel_id=1, source_target_pairs={{8,16},{12,20},{16,8},{20,12},{9,17},{13,21},{17,9},{21,13},{10,18... | collective-permute-start | bytes 1572872 | tf_op jit(solution)/shard_map/ppermute | solution.py:377
  251.5 31.2 %collective-permute-start.26 = (bf16[256,1024]{1,0:T(8,128)(2,1)S(1)}, bf16[256,1024]{1,0:T(8,128)(2,1)}, u32[]{:S(2)}, u32[]{:S(2)}) collective-permute-start(bf16[256,1024]{1,0:T(8,128)(2,1)S(1)} %collective-permute-done.21.refs_1_), channel_id=1, source_target_pairs={{8,24},{12,28},{16,0},{20,4},{9,25},{13,29},{17,1},{21,5},{10,26},... | collective-permute-start | bytes 1572872 | tf_op jit(solution)/shard_map/ppermute | solution.py:377
  257.9 28.1 %all-to-all-start.3 = ((bf16[8,64,512]{2,1,0:T(8,128)(2,1)}), bf16[8,64,512]{2,1,0:T(8,128)(2,1)}, u32[]{:S(2)}, u32[]{:S(2)}) async-start(bf16[8,64,512]{2,1,0:T(8,128)(2,1)} %bitcast.105), calls=%async_computation.3 | async-start | bytes 1048576 | tf_op jit(solution)/shard_map/all_to_all | solution.py:438
  285.1 18.5 %collective-permute-start.27 = (bf16[2,256,1024]{2,1,0:T(8,128)(2,1)S(1)}, bf16[2,256,1024]{2,1,0:T(8,128)(2,1)}, u32[]{:S(2)}, u32[]{:S(2)}) collective-permute-start(bf16[2,256,1024]{2,1,0:T(8,128)(2,1)S(1)} %pad_maximum_fusion.4.refs_2_), channel_id=1, source_target_pairs={{0,4},{4,0},{8,12},{12,8},{16,20},{20,16},{24,28},{28,24},{1,5},{5... | collective-permute-start | bytes 3145736 | tf_op jit(solution)/shard_map/ppermute | solution.py:382
  289.4 14.2 %copy-start.25 = (bf16[256,1024]{1,0:T(8,128)(2,1)S(1)}, bf16[256,1024]{1,0:T(8,128)(2,1)}, u32[]{:S(2)}) copy-start(bf16[256,1024]{1,0:T(8,128)(2,1)} %copy-done.24) | copy-start | bytes 1572868
  303.6 22.5 %copy-start.1 = (bf16[512,512]{1,0:T(8,128)(2,1)S(1)}, bf16[512,512]{1,0:T(8,128)(2,1)}, u32[]{:S(2)}) copy-start(bf16[512,512]{1,0:T(8,128)(2,1)} %param.28) | copy-start | bytes 1572868
  303.6 11.1 %copy-start.47 = (s32[16]{0:T(128)S(1)}, s32[16]{0:T(128)}, u32[]{:S(2)}) copy-start(s32[16]{0:T(128)} %param.33) | copy-start | bytes 196
  (35 other events, 85.5 us)
Sparse Core Ops, SparseCore 0:
  86.4 33.7 all-gather.12
  121.8 34.4 all-gather.10
  192.7 24.8 all-gather.14
  238.8 33.6 all-gather.16

commit v6 on v5

--- a/solution.py
+++ b/solution.py
@@ -448,14 +448,12 @@
     qkv_sent, enc_out, val = fence(qkv_sent, enc_out, cross_kv[1])
     qkv_got = swap(qkv_sent)
     val = jnp.concatenate(jnp.split(val, fold, axis=0), axis=1)
-    own_pair = jnp.stack([enc_out, val])
     qkv_own = jnp.concatenate([side_part(w, side) for w in enc_qkv], axis=1)
-    pair_next = to_next(own_pair) if by_pairs else own_pair
-    pair_inner = to_inner(own_pair) if by_pairs else own_pair
+    out_next, val_next = (to_next(a) if by_pairs else a for a in (enc_out, val))
+    out_inner, val_inner = (to_inner(a) if by_pairs else a for a in (enc_out, val))
     tokens = take_rows(cand_embed, parent, 0).reshape(beam_n * span, local_width)
-    lengths_got = swap(lengths)
-    qkv_got, pair_next, pair_inner, tokens, lengths_got, qkv_own = fence(
-        qkv_got, pair_next, pair_inner, tokens, lengths_got, qkv_own
+    qkv_got, out_next, val_next, out_inner, val_inner, tokens, qkv_own = fence(
+        qkv_got, out_next, val_next, out_inner, val_inner, tokens, qkv_own
     )
 
     both = jnp.zeros((side_n,) + qkv_own.shape, BF16)
@@ -465,14 +463,16 @@
     qkv_next = to_next(qkv_own) if by_pairs else qkv_own
     qkv_inner = to_inner(qkv_own) if by_pairs else qkv_own
     tokens_got = swap(tokens)
+    lengths_got = swap(lengths)
+    pair_next = jnp.stack([out_next, val_next])
     own_blocks = everyone(tokens)
     source_rows = lax.all_gather(source[0], "mp", axis=1, tiled=True)
     source_cut = source_rows.reshape(query_n, dp_n, -1).transpose(1, 0, 2)
     source_cut = exchange(source_cut)
     cache = take_rows(kv_cache, parent, 1)
     owns = jnp.stack([enc_out, val, cross_out])
-    qkv_next, qkv_inner, tokens_got, owns, pair_next, cache, source_cut = fence(
-        qkv_next, qkv_inner, tokens_got, owns, pair_next, cache, source_cut
+    qkv_next, qkv_inner, tokens_got, lengths_got, owns, pair_next, cache, source_cut = fence(
+        qkv_next, qkv_inner, tokens_got, lengths_got, owns, pair_next, cache, source_cut
     )
 
     qkv_far = far(qkv_own, qkv_next, qkv_inner)
@@ -490,7 +490,6 @@
     new_state, *sums = direct_state(context, wo_direct, hidden_share, w_direct[None])
     squares, direct_dot = lax.psum(tuple(a.reshape(-1) for a in sums), "mp")
     direct_score = direct_dot / jnp.sqrt(squares / features + EPSILON)
-    out_next, out_inner, val_next, val_inner = pair_next[0], pair_inner[0], pair_next[1], pair_inner[1]
     (
         qkv_far,
         owns_cross,

time: 334 us -> 330 us (0.988)
  starting transfers between devices: 60.8 us -> 65.4 us
  local copies, waits for them, and re-layouts: 37.9 us -> 33.5 us
  waiting for transfers between devices: 87.7 us -> 84.3 us
    ppermute x18 -> x20, waiting for transfers between devices: 14.3 us -> 28.4 us  [move(): lax.ppermute(a, 'dp', [(s * side_n + i, t * side_n + i) for s, t in pairs...]
    ppermute x10, waiting for transfers between devices: 17.2 us -> 7.57 us  [swap(): lax.ppermute(a, 'dp', [(i, i - i % side_n + (i + 1) % side_n) for i in ra...]
    all_to_all x3, waiting for transfers between devices: 55.3 us -> 47.6 us  [exchange(): return lax.all_to_all(a, 'dp', split_axis=0, concat_axis=0, tiled=True)]
    squeeze x2 -> x0, local copies, waits for them, and re-layouts: 3.5 us -> none  [the longest x1 2.47 us: shards(): pair_inner[1]]
    ppermute x10, starting transfers between devices: 9.87 us -> 13.3 us  [swap(): lax.ppermute(a, 'dp', [(i, i - i % side_n + (i + 1) % side_n) for i in ra...]
    ppermute x18 -> x20, starting transfers between devices: 29.5 us -> 30.8 us  [move(): lax.ppermute(a, 'dp', [(s * side_n + i, t * side_n + i) for s, t in pairs...]
    unnamed x96 -> x90, local copies, waits for them, and re-layouts: 25.5 us -> 24.5 us
  transfers between devices with their start and end apart: 35 -> 37, of which waited for: 7 -> 8; matrix products, arithmetic and copies ran while one was open for 6% -> 6% of each run, Pallas kernels for 9% -> 10%
where the time goes in v6:
time: 330 us; the launch traced here: 328 us
  waiting for transfers between devices  84.3 us (26%)
  blocking collectives  74.1 us (22%)
  starting transfers between devices  65.4 us (20%)
  Pallas kernels  40.2 us (12%)
  local copies, waits for them, and re-layouts  33.5 us (10%)
  between operations  14.4 us (4%)
  other arithmetic  14.2 us (4%)
    all_to_all x3, waiting for transfers between devices, exchange(): return lax.all_to_all(a, 'dp', split_axis=0, concat_axis=0, tiled=True)  47.6 us
    all_to_all x2, blocking collectives, exchange(): return lax.all_to_all(a, 'dp', split_axis=0, concat_axis=0, tiled=True)  35.5 us
    pallas_call x5, Pallas kernels, local_call(): pl.pallas_call(kernel, in_specs=[SMEM] + [VMEM] * (len(inputs) - 1), out_...  34.1 us
    ppermute x20, starting transfers between devices, move(): lax.ppermute(a, 'dp', [(s * side_n + i, t * side_n + i) for s, t in pairs...  30.8 us
    ppermute x20, waiting for transfers between devices, move(): lax.ppermute(a, 'dp', [(s * side_n + i, t * side_n + i) for s, t in pairs...  28.4 us
    unnamed x90, local copies, waits for them, and re-layouts  24.5 us
    all_to_all x3, starting transfers between devices, exchange(): return lax.all_to_all(a, 'dp', split_axis=0, concat_axis=0, tiled=True)  20.9 us
    ppermute x10, starting transfers between devices, swap(): lax.ppermute(a, 'dp', [(i, i - i % side_n + (i + 1) % side_n) for i in ra...  13.3 us
  transfers between devices with their start and end apart: 37, of which 8 were waited for; matrix products, arithmetic and copies ran while one was open for 6% of the time, Pallas kernels for 10%

profile of v6, /device:TPU:0, one launch (start us, length us, event | category | flops | bytes accessed | tf_op | source)
XLA Modules:
  0.0 328.2 jit_solution(11223298960512353218)
XLA Ops:
  7.2 1.6 fusion.8
  11.7 2.9 collective-permute-start
  14.6 1.6 collective-permute-start.1
  17.6 1.5 collective-permute-start.3
  19.1 1.5 collective-permute-start.4
  20.6 1.6 shard_map.184
  23.2 6.4 %collective-permute-done.1 = bf16[256,1024]{1,0:T(8,128)(2,1)} collective-permute-done((bf16[256,1024]{1,0:T(8,128)(2,1)S(1)}, bf16[256,1024]{1,0:T(8,128)(2,1)}, u32[]{:S(2)}, u32[]{:S(2)}) %collective-permute-start.1) | collective-permute-done | bytes 524320 | tf_op jit(solution)/shard_map/ppermute | solution.py:377
  29.6 9.8 %collective-permute-done.2 = bf16[256,1024]{1,0:T(8,128)(2,1)} collective-permute-done((bf16[256,1024]{1,0:T(8,128)(2,1)S(1)}, bf16[256,1024]{1,0:T(8,128)(2,1)}, u32[]{:S(2)}, u32[]{:S(2)}) %collective-permute-start.2) | collective-permute-done | bytes 524320 | tf_op jit(solution)/shard_map/ppermute | solution.py:377
  41.9 6.0 %collective-permute-start.5 = (bf16[1024,768]{1,0:T(8,128)(2,1)S(1)}, bf16[1024,768]{1,0:T(8,128)(2,1)}, u32[]{:S(2)}, u32[]{:S(2)}) collective-permute-start(bf16[1024,768]{1,0:T(8,128)(2,1)S(1)} %bitcast.83), channel_id=1, source_target_pairs={{0,8},{4,12},{8,0},{12,4},{16,24},{20,28},{24,16},{28,20},{1,9},{5... | collective-permute-start | bytes 4718600 | tf_op jit(solution)/shard_map/ppermute | solution.py:377
  47.8 1.8 collective-permute-start.6
  50.2 1.5 collective-permute-start.8
  51.7 5.7 %all-gather = bf16[1,8,4096]{2,1,0:T(8,128)(2,1)} all-gather(bf16[1,8,1024]{2,1,0:T(8,128)(2,1)S(1)} %copy-done.27), channel_id=2, replica_groups=mesh['dp'=8,'mp'=4] {'mp'}, dimensions={2}, use_global_device_ids=true | all-gather | bytes 81920 | tf_op jit(solution)/shard_map/all_gather | solution.py:469
  57.4 3.8 %all-to-all-start = ((bf16[8,8,512]{2,1,0:T(8,128)(2,1)}), bf16[8,8,512]{2,1,0:T(8,128)(2,1)S(1)}, u32[]{:S(2)}, u32[]{:S(2)}) async-start(bf16[8,8,512]{2,1,0:T(8,128)(2,1)} %bitcast.17), calls=%async_computation | async-start | bytes 131072 | tf_op jit(solution)/shard_map/all_to_all | solution.py:438
  66.6 6.3 %collective-permute-done.8 = s32[16]{0:T(128)S(1)} collective-permute-done((s32[16]{0:T(128)S(1)}, s32[16]{0:T(128)S(1)}, u32[]{:S(2)}, u32[]{:S(2)}) %collective-permute-start.8) | collective-permute-done | bytes 96 | tf_op jit(solution)/shard_map/ppermute | solution.py:382
  72.9 12.0 %all-to-all-done = bf16[8,8,512]{2,1,0:T(8,128)(2,1)S(1)} async-done(((bf16[8,8,512]{2,1,0:T(8,128)(2,1)}), bf16[8,8,512]{2,1,0:T(8,128)(2,1)S(1)}, u32[]{:S(2)}, u32[]{:S(2)}) %all-to-all-start) | async-done | bytes 65568 | tf_op jit(solution)/shard_map/all_to_all | solution.py:438
  87.0 1.8 collective-permute-start.10
  90.1 1.4 collective-permute-start.12
  93.3 8.7 %all-to-all-start.1 = ((f32[8,8,512]{2,1,0:T(8,128)}), f32[8,8,512]{2,1,0:T(8,128)S(1)}, u32[]{:S(2)}, u32[]{:S(2)}) async-start(f32[8,8,512]{2,1,0:T(8,128)} %fusion.1), calls=%async_computation.1 | async-start | bytes 262144 | tf_op jit(solution)/shard_map/all_to_all | solution.py:438
  102.1 3.4 %copy-done.2 = bf16[2,4096,512]{2,1,0:T(8,128)(2,1)S(1)} copy-done((bf16[2,4096,512]{2,1,0:T(8,128)(2,1)S(1)}, bf16[2,4096,512]{2,1,0:T(8,128)(2,1)}, u32[]{:S(2)}) %copy-start.2) | copy-done | bytes 8388632
  105.5 2.2 copy-done.3
  108.9 2.5 shard_map.186
  111.4 5.6 %all_gather.37.context_ref = bf16[16,2048]{1,0:T(8,128)(2,1)S(1)} all-gather(bf16[16,512]{1,0:T(8,128)(2,1)S(1)} %shard_map.186), channel_id=1, replica_groups=mesh['dp'=8,'mp'=4] {'mp'}, dimensions={1}, use_global_device_ids=true | all-gather | bytes 81920 | tf_op jit(solution)/shard_map/all_gather | solution.py:487
  118.5 7.6 %all-reduce.1 = (f32[16]{0:T(128)S(1)}, f32[16]{0:T(128)S(1)}) all-reduce(f32[16]{0:T(128)S(1)} %reduce.1, f32[16]{0:T(128)S(1)} %reduce.2), channel_id=1, replica_groups=mesh['dp'=8,'mp'=4] {'mp'}, use_global_device_ids=true, to_apply=%region_0.1 | all-reduce | flops 32 | bytes 256 | tf_op jit(solution)/shard_map/psum | solution.py:491
  126.1 35.6 %all-to-all-done.1 = f32[8,8,512]{2,1,0:T(8,128)S(1)} async-done(((f32[8,8,512]{2,1,0:T(8,128)}), f32[8,8,512]{2,1,0:T(8,128)S(1)}, u32[]{:S(2)}, u32[]{:S(2)}) %all-to-all-start.1) | async-done | bytes 131104 | tf_op jit(solution)/shard_map/all_to_all | solution.py:438
  161.7 1.5 collective-permute-start.16
  165.9 2.2 copy-done.5
  168.1 9.1 %shard_map.189 = bf16[512,256]{1,0:T(8,128)(2,1)S(1)} custom-call(s32[6]{0:T(128)S(1)} %stack.95.at_ref, bf16[4,512,1024]{2,1,0:T(8,128)(2,1)S(1)} %bitcast.88, s32[1,512]{1,0:T(1,128)S(1)} %reshape.223.live_ref, bf16[1024,768]{1,0:T(8,128)(2,1)S(1)} %bitcast.85, bf16[1024,768]{1,0:T(8,128)(2,1)} %collective-permute-done.5.refs_1_, ...), custom_call_target="tpu_custom_call" | custom-call | flops 1000 | bytes 1000 | tf_op jit(solution)/shard_map/pallas_call | solution.py:55
  177.2 1.7 collective-permute-start.14
  178.9 2.2 copy-done.4
  181.1 9.1 %shard_map.188 = bf16[512,256]{1,0:T(8,128)(2,1)S(1)} custom-call(s32[6]{0:T(128)S(1)} %stack.95.at_ref, bf16[4,512,1024]{2,1,0:T(8,128)(2,1)S(1)} %bitcast.87, s32[1,512]{1,0:T(1,128)S(1)} %reshape.221.live_ref, bf16[1024,768]{1,0:T(8,128)(2,1)S(1)} %bitcast.86, bf16[1024,768]{1,0:T(8,128)(2,1)} %collective-permute-done.5.refs_1_, ...), custom_call_target="tpu_custom_call" | custom-call | flops 1000 | bytes 1000 | tf_op jit(solution)/shard_map/pallas_call | solution.py:55
  197.5 26.2 %all_to_all.34 = bf16[8,8,512]{2,1,0:T(8,128)(2,1)S(1)} all-to-all(bf16[8,8,512]{2,1,0:T(8,128)(2,1)S(1)} %broadcast_in_dim.41), channel_id=1, replica_groups=mesh['dp'=8,'mp'=4] {'dp'}, dimensions={0} | all-to-all | bytes 131072 | tf_op jit(solution)/shard_map/all_to_all | solution.py:438
  226.3 1.6 copy-done.12
  229.1 5.3 %shard_map.190 = (bf16[2,512,512]{2,1,0:T(8,128)(2,1)S(1)}, f32[512,1]{1,0:T(8,128)S(1)}) custom-call(s32[6]{0:T(128)S(1)} %stack.95.at_ref, bf16[4,2,512,256]{3,2,1,0:T(8,128)(2,1)S(1)} %bitcast.91, bf16[512,1024]{1,0:T(8,128)(2,1)} %bitcast.4.tokens_ref, bf16[256,1024]{1,0:T(8,128)(2,1)S(1)} %copy-done.14, ...), custom_call_target="tpu_custom_call" | custom-call | flops 1000 | bytes 1000 | tf_op jit(solution)/shard_map/pallas_call | solution.py:55
  236.3 1.5 collective-permute-start.24
  240.1 5.1 %collective-permute-done.23.refs_1_ = bf16[256,1024]{1,0:T(8,128)(2,1)S(1)} collective-permute-done((bf16[256,1024]{1,0:T(8,128)(2,1)S(1)}, bf16[256,1024]{1,0:T(8,128)(2,1)S(1)}, u32[]{:S(2)}, u32[]{:S(2)}) %collective-permute-start.23) | collective-permute-done | bytes 524320 | tf_op jit(solution)/shard_map/ppermute | solution.py:377
  245.2 1.8 collective-permute-start.25
  248.3 1.5 collective-permute-start.27
  251.0 2.1 copy.34
  253.9 1.4 fusion
  256.1 8.4 %all-to-all-start.3 = ((bf16[8,64,512]{2,1,0:T(8,128)(2,1)}), bf16[8,64,512]{2,1,0:T(8,128)(2,1)}, u32[]{:S(2)}, u32[]{:S(2)}) async-start(bf16[8,64,512]{2,1,0:T(8,128)(2,1)} %bitcast.98), calls=%async_computation.3 | async-start | bytes 1048576 | tf_op jit(solution)/shard_map/all_to_all | solution.py:438
  264.6 6.1 %psum.37 = f32[1,512]{1,0:T(1,128)S(1)} all-reduce(f32[1,512]{1,0:T(1,128)S(1)} %bitcast.104), channel_id=1, replica_groups=mesh['dp'=8,'mp'=4] {'mp'}, use_global_device_ids=true, to_apply=%region_3.4 | all-reduce | flops 512 | bytes 4096 | tf_op jit(solution)/shard_map/psum | solution.py:564
  272.0 7.1 %collective-permute-done.28 = bf16[256,1024]{1,0:T(8,128)(2,1)} collective-permute-done((bf16[256,1024]{1,0:T(8,128)(2,1)S(1)}, bf16[256,1024]{1,0:T(8,128)(2,1)}, u32[]{:S(2)}, u32[]{:S(2)}) %collective-permute-start.28) | collective-permute-done | bytes 524320 | tf_op jit(solution)/shard_map/ppermute | solution.py:377
  283.1 2.2 copy-done.9
  286.5 7.0 %shard_map.191 = bf16[2,128,256]{2,1,0:T(8,128)(2,1)S(1)} custom-call(s32[6]{0:T(128)S(1)} %stack.95.at_ref, bf16[4,2,512,512]{3,2,1,0:T(8,128)(2,1)S(1)} %bitcast.90, bf16[4,2,64,512]{3,2,1,0:T(8,128)(2,1)} %bitcast.42.mixed_ref, f32[512,1]{1,0:T(8,128)S(1)} %copy.37.column_ref, f32[1,512]{1,0:T(1,128)S(1)} %bitcast.97, s32[1,512]{1,0:T(1,128)S(1)} %reshape.221.live_ref, ...), custom_call_target="tpu_custom_call" | custom-call | flops 1000 | bytes 1000 | tf_op jit(solution)/shard_map/pallas_call | solution.py:55
  293.5 7.2 %all-gather.5 = bf16[8,128,256]{2,1,0:T(8,128)(2,1)S(1)} all-gather(bf16[2,128,256]{2,1,0:T(8,128)(2,1)S(1)} %shard_map.191), channel_id=7, replica_groups=mesh['dp'=8,'mp'=4] {'mp'}, dimensions={0}, use_global_device_ids=true | all-gather | bytes 655360 | tf_op jit(solution)/shard_map/all_gather | solution.py:435
  300.7 3.6 %shard_map.192 = (f32[128,1]{1,0:T(8,128)S(1)}, f32[128,1]{1,0:T(8,128)S(1)}) custom-call(s32[6]{0:T(128)S(1)} %stack.95.at_ref, bf16[4,2,128,256]{3,2,1,0:T(8,128)(2,1)S(1)} %bitcast.93, bf16[8,1024]{1,0:T(8,128)(2,1)S(1)} %bitcast.96, bf16[1,1024]{1,0:T(2,128)(2,1)S(1)} %broadcast_in_dim.42.weight_ref, bf16[256,1024]{1,0:T(8,128)(2,1)S(1)} %copy-done.16, ...), custom_call_target="tpu_custom_call" | custom-call | flops 1000 | bytes 1000 | tf_op jit(solution)/shard_map/pallas_call | solution.py:55
  304.5 6.4 %all-reduce = (f32[1,128]{1,0:T(1,128)S(1)}, f32[1,128]{1,0:T(1,128)S(1)}) all-reduce(f32[1,128]{1,0:T(1,128)S(1)} %bitcast.105, f32[1,128]{1,0:T(1,128)S(1)} %bitcast.106), channel_id=1, replica_groups=mesh['dp'=8,'mp'=4] {'mp'}, use_global_device_ids=true, to_apply=%region_4.5 | all-reduce | flops 256 | bytes 2048 | tf_op jit(solution)/shard_map/psum | solution.py:592
  311.8 9.3 %all_to_all.35 = f32[8,1,16]{2,1,0:T(1,128)S(1)} all-to-all(f32[8,1,16]{2,1,0:T(1,128)S(1)} %compare_select_fusion), channel_id=1, replica_groups=mesh['dp'=8,'mp'=4] {'dp'}, dimensions={0} | all-to-all | bytes 1024 | tf_op jit(solution)/shard_map/all_to_all | solution.py:438
  (189 shorter events, 51.7 us)
Async XLA Ops:
  7.2 85.3 %copy-start = (bf16[512,512]{1,0:T(8,128)(2,1)S(1)}, bf16[512,512]{1,0:T(8,128)(2,1)}, u32[]{:S(2)}) copy-start(bf16[512,512]{1,0:T(8,128)(2,1)} %param.28) | copy-start | bytes 1572868
  11.7 27.7 %collective-permute-start = (bf16[512,768]{1,0:T(8,128)(2,1)}, bf16[512,768]{1,0:T(8,128)(2,1)}, u32[]{:S(2)}, u32[]{:S(2)}) collective-permute-start(bf16[512,768]{1,0:T(8,128)(2,1)} %pad_maximum_fusion.5), channel_id=1, source_target_pairs={{0,4},{4,0},{8,12},{12,8},{16,20},{20,16},{24,28},{28,24},{1,5},{5... | collective-permute-start | bytes 2359304 | tf_op jit(solution)/shard_map/ppermute | solution.py:382
  14.6 15.0 %collective-permute-start.1 = (bf16[256,1024]{1,0:T(8,128)(2,1)S(1)}, bf16[256,1024]{1,0:T(8,128)(2,1)}, u32[]{:S(2)}, u32[]{:S(2)}) collective-permute-start(bf16[256,1024]{1,0:T(8,128)(2,1)S(1)} %copy-done.13), channel_id=1, source_target_pairs={{0,8},{4,12},{8,0},{12,4},{16,24},{20,28},{24,16},{28,20},{1,9},{5... | collective-permute-start | bytes 1572872 | tf_op jit(solution)/shard_map/ppermute | solution.py:377
  17.2 22.2 %collective-permute-start.2 = (bf16[256,1024]{1,0:T(8,128)(2,1)S(1)}, bf16[256,1024]{1,0:T(8,128)(2,1)}, u32[]{:S(2)}, u32[]{:S(2)}) collective-permute-start(bf16[256,1024]{1,0:T(8,128)(2,1)S(1)} %get-tuple-element.143.refs_0_), channel_id=1, source_target_pairs={{0,8},{4,12},{8,0},{12,4},{16,24},{20,28},{24,16},{28,20},{1,9},{5... | collective-permute-start | bytes 1572872 | tf_op jit(solution)/shard_map/ppermute | solution.py:377
  17.6 21.7 %collective-permute-start.3 = (bf16[256,1024]{1,0:T(8,128)(2,1)S(1)}, bf16[256,1024]{1,0:T(8,128)(2,1)}, u32[]{:S(2)}, u32[]{:S(2)}) collective-permute-start(bf16[256,1024]{1,0:T(8,128)(2,1)S(1)} %copy-done.13), channel_id=1, source_target_pairs={{8,16},{12,20},{16,8},{20,12},{9,17},{13,21},{17,9},{21,13},{10,18... | collective-permute-start | bytes 1572872 | tf_op jit(solution)/shard_map/ppermute | solution.py:377
  19.1 20.3 %collective-permute-start.4 = (bf16[256,1024]{1,0:T(8,128)(2,1)S(1)}, bf16[256,1024]{1,0:T(8,128)(2,1)}, u32[]{:S(2)}, u32[]{:S(2)}) collective-permute-start(bf16[256,1024]{1,0:T(8,128)(2,1)S(1)} %get-tuple-element.143.refs_0_), channel_id=1, source_target_pairs={{8,16},{12,20},{16,8},{20,12},{9,17},{13,21},{17,9},{21,13},{10,18... | collective-permute-start | bytes 1572872 | tf_op jit(solution)/shard_map/ppermute | solution.py:377
  40.5 11.2 %copy-start.27 = (bf16[1,8,1024]{2,1,0:T(8,128)(2,1)S(1)}, bf16[1,8,1024]{2,1,0:T(8,128)(2,1)}, u32[]{:S(2)}) copy-start(bf16[1,8,1024]{2,1,0:T(8,128)(2,1)} %param.25) | copy-start | bytes 49156
  40.6 23.4 %copy-start.15 = (bf16[256,1024]{1,0:T(8,128)(2,1)S(1)}, bf16[256,1024]{1,0:T(8,128)(2,1)}, u32[]{:S(2)}) copy-start(bf16[256,1024]{1,0:T(8,128)(2,1)} %refs_0_.2) | copy-start | bytes 1572868
  41.9 43.1 %collective-permute-start.5 = (bf16[1024,768]{1,0:T(8,128)(2,1)S(1)}, bf16[1024,768]{1,0:T(8,128)(2,1)}, u32[]{:S(2)}, u32[]{:S(2)}) collective-permute-start(bf16[1024,768]{1,0:T(8,128)(2,1)S(1)} %bitcast.83), channel_id=1, source_target_pairs={{0,8},{4,12},{8,0},{12,4},{16,24},{20,28},{24,16},{28,20},{1,9},{5... | collective-permute-start | bytes 4718600 | tf_op jit(solution)/shard_map/ppermute | solution.py:377
  47.8 37.1 %collective-permute-start.6 = (bf16[1024,768]{1,0:T(8,128)(2,1)S(1)}, bf16[1024,768]{1,0:T(8,128)(2,1)}, u32[]{:S(2)}, u32[]{:S(2)}) collective-permute-start(bf16[1024,768]{1,0:T(8,128)(2,1)S(1)} %bitcast.84), channel_id=1, source_target_pairs={{8,16},{12,20},{16,8},{20,12},{9,17},{13,21},{17,9},{21,13},{10,18... | collective-permute-start | bytes 4718600 | tf_op jit(solution)/shard_map/ppermute | solution.py:377
  49.7 35.3 %collective-permute-start.7 = (bf16[512,1024]{1,0:T(8,128)(2,1)}, bf16[512,1024]{1,0:T(8,128)(2,1)}, u32[]{:S(2)}, u32[]{:S(2)}) collective-permute-start(bf16[512,1024]{1,0:T(8,128)(2,1)} %bitcast.4.tokens_ref), channel_id=1, source_target_pairs={{0,4},{4,0},{8,12},{12,8},{16,20},{20,16},{24,28},{28,24},{1,5},{5... | collective-permute-start | bytes 3145736 | tf_op jit(solution)/shard_map/ppermute | solution.py:382
  50.2 22.7 %collective-permute-start.8 = (s32[16]{0:T(128)S(1)}, s32[16]{0:T(128)S(1)}, u32[]{:S(2)}, u32[]{:S(2)}) collective-permute-start(s32[16]{0:T(128)S(1)} %copy-done.43), channel_id=1, source_target_pairs={{0,4},{4,0},{8,12},{12,8},{16,20},{20,16},{24,28},{28,24},{1,5},{5... | collective-permute-start | bytes 200 | tf_op jit(solution)/shard_map/ppermute | solution.py:382
  57.4 27.6 %all-to-all-start = ((bf16[8,8,512]{2,1,0:T(8,128)(2,1)}), bf16[8,8,512]{2,1,0:T(8,128)(2,1)S(1)}, u32[]{:S(2)}, u32[]{:S(2)}) async-start(bf16[8,8,512]{2,1,0:T(8,128)(2,1)} %bitcast.17), calls=%async_computation | async-start | bytes 131072 | tf_op jit(solution)/shard_map/all_to_all | solution.py:438
  61.1 104.8 %all-gather.13.cloned.1.call-start = ((), (), s32[]{:S(2)}) async-start(), calls=%async_computation.6 | async-start | bytes 5242880 | tf_op jit(solution)/shard_map/all_gather | solution.py:435
  66.6 25.7 %copy-start.41 = (bf16[1024]{0:T(1024)(128)(2,1)S(1)}, bf16[1024]{0:T(1024)(128)(2,1)}, u32[]{:S(2)}) copy-start(bf16[1024]{0:T(1024)(128)(2,1)} %param.31) | copy-start | bytes 6148
  66.6 25.8 %copy-start.26 = (bf16[16,4096]{1,0:T(8,128)(2,1)S(1)}, bf16[16,4096]{1,0:T(8,128)(2,1)}, u32[]{:S(2)}) copy-start(bf16[16,4096]{1,0:T(8,128)(2,1)} %hidden_ref.1) | copy-start | bytes 393220
  85.0 93.9 %all-gather.11.cloned.1.call-start = ((), (), s32[]{:S(2)}) async-start(), calls=%async_computation.5 | async-start | bytes 5242880 | tf_op jit(solution)/shard_map/all_gather | solution.py:435
  85.7 76.0 %collective-permute-start.9 = (bf16[1024,768]{1,0:T(8,128)(2,1)}, bf16[1024,768]{1,0:T(8,128)(2,1)}, u32[]{:S(2)}, u32[]{:S(2)}) collective-permute-start(bf16[1024,768]{1,0:T(8,128)(2,1)} %collective-permute-done.6.refs_2_), channel_id=1, source_target_pairs={{8,0},{12,4},{16,24},{20,28},{9,1},{13,5},{17,25},{21,29},{10,2},{... | collective-permute-start | bytes 4718600 | tf_op jit(solution)/shard_map/ppermute | solution.py:377
  87.0 74.7 %collective-permute-start.10 = (bf16[1024,768]{1,0:T(8,128)(2,1)}, bf16[1024,768]{1,0:T(8,128)(2,1)}, u32[]{:S(2)}, u32[]{:S(2)}) collective-permute-start(bf16[1024,768]{1,0:T(8,128)(2,1)} %collective-permute-done.5.refs_1_), channel_id=1, source_target_pairs={{8,16},{12,20},{16,8},{20,12},{9,17},{13,21},{17,9},{21,13},{10,18... | collective-permute-start | bytes 4718600 | tf_op jit(solution)/shard_map/ppermute | solution.py:377
  88.8 72.9 %collective-permute-start.11 = (bf16[1024,768]{1,0:T(8,128)(2,1)}, bf16[1024,768]{1,0:T(8,128)(2,1)}, u32[]{:S(2)}, u32[]{:S(2)}) collective-permute-start(bf16[1024,768]{1,0:T(8,128)(2,1)} %collective-permute-done.5.refs_1_), channel_id=1, source_target_pairs={{8,24},{12,28},{16,0},{20,4},{9,25},{13,29},{17,1},{21,5},{10,26},... | collective-permute-start | bytes 4718600 | tf_op jit(solution)/shard_map/ppermute | solution.py:377
  90.1 71.6 %collective-permute-start.12 = (bf16[3,256,1024]{2,1,0:T(8,128)(2,1)}, bf16[3,256,1024]{2,1,0:T(8,128)(2,1)}, u32[]{:S(2)}, u32[]{:S(2)}) collective-permute-start(bf16[3,256,1024]{2,1,0:T(8,128)(2,1)} %pad_maximum_fusion), channel_id=1, source_target_pairs={{0,4},{4,0},{8,12},{12,8},{16,20},{20,16},{24,28},{28,24},{1,5},{5... | collective-permute-start | bytes 4718600 | tf_op jit(solution)/shard_map/ppermute | solution.py:382
  91.6 70.1 %collective-permute-start.13 = (bf16[2,256,1024]{2,1,0:T(8,128)(2,1)S(1)}, bf16[2,256,1024]{2,1,0:T(8,128)(2,1)}, u32[]{:S(2)}, u32[]{:S(2)}) collective-permute-start(bf16[2,256,1024]{2,1,0:T(8,128)(2,1)S(1)} %pad_maximum_fusion.1.refs_1_), channel_id=1, source_target_pairs={{0,4},{4,0},{8,12},{12,8},{16,20},{20,16},{24,28},{28,24},{1,5},{5... | collective-permute-start | bytes 3145736 | tf_op jit(solution)/shard_map/ppermute | solution.py:382
  93.3 68.3 %all-to-all-start.1 = ((f32[8,8,512]{2,1,0:T(8,128)}), f32[8,8,512]{2,1,0:T(8,128)S(1)}, u32[]{:S(2)}, u32[]{:S(2)}) async-start(f32[8,8,512]{2,1,0:T(8,128)} %fusion.1), calls=%async_computation.1 | async-start | bytes 262144 | tf_op jit(solution)/shard_map/all_to_all | solution.py:438
  102.0 124.3 %all-gather.15.cloned.1.call-start = ((), (), s32[]{:S(2)}) async-start(), calls=%async_computation.7 | async-start | bytes 2621440 | tf_op jit(solution)/shard_map/all_gather | solution.py:435
  161.7 29.3 %collective-permute-start.16 = (bf16[256,1024]{1,0:T(8,128)(2,1)}, bf16[256,1024]{1,0:T(8,128)(2,1)}, u32[]{:S(2)}, u32[]{:S(2)}) collective-permute-start(bf16[256,1024]{1,0:T(8,128)(2,1)} %collective-permute-done.1), channel_id=1, source_target_pairs={{8,16},{12,20},{16,8},{20,12},{9,17},{13,21},{17,9},{21,13},{10,18... | collective-permute-start | bytes 1572872 | tf_op jit(solution)/shard_map/ppermute | solution.py:377
  163.2 27.8 %collective-permute-start.17 = (bf16[256,1024]{1,0:T(8,128)(2,1)}, bf16[256,1024]{1,0:T(8,128)(2,1)}, u32[]{:S(2)}, u32[]{:S(2)}) collective-permute-start(bf16[256,1024]{1,0:T(8,128)(2,1)} %collective-permute-done.1), channel_id=1, source_target_pairs={{8,24},{12,28},{16,0},{20,4},{9,25},{13,29},{17,1},{21,5},{10,26},... | collective-permute-start | bytes 1572872 | tf_op jit(solution)/shard_map/ppermute | solution.py:377
  164.5 26.5 %collective-permute-start.15 = (bf16[256,1024]{1,0:T(8,128)(2,1)}, bf16[256,1024]{1,0:T(8,128)(2,1)}, u32[]{:S(2)}, u32[]{:S(2)}) collective-permute-start(bf16[256,1024]{1,0:T(8,128)(2,1)} %collective-permute-done.3), channel_id=1, source_target_pairs={{8,0},{12,4},{16,24},{20,28},{9,1},{13,5},{17,25},{21,29},{10,2},{... | collective-permute-start | bytes 1572872 | tf_op jit(solution)/shard_map/ppermute | solution.py:377
  177.2 13.0 %collective-permute-start.14 = (bf16[512,256]{1,0:T(8,128)(2,1)S(1)}, bf16[512,256]{1,0:T(8,128)(2,1)S(1)}, u32[]{:S(2)}, u32[]{:S(2)}) collective-permute-start(bf16[512,256]{1,0:T(8,128)(2,1)S(1)} %shard_map.189), channel_id=1, source_target_pairs={{0,4},{4,0},{8,12},{12,8},{16,20},{20,16},{24,28},{28,24},{1,5},{5... | collective-permute-start | bytes 786440 | tf_op jit(solution)/shard_map/ppermute | solution.py:382
  191.0 92.0 %all-gather.17.cloned.1.call-start = ((), (), s32[]{:S(2)}) async-start(), calls=%async_computation.8 | async-start | bytes 5242880 | tf_op jit(solution)/shard_map/all_gather | solution.py:435
  193.5 32.7 %copy-start.14 = (bf16[256,1024]{1,0:T(8,128)(2,1)S(1)}, bf16[256,1024]{1,0:T(8,128)(2,1)}, u32[]{:S(2)}) copy-start(bf16[256,1024]{1,0:T(8,128)(2,1)} %refs_0_.1) | copy-start | bytes 1572868
  193.7 31.6 %collective-permute-start.18 = (bf16[2,256,1024]{2,1,0:T(8,128)(2,1)S(1)}, bf16[2,256,1024]{2,1,0:T(8,128)(2,1)S(1)}, u32[]{:S(2)}, u32[]{:S(2)}) collective-permute-start(bf16[2,256,1024]{2,1,0:T(8,128)(2,1)S(1)} %pad_maximum_fusion.2.refs_2_), channel_id=1, source_target_pairs={{0,4},{4,0},{8,12},{12,8},{16,20},{20,16},{24,28},{28,24},{1,5},{5... | collective-permute-start | bytes 3145736 | tf_op jit(solution)/shard_map/ppermute | solution.py:382
  194.1 29.5 %collective-permute-start.19 = (bf16[256,1024]{1,0:T(8,128)(2,1)}, bf16[256,1024]{1,0:T(8,128)(2,1)S(1)}, u32[]{:S(2)}, u32[]{:S(2)}) collective-permute-start(bf16[256,1024]{1,0:T(8,128)(2,1)} %collective-permute-done.4), channel_id=1, source_target_pairs={{8,0},{12,4},{16,24},{20,28},{9,1},{13,5},{17,25},{21,29},{10,2},{... | collective-permute-start | bytes 1572872 | tf_op jit(solution)/shard_map/ppermute | solution.py:377
  195.4 28.2 %collective-permute-start.20 = (bf16[256,1024]{1,0:T(8,128)(2,1)}, bf16[256,1024]{1,0:T(8,128)(2,1)S(1)}, u32[]{:S(2)}, u32[]{:S(2)}) collective-permute-start(bf16[256,1024]{1,0:T(8,128)(2,1)} %collective-permute-done.2), channel_id=1, source_target_pairs={{8,16},{12,20},{16,8},{20,12},{9,17},{13,21},{17,9},{21,13},{10,18... | collective-permute-start | bytes 1572872 | tf_op jit(solution)/shard_map/ppermute | solution.py:377
  196.1 28.4 %collective-permute-start.21 = (bf16[256,1024]{1,0:T(8,128)(2,1)}, bf16[256,1024]{1,0:T(8,128)(2,1)S(1)}, u32[]{:S(2)}, u32[]{:S(2)}) collective-permute-start(bf16[256,1024]{1,0:T(8,128)(2,1)} %collective-permute-done.2), channel_id=1, source_target_pairs={{8,24},{12,28},{16,0},{20,4},{9,25},{13,29},{17,1},{21,5},{10,26},... | collective-permute-start | bytes 1572872 | tf_op jit(solution)/shard_map/ppermute | solution.py:377
  235.5 9.7 %collective-permute-start.23 = (bf16[256,1024]{1,0:T(8,128)(2,1)S(1)}, bf16[256,1024]{1,0:T(8,128)(2,1)S(1)}, u32[]{:S(2)}, u32[]{:S(2)}) collective-permute-start(bf16[256,1024]{1,0:T(8,128)(2,1)S(1)} %copy-done.16), channel_id=1, source_target_pairs={{0,8},{4,12},{8,0},{12,4},{16,24},{20,28},{24,16},{28,20},{1,9},{5... | collective-permute-start | bytes 1572872 | tf_op jit(solution)/shard_map/ppermute | solution.py:377
  236.3 8.8 %collective-permute-start.24 = (bf16[256,1024]{1,0:T(8,128)(2,1)S(1)}, bf16[256,1024]{1,0:T(8,128)(2,1)}, u32[]{:S(2)}, u32[]{:S(2)}) collective-permute-start(bf16[256,1024]{1,0:T(8,128)(2,1)S(1)} %copy-done.16), channel_id=1, source_target_pairs={{8,16},{12,20},{16,8},{20,12},{9,17},{13,21},{17,9},{21,13},{10,18... | collective-permute-start | bytes 1572872 | tf_op jit(solution)/shard_map/ppermute | solution.py:377
  239.1 17.0 %copy-start.10 = (bf16[2,256,1024]{2,1,0:T(8,128)(2,1)}, bf16[2,256,1024]{2,1,0:T(8,128)(2,1)S(1)}, u32[]{:S(2)}) copy-start(bf16[2,256,1024]{2,1,0:T(8,128)(2,1)S(1)} %pad_maximum_fusion.3.refs_2_) | copy-start | bytes 3145732
  239.1 31.6 %collective-permute-start.22 = (bf16[2,256,1024]{2,1,0:T(8,128)(2,1)S(1)}, bf16[2,256,1024]{2,1,0:T(8,128)(2,1)}, u32[]{:S(2)}, u32[]{:S(2)}) collective-permute-start(bf16[2,256,1024]{2,1,0:T(8,128)(2,1)S(1)} %pad_maximum_fusion.3.refs_2_), channel_id=1, source_target_pairs={{0,4},{4,0},{8,12},{12,8},{16,20},{20,16},{24,28},{28,24},{1,5},{5... | collective-permute-start | bytes 3145736 | tf_op jit(solution)/shard_map/ppermute | solution.py:382
  245.2 10.9 %copy-start.24 = (bf16[256,1024]{1,0:T(8,128)(2,1)}, bf16[256,1024]{1,0:T(8,128)(2,1)S(1)}, u32[]{:S(2)}) copy-start(bf16[256,1024]{1,0:T(8,128)(2,1)S(1)} %collective-permute-done.23.refs_1_) | copy-start | bytes 1572868
  245.2 26.8 %collective-permute-start.25 = (bf16[256,1024]{1,0:T(8,128)(2,1)S(1)}, bf16[256,1024]{1,0:T(8,128)(2,1)}, u32[]{:S(2)}, u32[]{:S(2)}) collective-permute-start(bf16[256,1024]{1,0:T(8,128)(2,1)S(1)} %collective-permute-done.23.refs_1_), channel_id=1, source_target_pairs={{0,4},{4,0},{8,12},{12,8},{16,20},{20,16},{24,28},{28,24},{1,5},{5... | collective-permute-start | bytes 1572872 | tf_op jit(solution)/shard_map/ppermute | solution.py:382
  247.0 25.0 %collective-permute-start.26 = (bf16[256,1024]{1,0:T(8,128)(2,1)}, bf16[256,1024]{1,0:T(8,128)(2,1)}, u32[]{:S(2)}, u32[]{:S(2)}) collective-permute-start(bf16[256,1024]{1,0:T(8,128)(2,1)} %collective-permute-done.24), channel_id=1, source_target_pairs={{8,0},{12,4},{16,24},{20,28},{9,1},{13,5},{17,25},{21,29},{10,2},{... | collective-permute-start | bytes 1572872 | tf_op jit(solution)/shard_map/ppermute | solution.py:377
  248.3 23.8 %collective-permute-start.27 = (bf16[256,1024]{1,0:T(8,128)(2,1)S(1)}, bf16[256,1024]{1,0:T(8,128)(2,1)}, u32[]{:S(2)}, u32[]{:S(2)}) collective-permute-start(bf16[256,1024]{1,0:T(8,128)(2,1)S(1)} %collective-permute-done.23.refs_1_), channel_id=1, source_target_pairs={{8,16},{12,20},{16,8},{20,12},{9,17},{13,21},{17,9},{21,13},{10,18... | collective-permute-start | bytes 1572872 | tf_op jit(solution)/shard_map/ppermute | solution.py:377
  249.8 29.4 %collective-permute-start.28 = (bf16[256,1024]{1,0:T(8,128)(2,1)S(1)}, bf16[256,1024]{1,0:T(8,128)(2,1)}, u32[]{:S(2)}, u32[]{:S(2)}) collective-permute-start(bf16[256,1024]{1,0:T(8,128)(2,1)S(1)} %collective-permute-done.23.refs_1_), channel_id=1, source_target_pairs={{8,24},{12,28},{16,0},{20,4},{9,25},{13,29},{17,1},{21,5},{10,26},... | collective-permute-start | bytes 1572872 | tf_op jit(solution)/shard_map/ppermute | solution.py:377
  256.1 26.9 %all-to-all-start.3 = ((bf16[8,64,512]{2,1,0:T(8,128)(2,1)}), bf16[8,64,512]{2,1,0:T(8,128)(2,1)}, u32[]{:S(2)}, u32[]{:S(2)}) async-start(bf16[8,64,512]{2,1,0:T(8,128)(2,1)} %bitcast.98), calls=%async_computation.3 | async-start | bytes 1048576 | tf_op jit(solution)/shard_map/all_to_all | solution.py:438
  281.5 19.2 %collective-permute-start.29 = (bf16[2,256,1024]{2,1,0:T(8,128)(2,1)S(1)}, bf16[2,256,1024]{2,1,0:T(8,128)(2,1)}, u32[]{:S(2)}, u32[]{:S(2)}) collective-permute-start(bf16[2,256,1024]{2,1,0:T(8,128)(2,1)S(1)} %pad_maximum_fusion.4.refs_2_), channel_id=1, source_target_pairs={{0,4},{4,0},{8,12},{12,8},{16,20},{20,16},{24,28},{28,24},{1,5},{5... | collective-permute-start | bytes 3145736 | tf_op jit(solution)/shard_map/ppermute | solution.py:382
  286.5 14.2 %copy-start.25 = (bf16[256,1024]{1,0:T(8,128)(2,1)S(1)}, bf16[256,1024]{1,0:T(8,128)(2,1)}, u32[]{:S(2)}) copy-start(bf16[256,1024]{1,0:T(8,128)(2,1)} %copy-done.24) | copy-start | bytes 1572868
  300.7 20.9 %copy-start.1 = (bf16[512,512]{1,0:T(8,128)(2,1)S(1)}, bf16[512,512]{1,0:T(8,128)(2,1)}, u32[]{:S(2)}) copy-start(bf16[512,512]{1,0:T(8,128)(2,1)} %param.28) | copy-start | bytes 1572868
  300.7 11.1 %copy-start.44 = (s32[16]{0:T(128)S(1)}, s32[16]{0:T(128)}, u32[]{:S(2)}) copy-start(s32[16]{0:T(128)} %param.33) | copy-start | bytes 196
  (34 other events, 115.6 us)
Sparse Core Ops, SparseCore 0:
  85.1 34.8 all-gather.12
  121.6 34.4 all-gather.10
  191.2 24.6 all-gather.14
  235.6 33.0 all-gather.16

commit v7 on v6

--- a/solution.py
+++ b/solution.py
@@ -452,12 +452,12 @@
     out_next, val_next = (to_next(a) if by_pairs else a for a in (enc_out, val))
     out_inner, val_inner = (to_inner(a) if by_pairs else a for a in (enc_out, val))
     tokens = take_rows(cand_embed, parent, 0).reshape(beam_n * span, local_width)
-    qkv_got, out_next, val_next, out_inner, val_inner, tokens, qkv_own = fence(
-        qkv_got, out_next, val_next, out_inner, val_inner, tokens, qkv_own
-    )
-
     both = jnp.zeros((side_n,) + qkv_own.shape, BF16)
     both = lax.dynamic_update_index_in_dim(both, qkv_own, side, 0)
+    qkv_got, out_next, val_next, out_inner, val_inner, tokens, both = fence(
+        qkv_got, out_next, val_next, out_inner, val_inner, tokens, both
+    )
+
     both = lax.dynamic_update_index_in_dim(both, qkv_got, 1 - side, 0)
     qkv_own = both.reshape(-1, both.shape[2])
     qkv_next = to_next(qkv_own) if by_pairs else qkv_own

time: 330 us -> 329 us (level)
    unnamed x90 -> x84, local copies, waits for them, and re-layouts: 24.5 us -> 23.5 us
where the time goes in v7:
time: 329 us; the launch traced here: 328 us
  waiting for transfers between devices  83.8 us (25%)
  blocking collectives  74.1 us (23%)
  starting transfers between devices  65.4 us (20%)
  Pallas kernels  40.2 us (12%)
  local copies, waits for them, and re-layouts  33.2 us (10%)
  other arithmetic  14.4 us (4%)
  between operations  14.4 us (4%)
    all_to_all x3, waiting for transfers between devices, exchange(): return lax.all_to_all(a, 'dp', split_axis=0, concat_axis=0, tiled=True)  47.5 us
    all_to_all x2, blocking collectives, exchange(): return lax.all_to_all(a, 'dp', split_axis=0, concat_axis=0, tiled=True)  35.6 us
    pallas_call x5, Pallas kernels, local_call(): pl.pallas_call(kernel, in_specs=[SMEM] + [VMEM] * (len(inputs) - 1), out_...  34.1 us
    ppermute x20, starting transfers between devices, move(): lax.ppermute(a, 'dp', [(s * side_n + i, t * side_n + i) for s, t in pairs...  30.9 us
    ppermute x20, waiting for transfers between devices, move(): lax.ppermute(a, 'dp', [(s * side_n + i, t * side_n + i) for s, t in pairs...  28 us
    unnamed x84, local copies, waits for them, and re-layouts  23.5 us
    all_to_all x3, starting transfers between devices, exchange(): return lax.all_to_all(a, 'dp', split_axis=0, concat_axis=0, tiled=True)  20.8 us
    ppermute x10, starting transfers between devices, swap(): lax.ppermute(a, 'dp', [(i, i - i % side_n + (i + 1) % side_n) for i in ra...  13.4 us
  transfers between devices with their start and end apart: 37, of which 8 were waited for; matrix products, arithmetic and copies ran while one was open for 6% of the time, Pallas kernels for 10%

profile of v7, /device:TPU:0, one launch (start us, length us, event | category | flops | bytes accessed | tf_op | source)
XLA Modules:
  0.0 327.8 jit_solution(6581283303497375413)
XLA Ops:
  7.2 1.6 fusion.9
  12.5 2.9 collective-permute-start
  15.4 1.6 collective-permute-start.1
  18.4 1.5 collective-permute-start.3
  19.9 1.5 collective-permute-start.4
  21.4 1.7 shard_map.184
  24.3 6.0 %collective-permute-done.1 = bf16[256,1024]{1,0:T(8,128)(2,1)} collective-permute-done((bf16[256,1024]{1,0:T(8,128)(2,1)S(1)}, bf16[256,1024]{1,0:T(8,128)(2,1)}, u32[]{:S(2)}, u32[]{:S(2)}) %collective-permute-start.1) | collective-permute-done | bytes 524320 | tf_op jit(solution)/shard_map/ppermute | solution.py:377
  30.4 9.8 %collective-permute-done.2 = bf16[256,1024]{1,0:T(8,128)(2,1)} collective-permute-done((bf16[256,1024]{1,0:T(8,128)(2,1)S(1)}, bf16[256,1024]{1,0:T(8,128)(2,1)}, u32[]{:S(2)}, u32[]{:S(2)}) %collective-permute-start.2) | collective-permute-done | bytes 524320 | tf_op jit(solution)/shard_map/ppermute | solution.py:377
  41.4 5.9 %collective-permute-start.5 = (bf16[1024,768]{1,0:T(8,128)(2,1)S(1)}, bf16[1024,768]{1,0:T(8,128)(2,1)}, u32[]{:S(2)}, u32[]{:S(2)}) collective-permute-start(bf16[1024,768]{1,0:T(8,128)(2,1)S(1)} %bitcast.85), channel_id=1, source_target_pairs={{0,8},{4,12},{8,0},{12,4},{16,24},{20,28},{24,16},{28,20},{1,9},{5... | collective-permute-start | bytes 4718600 | tf_op jit(solution)/shard_map/ppermute | solution.py:377
  47.3 1.9 collective-permute-start.6
  49.7 1.5 collective-permute-start.8
  51.2 5.7 %all-gather = bf16[1,8,4096]{2,1,0:T(8,128)(2,1)} all-gather(bf16[1,8,1024]{2,1,0:T(8,128)(2,1)S(1)} %copy-done.27), channel_id=2, replica_groups=mesh['dp'=8,'mp'=4] {'mp'}, dimensions={2}, use_global_device_ids=true | all-gather | bytes 81920 | tf_op jit(solution)/shard_map/all_gather | solution.py:469
  56.9 3.8 %all-to-all-start = ((bf16[8,8,512]{2,1,0:T(8,128)(2,1)}), bf16[8,8,512]{2,1,0:T(8,128)(2,1)S(1)}, u32[]{:S(2)}, u32[]{:S(2)}) async-start(bf16[8,8,512]{2,1,0:T(8,128)(2,1)} %bitcast.17), calls=%async_computation | async-start | bytes 131072 | tf_op jit(solution)/shard_map/all_to_all | solution.py:438
  66.2 6.3 %collective-permute-done.8 = s32[16]{0:T(128)S(1)} collective-permute-done((s32[16]{0:T(128)S(1)}, s32[16]{0:T(128)S(1)}, u32[]{:S(2)}, u32[]{:S(2)}) %collective-permute-start.8) | collective-permute-done | bytes 96 | tf_op jit(solution)/shard_map/ppermute | solution.py:382
  72.5 12.0 %all-to-all-done = bf16[8,8,512]{2,1,0:T(8,128)(2,1)S(1)} async-done(((bf16[8,8,512]{2,1,0:T(8,128)(2,1)}), bf16[8,8,512]{2,1,0:T(8,128)(2,1)S(1)}, u32[]{:S(2)}, u32[]{:S(2)}) %all-to-all-start) | async-done | bytes 65568 | tf_op jit(solution)/shard_map/all_to_all | solution.py:438
  86.5 1.8 collective-permute-start.10
  89.6 1.4 collective-permute-start.12
  92.9 8.7 %all-to-all-start.1 = ((f32[8,8,512]{2,1,0:T(8,128)}), f32[8,8,512]{2,1,0:T(8,128)S(1)}, u32[]{:S(2)}, u32[]{:S(2)}) async-start(f32[8,8,512]{2,1,0:T(8,128)} %fusion.2), calls=%async_computation.1 | async-start | bytes 262144 | tf_op jit(solution)/shard_map/all_to_all | solution.py:438
  101.6 3.4 %copy-done.2 = bf16[2,4096,512]{2,1,0:T(8,128)(2,1)S(1)} copy-done((bf16[2,4096,512]{2,1,0:T(8,128)(2,1)S(1)}, bf16[2,4096,512]{2,1,0:T(8,128)(2,1)}, u32[]{:S(2)}) %copy-start.2) | copy-done | bytes 8388632
  105.0 2.2 copy-done.3
  108.4 2.5 shard_map.186
  110.9 5.6 %all_gather.37.context_ref = bf16[16,2048]{1,0:T(8,128)(2,1)S(1)} all-gather(bf16[16,512]{1,0:T(8,128)(2,1)S(1)} %shard_map.186), channel_id=1, replica_groups=mesh['dp'=8,'mp'=4] {'mp'}, dimensions={1}, use_global_device_ids=true | all-gather | bytes 81920 | tf_op jit(solution)/shard_map/all_gather | solution.py:487
  118.0 7.6 %all-reduce.1 = (f32[16]{0:T(128)S(1)}, f32[16]{0:T(128)S(1)}) all-reduce(f32[16]{0:T(128)S(1)} %reduce.1, f32[16]{0:T(128)S(1)} %reduce.2), channel_id=1, replica_groups=mesh['dp'=8,'mp'=4] {'mp'}, use_global_device_ids=true, to_apply=%region_0.1 | all-reduce | flops 32 | bytes 256 | tf_op jit(solution)/shard_map/psum | solution.py:491
  125.6 35.6 %all-to-all-done.1 = f32[8,8,512]{2,1,0:T(8,128)S(1)} async-done(((f32[8,8,512]{2,1,0:T(8,128)}), f32[8,8,512]{2,1,0:T(8,128)S(1)}, u32[]{:S(2)}, u32[]{:S(2)}) %all-to-all-start.1) | async-done | bytes 131104 | tf_op jit(solution)/shard_map/all_to_all | solution.py:438
  161.2 1.5 collective-permute-start.16
  165.5 2.2 copy-done.5
  167.6 9.1 %shard_map.189 = bf16[512,256]{1,0:T(8,128)(2,1)S(1)} custom-call(s32[6]{0:T(128)S(1)} %stack.95.at_ref, bf16[4,512,1024]{2,1,0:T(8,128)(2,1)S(1)} %bitcast.90, s32[1,512]{1,0:T(1,128)S(1)} %reshape.223.live_ref, bf16[1024,768]{1,0:T(8,128)(2,1)S(1)} %bitcast.87, bf16[1024,768]{1,0:T(8,128)(2,1)} %collective-permute-done.5.refs_1_, ...), custom_call_target="tpu_custom_call" | custom-call | flops 1000 | bytes 1000 | tf_op jit(solution)/shard_map/pallas_call | solution.py:55
  176.7 1.7 collective-permute-start.14
  178.4 2.2 copy-done.4
  180.6 9.1 %shard_map.188 = bf16[512,256]{1,0:T(8,128)(2,1)S(1)} custom-call(s32[6]{0:T(128)S(1)} %stack.95.at_ref, bf16[4,512,1024]{2,1,0:T(8,128)(2,1)S(1)} %bitcast.89, s32[1,512]{1,0:T(1,128)S(1)} %reshape.221.live_ref, bf16[1024,768]{1,0:T(8,128)(2,1)S(1)} %bitcast.88, bf16[1024,768]{1,0:T(8,128)(2,1)} %collective-permute-done.5.refs_1_, ...), custom_call_target="tpu_custom_call" | custom-call | flops 1000 | bytes 1000 | tf_op jit(solution)/shard_map/pallas_call | solution.py:55
  197.0 26.2 %all_to_all.34 = bf16[8,8,512]{2,1,0:T(8,128)(2,1)S(1)} all-to-all(bf16[8,8,512]{2,1,0:T(8,128)(2,1)S(1)} %broadcast_in_dim.41), channel_id=1, replica_groups=mesh['dp'=8,'mp'=4] {'dp'}, dimensions={0} | all-to-all | bytes 131072 | tf_op jit(solution)/shard_map/all_to_all | solution.py:438
  225.9 1.6 copy-done.12
  228.7 5.3 %shard_map.190 = (bf16[2,512,512]{2,1,0:T(8,128)(2,1)S(1)}, f32[512,1]{1,0:T(8,128)S(1)}) custom-call(s32[6]{0:T(128)S(1)} %stack.95.at_ref, bf16[4,2,512,256]{3,2,1,0:T(8,128)(2,1)S(1)} %bitcast.93, bf16[512,1024]{1,0:T(8,128)(2,1)} %bitcast.4.tokens_ref, bf16[256,1024]{1,0:T(8,128)(2,1)S(1)} %copy-done.14, ...), custom_call_target="tpu_custom_call" | custom-call | flops 1000 | bytes 1000 | tf_op jit(solution)/shard_map/pallas_call | solution.py:55
  235.9 1.5 collective-permute-start.24
  239.7 5.0 %collective-permute-done.23.refs_1_ = bf16[256,1024]{1,0:T(8,128)(2,1)S(1)} collective-permute-done((bf16[256,1024]{1,0:T(8,128)(2,1)S(1)}, bf16[256,1024]{1,0:T(8,128)(2,1)S(1)}, u32[]{:S(2)}, u32[]{:S(2)}) %collective-permute-start.23) | collective-permute-done | bytes 524320 | tf_op jit(solution)/shard_map/ppermute | solution.py:377
  244.7 1.8 collective-permute-start.25
  247.8 1.5 collective-permute-start.27
  250.6 2.1 copy.34
  253.5 1.4 fusion
  255.7 8.4 %all-to-all-start.3 = ((bf16[8,64,512]{2,1,0:T(8,128)(2,1)}), bf16[8,64,512]{2,1,0:T(8,128)(2,1)}, u32[]{:S(2)}, u32[]{:S(2)}) async-start(bf16[8,64,512]{2,1,0:T(8,128)(2,1)} %bitcast.100), calls=%async_computation.3 | async-start | bytes 1048576 | tf_op jit(solution)/shard_map/all_to_all | solution.py:438
  264.3 6.1 %psum.37 = f32[1,512]{1,0:T(1,128)S(1)} all-reduce(f32[1,512]{1,0:T(1,128)S(1)} %bitcast.106), channel_id=1, replica_groups=mesh['dp'=8,'mp'=4] {'mp'}, use_global_device_ids=true, to_apply=%region_3.4 | all-reduce | flops 512 | bytes 4096 | tf_op jit(solution)/shard_map/psum | solution.py:564
  271.6 7.1 %collective-permute-done.28 = bf16[256,1024]{1,0:T(8,128)(2,1)} collective-permute-done((bf16[256,1024]{1,0:T(8,128)(2,1)S(1)}, bf16[256,1024]{1,0:T(8,128)(2,1)}, u32[]{:S(2)}, u32[]{:S(2)}) %collective-permute-start.28) | collective-permute-done | bytes 524320 | tf_op jit(solution)/shard_map/ppermute | solution.py:377
  282.6 2.2 copy-done.9
  286.0 7.0 %shard_map.191 = bf16[2,128,256]{2,1,0:T(8,128)(2,1)S(1)} custom-call(s32[6]{0:T(128)S(1)} %stack.95.at_ref, bf16[4,2,512,512]{3,2,1,0:T(8,128)(2,1)S(1)} %bitcast.92, bf16[4,2,64,512]{3,2,1,0:T(8,128)(2,1)} %bitcast.42.mixed_ref, f32[512,1]{1,0:T(8,128)S(1)} %copy.37.column_ref, f32[1,512]{1,0:T(1,128)S(1)} %bitcast.99, s32[1,512]{1,0:T(1,128)S(1)} %reshape.221.live_ref, ...), custom_call_target="tpu_custom_call" | custom-call | flops 1000 | bytes 1000 | tf_op jit(solution)/shard_map/pallas_call | solution.py:55
  293.0 7.2 %all-gather.5 = bf16[8,128,256]{2,1,0:T(8,128)(2,1)S(1)} all-gather(bf16[2,128,256]{2,1,0:T(8,128)(2,1)S(1)} %shard_map.191), channel_id=7, replica_groups=mesh['dp'=8,'mp'=4] {'mp'}, dimensions={0}, use_global_device_ids=true | all-gather | bytes 655360 | tf_op jit(solution)/shard_map/all_gather | solution.py:435
  300.2 3.6 %shard_map.192 = (f32[128,1]{1,0:T(8,128)S(1)}, f32[128,1]{1,0:T(8,128)S(1)}) custom-call(s32[6]{0:T(128)S(1)} %stack.95.at_ref, bf16[4,2,128,256]{3,2,1,0:T(8,128)(2,1)S(1)} %bitcast.95, bf16[8,1024]{1,0:T(8,128)(2,1)S(1)} %bitcast.98, bf16[1,1024]{1,0:T(2,128)(2,1)S(1)} %broadcast_in_dim.42.weight_ref, bf16[256,1024]{1,0:T(8,128)(2,1)S(1)} %copy-done.16, ...), custom_call_target="tpu_custom_call" | custom-call | flops 1000 | bytes 1000 | tf_op jit(solution)/shard_map/pallas_call | solution.py:55
  304.1 6.4 %all-reduce = (f32[1,128]{1,0:T(1,128)S(1)}, f32[1,128]{1,0:T(1,128)S(1)}) all-reduce(f32[1,128]{1,0:T(1,128)S(1)} %bitcast.107, f32[1,128]{1,0:T(1,128)S(1)} %bitcast.108), channel_id=1, replica_groups=mesh['dp'=8,'mp'=4] {'mp'}, use_global_device_ids=true, to_apply=%region_4.5 | all-reduce | flops 256 | bytes 2048 | tf_op jit(solution)/shard_map/psum | solution.py:592
  311.3 9.4 %all_to_all.35 = f32[8,1,16]{2,1,0:T(1,128)S(1)} all-to-all(f32[8,1,16]{2,1,0:T(1,128)S(1)} %compare_select_fusion), channel_id=1, replica_groups=mesh['dp'=8,'mp'=4] {'dp'}, dimensions={0} | all-to-all | bytes 1024 | tf_op jit(solution)/shard_map/all_to_all | solution.py:438
  (182 shorter events, 51.7 us)
Async XLA Ops:
  7.2 84.8 %copy-start = (bf16[512,512]{1,0:T(8,128)(2,1)S(1)}, bf16[512,512]{1,0:T(8,128)(2,1)}, u32[]{:S(2)}) copy-start(bf16[512,512]{1,0:T(8,128)(2,1)} %param.28) | copy-start | bytes 1572868
  12.5 27.7 %collective-permute-start = (bf16[512,768]{1,0:T(8,128)(2,1)}, bf16[512,768]{1,0:T(8,128)(2,1)}, u32[]{:S(2)}, u32[]{:S(2)}) collective-permute-start(bf16[512,768]{1,0:T(8,128)(2,1)} %pad_maximum_fusion.5), channel_id=1, source_target_pairs={{0,4},{4,0},{8,12},{12,8},{16,20},{20,16},{24,28},{28,24},{1,5},{5... | collective-permute-start | bytes 2359304 | tf_op jit(solution)/shard_map/ppermute | solution.py:382
  15.4 15.0 %collective-permute-start.1 = (bf16[256,1024]{1,0:T(8,128)(2,1)S(1)}, bf16[256,1024]{1,0:T(8,128)(2,1)}, u32[]{:S(2)}, u32[]{:S(2)}) collective-permute-start(bf16[256,1024]{1,0:T(8,128)(2,1)S(1)} %copy-done.13), channel_id=1, source_target_pairs={{0,8},{4,12},{8,0},{12,4},{16,24},{20,28},{24,16},{28,20},{1,9},{5... | collective-permute-start | bytes 1572872 | tf_op jit(solution)/shard_map/ppermute | solution.py:377
  17.9 22.2 %collective-permute-start.2 = (bf16[256,1024]{1,0:T(8,128)(2,1)S(1)}, bf16[256,1024]{1,0:T(8,128)(2,1)}, u32[]{:S(2)}, u32[]{:S(2)}) collective-permute-start(bf16[256,1024]{1,0:T(8,128)(2,1)S(1)} %get-tuple-element.143.refs_0_), channel_id=1, source_target_pairs={{0,8},{4,12},{8,0},{12,4},{16,24},{20,28},{24,16},{28,20},{1,9},{5... | collective-permute-start | bytes 1572872 | tf_op jit(solution)/shard_map/ppermute | solution.py:377
  18.4 21.8 %collective-permute-start.3 = (bf16[256,1024]{1,0:T(8,128)(2,1)S(1)}, bf16[256,1024]{1,0:T(8,128)(2,1)}, u32[]{:S(2)}, u32[]{:S(2)}) collective-permute-start(bf16[256,1024]{1,0:T(8,128)(2,1)S(1)} %copy-done.13), channel_id=1, source_target_pairs={{8,16},{12,20},{16,8},{20,12},{9,17},{13,21},{17,9},{21,13},{10,18... | collective-permute-start | bytes 1572872 | tf_op jit(solution)/shard_map/ppermute | solution.py:377
  19.9 20.3 %collective-permute-start.4 = (bf16[256,1024]{1,0:T(8,128)(2,1)S(1)}, bf16[256,1024]{1,0:T(8,128)(2,1)}, u32[]{:S(2)}, u32[]{:S(2)}) collective-permute-start(bf16[256,1024]{1,0:T(8,128)(2,1)S(1)} %get-tuple-element.143.refs_0_), channel_id=1, source_target_pairs={{8,16},{12,20},{16,8},{20,12},{9,17},{13,21},{17,9},{21,13},{10,18... | collective-permute-start | bytes 1572872 | tf_op jit(solution)/shard_map/ppermute | solution.py:377
  23.1 26.6 %copy-start.40 = (s32[16]{0:T(128)S(1)}, s32[16]{0:T(128)}, u32[]{:S(2)}) copy-start(s32[16]{0:T(128)} %param.23) | copy-start | bytes 196
  23.2 28.1 %copy-start.27 = (bf16[1,8,1024]{2,1,0:T(8,128)(2,1)S(1)}, bf16[1,8,1024]{2,1,0:T(8,128)(2,1)}, u32[]{:S(2)}) copy-start(bf16[1,8,1024]{2,1,0:T(8,128)(2,1)} %param.25) | copy-start | bytes 49156
  40.1 23.4 %copy-start.15 = (bf16[256,1024]{1,0:T(8,128)(2,1)S(1)}, bf16[256,1024]{1,0:T(8,128)(2,1)}, u32[]{:S(2)}) copy-start(bf16[256,1024]{1,0:T(8,128)(2,1)} %refs_0_.2) | copy-start | bytes 1572868
  41.4 43.0 %collective-permute-start.5 = (bf16[1024,768]{1,0:T(8,128)(2,1)S(1)}, bf16[1024,768]{1,0:T(8,128)(2,1)}, u32[]{:S(2)}, u32[]{:S(2)}) collective-permute-start(bf16[1024,768]{1,0:T(8,128)(2,1)S(1)} %bitcast.85), channel_id=1, source_target_pairs={{0,8},{4,12},{8,0},{12,4},{16,24},{20,28},{24,16},{28,20},{1,9},{5... | collective-permute-start | bytes 4718600 | tf_op jit(solution)/shard_map/ppermute | solution.py:377
  47.3 37.1 %collective-permute-start.6 = (bf16[1024,768]{1,0:T(8,128)(2,1)S(1)}, bf16[1024,768]{1,0:T(8,128)(2,1)}, u32[]{:S(2)}, u32[]{:S(2)}) collective-permute-start(bf16[1024,768]{1,0:T(8,128)(2,1)S(1)} %bitcast.86), channel_id=1, source_target_pairs={{8,16},{12,20},{16,8},{20,12},{9,17},{13,21},{17,9},{21,13},{10,18... | collective-permute-start | bytes 4718600 | tf_op jit(solution)/shard_map/ppermute | solution.py:377
  49.2 35.3 %collective-permute-start.7 = (bf16[512,1024]{1,0:T(8,128)(2,1)}, bf16[512,1024]{1,0:T(8,128)(2,1)}, u32[]{:S(2)}, u32[]{:S(2)}) collective-permute-start(bf16[512,1024]{1,0:T(8,128)(2,1)} %bitcast.4.tokens_ref), channel_id=1, source_target_pairs={{0,4},{4,0},{8,12},{12,8},{16,20},{20,16},{24,28},{28,24},{1,5},{5... | collective-permute-start | bytes 3145736 | tf_op jit(solution)/shard_map/ppermute | solution.py:382
  49.7 22.7 %collective-permute-start.8 = (s32[16]{0:T(128)S(1)}, s32[16]{0:T(128)S(1)}, u32[]{:S(2)}, u32[]{:S(2)}) collective-permute-start(s32[16]{0:T(128)S(1)} %copy-done.40), channel_id=1, source_target_pairs={{0,4},{4,0},{8,12},{12,8},{16,20},{20,16},{24,28},{28,24},{1,5},{5... | collective-permute-start | bytes 200 | tf_op jit(solution)/shard_map/ppermute | solution.py:382
  56.9 27.5 %all-to-all-start = ((bf16[8,8,512]{2,1,0:T(8,128)(2,1)}), bf16[8,8,512]{2,1,0:T(8,128)(2,1)S(1)}, u32[]{:S(2)}, u32[]{:S(2)}) async-start(bf16[8,8,512]{2,1,0:T(8,128)(2,1)} %bitcast.17), calls=%async_computation | async-start | bytes 131072 | tf_op jit(solution)/shard_map/all_to_all | solution.py:438
  60.7 104.8 %all-gather.13.cloned.1.call-start = ((), (), s32[]{:S(2)}) async-start(), calls=%async_computation.6 | async-start | bytes 5242880 | tf_op jit(solution)/shard_map/all_gather | solution.py:435
  66.1 25.7 %copy-start.38 = (bf16[1024]{0:T(1024)(128)(2,1)S(1)}, bf16[1024]{0:T(1024)(128)(2,1)}, u32[]{:S(2)}) copy-start(bf16[1024]{0:T(1024)(128)(2,1)} %param.31) | copy-start | bytes 6148
  66.2 25.8 %copy-start.26 = (bf16[16,4096]{1,0:T(8,128)(2,1)S(1)}, bf16[16,4096]{1,0:T(8,128)(2,1)}, u32[]{:S(2)}) copy-start(bf16[16,4096]{1,0:T(8,128)(2,1)} %hidden_ref.1) | copy-start | bytes 393220
  84.5 93.9 %all-gather.11.cloned.1.call-start = ((), (), s32[]{:S(2)}) async-start(), calls=%async_computation.5 | async-start | bytes 5242880 | tf_op jit(solution)/shard_map/all_gather | solution.py:435
  85.2 76.0 %collective-permute-start.9 = (bf16[1024,768]{1,0:T(8,128)(2,1)}, bf16[1024,768]{1,0:T(8,128)(2,1)}, u32[]{:S(2)}, u32[]{:S(2)}) collective-permute-start(bf16[1024,768]{1,0:T(8,128)(2,1)} %collective-permute-done.6.refs_2_), channel_id=1, source_target_pairs={{8,0},{12,4},{16,24},{20,28},{9,1},{13,5},{17,25},{21,29},{10,2},{... | collective-permute-start | bytes 4718600 | tf_op jit(solution)/shard_map/ppermute | solution.py:377
  86.5 74.7 %collective-permute-start.10 = (bf16[1024,768]{1,0:T(8,128)(2,1)}, bf16[1024,768]{1,0:T(8,128)(2,1)}, u32[]{:S(2)}, u32[]{:S(2)}) collective-permute-start(bf16[1024,768]{1,0:T(8,128)(2,1)} %collective-permute-done.5.refs_1_), channel_id=1, source_target_pairs={{8,16},{12,20},{16,8},{20,12},{9,17},{13,21},{17,9},{21,13},{10,18... | collective-permute-start | bytes 4718600 | tf_op jit(solution)/shard_map/ppermute | solution.py:377
  88.3 72.9 %collective-permute-start.11 = (bf16[1024,768]{1,0:T(8,128)(2,1)}, bf16[1024,768]{1,0:T(8,128)(2,1)}, u32[]{:S(2)}, u32[]{:S(2)}) collective-permute-start(bf16[1024,768]{1,0:T(8,128)(2,1)} %collective-permute-done.5.refs_1_), channel_id=1, source_target_pairs={{8,24},{12,28},{16,0},{20,4},{9,25},{13,29},{17,1},{21,5},{10,26},... | collective-permute-start | bytes 4718600 | tf_op jit(solution)/shard_map/ppermute | solution.py:377
  89.6 71.6 %collective-permute-start.12 = (bf16[3,256,1024]{2,1,0:T(8,128)(2,1)}, bf16[3,256,1024]{2,1,0:T(8,128)(2,1)}, u32[]{:S(2)}, u32[]{:S(2)}) collective-permute-start(bf16[3,256,1024]{2,1,0:T(8,128)(2,1)} %pad_maximum_fusion), channel_id=1, source_target_pairs={{0,4},{4,0},{8,12},{12,8},{16,20},{20,16},{24,28},{28,24},{1,5},{5... | collective-permute-start | bytes 4718600 | tf_op jit(solution)/shard_map/ppermute | solution.py:382
  91.1 70.1 %collective-permute-start.13 = (bf16[2,256,1024]{2,1,0:T(8,128)(2,1)S(1)}, bf16[2,256,1024]{2,1,0:T(8,128)(2,1)}, u32[]{:S(2)}, u32[]{:S(2)}) collective-permute-start(bf16[2,256,1024]{2,1,0:T(8,128)(2,1)S(1)} %pad_maximum_fusion.1.refs_1_), channel_id=1, source_target_pairs={{0,4},{4,0},{8,12},{12,8},{16,20},{20,16},{24,28},{28,24},{1,5},{5... | collective-permute-start | bytes 3145736 | tf_op jit(solution)/shard_map/ppermute | solution.py:382
  92.9 68.3 %all-to-all-start.1 = ((f32[8,8,512]{2,1,0:T(8,128)}), f32[8,8,512]{2,1,0:T(8,128)S(1)}, u32[]{:S(2)}, u32[]{:S(2)}) async-start(f32[8,8,512]{2,1,0:T(8,128)} %fusion.2), calls=%async_computation.1 | async-start | bytes 262144 | tf_op jit(solution)/shard_map/all_to_all | solution.py:438
  101.6 124.3 %all-gather.15.cloned.1.call-start = ((), (), s32[]{:S(2)}) async-start(), calls=%async_computation.7 | async-start | bytes 2621440 | tf_op jit(solution)/shard_map/all_gather | solution.py:435
  161.2 29.3 %collective-permute-start.16 = (bf16[256,1024]{1,0:T(8,128)(2,1)}, bf16[256,1024]{1,0:T(8,128)(2,1)}, u32[]{:S(2)}, u32[]{:S(2)}) collective-permute-start(bf16[256,1024]{1,0:T(8,128)(2,1)} %collective-permute-done.1), channel_id=1, source_target_pairs={{8,16},{12,20},{16,8},{20,12},{9,17},{13,21},{17,9},{21,13},{10,18... | collective-permute-start | bytes 1572872 | tf_op jit(solution)/shard_map/ppermute | solution.py:377
  162.7 27.8 %collective-permute-start.17 = (bf16[256,1024]{1,0:T(8,128)(2,1)}, bf16[256,1024]{1,0:T(8,128)(2,1)}, u32[]{:S(2)}, u32[]{:S(2)}) collective-permute-start(bf16[256,1024]{1,0:T(8,128)(2,1)} %collective-permute-done.1), channel_id=1, source_target_pairs={{8,24},{12,28},{16,0},{20,4},{9,25},{13,29},{17,1},{21,5},{10,26},... | collective-permute-start | bytes 1572872 | tf_op jit(solution)/shard_map/ppermute | solution.py:377
  164.0 26.5 %collective-permute-start.15 = (bf16[256,1024]{1,0:T(8,128)(2,1)}, bf16[256,1024]{1,0:T(8,128)(2,1)}, u32[]{:S(2)}, u32[]{:S(2)}) collective-permute-start(bf16[256,1024]{1,0:T(8,128)(2,1)} %collective-permute-done.3), channel_id=1, source_target_pairs={{8,0},{12,4},{16,24},{20,28},{9,1},{13,5},{17,25},{21,29},{10,2},{... | collective-permute-start | bytes 1572872 | tf_op jit(solution)/shard_map/ppermute | solution.py:377
  176.7 13.0 %collective-permute-start.14 = (bf16[512,256]{1,0:T(8,128)(2,1)S(1)}, bf16[512,256]{1,0:T(8,128)(2,1)S(1)}, u32[]{:S(2)}, u32[]{:S(2)}) collective-permute-start(bf16[512,256]{1,0:T(8,128)(2,1)S(1)} %shard_map.189), channel_id=1, source_target_pairs={{0,4},{4,0},{8,12},{12,8},{16,20},{20,16},{24,28},{28,24},{1,5},{5... | collective-permute-start | bytes 786440 | tf_op jit(solution)/shard_map/ppermute | solution.py:382
  190.6 92.0 %all-gather.17.cloned.1.call-start = ((), (), s32[]{:S(2)}) async-start(), calls=%async_computation.8 | async-start | bytes 5242880 | tf_op jit(solution)/shard_map/all_gather | solution.py:435
  193.1 32.8 %copy-start.14 = (bf16[256,1024]{1,0:T(8,128)(2,1)S(1)}, bf16[256,1024]{1,0:T(8,128)(2,1)}, u32[]{:S(2)}) copy-start(bf16[256,1024]{1,0:T(8,128)(2,1)} %refs_0_.1) | copy-start | bytes 1572868
  193.2 31.7 %collective-permute-start.18 = (bf16[2,256,1024]{2,1,0:T(8,128)(2,1)S(1)}, bf16[2,256,1024]{2,1,0:T(8,128)(2,1)S(1)}, u32[]{:S(2)}, u32[]{:S(2)}) collective-permute-start(bf16[2,256,1024]{2,1,0:T(8,128)(2,1)S(1)} %pad_maximum_fusion.2.refs_2_), channel_id=1, source_target_pairs={{0,4},{4,0},{8,12},{12,8},{16,20},{20,16},{24,28},{28,24},{1,5},{5... | collective-permute-start | bytes 3145736 | tf_op jit(solution)/shard_map/ppermute | solution.py:382
  193.7 29.5 %collective-permute-start.19 = (bf16[256,1024]{1,0:T(8,128)(2,1)}, bf16[256,1024]{1,0:T(8,128)(2,1)S(1)}, u32[]{:S(2)}, u32[]{:S(2)}) collective-permute-start(bf16[256,1024]{1,0:T(8,128)(2,1)} %collective-permute-done.4), channel_id=1, source_target_pairs={{8,0},{12,4},{16,24},{20,28},{9,1},{13,5},{17,25},{21,29},{10,2},{... | collective-permute-start | bytes 1572872 | tf_op jit(solution)/shard_map/ppermute | solution.py:377
  195.0 28.2 %collective-permute-start.20 = (bf16[256,1024]{1,0:T(8,128)(2,1)}, bf16[256,1024]{1,0:T(8,128)(2,1)S(1)}, u32[]{:S(2)}, u32[]{:S(2)}) collective-permute-start(bf16[256,1024]{1,0:T(8,128)(2,1)} %collective-permute-done.2), channel_id=1, source_target_pairs={{8,16},{12,20},{16,8},{20,12},{9,17},{13,21},{17,9},{21,13},{10,18... | collective-permute-start | bytes 1572872 | tf_op jit(solution)/shard_map/ppermute | solution.py:377
  195.7 28.4 %collective-permute-start.21 = (bf16[256,1024]{1,0:T(8,128)(2,1)}, bf16[256,1024]{1,0:T(8,128)(2,1)S(1)}, u32[]{:S(2)}, u32[]{:S(2)}) collective-permute-start(bf16[256,1024]{1,0:T(8,128)(2,1)} %collective-permute-done.2), channel_id=1, source_target_pairs={{8,24},{12,28},{16,0},{20,4},{9,25},{13,29},{17,1},{21,5},{10,26},... | collective-permute-start | bytes 1572872 | tf_op jit(solution)/shard_map/ppermute | solution.py:377
  235.1 9.6 %collective-permute-start.23 = (bf16[256,1024]{1,0:T(8,128)(2,1)S(1)}, bf16[256,1024]{1,0:T(8,128)(2,1)S(1)}, u32[]{:S(2)}, u32[]{:S(2)}) collective-permute-start(bf16[256,1024]{1,0:T(8,128)(2,1)S(1)} %copy-done.16), channel_id=1, source_target_pairs={{0,8},{4,12},{8,0},{12,4},{16,24},{20,28},{24,16},{28,20},{1,9},{5... | collective-permute-start | bytes 1572872 | tf_op jit(solution)/shard_map/ppermute | solution.py:377
  235.9 8.8 %collective-permute-start.24 = (bf16[256,1024]{1,0:T(8,128)(2,1)S(1)}, bf16[256,1024]{1,0:T(8,128)(2,1)}, u32[]{:S(2)}, u32[]{:S(2)}) collective-permute-start(bf16[256,1024]{1,0:T(8,128)(2,1)S(1)} %copy-done.16), channel_id=1, source_target_pairs={{8,16},{12,20},{16,8},{20,12},{9,17},{13,21},{17,9},{21,13},{10,18... | collective-permute-start | bytes 1572872 | tf_op jit(solution)/shard_map/ppermute | solution.py:377
  238.7 17.0 %copy-start.10 = (bf16[2,256,1024]{2,1,0:T(8,128)(2,1)}, bf16[2,256,1024]{2,1,0:T(8,128)(2,1)S(1)}, u32[]{:S(2)}) copy-start(bf16[2,256,1024]{2,1,0:T(8,128)(2,1)S(1)} %pad_maximum_fusion.3.refs_2_) | copy-start | bytes 3145732
  238.7 31.7 %collective-permute-start.22 = (bf16[2,256,1024]{2,1,0:T(8,128)(2,1)S(1)}, bf16[2,256,1024]{2,1,0:T(8,128)(2,1)}, u32[]{:S(2)}, u32[]{:S(2)}) collective-permute-start(bf16[2,256,1024]{2,1,0:T(8,128)(2,1)S(1)} %pad_maximum_fusion.3.refs_2_), channel_id=1, source_target_pairs={{0,4},{4,0},{8,12},{12,8},{16,20},{20,16},{24,28},{28,24},{1,5},{5... | collective-permute-start | bytes 3145736 | tf_op jit(solution)/shard_map/ppermute | solution.py:382
  244.7 26.9 %collective-permute-start.25 = (bf16[256,1024]{1,0:T(8,128)(2,1)S(1)}, bf16[256,1024]{1,0:T(8,128)(2,1)}, u32[]{:S(2)}, u32[]{:S(2)}) collective-permute-start(bf16[256,1024]{1,0:T(8,128)(2,1)S(1)} %collective-permute-done.23.refs_1_), channel_id=1, source_target_pairs={{0,4},{4,0},{8,12},{12,8},{16,20},{20,16},{24,28},{28,24},{1,5},{5... | collective-permute-start | bytes 1572872 | tf_op jit(solution)/shard_map/ppermute | solution.py:382
  246.5 25.1 %collective-permute-start.26 = (bf16[256,1024]{1,0:T(8,128)(2,1)}, bf16[256,1024]{1,0:T(8,128)(2,1)}, u32[]{:S(2)}, u32[]{:S(2)}) collective-permute-start(bf16[256,1024]{1,0:T(8,128)(2,1)} %collective-permute-done.24), channel_id=1, source_target_pairs={{8,0},{12,4},{16,24},{20,28},{9,1},{13,5},{17,25},{21,29},{10,2},{... | collective-permute-start | bytes 1572872 | tf_op jit(solution)/shard_map/ppermute | solution.py:377
  247.8 23.8 %collective-permute-start.27 = (bf16[256,1024]{1,0:T(8,128)(2,1)S(1)}, bf16[256,1024]{1,0:T(8,128)(2,1)}, u32[]{:S(2)}, u32[]{:S(2)}) collective-permute-start(bf16[256,1024]{1,0:T(8,128)(2,1)S(1)} %collective-permute-done.23.refs_1_), channel_id=1, source_target_pairs={{8,16},{12,20},{16,8},{20,12},{9,17},{13,21},{17,9},{21,13},{10,18... | collective-permute-start | bytes 1572872 | tf_op jit(solution)/shard_map/ppermute | solution.py:377
  249.3 29.4 %collective-permute-start.28 = (bf16[256,1024]{1,0:T(8,128)(2,1)S(1)}, bf16[256,1024]{1,0:T(8,128)(2,1)}, u32[]{:S(2)}, u32[]{:S(2)}) collective-permute-start(bf16[256,1024]{1,0:T(8,128)(2,1)S(1)} %collective-permute-done.23.refs_1_), channel_id=1, source_target_pairs={{8,24},{12,28},{16,0},{20,4},{9,25},{13,29},{17,1},{21,5},{10,26},... | collective-permute-start | bytes 1572872 | tf_op jit(solution)/shard_map/ppermute | solution.py:377
  255.7 26.9 %all-to-all-start.3 = ((bf16[8,64,512]{2,1,0:T(8,128)(2,1)}), bf16[8,64,512]{2,1,0:T(8,128)(2,1)}, u32[]{:S(2)}, u32[]{:S(2)}) async-start(bf16[8,64,512]{2,1,0:T(8,128)(2,1)} %bitcast.100), calls=%async_computation.3 | async-start | bytes 1048576 | tf_op jit(solution)/shard_map/all_to_all | solution.py:438
  281.1 19.1 %collective-permute-start.29 = (bf16[2,256,1024]{2,1,0:T(8,128)(2,1)S(1)}, bf16[2,256,1024]{2,1,0:T(8,128)(2,1)}, u32[]{:S(2)}, u32[]{:S(2)}) collective-permute-start(bf16[2,256,1024]{2,1,0:T(8,128)(2,1)S(1)} %pad_maximum_fusion.4.refs_2_), channel_id=1, source_target_pairs={{0,4},{4,0},{8,12},{12,8},{16,20},{20,16},{24,28},{28,24},{1,5},{5... | collective-permute-start | bytes 3145736 | tf_op jit(solution)/shard_map/ppermute | solution.py:382
  286.0 14.2 %copy-start.25 = (bf16[256,1024]{1,0:T(8,128)(2,1)S(1)}, bf16[256,1024]{1,0:T(8,128)(2,1)}, u32[]{:S(2)}) copy-start(bf16[256,1024]{1,0:T(8,128)(2,1)} %copy-done.24) | copy-start | bytes 1572868
  300.2 21.0 %copy-start.1 = (bf16[512,512]{1,0:T(8,128)(2,1)S(1)}, bf16[512,512]{1,0:T(8,128)(2,1)}, u32[]{:S(2)}) copy-start(bf16[512,512]{1,0:T(8,128)(2,1)} %param.28) | copy-start | bytes 1572868
  300.2 11.1 %copy-start.41 = (s32[16]{0:T(128)S(1)}, s32[16]{0:T(128)}, u32[]{:S(2)}) copy-start(s32[16]{0:T(128)} %param.33) | copy-start | bytes 196
  (31 other events, 103.0 us)
Sparse Core Ops, SparseCore 0:
  84.6 34.8 all-gather.12
  121.1 34.4 all-gather.10
  190.7 24.6 all-gather.14
  235.2 33.0 all-gather.16
